TPU v7x, 32 devices: a whole 2x2x4 slice. The times are simulated.
32 devices in a mesh: wide: 16 (over z, y, core), tensor: 2 (over x).
Axes of the slice: x: 2, y: 2, z: 4, core: 2. Of those that a mesh axis runs over, the one named last changes fastest.
Arguments:
- block_in: bfloat16 [2, 2048, 2560], P(None, 'wide'), may hold values from -6 to 6
- segment_ids: int32 [2, 2048], P(None, 'wide'), may hold values from 0 to 6, as said below
- cotangent: bfloat16 [2, 2048, 2560], P(None, 'wide'), may hold values from -6 to 6
- first_gain: bfloat16 [2560], P('wide'), may hold values from 0.5 to 1.5
- gelu_weight: bfloat16 [2560, 10, 256], P('wide', 'tensor'), may hold values from -0.125 to 0.125
- gelu_bias: bfloat16 [10, 256], P('tensor', 'wide'), may hold values from -3 to 3
- input_weight: bfloat16 [2560, 10, 256], P('wide', 'tensor'), may hold values from -0.125 to 0.125
- input_bias: bfloat16 [10, 256], P('tensor', 'wide'), may hold values from -3 to 3
- conv_weight: bfloat16 [4, 10, 256], P(None, 'tensor', 'wide'), may hold values from -3 to 3
- conv_bias: bfloat16 [10, 256], P('tensor', 'wide'), may hold values from -2 to 2
- inlet_weight: bfloat16 [10, 256, 256], P('tensor', 'wide'), may hold values from -0.375 to 0.375
- inlet_bias: bfloat16 [10, 256], P('tensor', 'wide'), may hold values from -3 to 3
- forget_weight: bfloat16 [10, 256, 256], P('tensor', 'wide'), may hold values from -0.375 to 0.375
- forget_bias: bfloat16 [10, 256], P('tensor', 'wide'), may hold values from -3 to 3
- decay_rate: bfloat16 [10, 256], P('tensor', 'wide'), may hold values from -11.5 to -4
- out_weight: bfloat16 [10, 256, 2560], P('tensor', None, 'wide'), may hold values from -0.25 to 0.25
- out_bias: bfloat16 [2560], P('wide'), may hold values from -3 to 3
- second_gain: bfloat16 [2560], P('wide'), may hold values from 0.5 to 1.5
- mlp_gate: bfloat16 [2560, 7680], P('wide', 'tensor'), may hold values from -0.125 to 0.125
- mlp_up: bfloat16 [2560, 7680], P('wide', 'tensor'), may hold values from -0.125 to 0.125
- mlp_down: bfloat16 [7680, 2560], P('tensor', 'wide'), may hold values from -0.125 to 0.125
Outputs:
- block_out: bfloat16 [2, 2048, 2560], P(None, 'wide')
- input_grad: float32 [2, 2048, 2560], P(None, 'wide')
- first_gain_grad: float32 [2560], P('wide')
- gelu_weight_grad: float32 [2560, 10, 256], P('wide', 'tensor')
- gelu_bias_grad: float32 [10, 256], P('tensor', 'wide')
- input_weight_grad: float32 [2560, 10, 256], P('wide', 'tensor')
- input_bias_grad: float32 [10, 256], P('tensor', 'wide')
- conv_weight_grad: float32 [4, 10, 256], P(None, 'tensor', 'wide')
- conv_bias_grad: float32 [10, 256], P('tensor', 'wide')
- inlet_weight_grad: float32 [10, 256, 256], P('tensor', 'wide')
- inlet_bias_grad: float32 [10, 256], P('tensor', 'wide')
- forget_weight_grad: float32 [10, 256, 256], P('tensor', 'wide')
- forget_bias_grad: float32 [10, 256], P('tensor', 'wide')
- decay_rate_grad: float32 [10, 256], P('tensor', 'wide')
- out_weight_grad: float32 [10, 256, 2560], P('tensor', None, 'wide')
- out_bias_grad: float32 [2560], P('wide')
- second_gain_grad: float32 [2560], P('wide')
- mlp_gate_grad: float32 [2560, 7680], P('wide', 'tensor')
- mlp_up_grad: float32 [2560, 7680], P('wide', 'tensor')
- mlp_down_grad: float32 [7680, 2560], P('tensor', 'wide')
Inputs may be any that keep to these rules, and one draw needn't show every extreme that they name: `segment_ids`: along each sequence the ids start at 0 and rise by one at each of exactly 6 document starts. In one sequence, drawn from the seed, all starts lie within its first 128 or its last 128 tokens.
All inputs are finite; a program needn't handle non-finite values.
Results may differ from a plain program's by a relative error of at most 0.012.
Values may be sent and summed in bfloat16 or wider, within the bound.
A program may use at most 384 MiB of HBM per device.

v0:
```python
import jax
import jax.numpy as jnp
from jax import lax
from jax.sharding import PartitionSpec as P

CONV = 4


def shifted(shard, axis, by):
    size = lax.axis_size(axis)
    pairs = [(i, i + by) for i in range(size) if 0 <= i + by < size]
    return lax.ppermute(shard, axis, pairs)


def prefix(part, axis, combine, identity, reverse):
    count = lax.axis_size(axis)
    place = lax.axis_index(axis)
    ahead = count - 1 - place if reverse else place
    gathered = jax.tree.map(lambda a: lax.all_gather(a, axis), part)
    state = jax.tree.map(lambda a, e: jnp.zeros_like(a) + jnp.asarray(e, a.dtype), part, identity)

    def one(lap, state):
        source = count - 1 - lap if reverse else lap
        return combine(
            state, jax.tree.map(lambda a: lax.dynamic_index_in_dim(a, source, 0, False), gathered)
        )

    return lax.fori_loop(0, ahead, one, state)


def rms_norm(values, gain):
    scale = lax.rsqrt(jnp.mean(values * values, axis=-1, keepdims=True) + 1e-06)
    return values * scale * gain


def linear_combine(earlier, later):
    return (later[0] * earlier[0], later[0] * earlier[1] + later[1])


def causal_conv(extended, marks, weight, bias):
    margin = weight.shape[0] - 1
    tok_count = extended.shape[1] - margin
    current = marks[:, margin:]
    total = bias + weight[0] * extended[:, margin:]
    for offset in range(1, margin + 1):
        moved = extended[:, margin - offset : margin - offset + tok_count]
        same = (marks[:, margin - offset : margin - offset + tok_count] == current)[..., None]
        total = total + jnp.where(same, weight[offset] * moved, 0.0)
    return total


def lru_terms(inlet_pre, forget_pre, conv_vals, rate, starts):
    inlet = jax.nn.sigmoid(inlet_pre)
    forget = jax.nn.sigmoid(forget_pre)
    log_decay = -8.0 * forget * jax.nn.softplus(rate)
    decay = jnp.where(starts, 0.0, jnp.exp(log_decay))
    scaler = jnp.where(starts, 1.0, jnp.sqrt(-jnp.expm1(2.0 * log_decay)))
    return (decay, scaler * inlet * conv_vals)


def gelu_product(gate_pre, up_pre):
    return jax.nn.gelu(gate_pre) * up_pre


def local(
    block_in,
    segment_ids,
    cotangent,
    first_gain,
    gelu_weight,
    gelu_bias,
    input_weight,
    input_bias,
    conv_weight,
    conv_bias,
    inlet_weight,
    inlet_bias,
    forget_weight,
    forget_bias,
    decay_rate,
    out_weight,
    out_bias,
    second_gain,
    mlp_gate,
    mlp_up,
    mlp_down,
):
    seq_count, tok_count, width = block_in.shape
    head_count = gelu_weight.shape[1]
    block_size = gelu_weight.shape[2]
    channels = head_count * block_size
    margin = CONV - 1
    rows_all = seq_count * tok_count
    recurrent = (
        lax.all_gather(first_gain, "wide", axis=0, tiled=True),
        lax.all_gather(gelu_weight, "wide", axis=0, tiled=True),
        lax.all_gather(gelu_bias, "wide", axis=1, tiled=True),
        lax.all_gather(input_weight, "wide", axis=0, tiled=True),
        lax.all_gather(input_bias, "wide", axis=1, tiled=True),
        lax.all_gather(conv_weight, "wide", axis=2, tiled=True),
        lax.all_gather(conv_bias, "wide", axis=1, tiled=True),
        lax.all_gather(inlet_weight, "wide", axis=1, tiled=True),
        lax.all_gather(inlet_bias, "wide", axis=1, tiled=True),
        lax.all_gather(forget_weight, "wide", axis=1, tiled=True),
        lax.all_gather(forget_bias, "wide", axis=1, tiled=True),
        lax.all_gather(decay_rate, "wide", axis=1, tiled=True),
        lax.all_gather(out_weight, "wide", axis=2, tiled=True),
        lax.all_gather(out_bias, "wide", axis=0, tiled=True),
    )
    feeding = (
        lax.all_gather(second_gain, "wide", axis=0, tiled=True),
        lax.all_gather(mlp_gate, "wide", axis=0, tiled=True),
        lax.all_gather(mlp_up, "wide", axis=0, tiled=True),
        lax.all_gather(mlp_down, "wide", axis=1, tiled=True),
    )
    (
        gain_one,
        gelu_full,
        gelu_shift,
        input_full,
        input_shift,
        conv_full,
        conv_shift,
        inlet_full,
        inlet_shift,
        forget_full,
        forget_shift,
        rate_full,
        out_full,
        out_shift,
    ) = recurrent
    gain_two, gate_full, up_full, down_full = feeding
    inputs = block_in.astype(jnp.float32).reshape(rows_all, width)
    gain_first = gain_one.astype(jnp.float32)
    normed = rms_norm(inputs, gain_first).astype(jnp.bfloat16)
    gelu_pre = jnp.dot(
        normed, gelu_full.reshape(width, channels), preferred_element_type=jnp.float32
    ) + gelu_shift.astype(jnp.float32).reshape(channels)
    gelu_branch = jax.nn.gelu(gelu_pre)
    input_pre = jnp.dot(
        normed, input_full.reshape(width, channels), preferred_element_type=jnp.float32
    ) + input_shift.astype(jnp.float32).reshape(channels)
    input_branch = input_pre.astype(jnp.bfloat16).reshape(seq_count, tok_count, channels)
    marks = (segment_ids + 1).astype(jnp.bfloat16)
    rim_values, rim_marks = shifted(
        (input_branch[:, tok_count - margin :], marks[:, tok_count - margin :]), "wide", 1
    )
    extended = jnp.concatenate([rim_values, input_branch], axis=1).astype(jnp.float32)
    marks_ext = jnp.concatenate([rim_marks, marks], axis=1).astype(jnp.float32)
    conv_taps = conv_full.astype(jnp.float32).reshape(CONV, channels)
    conv_offset = conv_shift.astype(jnp.float32).reshape(channels)
    conv_out = causal_conv(extended, marks_ext, conv_taps, conv_offset)
    blocks = conv_out.astype(jnp.bfloat16).reshape(seq_count, tok_count, head_count, block_size)
    inlet_pre = jnp.einsum(
        "sthc,hcd->sthd", blocks, inlet_full, preferred_element_type=jnp.float32
    ) + inlet_shift.astype(jnp.float32)
    forget_pre = jnp.einsum(
        "sthc,hcd->sthd", blocks, forget_full, preferred_element_type=jnp.float32
    ) + forget_shift.astype(jnp.float32)
    starts = (marks_ext[:, margin:] != marks_ext[:, margin - 1 : margin - 1 + tok_count])[
        :, :, None, None
    ]
    blocks_wide = blocks.astype(jnp.float32)
    rate_wide = rate_full.astype(jnp.float32)
    decay, drive = lru_terms(inlet_pre, forget_pre, blocks_wide, rate_wide, starts)
    decay_cum, local_state = lax.associative_scan(linear_combine, (decay, drive), axis=1)
    unit = jnp.ones_like(decay[:, 0])
    empty = jnp.zeros_like(decay[:, 0])
    incoming = prefix(
        (decay_cum[:, -1], local_state[:, -1]), "wide", linear_combine, (unit, empty), False
    )
    state_in = incoming[1]
    state = local_state + decay_cum * state_in[:, None]
    gelu_grid = gelu_branch.reshape(seq_count, tok_count, head_count, block_size)
    mixed = (state * gelu_grid).astype(jnp.bfloat16).reshape(rows_all, channels)
    branch_part = jnp.dot(
        mixed, out_full.reshape(channels, width), preferred_element_type=jnp.float32
    )
    branch = lax.psum(branch_part, "tensor") + out_shift.astype(jnp.float32)
    resid = inputs + branch
    gain_second = gain_two.astype(jnp.float32)
    second = rms_norm(resid, gain_second).astype(jnp.bfloat16)
    gate_pre = jnp.dot(second, gate_full, preferred_element_type=jnp.float32)
    up_pre = jnp.dot(second, up_full, preferred_element_type=jnp.float32)
    hidden = gelu_product(gate_pre, up_pre).astype(jnp.bfloat16)
    feed_part = jnp.dot(hidden, down_full, preferred_element_type=jnp.float32)
    feed = lax.psum(feed_part.astype(jnp.bfloat16), "tensor").astype(jnp.float32)
    block_out = (resid + feed).astype(jnp.bfloat16).reshape(seq_count, tok_count, width)
    recurrent_back = (
        lax.all_gather(gelu_weight, "wide", axis=0, tiled=True),
        lax.all_gather(input_weight, "wide", axis=0, tiled=True),
        lax.all_gather(inlet_weight, "wide", axis=1, tiled=True),
        lax.all_gather(forget_weight, "wide", axis=1, tiled=True),
        lax.all_gather(out_weight, "wide", axis=2, tiled=True),
    )
    feeding_back = (
        lax.all_gather(mlp_gate, "wide", axis=0, tiled=True),
        lax.all_gather(mlp_up, "wide", axis=0, tiled=True),
        lax.all_gather(mlp_down, "wide", axis=1, tiled=True),
    )
    gelu_back, input_back, inlet_back, forget_back, out_back = recurrent_back
    gate_back, up_back, down_back = feeding_back
    grad_low = cotangent.reshape(rows_all, width)
    down_grad = jnp.einsum("tf,td->fd", hidden, grad_low, preferred_element_type=jnp.float32)
    hidden_grad = jnp.einsum("td,fd->tf", grad_low, down_back, preferred_element_type=jnp.float32)
    _, pull_feed = jax.vjp(gelu_product, gate_pre, up_pre)
    gate_pre_grad, up_pre_grad = pull_feed(hidden_grad)
    gate_low = gate_pre_grad.astype(jnp.bfloat16)
    up_low = up_pre_grad.astype(jnp.bfloat16)
    gate_grad = jnp.einsum("td,tf->df", second, gate_low, preferred_element_type=jnp.float32)
    up_grad = jnp.einsum("td,tf->df", second, up_low, preferred_element_type=jnp.float32)
    second_part = jnp.einsum(
        "tf,df->td", gate_low, gate_back, preferred_element_type=jnp.float32
    ) + jnp.einsum("tf,df->td", up_low, up_back, preferred_element_type=jnp.float32)
    second_grad = lax.psum(second_part, "tensor")
    _, pull_second = jax.vjp(rms_norm, resid, gain_second)
    resid_norm_grad, gain_two_grad = pull_second(second_grad)
    resid_grad = cotangent.astype(jnp.float32).reshape(rows_all, width) + resid_norm_grad
    feed_grads = (
        lax.psum_scatter(gain_two_grad, "wide", scatter_dimension=0, tiled=True),
        lax.psum_scatter(gate_grad, "wide", scatter_dimension=0, tiled=True),
        lax.psum_scatter(up_grad, "wide", scatter_dimension=0, tiled=True),
        lax.psum_scatter(down_grad, "wide", scatter_dimension=1, tiled=True),
    )
    branch_low = resid_grad.astype(jnp.bfloat16)
    out_shift_grad = jnp.sum(branch_low.astype(jnp.float32), axis=0)
    out_grad = jnp.einsum(
        "tc,td->cd", mixed, branch_low, preferred_element_type=jnp.float32
    ).reshape(head_count, block_size, width)
    mixed_grad = jnp.einsum(
        "td,cd->tc",
        branch_low,
        out_back.reshape(channels, width),
        preferred_element_type=jnp.float32,
    ).reshape(seq_count, tok_count, head_count, block_size)
    state_grad = mixed_grad * gelu_grid
    _, pull_gelu = jax.vjp(jax.nn.gelu, gelu_pre)
    (gelu_pre_grad,) = pull_gelu((mixed_grad * state).reshape(rows_all, channels))
    gelu_low = gelu_pre_grad.astype(jnp.bfloat16)
    next_decay = jnp.concatenate([decay[:, 1:], jnp.ones_like(decay[:, :1])], axis=1)
    tail_decay, local_carried = lax.associative_scan(
        linear_combine, (next_decay, state_grad), axis=1, reverse=True
    )
    head_decay = decay[:, 0]
    from_right = prefix(
        (head_decay * tail_decay[:, 0], head_decay * local_carried[:, 0]),
        "wide",
        linear_combine,
        (unit, empty),
        True,
    )
    carried = local_carried + tail_decay * from_right[1][:, None]
    prev_state = jnp.concatenate([state_in[:, None], state[:, :-1]], axis=1)

    def lru_local(inlet_arg, forget_arg, block_arg, rate_arg):
        return lru_terms(inlet_arg, forget_arg, block_arg, rate_arg, starts)

    _, pull_lru = jax.vjp(lru_local, inlet_pre, forget_pre, blocks_wide, rate_wide)
    inlet_grad, forget_grad, block_direct, rate_grad = pull_lru((carried * prev_state, carried))
    inlet_low = inlet_grad.astype(jnp.bfloat16)
    forget_low = forget_grad.astype(jnp.bfloat16)
    inlet_w_grad = jnp.einsum(
        "sthc,sthd->hcd", blocks, inlet_low, preferred_element_type=jnp.float32
    )
    inlet_b_grad = jnp.sum(inlet_low.astype(jnp.float32), axis=(0, 1))
    forget_w_grad = jnp.einsum(
        "sthc,sthd->hcd", blocks, forget_low, preferred_element_type=jnp.float32
    )
    forget_b_grad = jnp.sum(forget_low.astype(jnp.float32), axis=(0, 1))
    conv_grad = (
        block_direct
        + jnp.einsum("sthd,hcd->sthc", inlet_low, inlet_back, preferred_element_type=jnp.float32)
        + jnp.einsum("sthd,hcd->sthc", forget_low, forget_back, preferred_element_type=jnp.float32)
    )

    def conv_local(ext_arg, taps_arg, offset_arg):
        return causal_conv(ext_arg, marks_ext, taps_arg, offset_arg)

    _, pull_conv = jax.vjp(conv_local, extended, conv_taps, conv_offset)
    ext_grad, taps_grad, offset_grad = pull_conv(conv_grad.reshape(seq_count, tok_count, channels))
    rim_grad = shifted(ext_grad[:, :margin], "wide", -1)
    branch_input_grad = ext_grad[:, margin:] + jnp.concatenate(
        [jnp.zeros((seq_count, tok_count - margin, channels), jnp.float32), rim_grad], axis=1
    )
    input_low = branch_input_grad.astype(jnp.bfloat16).reshape(rows_all, channels)
    input_w_grad = jnp.einsum(
        "td,tc->dc", normed, input_low, preferred_element_type=jnp.float32
    ).reshape(width, head_count, block_size)
    input_b_grad = jnp.sum(input_low.astype(jnp.float32), axis=0).reshape(head_count, block_size)
    gelu_w_grad = jnp.einsum(
        "td,tc->dc", normed, gelu_low, preferred_element_type=jnp.float32
    ).reshape(width, head_count, block_size)
    gelu_b_grad = jnp.sum(gelu_low.astype(jnp.float32), axis=0).reshape(head_count, block_size)
    first_part = jnp.einsum(
        "tc,dc->td",
        input_low,
        input_back.reshape(width, channels),
        preferred_element_type=jnp.float32,
    ) + jnp.einsum(
        "tc,dc->td",
        gelu_low,
        gelu_back.reshape(width, channels),
        preferred_element_type=jnp.float32,
    )
    first_grad = lax.psum(first_part.astype(jnp.bfloat16), "tensor").astype(jnp.float32)
    _, pull_first = jax.vjp(rms_norm, inputs, gain_first)
    input_norm_grad, gain_one_grad = pull_first(first_grad)
    block_grad = (resid_grad + input_norm_grad).reshape(seq_count, tok_count, width)
    rec_grads = (
        lax.psum_scatter(gain_one_grad, "wide", scatter_dimension=0, tiled=True),
        lax.psum_scatter(gelu_w_grad, "wide", scatter_dimension=0, tiled=True),
        lax.psum_scatter(gelu_b_grad, "wide", scatter_dimension=1, tiled=True),
        lax.psum_scatter(input_w_grad, "wide", scatter_dimension=0, tiled=True),
        lax.psum_scatter(input_b_grad, "wide", scatter_dimension=1, tiled=True),
        lax.psum_scatter(
            taps_grad.reshape(CONV, head_count, block_size), "wide", scatter_dimension=2, tiled=True
        ),
        lax.psum_scatter(
            offset_grad.reshape(head_count, block_size), "wide", scatter_dimension=1, tiled=True
        ),
        lax.psum_scatter(inlet_w_grad, "wide", scatter_dimension=1, tiled=True),
        lax.psum_scatter(inlet_b_grad, "wide", scatter_dimension=1, tiled=True),
        lax.psum_scatter(forget_w_grad, "wide", scatter_dimension=1, tiled=True),
        lax.psum_scatter(forget_b_grad, "wide", scatter_dimension=1, tiled=True),
        lax.psum_scatter(rate_grad, "wide", scatter_dimension=1, tiled=True),
        lax.psum_scatter(out_grad, "wide", scatter_dimension=2, tiled=True),
        lax.psum_scatter(out_shift_grad, "wide", scatter_dimension=0, tiled=True),
    )
    return (
        block_out,
        block_grad,
        rec_grads[0],
        rec_grads[1],
        rec_grads[2],
        rec_grads[3],
        rec_grads[4],
        rec_grads[5],
        rec_grads[6],
        rec_grads[7],
        rec_grads[8],
        rec_grads[9],
        rec_grads[10],
        rec_grads[11],
        rec_grads[12],
        rec_grads[13],
        feed_grads[0],
        feed_grads[1],
        feed_grads[2],
        feed_grads[3],
    )


def solution(mesh):
    in_specs = (
        P(None, "wide", None),
        P(None, "wide"),
        P(None, "wide", None),
        P("wide"),
        P("wide", "tensor", None),
        P("tensor", "wide"),
        P("wide", "tensor", None),
        P("tensor", "wide"),
        P(None, "tensor", "wide"),
        P("tensor", "wide"),
        P("tensor", "wide", None),
        P("tensor", "wide"),
        P("tensor", "wide", None),
        P("tensor", "wide"),
        P("tensor", "wide"),
        P("tensor", None, "wide"),
        P("wide"),
        P("wide"),
        P("wide", "tensor"),
        P("wide", "tensor"),
        P("tensor", "wide"),
    )
    out_specs = (
        P(None, "wide", None),
        P(None, "wide", None),
        P("wide"),
        P("wide", "tensor", None),
        P("tensor", "wide"),
        P("wide", "tensor", None),
        P("tensor", "wide"),
        P(None, "tensor", "wide"),
        P("tensor", "wide"),
        P("tensor", "wide", None),
        P("tensor", "wide"),
        P("tensor", "wide", None),
        P("tensor", "wide"),
        P("tensor", "wide"),
        P("tensor", None, "wide"),
        P("wide"),
        P("wide"),
        P("wide", "tensor"),
        P("wide", "tensor"),
        P("tensor", "wide"),
    )
    return jax.shard_map(local, mesh=mesh, in_specs=in_specs, out_specs=out_specs, check_vma=False)
```

profile of v0, /device:TPU:27, one launch (start us, length us, event | category | flops | bytes accessed | tf_op | source)
XLA Modules:
  0.0 3471.1 jit_solution(13320943175260442800)
XLA Ops:
  14.0 16.0 all-gather.9
  32.1 55.8 %all-reduce.74 = (bf16[2560]{0:T(1024)(128)(2,1)S(1)}, bf16[2560]{0:T(1024)(128)(2,1)}, bf16[2560]{0:T(1024)(128)(2,1)}) all-reduce(bf16[2560]{0:T(1024)(128)(2,1)S(1)} %dynamic-update-slice, bf16[2560]{0:T(1024)(128)(2,1)S(1)} %dynamic-update-slice.1, ...), channel_id=1, replica_groups=mesh['wide'=16,'tensor'=2] {'wide'}, use_global_device_ids=true, to_apply=%add.67 | all-reduce | flops 7680 | bytes 30720
  88.0 21.6 all-gather.5
  109.8 19.9 all_gather.77
  130.5 18.5 all-gather.4
  149.1 18.3 all-gather.6
  167.5 18.5 all-gather.7
  186.0 18.4 all-gather.8
  204.9 21.2 all_gather.81
  226.1 21.5 all_gather.84
  248.3 9.7 copy.222
  267.6 9.5 copy.239
  277.1 6.4 multiply_multiply_fusion.5
  285.5 9.8 copy.244
  453.8 7.1 pad.226
  460.9 6.4 pad.210
  469.1 6.4 pad.209
  481.1 7.1 pad.225
  489.1 16.5 all-gather
  506.5 7.1 pad.212
  515.6 7.1 pad.211
  523.6 18.6 all-gather.1
  543.0 9.8 while.26
  559.4 6.5 fusion.88
  567.9 74.5 %all-reduce.80.cloned.1.call-done = f32[256,2560]{1,0:T(8,128)} async-done(((f32[256,2560]{1,0:T(8,128)}), f32[256,2560]{1,0:T(8,128)}) %all-reduce.80.cloned.1.call-update) | async-done | bytes 2621456 | tf_op jit(solution)/shard_map/psum | solution.py:179
  646.7 101.3 %all-gather.23.cloned.1.call-done = bf16[2560,3840]{1,0:T(8,128)(2,1)} async-done(((bf16[160,3840]{1,0:T(8,128)(2,1)}), bf16[2560,3840]{1,0:T(8,128)(2,1)}) %all-gather.23.cloned.1.call-update) | async-done | bytes 19660816 | tf_op jit(solution)/shard_map/all_gather | solution.py:112
  748.0 13.6 fusion.109
  761.6 90.6 %all-gather.25.cloned.1.call-done = bf16[2560,3840]{1,0:T(8,128)(2,1)} async-done(((bf16[160,3840]{1,0:T(8,128)(2,1)}), bf16[2560,3840]{1,0:T(8,128)(2,1)}) %all-gather.25.cloned.1.call-update) | async-done | bytes 19660816 | tf_op jit(solution)/shard_map/all_gather | solution.py:113
  852.2 13.6 fusion.110
  865.8 90.8 %all-gather.27.cloned.1.call-done = bf16[3840,2560]{0,1:T(8,128)(2,1)} async-done(((bf16[3840,160]{0,1:T(8,128)(2,1)}), bf16[3840,2560]{0,1:T(8,128)(2,1)}) %all-gather.27.cloned.1.call-update) | async-done | bytes 19660816 | tf_op jit(solution)/shard_map/all_gather | solution.py:114
  956.6 14.7 multiply_convert_fusion
  971.3 10.8 fusion.111
  982.1 12.1 convolution_add_fusion
  1013.6 53.7 %all-reduce.82.cloned.1.call-done = f32[256,2560]{1,0:T(8,128)} async-done(((f32[256,2560]{1,0:T(8,128)}), f32[256,2560]{1,0:T(8,128)}) %all-reduce.82.cloned.1.call-update) | async-done | bytes 2621456 | tf_op jit(solution)/shard_map/psum | solution.py:215
  1195.7 7.2 pad.254
  1206.8 10.8 rev.8
  1217.6 6.4 rev.9
  1224.0 17.8 all-gather.2
  1242.0 18.5 all-gather.3
  1281.4 10.7 convolution_convert_fusion
  1296.1 5.2 multiply_reduce_fusion.6
  1323.3 6.5 fusion.112
  1330.7 6.6 fusion.9
  1343.6 6.6 fusion.113
  1351.8 6.6 fusion.47
  1359.7 6.7 fusion.114
  1368.3 15.3 fusion.115
  1385.1 15.5 fusion.116
  1402.6 15.5 fusion.117
  1421.6 32.0 reduce-scatter.54.cloned.1.call-done
  1454.9 56.1 %reduce-scatter.56.cloned.1.call-done = f32[16,5]{1,0:T(8,128)} async-done(((f32[256,5]{1,0:T(8,128)}), f32[16,5]{1,0:T(8,128)}) %reduce-scatter.56.cloned.1.call-update) | async-done | bytes 336
  1512.4 56.3 %reduce-scatter.58.cloned.1.call-done = f32[16,5]{1,0:T(8,128)} async-done(((f32[256,5]{1,0:T(8,128)}), f32[16,5]{1,0:T(8,128)}) %reduce-scatter.58.cloned.1.call-update) | async-done | bytes 336
  1570.1 56.2 %reduce-scatter.50.cloned.1.call-done = f32[16,20]{1,0:T(8,128)} async-done(((f32[256,20]{1,0:T(8,128)}), f32[16,20]{1,0:T(8,128)}) %reduce-scatter.50.cloned.1.call-update) | async-done | bytes 1296
  1627.7 56.0 %reduce-scatter.48.cloned.1.call-done = f32[16,5]{1,0:T(8,128)} async-done(((f32[256,5]{1,0:T(8,128)}), f32[16,5]{1,0:T(8,128)}) %reduce-scatter.48.cloned.1.call-update) | async-done | bytes 336
  1685.0 77.2 %all-reduce.84.cloned.1.call-done = (bf16[256,2560]{1,0:T(8,128)(2,1)}, bf16[256,2560]{1,0:T(8,128)(2,1)}) async-done(((bf16[256,2560]{1,0:T(8,128)(2,1)}, bf16[256,2560]{1,0:T(8,128)(2,1)}), (bf16[256,2560]{1,0:T(8,128)(2,1)}, bf16[256,2560]{1,0:T(8,128)(2,1)})) %all-reduce.84.cloned.1.call-update) | async-done | bytes 2621456 | tf_op jit(solution)/shard_map/psum | solution.py:187
  1765.5 53.6 %all-reduce.73 = (f32[2560]{0:T(1024)S(1)}, f32[2560]{0:T(1024)S(1)}, f32[2560]{0:T(1024)S(1)}) all-reduce(f32[2560]{0:T(1024)S(1)} %get-tuple-element.216, f32[2560]{0:T(1024)S(1)} %copy-done.82, f32[2560]{0:T(1024)S(1)} %copy-done.81), channel_id=6, replica_groups=mesh['wide'=16,'tensor'=2] {'wide'}, use_global_device_ids=true, to_apply=%region_13.14.clone | all-reduce | flops 7680 | bytes 61440
  1821.1 5.4 fusion.15
  1826.6 58.4 %reduce-scatter.36.cloned.1.call-done = f32[5,16,256]{2,1,0:T(8,128)} async-done(((f32[5,256,256]{2,1,0:T(8,128)}), f32[5,16,256]{2,1,0:T(8,128)}) %reduce-scatter.36.cloned.1.call-update) | async-done | bytes 81936 | tf_op jit(solution)/shard_map/reduce_scatter | solution.py:323
  1885.0 143.8 %reduce-scatter.30.cloned.1.call-done = f32[160,5,256]{2,0,1:T(8,128)} async-done(((f32[2560,5,256]{2,0,1:T(8,128)}), f32[160,5,256]{2,0,1:T(8,128)}) %reduce-scatter.30.cloned.1.call-update) | async-done | bytes 819216 | tf_op jit(solution)/shard_map/reduce_scatter | solution.py:311
  2028.8 142.1 %reduce-scatter.38.cloned.1.call-done = f32[5,256,160]{1,2,0:T(8,128)} async-done(((f32[5,256,2560]{1,2,0:T(8,128)}), f32[5,256,160]{1,2,0:T(8,128)}) %reduce-scatter.38.cloned.1.call-update) | async-done | bytes 819216 | tf_op jit(solution)/shard_map/reduce_scatter | solution.py:326
  2170.9 142.7 %reduce-scatter.32.cloned.1.call-done = f32[160,5,256]{2,0,1:T(8,128)} async-done(((f32[2560,5,256]{2,0,1:T(8,128)}), f32[160,5,256]{2,0,1:T(8,128)}) %reduce-scatter.32.cloned.1.call-update) | async-done | bytes 819216 | tf_op jit(solution)/shard_map/reduce_scatter | solution.py:313
  2313.6 383.7 %reduce-scatter.40.cloned.1.call-done = f32[160,3840]{1,0:T(8,128)} async-done(((f32[2560,3840]{1,0:T(8,128)}), f32[160,3840]{1,0:T(8,128)}) %reduce-scatter.40.cloned.1.call-update) | async-done | bytes 2457616 | tf_op jit(solution)/shard_map/reduce_scatter | solution.py:221
  2697.2 383.8 %reduce-scatter.42.cloned.1.call-done = f32[160,3840]{1,0:T(8,128)} async-done(((f32[2560,3840]{1,0:T(8,128)}), f32[160,3840]{1,0:T(8,128)}) %reduce-scatter.42.cloned.1.call-update) | async-done | bytes 2457616 | tf_op jit(solution)/shard_map/reduce_scatter | solution.py:222
  3081.0 383.1 %reduce-scatter.44.cloned.1.call-done = f32[3840,160]{0,1:T(8,128)} async-done(((f32[3840,2560]{0,1:T(8,128)}), f32[3840,160]{0,1:T(8,128)}) %reduce-scatter.44.cloned.1.call-update) | async-done | bytes 2457616 | tf_op jit(solution)/shard_map/reduce_scatter | solution.py:223
  (665 shorter events, 444.6 us)
Async XLA Ops:
  7.2 80.8 %copy-start.116 = (bf16[5,16]{1,0:T(8,128)(2,1)S(1)}, bf16[5,16]{1,0:T(8,128)(2,1)}, u32[]{:S(2)}) copy-start(bf16[5,16]{1,0:T(8,128)(2,1)} %param.32) | copy-start | bytes 484
  7.2 102.4 %copy-start.109 = (bf16[4,5,16]{2,0,1:T(4,128)(2,1)S(1)}, bf16[4,5,16]{2,0,1:T(4,128)(2,1)}, u32[]{:S(2)}) copy-start(bf16[4,5,16]{2,0,1:T(4,128)(2,1)} %param.33) | copy-start | bytes 1924
  7.3 241.0 %all-gather.17.cloned.1.call-start = ((), (), s32[]{:S(2)}) async-start(), calls=%async_computation.15 | async-start | bytes 6963200 | tf_op jit(solution)/shard_map/all_gather | solution.py:98
  8.0 259.6 %all-gather.19.cloned.1.call-start = ((), (), s32[]{:S(2)}) async-start(), calls=%async_computation.16 | async-start | bytes 6963200 | tf_op jit(solution)/shard_map/all_gather | solution.py:96
  8.7 276.7 %all-gather.21.cloned.1.call-start = ((), (), s32[]{:S(2)}) async-start(), calls=%async_computation.17 | async-start | bytes 6963200 | tf_op jit(solution)/shard_map/all_gather | solution.py:107
  9.5 121.0 %copy-start.117 = (bf16[5,16]{1,0:T(8,128)(2,1)S(1)}, bf16[5,16]{1,0:T(8,128)(2,1)}, u32[]{:S(2)}) copy-start(bf16[5,16]{1,0:T(8,128)(2,1)} %param.34) | copy-start | bytes 484
  9.5 633.0 %all-reduce.80.cloned.1.call-start = ((), (), s32[]{:S(2)}) async-start(), calls=%async_computation.18 | async-start | bytes 5242880 | tf_op jit(solution)/shard_map/psum | solution.py:179
  10.3 237.7 %collective-permute-start = (bf16[2,3]{1,0:T(2,128)(2,1)S(1)}, bf16[2,3]{1,0:T(2,128)(2,1)S(1)}, u32[]{:S(2)}, u32[]{:S(2)}) collective-permute-start(bf16[2,3]{1,0:T(2,128)(2,1)S(1)} %slice.505), channel_id=1, source_target_pairs={{0,2},{2,4},{4,6},{6,8},{8,10},{10,12},{12,14},{14,16},{16,18},{18... | collective-permute-start | bytes 44 | tf_op jit(solution)/shard_map/ppermute | solution.py:12
  14.0 135.1 %copy-start.118 = (bf16[5,16]{1,0:T(8,128)(2,1)S(1)}, bf16[5,16]{1,0:T(8,128)(2,1)}, u32[]{:S(2)}) copy-start(bf16[5,16]{1,0:T(8,128)(2,1)} %param.38) | copy-start | bytes 484
  30.1 137.4 %copy-start.119 = (bf16[5,16]{1,0:T(8,128)(2,1)S(1)}, bf16[5,16]{1,0:T(8,128)(2,1)}, u32[]{:S(2)}) copy-start(bf16[5,16]{1,0:T(8,128)(2,1)} %param.39) | copy-start | bytes 484
  88.0 159.6 %copy-start.64 = (f32[2560]{0:T(1024)}, f32[2560]{0:T(1024)S(1)}, u32[]{:S(2)}) copy-start(f32[2560]{0:T(1024)S(1)} %convert_element_type.120) | copy-start | bytes 30724
  109.6 76.5 %copy-start.120 = (bf16[5,16]{1,0:T(8,128)(2,1)S(1)}, bf16[5,16]{1,0:T(8,128)(2,1)}, u32[]{:S(2)}) copy-start(bf16[5,16]{1,0:T(8,128)(2,1)} %param.36) | copy-start | bytes 484
  109.8 94.7 %copy-start.4 = (bf16[2,128,2560]{2,1,0:T(8,128)(2,1)S(1)}, bf16[2,128,2560]{2,1,0:T(8,128)(2,1)}, u32[]{:S(2)}) copy-start(bf16[2,128,2560]{2,1,0:T(8,128)(2,1)} %param.25) | copy-start | bytes 3932164
  130.1 74.8 %copy-start.92 = (bf16[5,16,256]{2,1,0:T(8,128)(2,1)S(1)}, bf16[5,16,256]{2,1,0:T(8,128)(2,1)}, u32[]{:S(2)}) copy-start(bf16[5,16,256]{2,1,0:T(8,128)(2,1)} %param.37) | copy-start | bytes 122884
  130.2 166.0 %copy-start.71 = (f32[1280]{0:T(1024)}, f32[1280]{0:T(1024)S(1)}, u32[]{:S(2)}) copy-start(f32[1280]{0:T(1024)S(1)} %mul.633) | copy-start | bytes 15364
  130.3 165.9 %copy-start.73 = (f32[1280]{0:T(1024)}, f32[1280]{0:T(1024)S(1)}, u32[]{:S(2)}) copy-start(f32[1280]{0:T(1024)S(1)} %mul.630) | copy-start | bytes 15364
  130.4 165.8 %copy-start.75 = (f32[1280]{0:T(1024)}, f32[1280]{0:T(1024)S(1)}, u32[]{:S(2)}) copy-start(f32[1280]{0:T(1024)S(1)} %mul.627) | copy-start | bytes 15364
  130.5 165.8 %copy-start.77 = (f32[1280]{0:T(1024)}, f32[1280]{0:T(1024)S(1)}, u32[]{:S(2)}) copy-start(f32[1280]{0:T(1024)S(1)} %mul.619) | copy-start | bytes 15364
  149.0 77.1 %copy-start.93 = (bf16[5,16,256]{2,1,0:T(8,128)(2,1)S(1)}, bf16[5,16,256]{2,1,0:T(8,128)(2,1)}, u32[]{:S(2)}) copy-start(bf16[5,16,256]{2,1,0:T(8,128)(2,1)} %param.35) | copy-start | bytes 122884
  186.0 61.6 %copy-start.79 = (f32[256,5]{0,1:T(8,128)}, f32[256,5]{0,1:T(8,128)S(1)}, u32[]{:S(2)}) copy-start(f32[256,5]{0,1:T(8,128)S(1)} %reshape.338) | copy-start | bytes 15364
  204.9 43.1 %copy-start.101 = (f32[2,128]{1,0:T(2,128)}, f32[2,128]{1,0:T(2,128)S(1)}, u32[]{:S(2)}) copy-start(f32[2,128]{1,0:T(2,128)S(1)} %fusion.16) | copy-start | bytes 3076
  204.9 95.7 %copy-start.68 = (f32[5,256]{1,0:T(8,128)}, f32[5,256]{1,0:T(8,128)S(1)}, u32[]{:S(2)}) copy-start(f32[5,256]{1,0:T(8,128)S(1)} %broadcast_multiply_fusion) | copy-start | bytes 15364
  248.0 29.1 copy-start.8
  248.2 48.1 %copy-start.110 = (pred[2,128]{1,0:T(4,128)(4,1)}, pred[2,128]{1,0:T(4,128)(4,1)S(1)}, u32[]{:S(2)}) copy-start(pred[2,128]{1,0:T(4,128)(4,1)S(1)} %get-tuple-element.347) | copy-start | bytes 772
  248.2 48.1 %copy-start.112 = (pred[2,128]{1,0:T(4,128)(4,1)}, pred[2,128]{1,0:T(4,128)(4,1)S(1)}, u32[]{:S(2)}) copy-start(pred[2,128]{1,0:T(4,128)(4,1)S(1)} %get-tuple-element.348) | copy-start | bytes 772
  248.2 48.1 %copy-start.114 = (pred[2,128]{1,0:T(4,128)(4,1)}, pred[2,128]{1,0:T(4,128)(4,1)S(1)}, u32[]{:S(2)}) copy-start(pred[2,128]{1,0:T(4,128)(4,1)S(1)} %get-tuple-element.349) | copy-start | bytes 772
  248.2 52.4 %copy-start.105 = (pred[2,128]{1,0:T(4,128)(4,1)}, pred[2,128]{1,0:T(4,128)(4,1)S(1)}, u32[]{:S(2)}) copy-start(pred[2,128]{1,0:T(4,128)(4,1)S(1)} %get-tuple-element.346) | copy-start | bytes 772
  262.8 32.5 collective-permute-start.1
  285.4 267.4 %copy-start.6 = (f32[2,128,5,256]{3,2,1,0:T(8,128)}, f32[2,128,5,256]{3,2,1,0:T(8,128)S(1)}, u32[]{:S(2)}) copy-start(f32[2,128,5,256]{3,2,1,0:T(8,128)S(1)} %reshape.369) | copy-start | bytes 3932164
  305.4 119.1 %copy-start.24 = (f32[2,128,5,256]{3,1,0,2:T(8,128)}, f32[2,128,5,256]{3,1,0,2:T(8,128)S(1)}, u32[]{:S(2)}) copy-start(f32[2,128,5,256]{3,1,0,2:T(8,128)S(1)} %get-tuple-element.269) | copy-start | bytes 3932164
  488.2 25.4 copy-start.83
  565.9 182.1 %all-gather.23.cloned.1.call-start = ((), (), s32[]{:S(2)}) async-start(), calls=%async_computation.19 | async-start | bytes 20889600 | tf_op jit(solution)/shard_map/all_gather | solution.py:112
  566.5 285.7 %all-gather.25.cloned.1.call-start = ((), (), s32[]{:S(2)}) async-start(), calls=%async_computation.20 | async-start | bytes 20889600 | tf_op jit(solution)/shard_map/all_gather | solution.py:113
  567.1 389.5 %all-gather.27.cloned.1.call-start = ((), (), s32[]{:S(2)}) async-start(), calls=%async_computation.21 | async-start | bytes 20889600 | tf_op jit(solution)/shard_map/all_gather | solution.py:114
  567.8 499.5 %all-reduce.82.cloned.1.call-start = ((), (), s32[]{:S(2)}) async-start(), calls=%async_computation.22 | async-start | bytes 5242880 | tf_op jit(solution)/shard_map/psum | solution.py:215
  567.9 502.6 %copy-start.62 = (f32[2560]{0:T(1024)}, f32[2560]{0:T(1024)S(1)}, u32[]{:S(2)}) copy-start(f32[2560]{0:T(1024)S(1)} %convert_element_type.132) | copy-start | bytes 30724
  645.1 425.4 %copy-start = (f32[256,2560]{1,0:T(8,128)}, f32[256,2560]{1,0:T(8,128)S(1)}, u32[]{:S(2)}) copy-start(f32[256,2560]{1,0:T(8,128)S(1)} %get-tuple-element.260) | copy-start | bytes 7864324
  645.1 425.4 %copy-start.99 = (f32[256]{0:T(256)}, f32[256]{0:T(256)S(1)}, u32[]{:S(2)}) copy-start(f32[256]{0:T(256)S(1)} %fusion.86) | copy-start | bytes 3076
  994.2 424.7 %reduce-scatter.46.cloned.1.call-start = ((), (), s32[]{:S(2)}) async-start(), calls=%async_computation.31 | async-start | bytes 139264
  1217.6 45.3 %copy-start.16 = (f32[2,128,5,256]{3,1,0,2:T(8,128)S(1)}, f32[2,128,5,256]{3,1,0,2:T(8,128)}, u32[]{:S(2)}) copy-start(f32[2,128,5,256]{3,1,0,2:T(8,128)} %copy-done.15) | copy-start | bytes 3932164
  1217.6 45.3 %copy-start.26 = (bf16[2,128,5,256]{3,1,0,2:T(8,128)(2,1)S(1)}, bf16[2,128,5,256]{3,1,0,2:T(8,128)(2,1)}, u32[]{:S(2)}) copy-start(bf16[2,128,5,256]{3,1,0,2:T(8,128)(2,1)} %copy-done.25) | copy-start | bytes 1966084
  1224.0 38.9 %copy-start.14 = (f32[2,128,5,256]{3,1,0,2:T(8,128)S(1)}, f32[2,128,5,256]{3,1,0,2:T(8,128)}, u32[]{:S(2)}) copy-start(f32[2,128,5,256]{3,1,0,2:T(8,128)} %get-tuple-element.262) | copy-start | bytes 3932164
  1276.3 144.0 %reduce-scatter.52.cloned.1.call-start = ((), (), s32[]{:S(2)}) async-start(), calls=%async_computation.34 | async-start | bytes 139264
  1281.4 172.2 %reduce-scatter.54.cloned.1.call-start = ((), (), s32[]{:S(2)}) async-start(), calls=%async_computation.35 | async-start | bytes 139264
  1296.0 215.1 %reduce-scatter.56.cloned.1.call-start = ((), (), s32[]{:S(2)}) async-start(), calls=%async_computation.36 | async-start | bytes 139264
  1302.2 266.5 %reduce-scatter.58.cloned.1.call-start = ((), (), s32[]{:S(2)}) async-start(), calls=%async_computation.37 | async-start | bytes 139264
  1310.1 7.4 collective-permute-start.2
  1314.0 312.2 %reduce-scatter.50.cloned.1.call-start = ((), (), s32[]{:S(2)}) async-start(), calls=%async_computation.33 | async-start | bytes 139264
  1317.5 366.1 %reduce-scatter.48.cloned.1.call-start = ((), (), s32[]{:S(2)}) async-start(), calls=%async_computation.32 | async-start | bytes 139264
  1330.6 431.6 %all-reduce.84.cloned.1.call-start = ((), (), s32[]{:S(2)}) async-start(), calls=%async_computation.38 | async-start | bytes 5242880 | tf_op jit(solution)/shard_map/psum | solution.py:187
  1337.3 489.3 %reduce-scatter.34.cloned.1.call-start = ((), (), s32[]{:S(2)}) async-start(), calls=%async_computation.25 | async-start | bytes 1392640 | tf_op jit(solution)/shard_map/reduce_scatter | solution.py:321
  1339.8 545.2 %reduce-scatter.36.cloned.1.call-start = ((), (), s32[]{:S(2)}) async-start(), calls=%async_computation.26 | async-start | bytes 1392640 | tf_op jit(solution)/shard_map/reduce_scatter | solution.py:323
  1342.3 686.5 %reduce-scatter.30.cloned.1.call-start = ((), (), s32[]{:S(2)}) async-start(), calls=%async_computation.23 | async-start | bytes 13926400 | tf_op jit(solution)/shard_map/reduce_scatter | solution.py:311
  1350.3 820.6 %reduce-scatter.38.cloned.1.call-start = ((), (), s32[]{:S(2)}) async-start(), calls=%async_computation.27 | async-start | bytes 13926400 | tf_op jit(solution)/shard_map/reduce_scatter | solution.py:326
  1358.4 955.2 %reduce-scatter.32.cloned.1.call-start = ((), (), s32[]{:S(2)}) async-start(), calls=%async_computation.24 | async-start | bytes 13926400 | tf_op jit(solution)/shard_map/reduce_scatter | solution.py:313
  1366.4 1330.9 %reduce-scatter.40.cloned.1.call-start = ((), (), s32[]{:S(2)}) async-start(), calls=%async_computation.28 | async-start | bytes 41779200 | tf_op jit(solution)/shard_map/reduce_scatter | solution.py:221
  1383.6 1697.4 %reduce-scatter.42.cloned.1.call-start = ((), (), s32[]{:S(2)}) async-start(), calls=%async_computation.29 | async-start | bytes 41779200 | tf_op jit(solution)/shard_map/reduce_scatter | solution.py:222
  1400.7 2063.4 %reduce-scatter.44.cloned.1.call-start = ((), (), s32[]{:S(2)}) async-start(), calls=%async_computation.30 | async-start | bytes 41779200 | tf_op jit(solution)/shard_map/reduce_scatter | solution.py:223
  1418.1 344.1 %copy-start.65 = (f32[2560]{0:T(1024)S(1)}, f32[2560]{0:T(1024)}, u32[]{:S(2)}) copy-start(f32[2560]{0:T(1024)} %copy-done.64) | copy-start | bytes 30724
  1418.1 347.4 %copy-start.82 = (f32[2560]{0:T(1024)S(1)}, f32[2560]{0:T(1024)}, u32[]{:S(2)}) copy-start(f32[2560]{0:T(1024)} %get-tuple-element.257) | copy-start | bytes 30724
  1762.2 58.8 %copy-start.1 = (f32[256,2560]{1,0:T(8,128)S(1)}, f32[256,2560]{1,0:T(8,128)}, u32[]{:S(2)}) copy-start(f32[256,2560]{1,0:T(8,128)} %copy-done) | copy-start | bytes 7864324
  1762.2 58.8 %copy-start.63 = (f32[2560]{0:T(1024)S(1)}, f32[2560]{0:T(1024)}, u32[]{:S(2)}) copy-start(f32[2560]{0:T(1024)} %copy-done.62) | copy-start | bytes 30724
  1762.3 58.9 %copy-start.100 = (f32[256]{0:T(256)S(1)}, f32[256]{0:T(256)}, u32[]{:S(2)}) copy-start(f32[256]{0:T(256)} %copy-done.99) | copy-start | bytes 3076
  1762.3 58.9 %copy-start.104 = (f32[256]{0:T(256)S(1)}, f32[256]{0:T(256)}, u32[]{:S(2)}) copy-start(f32[256]{0:T(256)} %copy-done.103) | copy-start | bytes 3076
  (90 other events, 371.2 us)
Sparse Core Ops, SparseCore 0:
  10.4 64.0 all-gather.16
  76.7 64.4 all-gather.18
  143.5 62.5 all-gather.20
  566.0 76.3 all-reduce.79
  644.0 103.9 all-gather.22
  749.5 102.6 all-gather.24
  853.9 102.6 all-gather.26
  994.3 72.9 all-reduce.81
  1276.4 62.0 reduce-scatter.45
  1341.8 54.1 reduce-scatter.51
  1399.4 54.1 reduce-scatter.53
  1456.9 54.1 reduce-scatter.55
  1514.5 54.1 reduce-scatter.57
  1572.0 54.1 reduce-scatter.49
  1629.5 54.0 reduce-scatter.47
  1686.4 75.7 all-reduce.83
  1766.7 56.6 reduce-scatter.33
  1827.5 57.4 reduce-scatter.35
  1890.2 138.5 reduce-scatter.29
  2033.3 137.4 reduce-scatter.37
  2176.1 137.4 reduce-scatter.31
  2318.4 378.7 reduce-scatter.39
  2702.1 378.8 reduce-scatter.41
  3085.7 378.3 reduce-scatter.43
where the time goes:
time: 3500 us; the launch traced here: 3470 us
  waiting for transfers between devices  2390 us (68%)
  local copies, waits for them, and re-layouts  390 us (11%)
  blocking collectives  355 us (10%)
  matrix products  190 us (5%)
  other arithmetic  118 us (3%)
    reduce_scatter x1, waiting for transfers between devices, local(): lax.psum_scatter(up_grad, 'wide', scatter_dimension=0, tiled=True)  384 us
    reduce_scatter x1, waiting for transfers between devices, local(): lax.psum_scatter(gate_grad, 'wide', scatter_dimension=0, tiled=True)  384 us
    reduce_scatter x1, waiting for transfers between devices, local(): lax.psum_scatter(down_grad, 'wide', scatter_dimension=1, tiled=True)  383 us
    unnamed x31, waiting for transfers between devices  261 us
    reduce_scatter x1, waiting for transfers between devices, local(): lax.psum_scatter(gelu_w_grad, 'wide', scatter_dimension=0, tiled=True)  144 us
    reduce_scatter x1, waiting for transfers between devices, local(): lax.psum_scatter(input_w_grad, 'wide', scatter_dimension=0, tiled=True)  143 us
    reduce_scatter x1, waiting for transfers between devices, local(): lax.psum_scatter(out_grad, 'wide', scatter_dimension=2, tiled=True)  142 us
    unnamed x2, blocking collectives  109 us
  transfers between devices with their start and end apart: 27, of which 18 were waited for; matrix products, arithmetic and copies ran while one was open for 7% of the time, Pallas kernels for 0%

commit v1 on v0

v1 whole, which is shorter than its diff:
```python
import functools

import jax
import jax.numpy as jnp
from jax import lax
from jax.experimental import pallas as pl
from jax.experimental.pallas import tpu as pltpu
from jax.sharding import PartitionSpec as P

CONV = 4
LANE = 128
GRANT = 60 * 1024 * 1024
F32 = jnp.float32
BF16 = jnp.bfloat16

LINE = 4


class Grid:
    def __init__(self):
        self.n = lax.axis_size("wide")
        self.hi = LINE
        self.inner_size = self.n // LINE
        self.tensor = lax.axis_size("tensor")
        self.w = lax.axis_index("wide")
        self.t = lax.axis_index("tensor")
        self.z = self.w // self.inner_size
        self.inner = lax.rem(self.w, self.inner_size)

    def flip(self, value, bit):
        return lax.ppermute(value, "wide", [(i, i ^ bit) for i in range(self.n)])

    def swap(self, value):
        size = self.tensor
        pairs = [(i, (i + 1) % size) for i in range(size)]
        return lax.ppermute(value, "tensor", pairs)


def shifted(shard, axis, by):
    size = lax.axis_size(axis)
    place = lax.axis_index(axis) - by
    there = jnp.logical_and(place >= 0, place < size)
    pairs = [(i, (i + by) % size) for i in range(size)]
    moved = lax.ppermute(shard, axis, pairs)
    return jax.tree.map(lambda a: jnp.where(there, a, jnp.zeros_like(a)), moved)


def pick(values, index, axis=0):
    return lax.dynamic_index_in_dim(values, index, axis, keepdims=False)


def reduce_small(grid, values):
    bit = grid.n // 2
    while bit:
        halves = values.reshape(2, bit, -1)
        mine = jnp.bitwise_and(lax.div(grid.w, bit), 1)
        got = grid.flip(pick(halves, 1 - mine), bit)
        values = pick(halves, mine) + got
        bit //= 2
    return values.reshape(-1)


def prefix_wide(grid, part, reverse):
    total = part
    entering = jnp.stack([jnp.ones_like(part[0]), jnp.zeros_like(part[1])])

    def joined(earlier, later):
        return jnp.stack([later[0] * earlier[0], later[0] * earlier[1] + later[1]])

    bit = 1
    while bit < grid.n:
        got = grid.flip(total, bit)
        set_here = jnp.bitwise_and(lax.div(grid.w, bit), 1) == 1
        after = jnp.logical_not(set_here) if reverse else set_here
        entering = jnp.where(after, joined(got, entering), entering)
        total = jnp.where(after, joined(got, total), joined(total, got))
        bit *= 2
    return entering[1]


def scan_kernel(reverse, a_ref, b_ref, cum_ref, out_ref):
    rows, width = a_ref.shape[1:]
    place = lax.broadcasted_iota(jnp.int32, (8, width), 0)
    tiles = rows // 8

    def one(i, carry):
        decay_in, state_in = carry
        tile = tiles - 1 - i if reverse else i
        at = pl.ds(pl.multiple_of(tile * 8, 8), 8)
        a = a_ref[0, at, :]
        b = b_ref[0, at, :]
        for by in (1, 2, 4):
            if reverse:
                moved_a = pltpu.roll(a, 8 - by, 0)
                moved_b = pltpu.roll(b, 8 - by, 0)
                ok = place < 8 - by
            else:
                moved_a = pltpu.roll(a, by, 0)
                moved_b = pltpu.roll(b, by, 0)
                ok = place >= by
            b = jnp.where(ok, a * moved_b + b, b)
            a = jnp.where(ok, a * moved_a, a)
        b = b + a * state_in
        a = a * decay_in
        cum_ref[0, at, :] = a
        out_ref[0, at, :] = b
        last = 0 if reverse else 7
        return (
            jnp.broadcast_to(a[last : last + 1], (8, width)),
            jnp.broadcast_to(b[last : last + 1], (8, width)),
        )

    start = (jnp.ones((8, width), F32), jnp.zeros((8, width), F32))
    lax.fori_loop(0, tiles, one, start)


def local_scan(decay, drive, reverse):
    seqs, rows, channels = decay.shape
    width = 256
    spec = pl.BlockSpec((1, rows, width), lambda s, c: (s, 0, c))
    shape = jax.ShapeDtypeStruct(decay.shape, F32)
    return pl.pallas_call(
        functools.partial(scan_kernel, reverse),
        grid=(seqs, channels // width),
        in_specs=[spec, spec],
        out_specs=[spec, spec],
        out_shape=[shape, shape],
        cost_estimate=pl.CostEstimate(
            flops=20 * decay.size, bytes_accessed=16 * decay.size, transcendentals=0
        ),
    )(decay, drive)


MESH = pl.DeviceIdType.MESH


class Spot:
    def __init__(self, n, tensor):
        self.n = n
        self.hi = LINE
        self.inner_size = n // LINE
        self.bits = [1 << i for i in range(self.inner_size.bit_length() - 1)]
        self.tensor = tensor
        self.w = lax.axis_index("wide")
        self.t = lax.axis_index("tensor")
        self.z = self.w // self.inner_size
        self.inner = lax.rem(self.w, self.inner_size)
        self.cross = {"tensor": lax.rem(self.t + 1, tensor)}

    def bit(self, which):
        return lax.rem(self.inner // which, 2)

    def flip(self, which):
        return {"wide": self.w + which - 2 * which * self.bit(which)}

    def line(self, place):
        return {"wide": place * self.inner_size + self.inner}

    def away(self, distance):
        return lax.rem(self.z + distance, self.hi)

    def greet(self, *sides):
        barrier = pltpu.get_barrier_semaphore()
        for side in sides:
            pl.semaphore_signal(barrier, inc=1, device_id=side, device_id_type=MESH)
        for distance in range(1, self.hi):
            pl.semaphore_signal(
                barrier, inc=1, device_id=self.line(self.away(distance)), device_id_type=MESH
            )
        pl.semaphore_wait(barrier, len(sides) + self.hi - 1)


def remote(src, dst, sems, index, side):
    return pltpu.make_async_remote_copy(
        src_ref=src,
        dst_ref=dst,
        send_sem=sems.at[0, index],
        recv_sem=sems.at[1, index],
        device_id=side,
        device_id_type=MESH,
    )


class Fans:
    def __init__(self, spot, at, sems, base, sides):
        self.spot, self.at, self.sems, self.base, self.sides = spot, at, sems, base, sides
        self.kinds = sorted(range(1 << len(sides)), key=lambda k: (bin(k).count("1"), -k))

    def onto(self, k):
        low = (k & -k) if k else 1 << len(self.sides)
        return [i for i in reversed(range(len(self.sides))) if (1 << i) < low]

    def copy(self, place, k, i, here=False):
        spot, hi = self.spot, self.spot.hi
        landed = k if here else k | (1 << i)
        index = self.base + (landed - 1) * hi + lax.rem(place - spot.z + hi, hi)
        ref = self.at(place, k)
        return remote(ref, ref, self.sems, index, self.sides[i])

    def hand_on(self, place, k):
        for i in self.onto(k):
            self.copy(place, k, i).start()

    def arrive(self, place, k):
        low = (k & -k).bit_length() - 1
        self.copy(place, k, low, here=True).wait_recv()

    def pass_on(self, place):
        for k in self.kinds:
            if k and self.onto(k):
                self.arrive(place, k)
                self.hand_on(place, k)

    def finish(self, place):
        for k in self.kinds:
            if k and not self.onto(k):
                self.arrive(place, k)
            for i in self.onto(k):
                self.copy(place, k, i).wait_send()

    def count(sides, hi):
        return ((1 << sides) - 1) * hi


class Chain:
    def __init__(self, spot, at, sems, sides):
        self.spot, self.at, self.sems = spot, at, sems
        self.fans = Fans(spot, at, sems, 2 * (spot.hi - 1), sides)

    def line_copy(self, s, up):
        spot, hi = self.spot, self.spot.hi
        owner = spot.z - (s - 1) if up else spot.z + (s - 1)
        other = spot.z + 1 if up else spot.z - 1
        ref = self.at(owner, 0)
        return remote(ref, ref, self.sems, (s - 1) if up else hi + s - 2, spot.line(other))

    def line_here(self, s, up):
        spot, hi = self.spot, self.spot.hi
        owner = spot.z - s if up else spot.z + s
        other = spot.z - 1 if up else spot.z + 1
        ref = self.at(owner, 0)
        return remote(ref, ref, self.sems, (s - 1) if up else hi + s - 2, spot.line(other))

    def first(self):
        spot, hi = self.spot, self.spot.hi

        @pl.when(spot.z < hi - 1)
        def _():
            self.line_copy(1, True).start()

        @pl.when(spot.z > 0)
        def _():
            self.line_copy(1, False).start()

        self.fans.hand_on(spot.z, 0)

    def onward(self, s):
        spot, hi = self.spot, self.spot.hi

        @pl.when(spot.z >= s)
        def _():
            self.line_here(s, True).wait_recv()

        if s < hi - 1:

            @pl.when(jnp.logical_and(spot.z >= s, spot.z < hi - 1))
            def _():
                self.line_copy(s + 1, True).start()

        @pl.when(spot.z >= s)
        def _():
            self.fans.hand_on(spot.z - s, 0)

        @pl.when(spot.z <= hi - 1 - s)
        def _():
            self.line_here(s, False).wait_recv()

        if s < hi - 1:

            @pl.when(jnp.logical_and(spot.z <= hi - 1 - s, spot.z > 0))
            def _():
                self.line_copy(s + 1, False).start()

        @pl.when(spot.z <= hi - 1 - s)
        def _():
            self.fans.hand_on(spot.z + s, 0)

    def places(self, s, act):
        spot = self.spot
        if s == 0:
            act(spot.z)
            return

        @pl.when(spot.z >= s)
        def _():
            act(spot.z - s)

        @pl.when(spot.z <= spot.hi - 1 - s)
        def _():
            act(spot.z + s)

    def second(self, s):
        self.places(s, self.fans.pass_on)

    def finish(self):
        spot, hi = self.spot, self.spot.hi
        for s in range(hi):
            self.places(s, self.fans.finish)
        for s in range(1, hi):

            @pl.when(jnp.logical_and(spot.z >= s - 1, spot.z < hi - 1))
            def _():
                self.line_copy(s, True).wait_send()

            @pl.when(jnp.logical_and(spot.z <= hi - s, spot.z > 0))
            def _():
                self.line_copy(s, False).wait_send()


def chain_sems(sides):
    return pltpu.SemaphoreType.DMA((2, 2 * (LINE - 1) + ((1 << sides) - 1) * LINE))


class Turns:
    def __init__(self, spot, window_of, at, sems, sides):
        self.spot, self.window_of, self.at, self.sems = spot, window_of, at, sems
        self.fans = Fans(spot, at, sems, spot.hi, sides)

    def line_copy(self, distance):
        spot = self.spot
        place = spot.away(distance)
        return remote(self.window_of(place), self.at(spot.z, 0), self.sems, distance, spot.line(place))

    def back(self, distance):
        return lax.rem(self.spot.z - distance + self.spot.hi, self.spot.hi)

    def line_here(self, distance):
        place = self.back(distance)
        ref = self.at(place, 0)
        return remote(ref, ref, self.sems, distance, self.spot.line(place))

    def first(self):
        for distance in range(1, self.spot.hi):
            self.line_copy(distance).start()
        self.fans.hand_on(self.spot.z, 0)

    def onward(self, distance):
        self.line_here(distance).wait_recv()
        self.fans.hand_on(self.back(distance), 0)

    def second(self, distance):
        self.fans.pass_on(self.back(distance))

    def finish(self):
        for distance in range(self.spot.hi):
            self.fans.finish(self.back(distance))
            if distance:
                self.line_copy(distance).wait_send()


def weights_kernel(
    n, tensor, rec, gates, feed, cot, rec_all, gates_all, feed_all, cot_all,
    rec_sems, gates_sems, feed_sems, cot_sems,
):
    del rec, gates, feed, cot
    spot = Spot(n, tensor)
    hi = spot.hi

    def index(place, k):
        return place * spot.inner_size + jnp.bitwise_xor(spot.inner, k)

    cube = [spot.flip(bit) for bit in spot.bits]
    moves = [
        Chain(spot, lambda place, k: gates_all.at[index(place, k)], gates_sems, cube),
        Chain(spot, lambda place, k: rec_all.at[:, index(place, k)], rec_sems, cube),
        Turns(
            spot,
            lambda place: feed_all.at[:, n + place],
            lambda place, k: feed_all.at[:, index(place, k)],
            feed_sems,
            cube,
        ),
        Chain(
            spot,
            lambda place, k: cot_all.at[place, lax.rem(spot.t + k, tensor)],
            cot_sems,
            [spot.cross],
        ),
    ]
    spot.greet(*cube, spot.cross)
    for move in moves:
        move.first()
    for s in range(1, hi):
        for move in moves:
            move.onward(s)
        for move in moves:
            move.second(s - 1)
    for move in moves:
        move.second(hi - 1)
    for move in moves:
        move.finish()


def blank(*shapes):
    return pl.pallas_call(
        lambda *refs: None,
        out_shape=[jax.ShapeDtypeStruct(shape, BF16) for shape in shapes],
        out_specs=[pl.BlockSpec(memory_space=pl.ANY)] * len(shapes),
        compiler_params=pltpu.CompilerParams(vmem_limit_bytes=GRANT),
        name="blank",
    )()


def bring_weights(grid, rec, gates, feed, cot):
    n, hi, tensor = grid.n, grid.hi, grid.tensor
    far = pl.BlockSpec(memory_space=pl.ANY)
    arrays = (rec, gates, feed, cot)
    cube = grid.inner_size.bit_length() - 1
    return pl.pallas_call(
        functools.partial(weights_kernel, n, tensor),
        out_shape=[jax.ShapeDtypeStruct(a.shape, a.dtype) for a in arrays],
        in_specs=[far] * 4,
        out_specs=[far] * 4,
        input_output_aliases={i: i for i in range(4)},
        scratch_shapes=[
            chain_sems(cube),
            chain_sems(cube),
            pltpu.SemaphoreType.DMA((2, grid.inner_size * hi)),
            chain_sems(1),
        ],
        compiler_params=pltpu.CompilerParams(
            collective_id=0, has_side_effects=True, vmem_limit_bytes=GRANT
        ),
        name="bring_weights",
    )(*arrays)


def by_rows(rows, step, act):
    def one(i, carry):
        act(pl.ds(pl.multiple_of(i * step, step), step))
        return carry

    lax.fori_loop(0, rows // step, one, 0)


STEP = 16


def second_kernel(n, tensor, part, inputs, shift, gain, resid, whole, held, out, got, swap_sems, sems):
    spot = Spot(n, tensor)
    rows = inputs.shape[0]

    def put(at):
        out[at, :] = part[1 - spot.t, at, :].astype(BF16)

    by_rows(rows, STEP, put)
    spot.greet(spot.cross)
    copy = remote(out, got, swap_sems, 0, spot.cross)
    copy.start()
    copy.wait()

    def norm(at):
        value = inputs[at, :] + (part[spot.t, at, :] + got[at, :].astype(F32) + shift[...])
        resid[at, :] = value
        scale = lax.rsqrt(jnp.mean(value * value, axis=-1, keepdims=True) + 1e-06)
        held[spot.z, spot.t, at, :] = (value * scale * gain[...]).astype(BF16)

    by_rows(rows, STEP, norm)
    chain = Chain(
        spot, lambda place, k: held.at[place, lax.rem(spot.t + k, tensor)], sems, [spot.cross]
    )
    chain.first()
    for s in range(1, spot.hi):
        chain.onward(s)
        chain.second(s - 1)
    chain.second(spot.hi - 1)
    chain.finish()
    for place in range(spot.hi):
        for side in range(tensor):

            def give(at, place=place, side=side):
                whole[place, side, at, :] = held[place, side, at, :]

            by_rows(rows, STEP, give)


def bring_second(grid, part, inputs, shift, gain):
    rows, width = inputs.shape
    near = pl.BlockSpec(memory_space=pltpu.VMEM)
    whole = (grid.hi, grid.tensor, rows, width)
    return pl.pallas_call(
        functools.partial(second_kernel, grid.n, grid.tensor),
        out_shape=[jax.ShapeDtypeStruct((rows, width), F32), jax.ShapeDtypeStruct(whole, BF16)],
        in_specs=[near] * 4,
        out_specs=[near] * 2,
        scratch_shapes=[
            pltpu.VMEM(whole, BF16),
            pltpu.VMEM((rows, width), BF16),
            pltpu.VMEM((rows, width), BF16),
            pltpu.SemaphoreType.DMA((2, 1)),
            chain_sems(1),
        ],
        compiler_params=pltpu.CompilerParams(
            collective_id=1, has_side_effects=True, vmem_limit_bytes=GRANT
        ),
        name="bring_second",
    )(part, inputs, shift, gain)


class Rows:
    def __init__(self, spot, part, out, got, line, cross_sems, line_sems):
        self.spot, self.part, self.out, self.got, self.line = spot, part, out, got, line
        self.cross_sems, self.line_sems = cross_sems, line_sems
        self.rows = out.shape[1]

    def place(self, k):
        spot, hi = self.spot, self.spot.hi
        last = hi - 1
        flipped = jnp.where(spot.z * 2 < hi, 0, 1)
        z = spot.z + flipped * (last - 2 * spot.z)
        if k == last:
            place = z
        else:
            place = jnp.where(k < last - z, last - k, k - (last - z))
        return place + flipped * (last - 2 * place)

    def cross_copy(self, place):
        return remote(
            self.out.at[place], self.got.at[place], self.cross_sems, place, self.spot.cross
        )

    def start(self):
        spot = self.spot
        for k in range(spot.hi):
            place = self.place(k)

            def put(at, place=place):
                self.out[place, at, :] = self.part[place, 1 - spot.t, at, :]

            by_rows(self.rows, STEP, put)
            self.cross_copy(place).start()

    def line_copy(self, s, up, here=False):
        spot, hi = self.spot, self.spot.hi
        slot = (s - 1) if up else hi + s - 2
        step = 1 if up != here else -1
        return remote(
            self.line.at[0, slot], self.line.at[1, slot], self.line_sems, slot, spot.line(spot.z + step)
        )

    def own(self, place, at):
        return self.part[place, self.spot.t, at, :].astype(F32) + self.got[place, at, :].astype(F32)

    def send(self, s, up):
        spot, hi = self.spot, self.spot.hi
        place = spot.z + hi - s if up else spot.z - hi + s
        slot = (s - 1) if up else hi + s - 2
        self.cross_copy(place).wait_recv()
        begins = spot.z == 0 if up else spot.z == hi - 1

        @pl.when(begins)
        def _():
            def put(at):
                self.line[0, slot, at, :] = self.own(place, at).astype(BF16)

            by_rows(self.rows, STEP, put)

        if s > 1:

            @pl.when(jnp.logical_not(begins))
            def _():
                self.line_copy(s - 1, up, here=True).wait_recv()

                def put(at):
                    before = self.line[1, slot - 1, at, :].astype(F32)
                    self.line[0, slot, at, :] = (self.own(place, at) + before).astype(BF16)

                by_rows(self.rows, STEP, put)

        self.line_copy(s, up).start()

    def sends_up(self, s):
        return self.spot.z <= s - 1

    def sends_down(self, s):
        return self.spot.z >= self.spot.hi - s

    def run(self, done):
        spot, hi = self.spot, self.spot.hi
        for s in range(1, hi):

            @pl.when(jnp.logical_and(self.sends_up(s), spot.z < hi - 1))
            def _():
                self.send(s, True)

            @pl.when(jnp.logical_and(self.sends_down(s), spot.z > 0))
            def _():
                self.send(s, False)

        self.cross_copy(spot.z).wait_recv()

        @pl.when(spot.z > 0)
        def _():
            self.line_copy(hi - 1, True, here=True).wait_recv()

        @pl.when(spot.z < hi - 1)
        def _():
            self.line_copy(hi - 1, False, here=True).wait_recv()

        def total(at):
            below = self.line[1, hi - 2, at, :].astype(F32)
            above = self.line[1, 2 * hi - 3, at, :].astype(F32)
            value = self.own(spot.z, at)
            value = value + jnp.where(spot.z > 0, below, 0.0)
            done(at, value + jnp.where(spot.z < hi - 1, above, 0.0))

        by_rows(self.rows, STEP, total)

    def finish(self):
        spot, hi = self.spot, self.spot.hi
        for place in range(hi):
            self.cross_copy(place).wait_send()
        for s in range(1, hi):

            @pl.when(jnp.logical_and(self.sends_up(s), spot.z < hi - 1))
            def _():
                self.line_copy(s, True).wait_send()

            @pl.when(jnp.logical_and(self.sends_down(s), spot.z > 0))
            def _():
                self.line_copy(s, False).wait_send()


def rows_kernel(
    second, n, tensor, part, resid, cot, gain, both, gain_grad,
    out, got, line, mine, other, cross_sems, line_sems, swap_sems,
):
    spot = Spot(n, tensor)
    sums = Rows(spot, part, out, got, line, cross_sems, line_sems)
    spot.greet(spot.cross)
    sums.start()
    if second:
        gain_grad[...] = jnp.zeros_like(gain_grad)

    def done(at, total):
        value = resid[at, :]
        if second:
            scale = lax.rsqrt(jnp.mean(value * value, axis=-1, keepdims=True) + 1e-06)
            turned = total * gain[...]
            inner = jnp.mean(turned * value, axis=-1, keepdims=True)
            grad = cot[at, :].astype(F32) + scale * turned - value * (scale * scale * scale * inner)
            gained = total * value * scale
            gain_grad[...] += jnp.sum(gained.reshape(2, 8, -1), axis=0)
            mine[at, :] = grad.astype(BF16)
        else:
            mine[at, :] = (value + total).astype(BF16)

    sums.run(done)
    copy = remote(mine, other, swap_sems, 0, spot.cross)
    copy.start()
    sums.finish()

    def keep(at):
        both[spot.t, at, :] = mine[at, :]

    by_rows(mine.shape[0], STEP, keep)
    copy.wait()

    def take(at):
        both[1 - spot.t, at, :] = other[at, :]

    by_rows(mine.shape[0], STEP, take)


def sum_rows(grid, second, part, resid, cot, gain):
    rows, width = resid.shape
    near = pl.BlockSpec(memory_space=pltpu.VMEM)
    hi, tensor = grid.hi, grid.tensor
    return pl.pallas_call(
        functools.partial(rows_kernel, second, grid.n, tensor),
        out_shape=[
            jax.ShapeDtypeStruct((tensor, rows, width), BF16),
            jax.ShapeDtypeStruct((8, width), F32),
        ],
        in_specs=[near] * 4,
        out_specs=[near] * 2,
        scratch_shapes=[
            pltpu.VMEM((hi, rows, width), BF16),
            pltpu.VMEM((hi, rows, width), BF16),
            pltpu.VMEM((2, 2 * (hi - 1), rows, width), BF16),
            pltpu.VMEM((rows, width), BF16),
            pltpu.VMEM((rows, width), BF16),
            pltpu.SemaphoreType.DMA((2, hi)),
            pltpu.SemaphoreType.DMA((2, 2 * (hi - 1))),
            pltpu.SemaphoreType.DMA((2, 1)),
        ],
        compiler_params=pltpu.CompilerParams(
            collective_id=2 if second else 3, has_side_effects=True, vmem_limit_bytes=GRANT
        ),
        name="sum_second" if second else "sum_feed",
    )(part, resid, cot, gain)


RING = 4


def tile_rows(rows):
    return 16 if rows % 16 == 0 else 8


def grads_kernel(n, tensor, spans, kept, *refs):
    count = len(spans)
    parts, apart, summed = refs[:count], refs[count], refs[count + 1]
    refs = refs[count + 2 :]
    stages = (n // LINE).bit_length() - 1
    sends, keeps, gots = refs[:stages], refs[stages : 2 * stages], refs[2 * stages : 3 * stages]
    ready, got_line, cube_sems, line_sems = refs[3 * stages :]
    spot = Spot(n, tensor)
    hi = spot.hi
    all_spans = sum(spans)
    units = all_spans * hi
    step = pl.program_id(0)
    rows = ready.shape[1]
    each = tile_rows(rows)

    def cube_copy(stage, unit):
        slot = lax.rem(unit, RING)
        return remote(
            sends[stage].at[slot],
            gots[stage].at[slot],
            cube_sems.at[stage],
            slot,
            spot.flip(spot.bits[stage]),
        )

    def line_copy(span, place, sender):
        return pltpu.make_async_remote_copy(
            src_ref=ready.at[span * hi + place],
            dst_ref=got_line.at[span, sender],
            send_sem=line_sems.at[0, span * hi + place],
            recv_sem=line_sems.at[1, span * hi + sender],
            device_id=spot.line(place),
            device_id_type=MESH,
        )

    @pl.when(step == 0)
    def _():
        spot.greet(*[spot.flip(bit) for bit in spot.bits])

    begin = 0
    for part, width in zip(parts, spans):
        first, begin = begin * hi, begin + width

        @pl.when(jnp.logical_and(step >= first, step < begin * hi))
        def _(part=part):
            slot = lax.rem(step, RING)

            @pl.when(step >= RING)
            def _():
                cube_copy(0, step - RING).wait_send()

            mine = spot.bit(1)
            for k in range(sends[0].shape[1]):

                def put(at, k=k):
                    sends[0][slot, k, at, :] = part[0, 2 * k + 1 - mine, at, :]
                    keeps[0][slot, k, at, :] = part[0, 2 * k + mine, at, :]

                by_rows(rows, each, put)
            cube_copy(0, step).start()

    for stage in range(stages):
        unit = step - stage - 1

        @pl.when(jnp.logical_and(unit >= 0, unit < units))
        def _(stage=stage, unit=unit):
            slot = lax.rem(unit, RING)
            cube_copy(stage, unit).wait_recv()

            def total(k, at):
                return (
                    keeps[stage][slot, k, at, :].astype(F32) + gots[stage][slot, k, at, :].astype(F32)
                ).astype(BF16)

            if stage < stages - 1:

                @pl.when(unit >= RING)
                def _():
                    cube_copy(stage + 1, unit - RING).wait_send()

                mine = spot.bit(spot.bits[stage + 1])
                for k in range(sends[stage + 1].shape[1]):

                    def put(at, k=k):
                        sends[stage + 1][slot, k, at, :] = total(2 * k + 1 - mine, at)
                        keeps[stage + 1][slot, k, at, :] = total(2 * k + mine, at)

                    by_rows(rows, each, put)
                cube_copy(stage + 1, unit).start()
            else:
                span, place = unit // hi, lax.rem(unit, hi)

                def put(at):
                    ready[unit, at, :] = total(0, at)

                by_rows(rows, each, put)

                @pl.when(place != spot.z)
                def _():
                    line_copy(span, place, spot.z).start()

    @pl.when(step == units + stages - 1)
    def _():
        for span in range(all_spans):
            for distance in range(1, hi):
                place = spot.away(distance)
                line_copy(span, place, place).wait_recv()
                line_copy(span, place, spot.z).wait_send()

            def give(at, span=span):
                own = ready[span * hi + spot.z, at, :]
                if span < kept:
                    for distance in range(hi):
                        place = spot.away(distance)
                        apart[span, place, at, :] = got_line[span, place, at, :] if distance else own
                else:
                    value = own.astype(F32)
                    for distance in range(1, hi):
                        value = value + got_line[span, spot.away(distance), at, :].astype(F32)
                    summed[span - kept, at, :] = value

            by_rows(rows, each, give)
        for stage in range(stages):
            for unit in range(units - RING, units):
                cube_copy(stage, unit).wait_send()


def send_grads(grid, parts, width, kept):
    hi, inner = grid.hi, grid.inner_size
    rows = parts[0].shape[0] // grid.n
    spans = [part.shape[1] // width for part in parts]
    all_spans = sum(spans)
    stages = inner.bit_length() - 1

    def part_spec(first, count):
        def index(i):
            unit = jnp.clip(i - first * hi, 0, count * hi - 1)
            return (lax.rem(unit, hi), 0, 0, unit // hi)

        return pl.BlockSpec((1, inner, rows, width), index)

    firsts = [sum(spans[:i]) for i in range(len(spans))]
    apart = (kept, hi, rows, width)
    summed = (all_spans - kept, rows, width)
    halves = [
        pltpu.VMEM((RING, inner >> (stage + 1), rows, width), BF16) for stage in range(stages)
    ]
    return pl.pallas_call(
        functools.partial(grads_kernel, grid.n, grid.tensor, spans, kept),
        grid=(all_spans * hi + stages,),
        out_shape=[jax.ShapeDtypeStruct(apart, BF16), jax.ShapeDtypeStruct(summed, F32)],
        in_specs=[part_spec(first, count) for first, count in zip(firsts, spans)],
        out_specs=[
            pl.BlockSpec(apart, lambda i: (0, 0, 0, 0)),
            pl.BlockSpec(summed, lambda i: (0, 0, 0)),
        ],
        scratch_shapes=halves * 3
        + [
            pltpu.VMEM((all_spans * hi, rows, width), BF16),
            pltpu.VMEM((all_spans, hi, rows, width), BF16),
            pltpu.SemaphoreType.DMA((stages, 2, RING)),
            pltpu.SemaphoreType.DMA((2, all_spans * hi)),
        ],
        compiler_params=pltpu.CompilerParams(
            collective_id=4, has_side_effects=True, vmem_limit_bytes=GRANT
        ),
        name="send_grads",
    )(*[part.reshape(hi, inner, rows, part.shape[1]) for part in parts])


def rms_norm(values, gain):
    scale = lax.rsqrt(jnp.mean(values * values, axis=-1, keepdims=True) + 1e-06)
    return values * scale * gain


def causal_conv(extended, marks, weight, bias):
    margin = weight.shape[0] - 1
    tok_count = extended.shape[1] - margin
    current = marks[:, margin:]
    total = bias + weight[0] * extended[:, margin:]
    for offset in range(1, margin + 1):
        moved = extended[:, margin - offset : margin - offset + tok_count]
        same = (marks[:, margin - offset : margin - offset + tok_count] == current)[..., None]
        total = total + jnp.where(same, weight[offset] * moved, 0.0)
    return total


def lru_terms(inlet_pre, forget_pre, conv_vals, rate, starts):
    inlet = jax.nn.sigmoid(inlet_pre)
    forget = jax.nn.sigmoid(forget_pre)
    log_decay = -8.0 * forget * jax.nn.softplus(rate)
    decay = jnp.where(starts, 0.0, jnp.exp(log_decay))
    scaler = jnp.where(starts, 1.0, jnp.sqrt(-jnp.expm1(2.0 * log_decay)))
    return (decay, scaler * inlet * conv_vals)


def gelu_product(gate_pre, up_pre):
    return jax.nn.gelu(gate_pre) * up_pre


def dot(left, right):
    return jnp.dot(left, right, preferred_element_type=F32)


def dot_nt(left, right):
    return jnp.einsum("ik,jk->ij", left, right, preferred_element_type=F32)


def dot_tn(left, right):
    return jnp.einsum("ki,kj->ij", left, right, preferred_element_type=F32)


def local(
    block_in,
    segment_ids,
    cotangent,
    first_gain,
    gelu_weight,
    gelu_bias,
    input_weight,
    input_bias,
    conv_weight,
    conv_bias,
    inlet_weight,
    inlet_bias,
    forget_weight,
    forget_bias,
    decay_rate,
    out_weight,
    out_bias,
    second_gain,
    mlp_gate,
    mlp_up,
    mlp_down,
):
    grid = Grid()
    seq_count, tok_count, width = block_in.shape
    head_count, block_size = gelu_weight.shape[1:]
    channels = head_count * block_size
    margin = CONV - 1
    rows_all = seq_count * tok_count
    rows_half = rows_all // grid.tensor
    d_own = gelu_weight.shape[0]
    lane_own = gelu_bias.shape[1]
    units = mlp_gate.shape[1]
    unit_tiles = units // LANE
    window_tiles = -(-unit_tiles // grid.hi)
    window = window_tiles * LANE

    rec_own = jnp.stack(
        [
            input_weight.reshape(d_own, channels),
            gelu_weight.reshape(d_own, channels),
            out_weight.reshape(channels, d_own).T,
        ]
    )
    gates_own = jnp.stack([inlet_weight, forget_weight]).reshape(-1, block_size)
    thin_own = jnp.concatenate(
        [
            v.reshape(-1)
            for v in (
                first_gain,
                out_bias,
                second_gain,
                gelu_bias,
                input_bias,
                conv_weight,
                conv_bias,
                inlet_bias,
                forget_bias,
                decay_rate,
            )
        ]
    )
    gate_rows = gates_own.shape[0]
    thin_size = thin_own.size
    thin_rows = -(-thin_size // block_size)
    spare = -(gate_rows + thin_rows) % 16
    thin_own = jnp.pad(thin_own, (0, (thin_rows + spare) * block_size - thin_size))
    gates_own = jnp.concatenate([gates_own, thin_own.reshape(-1, block_size)])
    feed_own = jnp.stack([mlp_gate, mlp_up, mlp_down.T])
    feed_windows = jnp.stack(
        [
            feed_own[:, :, tile * LANE : tile * LANE + window]
            for tile in (
                min(place * window_tiles, unit_tiles - window_tiles) for place in range(grid.hi)
            )
        ],
        axis=1,
    )
    cot_rows = cotangent.reshape(grid.tensor, rows_half, width)
    cot_own = pick(cot_rows, grid.t)
    rec_all, gates_all, feed_all, cot_all = blank(
        (3, grid.n, d_own, channels),
        (grid.n,) + gates_own.shape,
        (3, grid.n + grid.hi, d_own, window),
        (grid.hi, grid.tensor, rows_half, width),
    )
    rec_all = lax.dynamic_update_slice(rec_all, rec_own[:, None], (0, grid.w, 0, 0))
    gates_all = lax.dynamic_update_slice(gates_all, gates_own[None], (grid.w, 0, 0))
    feed_all = lax.dynamic_update_slice(feed_all, feed_windows, (0, grid.n, 0, 0))
    feed_all = lax.dynamic_update_slice(
        feed_all, lax.dynamic_slice_in_dim(feed_windows, grid.z, 1, 1), (0, grid.w, 0, 0)
    )
    cot_all = lax.dynamic_update_slice(cot_all, cot_own[None, None], (grid.z, grid.t, 0, 0))
    rec_all, gates_all, feed_all, cot_all = bring_weights(
        grid, rec_all, gates_all, feed_all, cot_all
    )
    feed_all = feed_all[:, : grid.n]
    rec_all = rec_all.reshape(3, width, channels)
    input_full, gelu_full, out_turned = rec_all[0], rec_all[1], rec_all[2]
    thin_all = gates_all[:, gate_rows:].reshape(grid.n, -1)[:, :thin_size]
    gates_all = gates_all[:, :gate_rows]
    gates_all = (
        gates_all.reshape(grid.n, 2, head_count, lane_own, block_size)
        .transpose(1, 2, 0, 3, 4)
        .reshape(2, head_count, block_size, block_size)
    )
    inlet_full, forget_full = gates_all[0], gates_all[1]

    thin_all = thin_all.astype(F32)
    gain_first, out_shift, gain_second = (
        thin_all[:, i * d_own : (i + 1) * d_own].reshape(width) for i in range(3)
    )
    per = head_count * lane_own
    lane_rows = (
        thin_all[:, 3 * d_own :]
        .reshape(grid.n, CONV + 6, head_count, lane_own)
        .transpose(1, 2, 0, 3)
        .reshape(CONV + 6, channels)
    )
    gelu_shift, input_shift = lane_rows[0], lane_rows[1]
    conv_taps = lane_rows[2 : 2 + CONV]
    conv_offset, inlet_shift, forget_shift, rate_wide = (lane_rows[2 + CONV + i] for i in range(4))
    inlet_shift = inlet_shift.reshape(head_count, block_size)
    forget_shift = forget_shift.reshape(head_count, block_size)
    rate_wide = rate_wide.reshape(head_count, block_size)

    feed_all = feed_all.reshape(3, width, window)
    gate_full, up_full, down_turned = feed_all[0], feed_all[1], feed_all[2]
    first_tile = jnp.minimum(grid.z * window_tiles, unit_tiles - window_tiles)
    unit_place = lax.iota(jnp.int32, window) + first_tile * LANE
    valid = (unit_place >= grid.z * window)[None, :]

    inputs = block_in.astype(F32).reshape(rows_all, width)
    normed = rms_norm(inputs, gain_first).astype(BF16)
    input_pre = dot(normed, input_full) + input_shift
    input_branch = input_pre.astype(BF16).reshape(seq_count, tok_count, channels)
    marks = (segment_ids + 1).astype(BF16)
    rim_values, rim_marks = shifted(
        (input_branch[:, tok_count - margin :], marks[:, tok_count - margin :]), "wide", 1
    )
    extended = jnp.concatenate([rim_values, input_branch], axis=1).astype(F32)
    marks_ext = jnp.concatenate([rim_marks, marks], axis=1).astype(F32)
    conv_out = causal_conv(extended, marks_ext, conv_taps, conv_offset)
    blocks = conv_out.astype(BF16).reshape(seq_count, tok_count, head_count, block_size)
    inlet_pre = (
        jnp.einsum("sthc,hcd->sthd", blocks, inlet_full, preferred_element_type=F32) + inlet_shift
    )
    forget_pre = (
        jnp.einsum("sthc,hcd->sthd", blocks, forget_full, preferred_element_type=F32) + forget_shift
    )
    starts = (marks_ext[:, margin:] != marks_ext[:, margin - 1 : margin - 1 + tok_count])[
        :, :, None, None
    ]
    blocks_wide = blocks.astype(F32)
    decay, drive = lru_terms(inlet_pre, forget_pre, blocks_wide, rate_wide, starts)
    flat = (seq_count, tok_count, channels)
    decay_cum, local_state = local_scan(decay.reshape(flat), drive.reshape(flat), False)
    gelu_pre = dot(normed, gelu_full) + gelu_shift
    gelu_branch = jax.nn.gelu(gelu_pre).reshape(flat)
    state_in = prefix_wide(grid, jnp.stack([decay_cum[:, -1], local_state[:, -1]]), False)
    state = local_state + decay_cum * state_in[:, None]
    mixed = (state * gelu_branch).astype(BF16).reshape(rows_all, channels)
    branch_part = dot_nt(mixed, out_turned).reshape(grid.tensor, rows_half, width)
    own_inputs = pick(inputs.reshape(grid.tensor, rows_half, width), grid.t)
    resid, second_all = bring_second(
        grid, branch_part, own_inputs, out_shift[None], gain_second[None]
    )

    rows_feed = grid.hi * rows_all
    second_all = second_all.reshape(rows_feed, width)
    cot_all = cot_all.reshape(rows_feed, width)
    gate_pre = dot(second_all, gate_full)
    up_pre = dot(second_all, up_full)
    product, pull_feed = jax.vjp(gelu_product, gate_pre, up_pre)
    hidden = jnp.where(valid, product, 0.0).astype(BF16)
    hidden_grad = jnp.where(valid, dot(cot_all, down_turned), 0.0)
    gate_pre_grad, up_pre_grad = pull_feed(hidden_grad)
    gate_low = gate_pre_grad.astype(BF16)
    up_low = up_pre_grad.astype(BF16)
    second_part = dot_nt(gate_low, gate_full) + dot_nt(up_low, up_full)
    shape_rows = (grid.hi, grid.tensor, rows_half, width)
    branch_low, gain_two_grad = sum_rows(
        grid, True, second_part.astype(BF16).reshape(shape_rows), resid, cot_own, gain_second[None]
    )
    branch_low = branch_low.reshape(rows_all, width)
    gain_two_grad = jnp.sum(gain_two_grad, axis=0)
    gain_two_grad = gain_two_grad + grid.swap(gain_two_grad)
    feed_part = dot_nt(hidden, down_turned).astype(BF16)
    block_out, _ = sum_rows(
        grid, False, feed_part.reshape(shape_rows), resid, cot_own, gain_second[None]
    )
    block_out = block_out.reshape(block_in.shape)
    pair_grad = dot_tn(second_all, jnp.concatenate([gate_low, up_low], axis=1)).astype(BF16)
    down_grad = dot_tn(cot_all, hidden).astype(BF16)

    out_shift_grad = jnp.sum(branch_low.astype(F32), axis=0)
    mixed_grad = dot(branch_low, out_turned).reshape(flat)
    out_grad = dot_tn(branch_low, mixed).astype(BF16)
    state_grad = mixed_grad * gelu_branch
    _, pull_gelu = jax.vjp(jax.nn.gelu, gelu_pre)
    (gelu_pre_grad,) = pull_gelu((mixed_grad * state).reshape(rows_all, channels))
    gelu_low = gelu_pre_grad.astype(BF16)
    gelu_b_grad = jnp.sum(gelu_low.astype(F32), axis=0)
    decay_flat = decay.reshape(flat)
    next_decay = jnp.concatenate([decay_flat[:, 1:], jnp.ones_like(decay_flat[:, :1])], axis=1)
    tail_decay, local_carried = local_scan(next_decay, state_grad, True)
    head_decay = decay_flat[:, 0]
    from_right = prefix_wide(
        grid,
        jnp.stack([head_decay * tail_decay[:, 0], head_decay * local_carried[:, 0]]),
        True,
    )
    carried = (local_carried + tail_decay * from_right[:, None]).reshape(blocks.shape)
    prev_state = jnp.concatenate([state_in[:, None], state[:, :-1]], axis=1).reshape(blocks.shape)

    def lru_local(inlet_arg, forget_arg, block_arg, rate_arg):
        return lru_terms(inlet_arg, forget_arg, block_arg, rate_arg, starts)

    _, pull_lru = jax.vjp(lru_local, inlet_pre, forget_pre, blocks_wide, rate_wide)
    inlet_grad, forget_grad, block_direct, rate_grad = pull_lru((carried * prev_state, carried))
    inlet_low = inlet_grad.astype(BF16)
    forget_low = forget_grad.astype(BF16)
    inlet_b_grad = jnp.sum(inlet_low.astype(F32), axis=(0, 1))
    forget_b_grad = jnp.sum(forget_low.astype(F32), axis=(0, 1))
    gate_w_grads = jnp.stack(
        [
            jnp.einsum("sthc,sthd->hcd", blocks, low, preferred_element_type=F32)
            for low in (inlet_low, forget_low)
        ]
    )
    gate_w_grads = (
        gate_w_grads.reshape(2, head_count, grid.n, lane_own, block_size)
        .transpose(2, 0, 1, 3, 4)
        .reshape(width, block_size)
        .astype(BF16)
    )
    conv_grad = (
        block_direct
        + jnp.einsum("sthd,hcd->sthc", inlet_low, inlet_full, preferred_element_type=F32)
        + jnp.einsum("sthd,hcd->sthc", forget_low, forget_full, preferred_element_type=F32)
    )

    def conv_local(ext_arg, taps_arg, offset_arg):
        return causal_conv(ext_arg, marks_ext, taps_arg, offset_arg)

    _, pull_conv = jax.vjp(conv_local, extended, conv_taps, conv_offset)
    ext_grad, taps_grad, offset_grad = pull_conv(conv_grad.reshape(flat))
    rim_grad = shifted(ext_grad[:, :margin], "wide", -1)
    branch_input_grad = ext_grad[:, margin:] + jnp.concatenate(
        [jnp.zeros((seq_count, tok_count - margin, channels), F32), rim_grad], axis=1
    )
    input_low = branch_input_grad.astype(BF16).reshape(rows_all, channels)
    both_grad = dot_tn(normed, jnp.concatenate([gelu_low, input_low], axis=1)).astype(BF16)
    rec_grad = jnp.concatenate([both_grad, out_grad, gate_w_grads], axis=1)
    feed_grads, rec_grads = send_grads(grid, (pair_grad, down_grad, rec_grad), window, 3)
    rec_grads = jnp.concatenate(list(rec_grads), axis=1)
    gelu_w_grad = rec_grads[:, :channels]
    input_w_grad = rec_grads[:, channels : 2 * channels]
    out_grad = rec_grads[:, 2 * channels : 3 * channels]
    gate_w_grads = rec_grads[:, 3 * channels :].reshape(2, head_count, lane_own, block_size)

    def feed_weight_grad(got):
        pieces = []
        for place in range(grid.hi):
            begin = min(place * window_tiles, unit_tiles - window_tiles)
            skip = min(place * window_tiles - begin, window_tiles)
            if skip < window_tiles:
                pieces.append(got[place, :, skip * LANE :])
        return jnp.concatenate(pieces, axis=1).astype(F32)

    gate_grad, up_grad, down_grad = (feed_weight_grad(got) for got in feed_grads)
    down_grad = down_grad.T
    input_b_grad = jnp.sum(input_low.astype(F32), axis=0)
    first_part = (dot_nt(input_low, input_full) + dot_nt(gelu_low, gelu_full)).astype(BF16)
    first_grad = first_part.astype(F32) + grid.swap(first_part).astype(F32)
    _, pull_first = jax.vjp(rms_norm, inputs, gain_first)
    input_norm_grad, gain_one_grad = pull_first(first_grad)
    block_grad = (branch_low.astype(F32) + input_norm_grad).reshape(block_in.shape)

    lane_grads = jnp.stack(
        [
            v.reshape(channels)
            for v in (
                gelu_b_grad,
                input_b_grad,
                taps_grad[0],
                taps_grad[1],
                taps_grad[2],
                taps_grad[3],
                offset_grad,
                inlet_b_grad,
                forget_b_grad,
                rate_grad,
            )
        ]
    )
    lane_grads = (
        lane_grads.reshape(CONV + 6, head_count, grid.n, lane_own)
        .transpose(2, 0, 1, 3)
        .reshape(grid.n, -1)
    )
    thin_grads = jnp.concatenate(
        [v.reshape(grid.n, d_own) for v in (gain_one_grad, out_shift_grad, gain_two_grad)]
        + [lane_grads],
        axis=1,
    )
    thin = reduce_small(grid, thin_grads)
    gain_one_own, out_shift_own, gain_two_own = (
        thin[i * d_own : (i + 1) * d_own] for i in range(3)
    )
    lanes = thin[3 * d_own :].reshape(CONV + 6, head_count, lane_own)
    weight_shape = gelu_weight.shape
    return (
        block_out,
        block_grad,
        gain_one_own,
        gelu_w_grad.reshape(weight_shape),
        lanes[0],
        input_w_grad.reshape(weight_shape),
        lanes[1],
        lanes[2 : 2 + CONV],
        lanes[2 + CONV],
        gate_w_grads[0],
        lanes[3 + CONV],
        gate_w_grads[1],
        lanes[4 + CONV],
        lanes[5 + CONV],
        out_grad.T.reshape(out_weight.shape),
        out_shift_own,
        gain_two_own,
        gate_grad,
        up_grad,
        down_grad,
    )


def solution(mesh):
    in_specs = (
        P(None, "wide", None),
        P(None, "wide"),
        P(None, "wide", None),
        P("wide"),
        P("wide", "tensor", None),
        P("tensor", "wide"),
        P("wide", "tensor", None),
        P("tensor", "wide"),
        P(None, "tensor", "wide"),
        P("tensor", "wide"),
        P("tensor", "wide", None),
        P("tensor", "wide"),
        P("tensor", "wide", None),
        P("tensor", "wide"),
        P("tensor", "wide"),
        P("tensor", None, "wide"),
        P("wide"),
        P("wide"),
        P("wide", "tensor"),
        P("wide", "tensor"),
        P("tensor", "wide"),
    )
    out_specs = (
        P(None, "wide", None),
        P(None, "wide", None),
        P("wide"),
        P("wide", "tensor", None),
        P("tensor", "wide"),
        P("wide", "tensor", None),
        P("tensor", "wide"),
        P(None, "tensor", "wide"),
        P("tensor", "wide"),
        P("tensor", "wide", None),
        P("tensor", "wide"),
        P("tensor", "wide", None),
        P("tensor", "wide"),
        P("tensor", "wide"),
        P("tensor", None, "wide"),
        P("wide"),
        P("wide"),
        P("wide", "tensor"),
        P("wide", "tensor"),
        P("tensor", "wide"),
    )
    return jax.shard_map(local, mesh=mesh, in_specs=in_specs, out_specs=out_specs, check_vma=False)
```

time: 3500 us -> 1150 us (0.33)
  waiting for transfers between devices: 2390 us -> 40.2 us
  Pallas kernels: 0 us -> 715 us
  blocking collectives: 355 us -> 0 us
  local copies, waits for them, and re-layouts: 390 us -> 143 us
  matrix products: 190 us -> 143 us
  other arithmetic: 118 us -> 72.9 us
    reduce_scatter x8 -> x0, waiting for transfers between devices: 1640 us -> none  [the longest x1 384 us: local(): lax.psum_scatter(up_grad, 'wide', scatter_dimension=0, tiled=True)]
    pallas_call x0 -> x8, Pallas kernels: none -> 715 us  [the longest x1 239 us: bring_weights(): pl.pallas_call(functools.partial(weights_kernel, n, tensor), out_shape=[j...]
    all_gather x6 -> x0, waiting for transfers between devices: 283 us -> none  [the longest x1 101 us: local(): lax.all_gather(mlp_gate, 'wide', axis=0, tiled=True)]
    unnamed x31 -> x0, waiting for transfers between devices: 261 us -> none
    all_gather x13 -> x0, blocking collectives: 245 us -> none  [the longest x4 71.5 us: prefix(): gathered = jax.tree.map(lambda a: lax.all_gather(a, axis), part)]
    psum x3 -> x0, waiting for transfers between devices: 205 us -> none  [the longest x1 77.2 us: local(): lax.psum(feed_part.astype(jnp.bfloat16), 'tensor').astype(jnp.float32)]
    slice x99 -> x15, local copies, waits for them, and re-layouts: 205 us -> 35.6 us  [the longest x1 12.9 us: local(): input_full, gelu_full, out_turned = (rec_all[0], rec_all[1], rec_all[2])]
    unnamed x2 -> x0, blocking collectives: 109 us -> none
  transfers between devices with their start and end apart: 27 -> 17, of which waited for: 18 -> 10; matrix products, arithmetic and copies ran while one was open for 7% -> 6% of each run, Pallas kernels for 0% -> 7%
where the time goes in v1:
time: 1150 us; the launch traced here: 1140 us
  Pallas kernels  715 us (62%)
  local copies, waits for them, and re-layouts  143 us (12%)
  matrix products  143 us (12%)
  other arithmetic  72.9 us (6%)
  waiting for transfers between devices  40.2 us (3%)
  starting transfers between devices  22.9 us (2%)
    pallas_call x1, Pallas kernels, bring_weights(): pl.pallas_call(functools.partial(weights_kernel, n, tensor), out_shape=[j...  239 us
    pallas_call x1, Pallas kernels, send_grads(): pl.pallas_call(functools.partial(grads_kernel, grid.n, grid.tensor, spans...  232 us
    pallas_call x2, Pallas kernels, sum_rows(): pl.pallas_call(functools.partial(rows_kernel, second, grid.n, tensor), ou...  152 us
    pallas_call x1, Pallas kernels, bring_second(): pl.pallas_call(functools.partial(second_kernel, grid.n, grid.tensor), out...  76.7 us
    dot_general x6, matrix products, dot(): return jnp.dot(left, right, preferred_element_type=F32)  47.7 us
    dot_general x6, matrix products, dot_nt(): return jnp.einsum('ik,jk->ij', left, right, preferred_element_type=F32)  46.2 us
    dot_general x4, matrix products, dot_tn(): return jnp.einsum('ki,kj->ij', left, right, preferred_element_type=F32)  40.9 us
    concatenate x1, local copies, waits for them, and re-layouts, local(): rec_grad = jnp.concatenate([both_grad, out_grad, gate_w_grads], axis=1)  28.3 us
  transfers between devices with their start and end apart: 17, of which 10 were waited for; matrix products, arithmetic and copies ran while one was open for 6% of the time, Pallas kernels for 7%

profile of v1, /device:TPU:27, one launch (start us, length us, event | category | flops | bytes accessed | tf_op | source)
XLA Modules:
  0.0 1140.0 jit_solution(2996091295305462697)
XLA Ops:
  0.7 2.2 pad_maximum_fusion.2
  5.5 2.3 stack_reshape.10
  9.1 2.3 stack_reshape.4
  13.2 3.3 pad_maximum_fusion.1
  20.9 239.0 %bring_weights.1 = (bf16[3,16,160,1280]{3,2,1,0:T(8,128)(2,1)}, bf16[16,176,256]{2,1,0:T(8,128)(2,1)}, bf16[3,20,160,1024]{3,2,1,0:T(8,128)(2,1)}, bf16[4,2,128,2560]{3,2,1,0:T(8,128)(2,1)}) custom-call(bf16[3,16,160,1280]{3,2,1,0:T(8,128)(2,1)} %fusion.62.rec, ...), custom_call_target="tpu_custom_call", output_to_operand_aliasing={{0}: (0, {}), {1}: (1, {}), {2}: (2, {}), {3}: (3, {})} | custom-call | tf_op jit(solution)/shard_map/bring_weights/pallas_call | solution.py:419
  261.7 12.9 %fusion.91 = (bf16[1,16,160,1280]{3,2,1,0:T(8,128)(2,1)}, bf16[1,16,160,1280]{3,2,1,0:T(8,128)(2,1)}, bf16[1,16,160,1280]{3,2,1,0:T(8,128)(2,1)}) fusion(bf16[3,16,160,1280]{3,2,1,0:T(8,128)(2,1)} %get-tuple-element.44), kind=kLoop, calls=%fused_computation.294 | loop fusion | bytes 39321600 | tf_op jit(solution)/shard_map/slice | solution.py:1021
  277.3 5.2 fusion.20
  288.2 1.8 convert_element_type.126
  298.6 12.2 %fusion.90 = (bf16[1,16,160,1024]{3,2,1,0:T(8,128)(2,1)}, bf16[1,16,160,1024]{3,2,1,0:T(8,128)(2,1)}, bf16[1,16,160,1024]{3,2,1,0:T(8,128)(2,1)}) fusion(bf16[3,20,160,1024]{3,2,1,0:T(8,128)(2,1)} %get-tuple-element.48), kind=kLoop, calls=%fused_computation.293 | loop fusion | bytes 31457280 | tf_op jit(solution)/shard_map/slice | solution.py:1050
  310.8 6.4 multiply_multiply_fusion.5
  319.9 1.6 maximum_convert_fusion
  321.6 2.1 add_convert_fusion.1
  324.9 3.1 convert_multiply_fusion.3
  329.1 2.8 copy.271.a_ref
  331.9 2.5 copy.270
  334.4 2.8 copy.272.b_ref
  337.1 7.9 shard_map.356
  351.0 3.0 collective-permute-start.3
  355.4 2.6 collective-permute-done.4
  358.2 3.5 collective-permute-done.5
  364.5 6.2 fusion.99.part
  370.7 76.7 %bring_second.1 = (f32[128,2560]{1,0:T(8,128)}, bf16[4,2,128,2560]{3,2,1,0:T(8,128)(2,1)}) custom-call(f32[2,128,2560]{2,1,0:T(8,128)} %fusion.99.part, f32[128,2560]{1,0:T(8,128)} %dynamic-slice_bitcast_fusion.inputs, f32[1,2560]{1,0:T(1,128)} %broadcast_in_dim_reshape.4.shift, f32[1,2560]{1,0:T(1,128)} %broadcast_in_dim_reshape.5.gain), custom_call_target="tpu_custom_call" | custom-call | tf_op jit(solution)/shard_map/bring_second/pallas_call | solution.py:491
  447.5 9.9 fusion.101
  457.4 9.0 fusion.100
  466.4 13.9 %multiply_convert_fusion = (bf16[1024,1024]{0,1:T(8,128)(2,1)}, bf16[1024,1024]{0,1:T(8,128)(2,1)}, bf16[1024,1024]{0,1:T(8,128)(2,1)}) fusion(pred[1024]{0:T(1024)(128)(4,1)S(1)} %add_compare_fusion, f32[1024,1024]{0,1:T(8,128)} %fusion.100, f32[1024,1024]{0,1:T(8,128)S(1)} %fusion.101, bf16[1024,2560]{1,0:T(8,128)(2,1)} %bitcast.47, ...), kind=kOutput, calls=%fused_computation.19 | convolution fusion | flops 5398069248 | bytes 25166848 | tf_op jit(solution)/shard_map/dot_general | solution.py:912
  480.3 11.7 %fusion.102 = f32[1024,2560]{1,0:T(8,128)} fusion(bf16[1024,1024]{0,1:T(8,128)(2,1)} %get-tuple-element.191, bf16[2560,1024]{1,0:T(8,128)(2,1)} %bitcast.370), kind=kOutput, calls=%fused_computation.305 | convolution fusion | flops 5368709120 | bytes 17825792 | tf_op jit(solution)/shard_map/ik,jk->ij/dot_general | solution.py:916
  492.0 17.9 %convolution_convert_fusion.1 = bf16[2560,2048]{1,0:T(8,128)(2,1)} fusion(bf16[1024,2560]{1,0:T(8,128)(2,1)} %bitcast.411, bf16[1024,1024]{0,1:T(8,128)(2,1)S(1)} %copy-done.89, bf16[1024,1024]{0,1:T(8,128)(2,1)S(1)} %copy-done.90), kind=kOutput, calls=%fused_computation.3 | convolution fusion | flops 10751049728 | bytes 19922944 | tf_op jit(solution)/shard_map/ki,kj->ij/dot_general | solution.py:920
  509.9 9.9 add_convert_fusion
  519.9 73.0 %sum_second.1 = (bf16[2,128,2560]{2,1,0:T(8,128)(2,1)}, f32[8,2560]{1,0:T(8,128)}) custom-call(bf16[4,2,128,2560]{3,2,1,0:T(8,128)(2,1)} %bitcast.350, f32[128,2560]{1,0:T(8,128)} %get-tuple-element.49.resid, bf16[128,2560]{1,0:T(8,128)(2,1)} %dynamic-slice_bitcast_fusion.1.cot, f32[1,2560]{1,0:T(1,128)} %broadcast_in_dim_reshape.5.gain), custom_call_target="tpu_custom_call" | custom-call | tf_op jit(solution)/shard_map/sum_second/pallas_call | solution.py:679
  592.9 6.3 bitcast_convert_fusion
  599.4 10.1 convolution_convert_fusion.2
  609.5 7.4 convolution_convert_fusion.3
  616.9 3.4 fusion.92
  620.3 7.9 shard_map.357
  629.8 4.7 collective-permute-start.6
  634.5 3.5 convert_reduce_fusion.3
  639.1 2.8 copy.279
  644.1 79.2 %sum_feed.1 = (bf16[2,128,2560]{2,1,0:T(8,128)(2,1)}, f32[8,2560]{1,0:T(8,128)}) custom-call(bf16[4,2,128,2560]{3,2,1,0:T(8,128)(2,1)} %bitcast.349, f32[128,2560]{1,0:T(8,128)} %get-tuple-element.49.resid, bf16[128,2560]{1,0:T(8,128)(2,1)} %dynamic-slice_bitcast_fusion.1.cot, f32[1,2560]{1,0:T(1,128)} %broadcast_in_dim_reshape.5.gain), custom_call_target="tpu_custom_call" | custom-call | tf_op jit(solution)/shard_map/sum_feed/pallas_call | solution.py:679
  727.6 2.0 collective-permute-done.8
  730.2 3.0 collective-permute-done.9
  733.3 2.9 multiply_add_fusion
  736.2 2.8 copy.275
  739.0 4.5 convert_reduce_fusion.1
  748.6 2.6 multiply_reduce_fusion.3
  751.2 2.1 pad_add_fusion
  754.5 1.7 copy.285
  756.2 6.3 collective-permute-start.10
  762.5 2.3 fusion.34
  768.3 1.6 convert_reduce_fusion.2
  771.3 5.0 fusion.103
  776.3 5.9 fusion.10
  789.8 23.2 %collective-permute-done.11 = bf16[256,2560]{1,0:T(8,128)(2,1)} collective-permute-done((bf16[256,2560]{1,0:T(8,128)(2,1)}, bf16[256,2560]{1,0:T(8,128)(2,1)}, u32[]{:S(2)}, u32[]{:S(2)}) %collective-permute-start.11) | collective-permute-done | bytes 1310752 | tf_op jit(solution)/shard_map/ppermute | solution.py:36
  813.0 3.7 fusion.14
  816.7 6.7 convolution_convert_fusion
  823.4 16.9 %pad_maximum_fusion = bf16[2560,4096]{0,1:T(8,128)(2,1)} fusion(bf16[2560,256]{0,1:T(8,128)(2,1)S(1)} %copy.294, bf16[2560,1280]{0,1:T(8,128)(2,1)} %bitcast_convert_fusion, bf16[2560,2560]{0,1:T(8,128)(2,1)} %convolution_convert_fusion), kind=kLoop, calls=%fused_computation | loop fusion | flops 62914560 | bytes 41943040 | tf_op jit(solution)/shard_map/concatenate | solution.py:1176
  840.3 28.3 %copy.295 = bf16[2560,4096]{1,0:T(8,128)(2,1)} copy(bf16[2560,4096]{0,1:T(8,128)(2,1)} %pad_maximum_fusion) | data formatting | bytes 41943040 | tf_op jit(solution)/shard_map/concatenate | solution.py:1176
  868.6 231.7 %send_grads.1 = (bf16[3,4,160,1024]{3,2,1,0:T(8,128)(2,1)}, f32[4,160,1024]{2,1,0:T(8,128)}) custom-call(bf16[4,4,160,2048]{3,2,1,0:T(8,128)(2,1)} %bitcast.338, bf16[4,4,160,1024]{3,2,1,0:T(8,128)(2,1)} %bitcast.348, bf16[4,4,160,4096]{3,2,1,0:T(8,128)(2,1)} %bitcast.330), custom_call_target="tpu_custom_call" | custom-call | tf_op jit(solution)/shard_map/send_grads/pallas_call | solution.py:858
  1100.3 2.7 slice_bitcast_fusion
  1110.6 2.9 convert_bitcast_fusion
  1113.6 1.6 maximum_convert_fusion.2
  1115.4 4.2 fusion.11
  1121.4 1.9 slice_bitcast_fusion.7
  1124.4 2.2 collective-permute-done.15
  1126.7 2.8 collective-permute-start.16
  (399 shorter events, 93.1 us)
Async XLA Ops:
  7.9 4.7 copy-start.77
  7.9 4.8 copy-start.78
  7.9 4.9 copy-start.79
  7.9 5.0 copy-start.80
  7.9 5.0 copy-start.81
  7.9 5.1 copy-start.82
  7.9 5.1 copy-start.83
  8.0 5.1 copy-start.84
  8.0 5.2 copy-start.57
  8.0 5.2 copy-start.58
  276.9 14.0 %copy-start.62 = (f32[2,128]{1,0:T(2,128)}, f32[2,128]{1,0:T(2,128)S(1)}, u32[]{:S(2)}) copy-start(f32[2,128]{1,0:T(2,128)S(1)} %fusion.16) | copy-start | bytes 3076
  277.3 5.2 copy-start.36
  277.3 7.1 copy-start.88
  277.3 9.6 copy-start.13
  284.0 34.0 %collective-permute-start.1 = (bf16[2,3,1280]{2,0,1:T(2,128)(2,1)}, bf16[2,3,1280]{2,0,1:T(2,128)(2,1)}, u32[]{:S(2)}, u32[]{:S(2)}) collective-permute-start(bf16[2,3,1280]{2,0,1:T(2,128)(2,1)} %copy.322), channel_id=1, source_target_pairs={{0,2},{2,4},{4,6},{6,8},{8,10},{10,12},{12,14},{14,16},{16,18},{18... | collective-permute-start | bytes 46088 | tf_op jit(solution)/shard_map/ppermute | solution.py:44
  285.0 32.2 %collective-permute-start = (bf16[2,3]{1,0:T(2,128)(2,1)}, bf16[2,3]{1,0:T(2,128)(2,1)}, u32[]{:S(2)}, u32[]{:S(2)}) collective-permute-start(bf16[2,3]{1,0:T(2,128)(2,1)} %slice.489), channel_id=1, source_target_pairs={{0,2},{2,4},{4,6},{6,8},{8,10},{10,12},{12,14},{14,16},{16,18},{18... | collective-permute-start | bytes 44 | tf_op jit(solution)/shard_map/ppermute | solution.py:44
  288.2 5.6 copy-start.50
  298.6 12.2 %copy-start.37 = (bf16[2,128,2560]{2,1,0:T(8,128)(2,1)S(1)}, bf16[2,128,2560]{2,1,0:T(8,128)(2,1)}, u32[]{:S(2)}) copy-start(bf16[2,128,2560]{2,1,0:T(8,128)(2,1)} %copy-done.36) | copy-start | bytes 3932164
  310.8 7.0 copy-start.86
  318.0 6.5 copy-start.74
  337.1 9.1 copy-start.56
  337.1 9.8 copy-start.55
  346.0 4.3 collective-permute-start.2
  349.1 4.9 copy-start.52
  349.1 13.2 %copy-start.16 = (f32[256,1280]{1,0:T(8,128)S(1)}, f32[256,1280]{1,0:T(8,128)}, u32[]{:S(2)}) copy-start(f32[256,1280]{1,0:T(8,128)} %get-tuple-element.297) | copy-start | bytes 3932164
  351.0 4.2 collective-permute-start.3
  355.3 2.7 collective-permute-start.4
  358.1 3.6 collective-permute-start.5
  447.5 9.9 copy-start.87
  447.5 18.9 %slice-start.2 = ((s8[5242880]{0:T(1024)(128)(4,1)}), s8[4194304]{0:T(1024)(128)(4,1)S(1)}, s32[]{:S(2)}) async-start(s8[5242880]{0:T(1024)(128)(4,1)} %bitcast.359), calls=%async_computation.2 | async-start | bytes 8388608
  457.4 9.0 slice-start.3
  480.3 11.7 %copy-start.89 = (bf16[1024,1024]{0,1:T(8,128)(2,1)S(1)}, bf16[1024,1024]{0,1:T(8,128)(2,1)}, u32[]{:S(2)}) copy-start(bf16[1024,1024]{0,1:T(8,128)(2,1)} %get-tuple-element.190) | copy-start | bytes 6291460
  480.3 11.7 %copy-start.90 = (bf16[1024,1024]{0,1:T(8,128)(2,1)S(1)}, bf16[1024,1024]{0,1:T(8,128)(2,1)}, u32[]{:S(2)}) copy-start(bf16[1024,1024]{0,1:T(8,128)(2,1)} %get-tuple-element.191) | copy-start | bytes 6291460
  480.3 29.6 %slice-start.6 = ((s8[5242880]{0:T(1024)(128)(4,1)}), s8[4194304]{0:T(1024)(128)(4,1)S(1)}, s32[]{:S(2)}) async-start(s8[5242880]{0:T(1024)(128)(4,1)} %bitcast.366), calls=%async_computation.6 | async-start | bytes 8388608
  492.0 17.9 %slice-start.7 = ((s8[5242880]{0:T(1024)(128)(4,1)}), s8[1048576]{0:T(1024)(128)(4,1)S(1)}, s32[]{:S(2)}) async-start(s8[5242880]{0:T(1024)(128)(4,1)} %bitcast.366), calls=%async_computation.7 | async-start | bytes 2097152
  592.8 6.3 copy-start.2
  592.9 6.5 copy-start.91
  592.9 16.6 %slice-start.4 = ((s8[5242880]{0:T(1024)(128)(4,1)}), s8[4194304]{0:T(1024)(128)(4,1)S(1)}, s32[]{:S(2)}) async-start(s8[5242880]{0:T(1024)(128)(4,1)} %bitcast.362), calls=%async_computation.4 | async-start | bytes 8388608
  592.9 24.0 %slice-start = ((s8[6553600]{0:T(1024)(128)(4,1)}), s8[4194304]{0:T(1024)(128)(4,1)S(1)}, s32[]{:S(2)}) async-start(s8[6553600]{0:T(1024)(128)(4,1)} %bitcast.332), calls=%async_computation | async-start | bytes 8388608
  599.4 10.1 slice-start.5
  599.4 17.5 %slice-start.1 = ((s8[6553600]{0:T(1024)(128)(4,1)}), s8[2359296]{0:T(1024)(128)(4,1)S(1)}, s32[]{:S(2)}) async-start(s8[6553600]{0:T(1024)(128)(4,1)} %bitcast.332), calls=%async_computation.1 | async-start | bytes 4718592
  609.5 7.4 copy-start.7
  609.5 7.4 copy-start.17
  629.8 94.2 %collective-permute-start.6 = (f32[2,2,1280]{2,0,1:T(2,128)}, f32[2,2,1280]{2,0,1:T(2,128)S(1)}, u32[]{:S(2)}, u32[]{:S(2)}) collective-permute-start(f32[2,2,1280]{2,0,1:T(2,128)} %pad_maximum_fusion.21), channel_id=1, source_target_pairs={{0,2},{2,0},{4,6},{6,4},{8,10},{10,8},{12,14},{14,12},{16,18},{18,... | collective-permute-start | bytes 61448 | tf_op jit(solution)/shard_map/ppermute | solution.py:31
  638.2 85.1 %collective-permute-start.12 = (f32[2560]{0:T(1024)S(1)}, f32[2560]{0:T(1024)S(1)}, u32[]{:S(2)}, u32[]{:S(2)}) collective-permute-start(f32[2560]{0:T(1024)S(1)} %reduce_sum.141), channel_id=1, source_target_pairs={{0,1},{1,0},{2,3},{3,2},{4,5},{5,4},{6,7},{7,6},{8,9},{9,8},{10,11... | collective-permute-start | bytes 30728 | tf_op jit(solution)/shard_map/ppermute | solution.py:36
  724.0 2.7 collective-permute-start.7
  726.9 2.7 collective-permute-start.8
  729.6 3.6 collective-permute-start.9
  756.2 9.2 collective-permute-start.10
  771.3 5.0 copy-start.18
  771.3 5.0 copy-start.20
  776.3 7.4 copy-start.11
  782.2 30.8 %collective-permute-start.11 = (bf16[256,2560]{1,0:T(8,128)(2,1)}, bf16[256,2560]{1,0:T(8,128)(2,1)}, u32[]{:S(2)}, u32[]{:S(2)}) collective-permute-start(bf16[256,2560]{1,0:T(8,128)(2,1)} %fusion.10), channel_id=1, source_target_pairs={{0,1},{1,0},{2,3},{3,2},{4,5},{5,4},{6,7},{7,6},{8,9},{9,8},{10,11... | collective-permute-start | bytes 3932168 | tf_op jit(solution)/shard_map/ppermute | solution.py:36
  785.9 27.1 %copy-start.1 = (bf16[2,128,2560]{2,1,0:T(8,128)(2,1)S(1)}, bf16[2,128,2560]{2,1,0:T(8,128)(2,1)}, u32[]{:S(2)}) copy-start(bf16[2,128,2560]{2,1,0:T(8,128)(2,1)} %param.21) | copy-start | bytes 3932164
  785.9 27.1 %copy-start.46 = (f32[2560]{0:T(1024)S(1)}, f32[2560]{0:T(1024)}, u32[]{:S(2)}) copy-start(f32[2560]{0:T(1024)} %copy-done.45) | copy-start | bytes 30724
  785.9 27.1 %copy-start.64 = (f32[256]{0:T(256)S(1)}, f32[256]{0:T(256)}, u32[]{:S(2)}) copy-start(f32[256]{0:T(256)} %bitcast_rsqrt_fusion) | copy-start | bytes 3076
  789.8 26.9 %copy-start.19 = (bf16[2,128,1280]{2,1,0:T(8,128)(2,1)S(1)}, bf16[2,128,1280]{2,1,0:T(8,128)(2,1)}, u32[]{:S(2)}) copy-start(bf16[2,128,1280]{2,1,0:T(8,128)(2,1)} %copy-done.18) | copy-start | bytes 1966084
  789.8 26.9 %copy-start.21 = (bf16[256,1280]{1,0:T(8,128)(2,1)S(1)}, bf16[256,1280]{1,0:T(8,128)(2,1)}, u32[]{:S(2)}) copy-start(bf16[256,1280]{1,0:T(8,128)(2,1)} %get-tuple-element.179) | copy-start | bytes 1966084
  1104.7 5.2 copy-start.63
  1109.9 11.3 collective-permute-start.13
  1121.3 2.7 collective-permute-start.14
  1124.0 2.6 collective-permute-start.15
  1126.7 6.3 collective-permute-start.16
  1131.1 7.4 copy-start.35
  (53 other events, 120.8 us)

commit v2 on v1

--- a/solution.py
+++ b/solution.py
@@ -47,17 +47,6 @@
 
 def pick(values, index, axis=0):
     return lax.dynamic_index_in_dim(values, index, axis, keepdims=False)
-
-
-def reduce_small(grid, values):
-    bit = grid.n // 2
-    while bit:
-        halves = values.reshape(2, bit, -1)
-        mine = jnp.bitwise_and(lax.div(grid.w, bit), 1)
-        got = grid.flip(pick(halves, 1 - mine), bit)
-        values = pick(halves, mine) + got
-        bit //= 2
-    return values.reshape(-1)
 
 
 def prefix_wide(grid, part, reverse):
@@ -708,20 +697,34 @@
     return 16 if rows % 16 == 0 else 8
 
 
-def grads_kernel(n, tensor, spans, kept, *refs):
-    count = len(spans)
-    parts, apart, summed = refs[:count], refs[count], refs[count + 1]
-    refs = refs[count + 2 :]
+def grads_kernel(
+    n, tensor, spans, kept,
+    second, cot, normed, branch, gate_low, up_low, hidden, gelu_low, input_low, mixed, gates, first, thin,
+    apart, summed, first_other, thin_own, *refs,
+):
     stages = (n // LINE).bit_length() - 1
-    sends, keeps, gots = refs[:stages], refs[stages : 2 * stages], refs[2 * stages : 3 * stages]
-    ready, got_line, cube_sems, line_sems = refs[3 * stages :]
+    lists = [refs[i * stages : (i + 1) * stages] for i in range(6)]
+    sends, keeps, gots, thin_sends, thin_keeps, thin_gots = lists
+    (
+        made, ready, got_line, first_out, first_got, thin_ready, thin_line,
+        cube_sems, line_sems, first_sems, thin_sems, thin_line_sems,
+    ) = refs[6 * stages :]
     spot = Spot(n, tensor)
     hi = spot.hi
-    all_spans = sum(spans)
+    all_spans = len(spans)
     units = all_spans * hi
     step = pl.program_id(0)
     rows = ready.shape[1]
     each = tile_rows(rows)
+    last_step = units + stages - 1
+    sources = {
+        "gate": (second, gate_low),
+        "up": (second, up_low),
+        "down": (cot, hidden),
+        "gelu": (normed, gelu_low),
+        "input": (normed, input_low),
+        "out": (branch, mixed),
+    }
 
     def cube_copy(stage, unit):
         slot = lax.rem(unit, RING)
@@ -743,31 +746,109 @@
             device_id_type=MESH,
         )
 
+    def thin_copy(stage):
+        return remote(
+            thin_sends[stage], thin_gots[stage], thin_sems, stage, spot.flip(spot.bits[stage])
+        )
+
+    def thin_line_copy(place, sender):
+        return pltpu.make_async_remote_copy(
+            src_ref=thin_ready.at[place],
+            dst_ref=thin_line.at[sender],
+            send_sem=thin_line_sems.at[0, place],
+            recv_sem=thin_line_sems.at[1, sender],
+            device_id=spot.line(place),
+            device_id_type=MESH,
+        )
+
+    first_copy = remote(first_out, first_got, first_sems, 0, spot.cross)
+
     @pl.when(step == 0)
     def _():
-        spot.greet(*[spot.flip(bit) for bit in spot.bits])
-
-    begin = 0
-    for part, width in zip(parts, spans):
-        first, begin = begin * hi, begin + width
-
-        @pl.when(jnp.logical_and(step >= first, step < begin * hi))
-        def _(part=part):
-            slot = lax.rem(step, RING)
-
-            @pl.when(step >= RING)
-            def _():
-                cube_copy(0, step - RING).wait_send()
-
-            mine = spot.bit(1)
-            for k in range(sends[0].shape[1]):
-
-                def put(at, k=k):
-                    sends[0][slot, k, at, :] = part[0, 2 * k + 1 - mine, at, :]
-                    keeps[0][slot, k, at, :] = part[0, 2 * k + mine, at, :]
-
-                by_rows(rows, each, put)
-            cube_copy(0, step).start()
+        spot.greet(*[spot.flip(bit) for bit in spot.bits], spot.cross)
+
+        def put(at):
+            first_out[at, :] = first[at, :]
+
+        by_rows(first.shape[0], STEP, put)
+        first_copy.start()
+        mine = spot.bit(1)
+        for place in range(hi):
+            for k in range(thin_sends[0].shape[1]):
+                thin_sends[0][place, k] = thin[place, 2 * k + 1 - mine]
+                thin_keeps[0][place, k] = thin[place, 2 * k + mine]
+        thin_copy(0).start()
+
+    for stage in range(stages):
+
+        @pl.when(step == stage + 1)
+        def _(stage=stage):
+            thin_copy(stage).wait_recv()
+            if stage < stages - 1:
+                mine = spot.bit(spot.bits[stage + 1])
+                for place in range(hi):
+                    for k in range(thin_sends[stage + 1].shape[1]):
+                        a, b = 2 * k + 1 - mine, 2 * k + mine
+                        thin_sends[stage + 1][place, k] = (
+                            thin_keeps[stage][place, a] + thin_gots[stage][place, a]
+                        )
+                        thin_keeps[stage + 1][place, k] = (
+                            thin_keeps[stage][place, b] + thin_gots[stage][place, b]
+                        )
+                thin_copy(stage + 1).start()
+            else:
+                for place in range(hi):
+                    thin_ready[place] = thin_keeps[stage][place, 0] + thin_gots[stage][place, 0]
+                for distance in range(1, hi):
+                    thin_line_copy(spot.away(distance), spot.z).start()
+
+    @pl.when(step < units)
+    def _():
+        slot = lax.rem(step, RING)
+
+        @pl.when(step >= RING)
+        def _():
+            cube_copy(0, step - RING).wait_send()
+
+        for span, pieces in enumerate(spans):
+
+            @pl.when(step // hi == span)
+            def _(pieces=pieces):
+                for name, begin, width, to in pieces:
+                    if name == "gates":
+
+                        def put(at, width=width, to=to):
+                            made[at, to : to + width] = gates[0, at, :].astype(made.dtype)
+
+                        by_rows(made.shape[0], STEP, put)
+                        continue
+                    left, right = sources[name]
+
+                    def one(j, carry, left=left, right=right, begin=begin, width=width, to=to):
+                        at = pl.ds(pl.multiple_of(j * LANE, LANE), LANE)
+                        made[at, to : to + width] = lax.dot_general(
+                            left[:, at],
+                            right[:, begin : begin + width],
+                            (((0,), (0,)), ((), ())),
+                            preferred_element_type=F32,
+                        ).astype(made.dtype)
+                        return carry
+
+                    lax.fori_loop(0, made.shape[0] // LANE, one, 0)
+
+        mine = spot.bit(1)
+        for k in range(sends[0].shape[1]):
+
+            def put(at, k=k):
+                def block(i):
+                    at_made = pl.ds(pl.multiple_of(i * rows + at.start, each), each)
+                    return made[at_made, :].astype(BF16)
+
+                sends[0][slot, k, at, :] = block(2 * k + 1 - mine)
+                keeps[0][slot, k, at, :] = block(2 * k + mine)
+
+            by_rows(rows, each, put)
+        cube_copy(0, step).start()
 
     for stage in range(stages):
         unit = step - stage - 1
@@ -809,7 +890,7 @@
                 def _():
                     line_copy(span, place, spot.z).start()
 
-    @pl.when(step == units + stages - 1)
+    @pl.when(step == last_step)
     def _():
         for span in range(all_spans):
             for distance in range(1, hi):
@@ -833,49 +914,110 @@
         for stage in range(stages):
             for unit in range(units - RING, units):
                 cube_copy(stage, unit).wait_send()
-
-
-def send_grads(grid, parts, width, kept):
+            thin_copy(stage).wait_send()
+        value = thin_ready[spot.z]
+        for distance in range(1, hi):
+            place = spot.away(distance)
+            thin_line_copy(place, place).wait_recv()
+            thin_line_copy(place, spot.z).wait_send()
+            value = value + thin_line[place]
+        thin_own[...] = value
+        first_copy.wait()
+
+        def take(at):
+            first_other[at, :] = first_got[at, :]
+
+        by_rows(first.shape[0], STEP, take)
+
+
+def column_spans(widths, width):
+    spans, here, room = [], [], width
+    for name, size in widths:
+        begin = 0
+        while begin < size:
+            count = min(size - begin, room)
+            here.append((name, begin, count, width - room))
+            begin, room = begin + count, room - count
+            if room == 0:
+                spans, here, room = spans + [here], [], width
+    assert not here
+    return spans
+
+
+def send_grads(grid, feed, rec, gates, first, thin):
     hi, inner = grid.hi, grid.inner_size
-    rows = parts[0].shape[0] // grid.n
-    spans = [part.shape[1] // width for part in parts]
-    all_spans = sum(spans)
+    second, cot, gate_low, up_low, hidden = feed
+    normed, branch, gelu_low, input_low, mixed = rec
+    d = second.shape[1]
+    rows = d // grid.n
+    slab = d // hi
+    width = gate_low.shape[1]
+    kept = 3
+    channels = mixed.shape[1]
+    spans = column_spans([(name, width) for name in ("gate", "up", "down")], width) + column_spans(
+        [(name, channels) for name in ("gelu", "input", "out")] + [("gates", gates.shape[1])], width
+    )
+    all_spans = len(spans)
+    units = all_spans * hi
     stages = inner.bit_length() - 1
 
-    def part_spec(first, count):
-        def index(i):
-            unit = jnp.clip(i - first * hi, 0, count * hi - 1)
-            return (lax.rem(unit, hi), 0, 0, unit // hi)
-
-        return pl.BlockSpec((1, inner, rows, width), index)
-
-    firsts = [sum(spans[:i]) for i in range(len(spans))]
-    apart = (kept, hi, rows, width)
-    summed = (all_spans - kept, rows, width)
-    halves = [
-        pltpu.VMEM((RING, inner >> (stage + 1), rows, width), BF16) for stage in range(stages)
-    ]
+    def place_of(i):
+        return lax.rem(jnp.minimum(i, units - 1), hi)
+
+    def slab_of(a):
+        return pl.BlockSpec((a.shape[0], slab), lambda i: (0, place_of(i)))
+
+    def whole(a):
+        zeros = (0,) * a.ndim
+        return pl.BlockSpec(a.shape, lambda i: zeros, pipeline_mode=pl.Buffered(1))
+
+    apart = jax.ShapeDtypeStruct((kept, hi, rows, width), BF16)
+    summed = jax.ShapeDtypeStruct((all_spans - kept, rows, width), F32)
+    other = jax.ShapeDtypeStruct(first.shape, BF16)
+    thin = thin.reshape(hi, inner, 8, thin.shape[1] // 8)
+    thin_shape = thin.shape[2:]
+    thin_own = jax.ShapeDtypeStruct(thin_shape, F32)
+    outs = [apart, summed, other, thin_own]
+
+    def halves(lead, tail, kind):
+        return [
+            pltpu.VMEM((lead, inner >> (stage + 1)) + tail, kind) for stage in range(stages)
+        ]
+
+    gates = gates.reshape(hi, slab, gates.shape[1])
     return pl.pallas_call(
         functools.partial(grads_kernel, grid.n, grid.tensor, spans, kept),
-        grid=(all_spans * hi + stages,),
-        out_shape=[jax.ShapeDtypeStruct(apart, BF16), jax.ShapeDtypeStruct(summed, F32)],
-        in_specs=[part_spec(first, count) for first, count in zip(firsts, spans)],
-        out_specs=[
-            pl.BlockSpec(apart, lambda i: (0, 0, 0, 0)),
-            pl.BlockSpec(summed, lambda i: (0, 0, 0)),
-        ],
-        scratch_shapes=halves * 3
+        grid=(units + stages,),
+        out_shape=outs,
+        in_specs=[slab_of(a) for a in (second, cot, normed, branch)]
+        + [whole(a) for a in (gate_low, up_low, hidden, gelu_low, input_low, mixed)]
+        + [pl.BlockSpec((1,) + gates.shape[1:], lambda i: (place_of(i), 0, 0))]
+        + [whole(first), whole(thin)],
+        out_specs=[whole(a) for a in outs],
+        scratch_shapes=halves(RING, (rows, width), BF16) * 3
+        + halves(hi, thin_shape, F32) * 3
         + [
-            pltpu.VMEM((all_spans * hi, rows, width), BF16),
+            pltpu.VMEM((slab, width), BF16 if rows % 16 == 0 else F32),
+            pltpu.VMEM((units, rows, width), BF16),
             pltpu.VMEM((all_spans, hi, rows, width), BF16),
+            pltpu.VMEM(first.shape, BF16),
+            pltpu.VMEM(first.shape, BF16),
+            pltpu.VMEM((hi,) + thin_shape, F32),
+            pltpu.VMEM((hi,) + thin_shape, F32),
             pltpu.SemaphoreType.DMA((stages, 2, RING)),
-            pltpu.SemaphoreType.DMA((2, all_spans * hi)),
+            pltpu.SemaphoreType.DMA((2, units)),
+            pltpu.SemaphoreType.DMA((2, 1)),
+            pltpu.SemaphoreType.DMA((2, stages)),
+            pltpu.SemaphoreType.DMA((2, hi)),
         ],
         compiler_params=pltpu.CompilerParams(
             collective_id=4, has_side_effects=True, vmem_limit_bytes=GRANT
         ),
         name="send_grads",
-    )(*[part.reshape(hi, inner, rows, part.shape[1]) for part in parts])
+    )(
+        second, cot, normed, branch, gate_low, up_low, hidden, gelu_low, input_low, mixed, gates,
+        first, thin,
+    )
 
 
 def rms_norm(values, gain):
@@ -1106,18 +1248,14 @@
     )
     branch_low = branch_low.reshape(rows_all, width)
     gain_two_grad = jnp.sum(gain_two_grad, axis=0)
-    gain_two_grad = gain_two_grad + grid.swap(gain_two_grad)
     feed_part = dot_nt(hidden, down_turned).astype(BF16)
     block_out, _ = sum_rows(
         grid, False, feed_part.reshape(shape_rows), resid, cot_own, gain_second[None]
     )
     block_out = block_out.reshape(block_in.shape)
-    pair_grad = dot_tn(second_all, jnp.concatenate([gate_low, up_low], axis=1)).astype(BF16)
-    down_grad = dot_tn(cot_all, hidden).astype(BF16)
 
     out_shift_grad = jnp.sum(branch_low.astype(F32), axis=0)
     mixed_grad = dot(branch_low, out_turned).reshape(flat)
-    out_grad = dot_tn(branch_low, mixed).astype(BF16)
     state_grad = mixed_grad * gelu_branch
     _, pull_gelu = jax.vjp(jax.nn.gelu, gelu_pre)
     (gelu_pre_grad,) = pull_gelu((mixed_grad * state).reshape(rows_all, channels))
@@ -1172,32 +1310,13 @@
         [jnp.zeros((seq_count, tok_count - margin, channels), F32), rim_grad], axis=1
     )
     input_low = branch_input_grad.astype(BF16).reshape(rows_all, channels)
-    both_grad = dot_tn(normed, jnp.concatenate([gelu_low, input_low], axis=1)).astype(BF16)
-    rec_grad = jnp.concatenate([both_grad, out_grad, gate_w_grads], axis=1)
-    feed_grads, rec_grads = send_grads(grid, (pair_grad, down_grad, rec_grad), window, 3)
-    rec_grads = jnp.concatenate(list(rec_grads), axis=1)
-    gelu_w_grad = rec_grads[:, :channels]
-    input_w_grad = rec_grads[:, channels : 2 * channels]
-    out_grad = rec_grads[:, 2 * channels : 3 * channels]
-    gate_w_grads = rec_grads[:, 3 * channels :].reshape(2, head_count, lane_own, block_size)
-
-    def feed_weight_grad(got):
-        pieces = []
-        for place in range(grid.hi):
-            begin = min(place * window_tiles, unit_tiles - window_tiles)
-            skip = min(place * window_tiles - begin, window_tiles)
-            if skip < window_tiles:
-                pieces.append(got[place, :, skip * LANE :])
-        return jnp.concatenate(pieces, axis=1).astype(F32)
-
-    gate_grad, up_grad, down_grad = (feed_weight_grad(got) for got in feed_grads)
-    down_grad = down_grad.T
     input_b_grad = jnp.sum(input_low.astype(F32), axis=0)
-    first_part = (dot_nt(input_low, input_full) + dot_nt(gelu_low, gelu_full)).astype(BF16)
-    first_grad = first_part.astype(F32) + grid.swap(first_part).astype(F32)
-    _, pull_first = jax.vjp(rms_norm, inputs, gain_first)
-    input_norm_grad, gain_one_grad = pull_first(first_grad)
-    block_grad = (branch_low.astype(F32) + input_norm_grad).reshape(block_in.shape)
+    first_part = dot_nt(input_low, input_full) + dot_nt(gelu_low, gelu_full)
+    scale_first = lax.rsqrt(jnp.mean(inputs * inputs, axis=-1, keepdims=True) + 1e-06)
+    gain_one_grad = jnp.sum(first_part * inputs * scale_first, axis=0)
+    first_part = first_part.astype(BF16)
+    gain_grads = jnp.stack([gain_one_grad, gain_two_grad])
+    gain_grads = gain_grads + grid.swap(gain_grads)
 
     lane_grads = jnp.stack(
         [
@@ -1222,11 +1341,40 @@
         .reshape(grid.n, -1)
     )
     thin_grads = jnp.concatenate(
-        [v.reshape(grid.n, d_own) for v in (gain_one_grad, out_shift_grad, gain_two_grad)]
+        [v.reshape(grid.n, d_own) for v in (gain_grads[0], out_shift_grad, gain_grads[1])]
         + [lane_grads],
         axis=1,
     )
-    thin = reduce_small(grid, thin_grads)
+    feed_grads, rec_grads, first_other, thin = send_grads(
+        grid,
+        (second_all, cot_all, gate_low, up_low, hidden),
+        (normed, branch_low, gelu_low, input_low, mixed),
+        gate_w_grads,
+        first_part,
+        thin_grads,
+    )
+    thin = thin.reshape(-1)
+    rec_grads = jnp.concatenate(list(rec_grads), axis=1)
+    gelu_w_grad = rec_grads[:, :channels]
+    input_w_grad = rec_grads[:, channels : 2 * channels]
+    out_grad = rec_grads[:, 2 * channels : 3 * channels]
+    gate_w_grads = rec_grads[:, 3 * channels :].reshape(2, head_count, lane_own, block_size)
+
+    def feed_weight_grad(got):
+        pieces = []
+        for place in range(grid.hi):
+            begin = min(place * window_tiles, unit_tiles - window_tiles)
+            skip = min(place * window_tiles - begin, window_tiles)
+            if skip < window_tiles:
+                pieces.append(got[place, :, skip * LANE :])
+        return jnp.concatenate(pieces, axis=1).astype(F32)
+
+    gate_grad, up_grad, down_grad = (feed_weight_grad(got) for got in feed_grads)
+    down_grad = down_grad.T
+    first_grad = first_part.astype(F32) + first_other.astype(F32)
+    _, pull_first = jax.vjp(rms_norm, inputs, gain_first)
+    input_norm_grad, _ = pull_first(first_grad)
+    block_grad = (branch_low.astype(F32) + input_norm_grad).reshape(block_in.shape)
     gain_one_own, out_shift_own, gain_two_own = (
         thin[i * d_own : (i + 1) * d_own] for i in range(3)
     )

time: 1150 us -> 1040 us (0.904)
  matrix products: 143 us -> 106 us
  local copies, waits for them, and re-layouts: 143 us -> 107 us
  waiting for transfers between devices: 40.2 us -> 13.3 us
  other arithmetic: 72.9 us -> 54.6 us
    dot_general x4 -> x0, matrix products: 40.9 us -> none  [dot_tn(): return jnp.einsum('ki,kj->ij', left, right, preferred_element_type=F32)]
    concatenate x6 -> x1, local copies, waits for them, and re-layouts: 33.4 us -> 0.1 us  [local(): jnp.concatenate([v.reshape(grid.n, d_own) for v in (gain_grads[0], out_sh...]
    ppermute x2 -> x1, waiting for transfers between devices: 23.2 us -> 1.16 us  [swap(): return lax.ppermute(value, 'tensor', pairs)]
    concatenate x1 -> x0, other arithmetic: 16.9 us -> none  [local(): rec_grad = jnp.concatenate([both_grad, out_grad, gate_w_grads], axis=1)]
  transfers between devices with their start and end apart: 17 -> 12, of which waited for: 10 -> 7; matrix products, arithmetic and copies ran while one was open for 6% -> 6% of each run, Pallas kernels for 7% -> 8%
where the time goes in v2:
time: 1040 us; the launch traced here: 1030 us
  Pallas kernels  724 us (70%)
  local copies, waits for them, and re-layouts  107 us (10%)
  matrix products  106 us (10%)
  other arithmetic  54.6 us (5%)
  starting transfers between devices  19.9 us (2%)
  waiting for transfers between devices  13.3 us (1%)
    pallas_call x1, Pallas kernels, send_grads(): pl.pallas_call(functools.partial(grads_kernel, grid.n, grid.tensor, spans...  240 us
    pallas_call x1, Pallas kernels, bring_weights(): pl.pallas_call(functools.partial(weights_kernel, n, tensor), out_shape=[j...  239 us
    pallas_call x2, Pallas kernels, sum_rows(): pl.pallas_call(functools.partial(rows_kernel, second, grid.n, tensor), ou...  153 us
    pallas_call x1, Pallas kernels, bring_second(): pl.pallas_call(functools.partial(second_kernel, grid.n, grid.tensor), out...  76.6 us
    dot_general x6, matrix products, dot(): return jnp.dot(left, right, preferred_element_type=F32)  52.4 us
    dot_general x6, matrix products, dot_nt(): return jnp.einsum('ik,jk->ij', left, right, preferred_element_type=F32)  46.2 us
  transfers between devices with their start and end apart: 12, of which 7 were waited for; matrix products, arithmetic and copies ran while one was open for 6% of the time, Pallas kernels for 8%

profile of v2, /device:TPU:27, one launch (start us, length us, event | category | flops | bytes accessed | tf_op | source)
XLA Modules:
  0.0 1027.9 jit_solution(11083436467134059088)
XLA Ops:
  0.7 2.2 pad_maximum_fusion.1
  2.9 1.5 slice_bitcast_fusion.6
  5.5 2.3 stack_reshape.10
  9.1 2.3 stack_reshape.4
  13.2 3.3 pad_maximum_fusion
  20.9 239.2 %bring_weights.1 = (bf16[3,16,160,1280]{3,2,1,0:T(8,128)(2,1)}, bf16[16,176,256]{2,1,0:T(8,128)(2,1)}, bf16[3,20,160,1024]{3,2,1,0:T(8,128)(2,1)}, bf16[4,2,128,2560]{3,2,1,0:T(8,128)(2,1)}) custom-call(bf16[3,16,160,1280]{3,2,1,0:T(8,128)(2,1)} %fusion.54.rec, ...), custom_call_target="tpu_custom_call", output_to_operand_aliasing={{0}: (0, {}), {1}: (1, {}), {2}: (2, {}), {3}: (3, {})} | custom-call | tf_op jit(solution)/shard_map/bring_weights/pallas_call | solution.py:408
  261.9 12.9 %fusion.82 = (bf16[1,16,160,1280]{3,2,1,0:T(8,128)(2,1)}, bf16[1,16,160,1280]{3,2,1,0:T(8,128)(2,1)}, bf16[1,16,160,1280]{3,2,1,0:T(8,128)(2,1)}) fusion(bf16[3,16,160,1280]{3,2,1,0:T(8,128)(2,1)} %get-tuple-element.46), kind=kLoop, calls=%fused_computation.275 | loop fusion | bytes 39321600 | tf_op jit(solution)/shard_map/slice | solution.py:1163
  277.5 5.2 fusion.16
  285.2 1.4 copy.253
  287.9 1.8 convert_element_type.110
  297.8 12.4 %fusion.81 = (bf16[1,16,160,1024]{3,2,1,0:T(8,128)(2,1)}, bf16[1,16,160,1024]{3,2,1,0:T(8,128)(2,1)}, bf16[1,16,160,1024]{3,2,1,0:T(8,128)(2,1)}) fusion(bf16[3,20,160,1024]{3,2,1,0:T(8,128)(2,1)} %get-tuple-element.50), kind=kLoop, calls=%fused_computation.274 | loop fusion | bytes 31457280 | tf_op jit(solution)/shard_map/slice | solution.py:1192
  310.2 6.4 multiply_multiply_fusion.5
  318.6 1.6 maximum_convert_fusion
  320.3 2.2 add_convert_fusion.1
  323.6 3.1 convert_multiply_fusion.3
  327.8 2.8 copy.261.a_ref
  330.6 2.5 copy.260
  333.1 2.8 copy.262.b_ref
  335.9 7.9 shard_map.356
  346.3 1.5 slice.654
  349.7 3.3 collective-permute-start.3
  354.4 2.6 collective-permute-done.4
  357.2 3.5 collective-permute-done.5
  363.5 6.2 fusion.90.part
  369.8 76.6 %bring_second.1 = (f32[128,2560]{1,0:T(8,128)}, bf16[4,2,128,2560]{3,2,1,0:T(8,128)(2,1)}) custom-call(f32[2,128,2560]{2,1,0:T(8,128)} %fusion.90.part, f32[128,2560]{1,0:T(8,128)} %dynamic-slice_bitcast_fusion.inputs, f32[1,2560]{1,0:T(1,128)} %broadcast_in_dim_reshape.4.shift, f32[1,2560]{1,0:T(1,128)} %broadcast_in_dim_reshape.5.gain), custom_call_target="tpu_custom_call" | custom-call | tf_op jit(solution)/shard_map/bring_second/pallas_call | solution.py:480
  446.4 10.5 %fusion.92 = f32[1024,1024]{1,0:T(8,128)} fusion(bf16[1024,2560]{1,0:T(8,128)(2,1)} %bitcast.343, bf16[2560,1024]{1,0:T(8,128)(2,1)} %bitcast.353), kind=kOutput, calls=%fused_computation.285 | convolution fusion | flops 5368709120 | bytes 14680064 | tf_op jit(solution)/shard_map/dot_general | solution.py:1054
  457.0 9.5 fusion.91
  466.5 13.8 %multiply_convert_fusion = (bf16[1024,1024]{1,0:T(8,128)(2,1)S(1)}, bf16[1024,1024]{1,0:T(8,128)(2,1)S(1)}, bf16[1024,1024]{1,0:T(8,128)(2,1)}) fusion(pred[1024]{0:T(1024)(128)(4,1)S(1)} %add_compare_fusion, f32[1024,1024]{1,0:T(8,128)} %fusion.91, f32[1024,1024]{1,0:T(8,128)} %fusion.92, bf16[1024,2560]{1,0:T(8,128)(2,1)} %bitcast.47.cot, ...), kind=kOutput, calls=%fused_computation.11 | convolution fusion | flops 5398069248 | bytes 25166848 | tf_op jit(solution)/shard_map/dot_general | solution.py:1054
  480.3 8.4 fusion.93
  488.7 9.9 add_convert_fusion
  498.6 73.1 %sum_second.1 = (bf16[2,128,2560]{2,1,0:T(8,128)(2,1)}, f32[8,2560]{1,0:T(8,128)}) custom-call(bf16[4,2,128,2560]{3,2,1,0:T(8,128)(2,1)} %bitcast.338, f32[128,2560]{1,0:T(8,128)} %get-tuple-element.51.resid, bf16[128,2560]{1,0:T(8,128)(2,1)} %dynamic-slice_bitcast_fusion.1.cot, f32[1,2560]{1,0:T(1,128)} %broadcast_in_dim_reshape.5.gain), custom_call_target="tpu_custom_call" | custom-call | tf_op jit(solution)/shard_map/sum_second/pallas_call | solution.py:668
  571.8 2.2 convert_reduce_fusion
  574.0 7.1 fusion.83
  581.0 8.0 shard_map.357
  590.6 4.7 collective-permute-start.6
  595.3 3.5 convert_reduce_fusion.4
  598.9 10.2 convolution_convert_fusion
  609.7 2.9 copy.269
  612.6 1.6 copy.270
  614.9 79.6 %sum_feed.1 = (bf16[2,128,2560]{2,1,0:T(8,128)(2,1)}, f32[8,2560]{1,0:T(8,128)}) custom-call(bf16[4,2,128,2560]{3,2,1,0:T(8,128)(2,1)} %bitcast.337, f32[128,2560]{1,0:T(8,128)} %get-tuple-element.51.resid, bf16[128,2560]{1,0:T(8,128)(2,1)} %dynamic-slice_bitcast_fusion.1.cot, f32[1,2560]{1,0:T(1,128)} %broadcast_in_dim_reshape.5.gain), custom_call_target="tpu_custom_call" | custom-call | tf_op jit(solution)/shard_map/sum_feed/pallas_call | solution.py:668
  694.6 1.6 collective-permute-start.7
  697.4 2.1 collective-permute-start.8
  699.6 1.4 collective-permute-done.8
  702.4 2.4 collective-permute-done.9
  704.9 2.9 multiply_add_fusion
  707.8 2.8 copy.265
  710.6 5.1 convert_reduce_fusion.2
  722.1 2.6 multiply_reduce_fusion.3
  724.8 2.1 pad_add_fusion
  728.0 2.4 copy.275
  730.4 5.8 collective-permute-start.10
  736.3 2.3 pad_maximum_fusion.2
  739.5 1.4 reduce_sum.160
  740.9 2.5 copy.305
  743.5 2.2 copy.276
  745.7 1.4 broadcast_select_fusion
  749.1 5.0 fusion.94
  754.2 6.4 fusion.14
  764.4 239.6 %send_grads.1 = (bf16[3,4,160,1024]{3,2,1,0:T(8,128)(2,1)}, f32[4,160,1024]{2,1,0:T(8,128)}, bf16[256,2560]{1,0:T(8,128)(2,1)}, f32[8,160]{1,0:T(8,128)}) custom-call(bf16[1024,2560]{1,0:T(8,128)(2,1)} %bitcast.344, bf16[1024,2560]{1,0:T(8,128)(2,1)} %bitcast.47.cot, bf16[256,2560]{1,0:T(8,128)(2,1)} %get-tuple-element.222.normed, ...), custom_call_target="tpu_custom_call" | custom-call | tf_op jit(solution)/shard_map/send_grads/pallas_call | solution.py:988
  1004.0 2.7 slice_bitcast_fusion
  1016.0 2.6 fusion.7
  1019.9 2.9 convert_bitcast_fusion
  1022.9 1.6 maximum_convert_fusion.2
  1024.5 1.6 maximum_convert_fusion.1
  (360 shorter events, 69.7 us)
Async XLA Ops:
  7.9 4.5 copy-start.66
  7.9 4.6 copy-start.76
  7.9 4.7 copy-start.77
  7.9 4.8 copy-start.78
  7.9 4.9 copy-start.79
  7.9 5.0 copy-start.80
  7.9 5.0 copy-start.81
  7.9 5.1 copy-start.82
  7.9 5.1 copy-start.83
  8.0 5.1 copy-start.84
  8.0 5.2 copy-start.56
  8.0 5.2 copy-start.57
  277.1 13.5 %copy-start.62 = (f32[2,128]{1,0:T(2,128)}, f32[2,128]{1,0:T(2,128)S(1)}, u32[]{:S(2)}) copy-start(f32[2,128]{1,0:T(2,128)S(1)} %fusion.8) | copy-start | bytes 3076
  277.4 5.2 copy-start.35
  277.5 6.8 copy-start.87
  277.5 9.2 copy-start.10
  284.2 32.6 %collective-permute-start.1 = (bf16[2,3,1280]{2,0,1:T(2,128)(2,1)}, bf16[2,3,1280]{2,0,1:T(2,128)(2,1)}, u32[]{:S(2)}, u32[]{:S(2)}) collective-permute-start(bf16[2,3,1280]{2,0,1:T(2,128)(2,1)} %copy.308), channel_id=1, source_target_pairs={{0,2},{2,4},{4,6},{6,8},{8,10},{10,12},{12,14},{14,16},{16,18},{18... | collective-permute-start | bytes 46088 | tf_op jit(solution)/shard_map/ppermute | solution.py:44
  284.3 3.6 copy-start.85
  284.9 31.7 %collective-permute-start = (bf16[2,3]{1,0:T(2,128)(2,1)}, bf16[2,3]{1,0:T(2,128)(2,1)S(1)}, u32[]{:S(2)}, u32[]{:S(2)}) collective-permute-start(bf16[2,3]{1,0:T(2,128)(2,1)} %slice.485), channel_id=1, source_target_pairs={{0,2},{2,4},{4,6},{6,8},{8,10},{10,12},{12,14},{14,16},{16,18},{18... | collective-permute-start | bytes 44 | tf_op jit(solution)/shard_map/ppermute | solution.py:44
  287.9 5.0 copy-start.46
  289.7 3.4 copy-start.44
  289.7 3.4 copy-start.12
  293.3 3.3 copy-start.9
  297.8 12.4 %copy-start.36 = (bf16[2,128,2560]{2,1,0:T(8,128)(2,1)S(1)}, bf16[2,128,2560]{2,1,0:T(8,128)(2,1)}, u32[]{:S(2)}) copy-start(bf16[2,128,2560]{2,1,0:T(8,128)(2,1)} %copy-done.35) | copy-start | bytes 3932164
  310.2 6.4 copy-start.86
  316.7 3.5 copy-start.67
  316.7 3.5 copy-start.69
  316.7 3.5 copy-start.71
  316.7 6.4 copy-start.73
  323.1 3.5 copy-start.6
  335.9 9.1 copy-start.54
  335.9 9.8 copy-start.53
  344.7 4.4 collective-permute-start.2
  347.8 5.2 copy-start.51
  347.8 13.5 %copy-start.15 = (f32[256,1280]{1,0:T(8,128)S(1)}, f32[256,1280]{1,0:T(8,128)}, u32[]{:S(2)}) copy-start(f32[256,1280]{1,0:T(8,128)} %get-tuple-element.303) | copy-start | bytes 3932164
  349.7 4.5 collective-permute-start.3
  354.3 2.7 collective-permute-start.4
  357.1 3.6 collective-permute-start.5
  446.4 10.6 %copy-start.13 = (bf16[4,2,128,2560]{3,2,1,0:T(8,128)(2,1)S(1)}, bf16[4,2,128,2560]{3,2,1,0:T(8,128)(2,1)}, u32[]{:S(2)}) copy-start(bf16[4,2,128,2560]{3,2,1,0:T(8,128)(2,1)} %get-tuple-element.49) | copy-start | bytes 15728644
  446.4 20.0 %slice-start = ((s8[5242880]{0:T(1024)(128)(4,1)}), s8[4194304]{0:T(1024)(128)(4,1)S(1)}, s32[]{:S(2)}) async-start(s8[5242880]{0:T(1024)(128)(4,1)} %bitcast.350), calls=%async_computation | async-start | bytes 8388608
  457.0 9.5 slice-start.1
  457.0 23.3 %slice-start.4 = ((s8[5242880]{0:T(1024)(128)(4,1)}), s8[4194304]{0:T(1024)(128)(4,1)S(1)}, s32[]{:S(2)}) async-start(s8[5242880]{0:T(1024)(128)(4,1)} %bitcast.358), calls=%async_computation.4 | async-start | bytes 8388608
  457.0 31.7 %slice-start.2 = ((s8[5242880]{0:T(1024)(128)(4,1)}), s8[4194304]{0:T(1024)(128)(4,1)S(1)}, s32[]{:S(2)}) async-start(s8[5242880]{0:T(1024)(128)(4,1)} %bitcast.354), calls=%async_computation.2 | async-start | bytes 8388608
  466.5 13.8 %slice-start.5 = ((s8[5242880]{0:T(1024)(128)(4,1)}), s8[1048576]{0:T(1024)(128)(4,1)S(1)}, s32[]{:S(2)}) async-start(s8[5242880]{0:T(1024)(128)(4,1)} %bitcast.358), calls=%async_computation.5 | async-start | bytes 2097152
  466.5 22.2 %slice-start.3 = ((s8[5242880]{0:T(1024)(128)(4,1)}), s8[1048576]{0:T(1024)(128)(4,1)S(1)}, s32[]{:S(2)}) async-start(s8[5242880]{0:T(1024)(128)(4,1)} %bitcast.354), calls=%async_computation.3 | async-start | bytes 2097152
  480.2 8.4 copy-start.26
  480.2 8.4 copy-start.25
  590.6 103.9 %collective-permute-start.6 = (f32[2,2,1280]{2,0,1:T(2,128)}, f32[2,2,1280]{2,0,1:T(2,128)S(1)}, u32[]{:S(2)}, u32[]{:S(2)}) collective-permute-start(f32[2,2,1280]{2,0,1:T(2,128)} %pad_maximum_fusion.20), channel_id=1, source_target_pairs={{0,2},{2,0},{4,6},{6,4},{8,10},{10,8},{12,14},{14,12},{16,18},{18,... | collective-permute-start | bytes 61448 | tf_op jit(solution)/shard_map/ppermute | solution.py:31
  694.6 2.8 collective-permute-start.7
  697.4 3.6 collective-permute-start.8
  701.1 3.7 collective-permute-start.9
  710.6 5.1 copy-start.7
  710.6 5.1 copy-start.59
  728.0 8.2 copy-start.22
  730.4 13.1 %collective-permute-start.10 = (f32[2,3,1280]{2,0,1:T(2,128)}, f32[2,3,1280]{2,0,1:T(2,128)}, u32[]{:S(2)}, u32[]{:S(2)}) collective-permute-start(f32[2,3,1280]{2,0,1:T(2,128)} %copy.275), channel_id=1, source_target_pairs={{0,30},{2,0},{4,2},{6,4},{8,6},{10,8},{12,10},{14,12},{16,14},{18,... | collective-permute-start | bytes 92168 | tf_op jit(solution)/shard_map/ppermute | solution.py:44
  749.0 5.1 copy-start.16
  749.1 5.1 copy-start.1
  749.1 5.1 copy-start.17
  749.1 5.1 copy-start.75
  754.1 6.7 copy-start.39
  754.1 6.7 copy-start.48
  754.2 6.7 copy-start.47
  754.2 6.8 copy-start.49
  760.6 2.7 collective-permute-start.11
  (42 other events, 80.0 us)

commit v3 on v2

--- a/solution.py
+++ b/solution.py
@@ -47,77 +47,6 @@
 
 def pick(values, index, axis=0):
     return lax.dynamic_index_in_dim(values, index, axis, keepdims=False)
-
-
-def prefix_wide(grid, part, reverse):
-    total = part
-    entering = jnp.stack([jnp.ones_like(part[0]), jnp.zeros_like(part[1])])
-
-    def joined(earlier, later):
-        return jnp.stack([later[0] * earlier[0], later[0] * earlier[1] + later[1]])
-
-    bit = 1
-    while bit < grid.n:
-        got = grid.flip(total, bit)
-        set_here = jnp.bitwise_and(lax.div(grid.w, bit), 1) == 1
-        after = jnp.logical_not(set_here) if reverse else set_here
-        entering = jnp.where(after, joined(got, entering), entering)
-        total = jnp.where(after, joined(got, total), joined(total, got))
-        bit *= 2
-    return entering[1]
-
-
-def scan_kernel(reverse, a_ref, b_ref, cum_ref, out_ref):
-    rows, width = a_ref.shape[1:]
-    place = lax.broadcasted_iota(jnp.int32, (8, width), 0)
-    tiles = rows // 8
-
-    def one(i, carry):
-        decay_in, state_in = carry
-        tile = tiles - 1 - i if reverse else i
-        at = pl.ds(pl.multiple_of(tile * 8, 8), 8)
-        a = a_ref[0, at, :]
-        b = b_ref[0, at, :]
-        for by in (1, 2, 4):
-            if reverse:
-                moved_a = pltpu.roll(a, 8 - by, 0)
-                moved_b = pltpu.roll(b, 8 - by, 0)
-                ok = place < 8 - by
-            else:
-                moved_a = pltpu.roll(a, by, 0)
-                moved_b = pltpu.roll(b, by, 0)
-                ok = place >= by
-            b = jnp.where(ok, a * moved_b + b, b)
-            a = jnp.where(ok, a * moved_a, a)
-        b = b + a * state_in
-        a = a * decay_in
-        cum_ref[0, at, :] = a
-        out_ref[0, at, :] = b
-        last = 0 if reverse else 7
-        return (
-            jnp.broadcast_to(a[last : last + 1], (8, width)),
-            jnp.broadcast_to(b[last : last + 1], (8, width)),
-        )
-
-    start = (jnp.ones((8, width), F32), jnp.zeros((8, width), F32))
-    lax.fori_loop(0, tiles, one, start)
-
-
-def local_scan(decay, drive, reverse):
-    seqs, rows, channels = decay.shape
-    width = 256
-    spec = pl.BlockSpec((1, rows, width), lambda s, c: (s, 0, c))
-    shape = jax.ShapeDtypeStruct(decay.shape, F32)
-    return pl.pallas_call(
-        functools.partial(scan_kernel, reverse),
-        grid=(seqs, channels // width),
-        in_specs=[spec, spec],
-        out_specs=[spec, spec],
-        out_shape=[shape, shape],
-        cost_estimate=pl.CostEstimate(
-            flops=20 * decay.size, bytes_accessed=16 * decay.size, transcendentals=0
-        ),
-    )(decay, drive)
 
 
 MESH = pl.DeviceIdType.MESH
@@ -204,6 +133,10 @@
         for k in self.kinds:
             if k and not self.onto(k):
                 self.arrive(place, k)
+        self.finish_sends(place)
+
+    def finish_sends(self, place):
+        for k in self.kinds:
             for i in self.onto(k):
                 self.copy(place, k, i).wait_send()
 
@@ -292,9 +225,17 @@
         self.places(s, self.fans.pass_on)
 
     def finish(self):
+        for s in range(self.spot.hi):
+            self.places(s, self.fans.finish)
+        self.finish_line()
+
+    def finish_sends(self):
+        for s in range(self.spot.hi):
+            self.places(s, self.fans.finish_sends)
+        self.finish_line()
+
+    def finish_line(self):
         spot, hi = self.spot, self.spot.hi
-        for s in range(hi):
-            self.places(s, self.fans.finish)
         for s in range(1, hi):
 
             @pl.when(jnp.logical_and(spot.z >= s - 1, spot.z < hi - 1))
@@ -348,10 +289,10 @@
 
 
 def weights_kernel(
-    n, tensor, rec, gates, feed, cot, rec_all, gates_all, feed_all, cot_all,
-    rec_sems, gates_sems, feed_sems, cot_sems,
+    n, tensor, rec, gates, thin, feed, cot, rec_all, gates_all, thin_all, feed_all, cot_all,
+    rec_sems, gates_sems, thin_sems, feed_sems, cot_sems,
 ):
-    del rec, gates, feed, cot
+    del rec, gates, thin, feed, cot
     spot = Spot(n, tensor)
     hi = spot.hi
 
@@ -360,7 +301,8 @@
 
     cube = [spot.flip(bit) for bit in spot.bits]
     moves = [
-        Chain(spot, lambda place, k: gates_all.at[index(place, k)], gates_sems, cube),
+        Chain(spot, lambda place, k: thin_all.at[index(place, k)], thin_sems, cube),
+        Chain(spot, lambda place, k: gates_all.at[:, index(place, k)], gates_sems, cube),
         Chain(spot, lambda place, k: rec_all.at[:, index(place, k)], rec_sems, cube),
         Turns(
             spot,
@@ -400,18 +342,19 @@
     )()
 
 
-def bring_weights(grid, rec, gates, feed, cot):
+def bring_weights(grid, rec, gates, thin, feed, cot):
     n, hi, tensor = grid.n, grid.hi, grid.tensor
     far = pl.BlockSpec(memory_space=pl.ANY)
-    arrays = (rec, gates, feed, cot)
+    arrays = (rec, gates, thin, feed, cot)
     cube = grid.inner_size.bit_length() - 1
     return pl.pallas_call(
         functools.partial(weights_kernel, n, tensor),
         out_shape=[jax.ShapeDtypeStruct(a.shape, a.dtype) for a in arrays],
-        in_specs=[far] * 4,
-        out_specs=[far] * 4,
-        input_output_aliases={i: i for i in range(4)},
+        in_specs=[far] * len(arrays),
+        out_specs=[far] * len(arrays),
+        input_output_aliases={i: i for i in range(len(arrays))},
         scratch_shapes=[
+            chain_sems(cube),
             chain_sems(cube),
             chain_sems(cube),
             pltpu.SemaphoreType.DMA((2, grid.inner_size * hi)),
@@ -435,72 +378,494 @@
 STEP = 16
 
 
-def second_kernel(n, tensor, part, inputs, shift, gain, resid, whole, held, out, got, swap_sems, sems):
+GELU_SLOPE = 0.7978845608028654
+GELU_CUBE = 0.044715
+HALO = 8
+GELU_SHIFT, INPUT_SHIFT, TAPS, CONV_SHIFT, INLET_SHIFT, FORGET_SHIFT, RATE_SOFT, RATE_SIGMOID = 0, 1, 2, 6, 7, 8, 9, 10
+LANE_ROWS = 16
+
+
+def gelu_of(v):
+    bent = jnp.tanh(GELU_SLOPE * (v + GELU_CUBE * (v * v * v)))
+    half = 0.5 * (1.0 + bent)
+    slope = half + 0.5 * v * (1.0 - bent * bent) * (GELU_SLOPE * (1.0 + 3.0 * GELU_CUBE * (v * v)))
+    return v * half, slope
+
+
+def minus_expm1(x):
+    series = jnp.ones_like(x)
+    for k in range(9, 1, -1):
+        series = 1.0 + series * x * (1.0 / k)
+    return jnp.where(x > -0.5, -x * series, 1.0 - jnp.exp(x))
+
+
+def decay_of(forget, soft, starts):
+    log_decay = -8.0 * forget * soft
+    decay = jnp.where(starts, 0.0, jnp.exp(log_decay))
+    scaler = jnp.where(starts, 1.0, jnp.sqrt(minus_expm1(2.0 * log_decay)))
+    return decay, scaler
+
+
+def tile_scan(a, b, state_in, decay_in, reverse):
+    place = lax.broadcasted_iota(jnp.int32, a.shape, 0)
+    for by in (1, 2, 4):
+        turn = 8 - by if reverse else by
+        ok = place < 8 - by if reverse else place >= by
+        b = jnp.where(ok, a * pltpu.roll(b, turn, 0) + b, b)
+        a = jnp.where(ok, a * pltpu.roll(a, turn, 0), a)
+    return a * decay_in, b + a * state_in
+
+
+def scan_rows(seqs, length, width, read, write, reverse):
+    tiles = length // 8
+    last = 0 if reverse else 7
+
+    def one(i, carry):
+        tile = tiles - 1 - i if reverse else i
+        after = []
+        for s in range(seqs):
+            decay_in, state_in = carry[s]
+            at = pl.ds(pl.multiple_of(s * length + tile * 8, 8), 8)
+            a, b = tile_scan(*read(at), state_in, decay_in, reverse)
+            write(at, a, b)
+            after.append(
+                tuple(jnp.broadcast_to(v[last : last + 1], (8, width)) for v in (a, b))
+            )
+        return tuple(after)
+
+    start = (jnp.ones((8, width), F32), jnp.zeros((8, width), F32))
+    lax.fori_loop(0, tiles, one, (start,) * seqs)
+
+
+def enter_kernel(
+    seqs, x, halo, gain, w_input, w_gelu, w_inlet, w_forget, lanes, flags,
+    normed, ext, conv, gelu_pre, inlet_pre, forget_pre, cum, local, held, factor, addend,
+):
+    rows = x.shape[0]
+    length = rows // seqs
+    width = conv.shape[1]
+
+    @pl.when(pl.program_id(0) == 0)
+    def _():
+        def norm(source, at, to):
+            value = source[at, :].astype(F32)
+            scale = lax.rsqrt(jnp.mean(value * value, axis=-1, keepdims=True) + 1e-06)
+            value = (value * scale * gain[...]).astype(BF16)
+            held[pl.ds(pl.multiple_of(at.start + to, STEP), STEP), :] = value
+            return value
+
+        def main(at):
+            normed[at, :] = norm(x, at, 0)
+
+        by_rows(rows, STEP, main)
+        by_rows(halo.shape[0], STEP, lambda at: norm(halo, at, rows))
+
+    table = lanes[...]
+
+    def row(i):
+        return table[i : i + 1]
+
+    branch = (dot(held[...], w_input[0]) + row(INPUT_SHIFT)).astype(BF16)
+    gelu_pre[...] = dot(held[0:rows, :], w_gelu[0]) + row(GELU_SHIFT)
+    for s in range(seqs):
+        here = slice(s * length, (s + 1) * length)
+        front = rows + s * HALO
+        longer = jnp.concatenate(
+            [branch[front : front + HALO].astype(F32), branch[here].astype(F32)], axis=0
+        )
+        ext[s] = longer.astype(BF16)
+        total = row(CONV_SHIFT) + row(TAPS) * longer[HALO:]
+        for k in range(1, CONV):
+            moved = pltpu.roll(longer, k, 0)[HALO:]
+            total = total + jnp.where(flags[here, k : k + 1] > 0.5, row(TAPS + k) * moved, 0.0)
+        conv[here, :] = total.astype(BF16)
+    blocks = conv[...]
+    inlet_pre[...] = dot(blocks, w_inlet[0]) + row(INLET_SHIFT)
+    forget_pre[...] = dot(blocks, w_forget[0]) + row(FORGET_SHIFT)
+
+    def terms(at):
+        starts = flags[at, 0:1] > 0.5
+        decay, scaler = decay_of(jax.nn.sigmoid(forget_pre[at, :]), row(RATE_SOFT), starts)
+        factor[at, :] = decay
+        addend[at, :] = scaler * jax.nn.sigmoid(inlet_pre[at, :]) * conv[at, :].astype(F32)
+
+    by_rows(rows, 32, terms)
+
+    def write(at, a, b):
+        cum[at, :] = a
+        local[at, :] = b
+
+    scan_rows(seqs, length, width, lambda at: (factor[at, :], addend[at, :]), write, False)
+
+
+def enter_recurrence(x, halo, gain, rec, inlet, forget, lanes, flags, seqs):
+    rows, d = x.shape
+    heads, width = inlet.shape[:2]
+    channels = heads * width
+    longer = rows // seqs + HALO
+
+    def fixed(a):
+        return pl.BlockSpec(a.shape, lambda h: (0, 0))
+
+    def column(count):
+        return pl.BlockSpec((count, width), lambda h: (0, h))
+
+    def weight(k):
+        return pl.BlockSpec((1, d, width), lambda h: (k, 0, h))
+
+    head = pl.BlockSpec((1, width, width), lambda h: (h, 0, 0))
+    wide = jax.ShapeDtypeStruct((rows, channels), F32)
+    return pl.pallas_call(
+        functools.partial(enter_kernel, seqs),
+        grid=(heads,),
+        out_shape=[
+            jax.ShapeDtypeStruct((rows, d), BF16),
+            jax.ShapeDtypeStruct((seqs, longer, channels), BF16),
+            jax.ShapeDtypeStruct((rows, channels), BF16),
+        ]
+        + [wide] * 5,
+        in_specs=[fixed(x), fixed(halo), fixed(gain), weight(0), weight(1), head, head]
+        + [column(LANE_ROWS), fixed(flags)],
+        out_specs=[
+            fixed(x),
+            pl.BlockSpec((seqs, longer, width), lambda h: (0, 0, h)),
+            column(rows),
+        ]
+        + [column(rows)] * 5,
+        scratch_shapes=[
+            pltpu.VMEM((rows + halo.shape[0], d), BF16),
+            pltpu.VMEM((rows, width), F32),
+            pltpu.VMEM((rows, width), F32),
+        ],
+        compiler_params=pltpu.CompilerParams(vmem_limit_bytes=GRANT),
+        name="enter_recurrence",
+    )(x, halo, gain, rec, rec, inlet, forget, lanes, flags)
+
+
+class Prefix:
+    def __init__(self, spot, seqs, reverse, tots, gots, line, cube_sems, line_sems):
+        self.spot, self.seqs, self.reverse = spot, seqs, reverse
+        self.tots, self.gots, self.line = tots, gots, line
+        self.cube_sems, self.line_sems = cube_sems, line_sems
+
+    def line_copy(self, place, sender):
+        stages = len(self.spot.bits)
+        return pltpu.make_async_remote_copy(
+            src_ref=self.tots.at[stages],
+            dst_ref=self.line.at[sender],
+            send_sem=self.line_sems.at[0, place],
+            recv_sem=self.line_sems.at[1, sender],
+            device_id=self.spot.line(place),
+            device_id_type=MESH,
+        )
+
+    def run(self):
+        spot, seqs, hi = self.spot, self.seqs, self.spot.hi
+        a, b = slice(0, seqs), slice(seqs, 2 * seqs)
+        width = self.tots.shape[2]
+        enter_a, enter_b = jnp.ones((seqs, width), F32), jnp.zeros((seqs, width), F32)
+        for stage, bit in enumerate(spot.bits):
+            copy = remote(
+                self.tots.at[stage], self.gots.at[stage], self.cube_sems, stage, spot.flip(bit)
+            )
+            copy.start()
+            copy.wait()
+            mine_a, mine_b = self.tots[stage, a, :], self.tots[stage, b, :]
+            got_a, got_b = self.gots[stage, a, :], self.gots[stage, b, :]
+            after = spot.bit(bit) == (0 if self.reverse else 1)
+            enter_b = jnp.where(after, enter_a * got_b + enter_b, enter_b)
+            enter_a = jnp.where(after, enter_a * got_a, enter_a)
+            self.tots[stage + 1, a, :] = mine_a * got_a
+            self.tots[stage + 1, b, :] = jnp.where(
+                after, mine_a * got_b + mine_b, got_a * mine_b + got_b
+            )
+            self.tots[stage + 1, 2 * seqs :, :] = jnp.zeros((8 - 2 * seqs, width), F32)
+        for distance in range(1, hi):
+            self.line_copy(spot.away(distance), spot.z).start()
+        for distance in range(1, hi):
+            place = spot.away(distance)
+            self.line_copy(place, place).wait_recv()
+            self.line_copy(place, spot.z).wait_send()
+        come = jnp.zeros((seqs, width), F32)
+        for place in reversed(range(hi)) if self.reverse else range(hi):
+            before = spot.z < place if self.reverse else spot.z > place
+            come = jnp.where(before, self.line[place, a, :] * come + self.line[place, b, :], come)
+        return enter_a * come + enter_b
+
+
+def prefix_scratch(grid, channels):
+    stages = grid.inner_size.bit_length() - 1
+    return [
+        pltpu.VMEM((stages + 1, 8, channels), F32),
+        pltpu.VMEM((stages, 8, channels), F32),
+        pltpu.VMEM((grid.hi, 8, channels), F32),
+        pltpu.SemaphoreType.DMA((2, stages)),
+        pltpu.SemaphoreType.DMA((2, grid.hi)),
+    ]
+
+
+def second_kernel(
+    n, tensor, seqs, cum, local, gelu_pre, w_out, x, shift, gain,
+    entered, mixed, resid, second,
+    part, out, got, tots, gots, line, cube_sems, line_sems, swap_sems,
+):
     spot = Spot(n, tensor)
-    rows = inputs.shape[0]
+    rows = resid.shape[0]
+    every = x.shape[0]
+    length = every // seqs
+    spot.greet(*[spot.flip(bit) for bit in spot.bits], spot.cross)
+    tots[0] = jnp.zeros_like(tots[0])
+    for s in range(seqs):
+        last = slice((s + 1) * length - 1, (s + 1) * length)
+        tots[0, s : s + 1, :] = cum[last, :]
+        tots[0, seqs + s : seqs + s + 1, :] = local[last, :]
+    enter = Prefix(spot, seqs, False, tots, gots, line, cube_sems, line_sems).run()
+    entered[...] = jnp.zeros_like(entered)
+    entered[0:seqs, :] = enter
+    for s in range(seqs):
+
+        def mix(at, s=s):
+            here = pl.ds(pl.multiple_of(s * length + at.start, STEP), STEP)
+            state = local[here, :] + cum[here, :] * enter[s : s + 1]
+            mixed[here, :] = (state * gelu_of(gelu_pre[here, :])[0]).astype(BF16)
+
+        by_rows(length, STEP, mix)
+    values = mixed[...]
+
+    def branch(j, carry):
+        at = pl.ds(pl.multiple_of(j * 256, 256), 256)
+        value = dot_nt(values, w_out[0, at, :])
+        for side in range(tensor):
+            part[side, :, at] = value[side * rows : (side + 1) * rows]
+        return carry
+
+    lax.fori_loop(0, x.shape[1] // 256, branch, 0)
 
     def put(at):
         out[at, :] = part[1 - spot.t, at, :].astype(BF16)
 
     by_rows(rows, STEP, put)
-    spot.greet(spot.cross)
     copy = remote(out, got, swap_sems, 0, spot.cross)
     copy.start()
     copy.wait()
 
     def norm(at):
-        value = inputs[at, :] + (part[spot.t, at, :] + got[at, :].astype(F32) + shift[...])
+        own = x[pl.ds(pl.multiple_of(spot.t * rows + at.start, STEP), STEP), :].astype(F32)
+        value = own + (part[spot.t, at, :] + got[at, :].astype(F32) + shift[...])
         resid[at, :] = value
         scale = lax.rsqrt(jnp.mean(value * value, axis=-1, keepdims=True) + 1e-06)
-        held[spot.z, spot.t, at, :] = (value * scale * gain[...]).astype(BF16)
+        second[at, :] = (value * scale * gain[...]).astype(BF16)
 
     by_rows(rows, STEP, norm)
-    chain = Chain(
-        spot, lambda place, k: held.at[place, lax.rem(spot.t + k, tensor)], sems, [spot.cross]
-    )
-    chain.first()
-    for s in range(1, spot.hi):
-        chain.onward(s)
-        chain.second(s - 1)
-    chain.second(spot.hi - 1)
-    chain.finish()
-    for place in range(spot.hi):
-        for side in range(tensor):
-
-            def give(at, place=place, side=side):
-                whole[place, side, at, :] = held[place, side, at, :]
-
-            by_rows(rows, STEP, give)
-
-
-def bring_second(grid, part, inputs, shift, gain):
-    rows, width = inputs.shape
+
+
+def make_second(grid, cum, local, gelu_pre, rec, x, shift, gain, seqs):
+    every, d = x.shape
+    channels = cum.shape[1]
+    rows = every // grid.tensor
     near = pl.BlockSpec(memory_space=pltpu.VMEM)
-    whole = (grid.hi, grid.tensor, rows, width)
     return pl.pallas_call(
-        functools.partial(second_kernel, grid.n, grid.tensor),
-        out_shape=[jax.ShapeDtypeStruct((rows, width), F32), jax.ShapeDtypeStruct(whole, BF16)],
-        in_specs=[near] * 4,
-        out_specs=[near] * 2,
+        functools.partial(second_kernel, grid.n, grid.tensor, seqs),
+        grid=(1,),
+        out_shape=[
+            jax.ShapeDtypeStruct((8, channels), F32),
+            jax.ShapeDtypeStruct((every, channels), BF16),
+            jax.ShapeDtypeStruct((rows, d), F32),
+            jax.ShapeDtypeStruct((rows, d), BF16),
+        ],
+        in_specs=[near] * 3 + [pl.BlockSpec((1, d, channels), lambda i: (2, 0, 0))] + [near] * 3,
+        out_specs=[near] * 4,
         scratch_shapes=[
-            pltpu.VMEM(whole, BF16),
-            pltpu.VMEM((rows, width), BF16),
-            pltpu.VMEM((rows, width), BF16),
-            pltpu.SemaphoreType.DMA((2, 1)),
-            chain_sems(1),
-        ],
+            pltpu.VMEM((grid.tensor, rows, d), F32),
+            pltpu.VMEM((rows, d), BF16),
+            pltpu.VMEM((rows, d), BF16),
+        ]
+        + prefix_scratch(grid, channels)
+        + [pltpu.SemaphoreType.DMA((2, 1))],
         compiler_params=pltpu.CompilerParams(
             collective_id=1, has_side_effects=True, vmem_limit_bytes=GRANT
         ),
-        name="bring_second",
-    )(part, inputs, shift, gain)
+        name="make_second",
+    )(cum, local, gelu_pre, rec, x, shift, gain)
+
+
+def leave_kernel(
+    n, tensor, seqs, branch, w_out, gelu_pre, local, cum, inlet_pre, forget_pre, conv, ext, entered,
+    w_inlet, w_forget, lanes, flags,
+    gelu_low, input_low, gate_grads, lane_grads, shift_grad,
+    tail, carried, factor, addend, back, rim, tots, gots, line, cube_sems, line_sems, rim_sems,
+):
+    spot = Spot(n, tensor)
+    every, channels = conv.shape
+    length = every // seqs
+    heads, width = w_inlet.shape[:2]
+    behind = {"wide": lax.rem(spot.w + n - 1, n)}
+    ahead = {"wide": lax.rem(spot.w + 1, n)}
+    spot.greet(*[spot.flip(bit) for bit in spot.bits], behind, ahead)
+    tots[0] = jnp.zeros_like(tots[0])
+    lane_grads[...] = jnp.zeros_like(lane_grads)
+    shift_grad[...] = jnp.zeros_like(shift_grad)
+
+    def add(at):
+        shift_grad[...] += jnp.sum(branch[at, :].astype(F32).reshape(2, 8, -1), axis=0)
+
+    by_rows(every, STEP, add)
+
+    def decays(at, cols):
+        soft = lanes[RATE_SOFT : RATE_SOFT + 1, cols]
+        return decay_of(jax.nn.sigmoid(forget_pre[at, cols]), soft, flags[at, 0:1] > 0.5)
+
+    def upward(h, none):
+        cols = pl.ds(pl.multiple_of(h * width, width), width)
+        grad = dot(branch[...], w_out[0, :, cols])
+        gelu, slope = gelu_of(gelu_pre[:, cols])
+        for s in range(seqs):
+            here = slice(s * length, (s + 1) * length)
+            state = local[here, cols] + cum[here, cols] * entered[s : s + 1, cols]
+            low = (grad[here] * state * slope[here]).astype(BF16)
+            gelu_low[here, cols] = low
+            lane_grads[0:1, cols] += jnp.sum(low.astype(F32), axis=0, keepdims=True)
+            decay, _ = decays(here, cols)
+            place = lax.broadcasted_iota(jnp.int32, (length, width), 0)
+            factor[here, :] = jnp.where(place < length - 1, pltpu.roll(decay, length - 1, 0), 1.0)
+        addend[...] = grad * gelu
+
+        def write(at, a, b):
+            tail[at, cols] = a
+            carried[at, cols] = b
+
+        scan_rows(seqs, length, width, lambda at: (factor[at, :], addend[at, :]), write, True)
+        for s in range(seqs):
+            first = slice(s * length, s * length + 8)
+            decay, _ = decays(first, cols)
+            tots[0, s : s + 1, cols] = decay[0:1] * tail[first, cols][0:1]
+            tots[0, seqs + s : seqs + s + 1, cols] = decay[0:1] * carried[first, cols][0:1]
+        return none
+
+    lax.fori_loop(0, heads, upward, 0)
+    come = Prefix(spot, seqs, True, tots, gots, line, cube_sems, line_sems).run()
+    tots[0, 0:seqs, :] = come
+
+    def downward(h, none):
+        cols = pl.ds(pl.multiple_of(h * width, width), width)
+
+        def row(i):
+            return lanes[i : i + 1, cols]
+
+        sums = []
+        for s in range(seqs):
+            here = slice(s * length, (s + 1) * length)
+            place = lax.broadcasted_iota(jnp.int32, (length, width), 0)
+            starts = flags[here, 0:1] > 0.5
+            blocks = conv[here, cols].astype(F32)
+            enter = entered[s : s + 1, cols]
+            state = local[here, cols] + cum[here, cols] * enter
+            before = jnp.where(place > 0, pltpu.roll(state, 1, 0), enter)
+            carry = carried[here, cols] + tail[here, cols] * tots[0, s : s + 1, cols]
+            inlet = jax.nn.sigmoid(inlet_pre[here, cols])
+            forget = jax.nn.sigmoid(forget_pre[here, cols])
+            soft = row(RATE_SOFT)
+            decay, scaler = decay_of(forget, soft, starts)
+            log_grad = jnp.where(
+                starts, 0.0, carry * before * decay - carry * inlet * blocks * (decay * decay) / scaler
+            )
+            rate_grad = jnp.sum(log_grad * (-8.0 * forget), axis=0, keepdims=True) * row(RATE_SIGMOID)
+            inlet_low = (carry * scaler * blocks * (inlet * (1.0 - inlet))).astype(BF16)
+            forget_low = (log_grad * (-8.0 * soft) * (forget * (1.0 - forget))).astype(BF16)
+            conv_grad = (
+                carry * scaler * inlet
+                + dot_nt(inlet_low, w_inlet[h])
+                + dot_nt(forget_low, w_forget[h])
+            )
+            longer = ext[s, :, cols].astype(F32)
+            zeros = jnp.zeros((HALO, width), F32)
+            total = jnp.concatenate([zeros, row(TAPS) * conv_grad], axis=0)
+            taps = [jnp.sum(conv_grad * longer[HALO:], axis=0, keepdims=True)]
+            for k in range(1, CONV):
+                masked = jnp.where(flags[here, k : k + 1] > 0.5, conv_grad, 0.0)
+                moved = pltpu.roll(longer, k, 0)[HALO:]
+                taps.append(jnp.sum(masked * moved, axis=0, keepdims=True))
+                sent = jnp.concatenate([zeros, row(TAPS + k) * masked], axis=0)
+                total = total + pltpu.roll(sent, HALO + length - k, 0)
+            back[s, :, cols] = total
+            lows = [jnp.sum(v.astype(F32), axis=0, keepdims=True) for v in (inlet_low, forget_low)]
+            sums.append(taps + [jnp.sum(conv_grad, axis=0, keepdims=True)] + lows + [rate_grad])
+            for m, low in enumerate((inlet_low, forget_low)):
+                factor[here, :] = low.astype(F32) if m == 0 else factor[here, :]
+                addend[here, :] = low.astype(F32) if m == 1 else addend[here, :]
+        for i in range(len(sums[0])):
+            lane_grads[2 + i : 3 + i, cols] = sum(each[i] for each in sums[1:]) + sums[0][i]
+        for m, low in enumerate((factor, addend)):
+            gate_grads[m, h] = dot_tn(conv[:, cols], low[...].astype(BF16)).astype(BF16)
+        return none
+
+    lax.fori_loop(0, heads, downward, 0)
+    copy = remote(back.at[:, 0:HALO, :], rim, rim_sems, 0, behind)
+    copy.start()
+    copy.wait()
+
+    def give(h, none):
+        cols = pl.ds(pl.multiple_of(h * width, width), width)
+        total = jnp.zeros((1, width), F32)
+        for s in range(seqs):
+            edge = jnp.where(spot.w < n - 1, rim[s, :, cols], 0.0)
+            value = back[s, HALO:, cols]
+            value = jnp.concatenate([value[: length - HALO], value[length - HALO :] + edge], axis=0)
+            low = value.astype(BF16)
+            input_low[s * length : (s + 1) * length, cols] = low
+            total = total + jnp.sum(low.astype(F32), axis=0, keepdims=True)
+        lane_grads[1:2, cols] = total
+        return none
+
+    lax.fori_loop(0, heads, give, 0)
+
+
+def leave_recurrence(
+    grid, branch, rec, gelu_pre, local, cum, inlet_pre, forget_pre, conv, ext, entered, inlet, forget, lanes,
+    flags, seqs,
+):
+    every, channels = conv.shape
+    d = branch.shape[1]
+    heads, width = inlet.shape[:2]
+    near = pl.BlockSpec(memory_space=pltpu.VMEM)
+    low = jax.ShapeDtypeStruct((every, channels), BF16)
+    return pl.pallas_call(
+        functools.partial(leave_kernel, grid.n, grid.tensor, seqs),
+        grid=(1,),
+        out_shape=[
+            low,
+            low,
+            jax.ShapeDtypeStruct((2, heads, width, width), BF16),
+            jax.ShapeDtypeStruct((LANE_ROWS, channels), F32),
+            jax.ShapeDtypeStruct((8, d), F32),
+        ],
+        in_specs=[near, pl.BlockSpec((1, d, channels), lambda i: (2, 0, 0))] + [near] * 12,
+        out_specs=[near] * 5,
+        scratch_shapes=[
+            pltpu.VMEM((every, channels), F32),
+            pltpu.VMEM((every, channels), F32),
+            pltpu.VMEM((every, width), F32),
+            pltpu.VMEM((every, width), F32),
+            pltpu.VMEM((seqs, every // seqs + HALO, channels), F32),
+            pltpu.VMEM((seqs, HALO, channels), F32),
+        ]
+        + prefix_scratch(grid, channels)
+        + [pltpu.SemaphoreType.DMA((2, 1))],
+        compiler_params=pltpu.CompilerParams(
+            collective_id=5, has_side_effects=True, vmem_limit_bytes=GRANT
+        ),
+        name="leave_recurrence",
+    )(
+        branch, rec, gelu_pre, local, cum, inlet_pre, forget_pre, conv, ext, entered, inlet, forget,
+        lanes, flags,
+    )
 
 
 class Rows:
-    def __init__(self, spot, part, out, got, line, cross_sems, line_sems):
-        self.spot, self.part, self.out, self.got, self.line = spot, part, out, got, line
+    def __init__(self, spot, part, got, line, cross_sems, line_sems):
+        self.spot, self.part, self.got, self.line = spot, part, got, line
         self.cross_sems, self.line_sems = cross_sems, line_sems
-        self.rows = out.shape[1]
+        self.rows = got.shape[1]
 
     def place(self, k):
         spot, hi = self.spot, self.spot.hi
@@ -514,20 +879,14 @@
         return place + flipped * (last - 2 * place)
 
     def cross_copy(self, place):
+        spot = self.spot
         return remote(
-            self.out.at[place], self.got.at[place], self.cross_sems, place, self.spot.cross
+            self.part.at[place, 1 - spot.t], self.got.at[place], self.cross_sems, place, spot.cross
         )
 
     def start(self):
-        spot = self.spot
-        for k in range(spot.hi):
-            place = self.place(k)
-
-            def put(at, place=place):
-                self.out[place, at, :] = self.part[place, 1 - spot.t, at, :]
-
-            by_rows(self.rows, STEP, put)
-            self.cross_copy(place).start()
+        for k in range(self.spot.hi):
+            self.cross_copy(self.place(k)).start()
 
     def line_copy(self, s, up, here=False):
         spot, hi = self.spot, self.spot.hi
@@ -620,35 +979,89 @@
                 self.line_copy(s, False).wait_send()
 
 
-def rows_kernel(
-    second, n, tensor, part, resid, cot, gain, both, gain_grad,
-    out, got, line, mine, other, cross_sems, line_sems, swap_sems,
+def feed_kernel(
+    n, tensor, unit_tiles, own, w_gate, w_up, w_down, cot, resid, gain,
+    whole, gate_low, up_low, hidden, both, gain_grad,
+    part, got, line, mine, other, sems, cross_sems, line_sems, swap_sems,
 ):
     spot = Spot(n, tensor)
-    sums = Rows(spot, part, out, got, line, cross_sems, line_sems)
+    hi = spot.hi
+    rows, d = own.shape
+    width = w_gate.shape[2]
+    every = tensor * rows
     spot.greet(spot.cross)
+
+    def put(at):
+        whole[spot.z, spot.t, at, :] = own[at, :]
+
+    by_rows(rows, STEP, put)
+    chain = Chain(
+        spot, lambda place, k: whole.at[place, lax.rem(spot.t + k, tensor)], sems, [spot.cross]
+    )
+    chain.first()
+    gain_grad[...] = jnp.zeros_like(gain_grad)
+    tiles = width // LANE
+    skip = spot.z * tiles - jnp.minimum(spot.z * tiles, unit_tiles - tiles)
+    chunk = 256
+
+    def work(place):
+        def ahead(j, none):
+            cols = pl.ds(pl.multiple_of(j * chunk, chunk), chunk)
+            rows_in = whole[place].reshape(every, d)
+            gate, slope = gelu_of(dot(rows_in, w_gate[0, :, cols]))
+            up = dot(rows_in, w_up[0, :, cols])
+            grad = dot(cot[place].reshape(every, d), w_down[0, :, cols])
+            at = lax.broadcasted_iota(jnp.int32, (1, chunk), 1) + j * chunk
+            ok = at >= skip * LANE
+            grad = jnp.where(ok, grad, 0.0)
+            hidden[place, :, cols] = jnp.where(ok, gate * up, 0.0).astype(BF16)
+            gate_low[place, :, cols] = (grad * up * slope).astype(BF16)
+            up_low[place, :, cols] = (grad * gate).astype(BF16)
+            return none
+
+        lax.fori_loop(0, width // chunk, ahead, 0)
+
+        def back(j, none):
+            cols = pl.ds(pl.multiple_of(j * chunk, chunk), chunk)
+            value = dot_nt(gate_low[place], w_gate[0, cols, :])
+            value = (value + dot_nt(up_low[place], w_up[0, cols, :])).astype(BF16)
+            for side in range(tensor):
+                part[place, side, :, cols] = value[side * rows : (side + 1) * rows]
+            return none
+
+        lax.fori_loop(0, d // chunk, back, 0)
+
+    def come_and_work(place):
+        chain.fans.arrive(place, 1)
+        work(place)
+
+    for s in range(1, hi):
+        chain.onward(s)
+        chain.places(s - 1, come_and_work)
+    chain.places(hi - 1, come_and_work)
+    sums = Rows(spot, part, got, line, cross_sems, line_sems)
     sums.start()
-    if second:
-        gain_grad[...] = jnp.zeros_like(gain_grad)
+    chain.finish_sends()
 
     def done(at, total):
         value = resid[at, :]
-        if second:
-            scale = lax.rsqrt(jnp.mean(value * value, axis=-1, keepdims=True) + 1e-06)
-            turned = total * gain[...]
-            inner = jnp.mean(turned * value, axis=-1, keepdims=True)
-            grad = cot[at, :].astype(F32) + scale * turned - value * (scale * scale * scale * inner)
-            gained = total * value * scale
-            gain_grad[...] += jnp.sum(gained.reshape(2, 8, -1), axis=0)
-            mine[at, :] = grad.astype(BF16)
-        else:
-            mine[at, :] = (value + total).astype(BF16)
+        scale = lax.rsqrt(jnp.mean(value * value, axis=-1, keepdims=True) + 1e-06)
+        turned = total * gain[...]
+        inner = jnp.mean(turned * value, axis=-1, keepdims=True)
+        grad = cot[spot.z, spot.t, at, :].astype(F32)
+        grad = grad + scale * turned - value * (scale * scale * scale * inner)
+        gained = total * value * scale
+        gain_grad[...] += jnp.sum(gained.reshape(2, 8, -1), axis=0)
+        mine[at, :] = grad.astype(BF16)
 
     sums.run(done)
     copy = remote(mine, other, swap_sems, 0, spot.cross)
     copy.start()
     sums.finish()
-
+    share(spot, copy, mine, other, both)
+
+
+def share(spot, copy, mine, other, both):
     def keep(at):
         both[spot.t, at, :] = mine[at, :]
 
@@ -661,33 +1074,101 @@
     by_rows(mine.shape[0], STEP, take)
 
 
-def sum_rows(grid, second, part, resid, cot, gain):
+def rows_scratch(grid, rows, width):
+    hi = grid.hi
+    return [
+        pltpu.VMEM((hi, rows, width), BF16),
+        pltpu.VMEM((2, 2 * (hi - 1), rows, width), BF16),
+        pltpu.VMEM((rows, width), BF16),
+        pltpu.VMEM((rows, width), BF16),
+    ]
+
+
+def rows_sems(grid):
+    hi = grid.hi
+    return [
+        pltpu.SemaphoreType.DMA((2, hi)),
+        pltpu.SemaphoreType.DMA((2, 2 * (hi - 1))),
+        pltpu.SemaphoreType.DMA((2, 1)),
+    ]
+
+
+def feed_forward(grid, own, feed, cot, resid, gain, unit_tiles):
+    rows, d = own.shape
+    hi, tensor = grid.hi, grid.tensor
+    width = feed.shape[-1]
+    near = pl.BlockSpec(memory_space=pltpu.VMEM)
+    whole = jax.ShapeDtypeStruct((hi, tensor, rows, d), BF16)
+    low = jax.ShapeDtypeStruct((hi, tensor * rows, width), BF16)
+    feed = feed.reshape(3, -1, width)
+
+    def weight(k):
+        return pl.BlockSpec((1, d, width), lambda i: (k, 0, 0))
+
+    return pl.pallas_call(
+        functools.partial(feed_kernel, grid.n, tensor, unit_tiles),
+        grid=(1,),
+        out_shape=[
+            whole,
+            low,
+            low,
+            low,
+            jax.ShapeDtypeStruct((tensor, rows, d), BF16),
+            jax.ShapeDtypeStruct((8, d), F32),
+        ],
+        in_specs=[near] + [weight(k) for k in range(3)] + [near] * 3,
+        out_specs=[near] * 6,
+        scratch_shapes=[pltpu.VMEM(whole.shape, BF16)]
+        + rows_scratch(grid, rows, d)
+        + [chain_sems(1)]
+        + rows_sems(grid),
+        compiler_params=pltpu.CompilerParams(
+            collective_id=2, has_side_effects=True, vmem_limit_bytes=GRANT
+        ),
+        name="feed_forward",
+    )(own, feed, feed, feed, cot, resid, gain)
+
+
+def out_kernel(
+    n, tensor, part_in, resid, both, part, got, line, mine, other, cross_sems, line_sems, swap_sems
+):
+    spot = Spot(n, tensor)
+    spot.greet(spot.cross)
+    rows = resid.shape[0]
+    for place in range(spot.hi):
+        for side in range(tensor):
+
+            def put(at, place=place, side=side):
+                part[place, side, at, :] = part_in[place, side, at, :]
+
+            by_rows(rows, STEP, put)
+    sums = Rows(spot, part, got, line, cross_sems, line_sems)
+    sums.start()
+
+    def done(at, total):
+        mine[at, :] = (resid[at, :] + total).astype(BF16)
+
+    sums.run(done)
+    copy = remote(mine, other, swap_sems, 0, spot.cross)
+    copy.start()
+    sums.finish()
+    share(spot, copy, mine, other, both)
+
+
+def block_output(grid, part, resid):
     rows, width = resid.shape
     near = pl.BlockSpec(memory_space=pltpu.VMEM)
-    hi, tensor = grid.hi, grid.tensor
     return pl.pallas_call(
-        functools.partial(rows_kernel, second, grid.n, tensor),
-        out_shape=[
-            jax.ShapeDtypeStruct((tensor, rows, width), BF16),
-            jax.ShapeDtypeStruct((8, width), F32),
-        ],
-        in_specs=[near] * 4,
-        out_specs=[near] * 2,
-        scratch_shapes=[
-            pltpu.VMEM((hi, rows, width), BF16),
-            pltpu.VMEM((hi, rows, width), BF16),
-            pltpu.VMEM((2, 2 * (hi - 1), rows, width), BF16),
-            pltpu.VMEM((rows, width), BF16),
-            pltpu.VMEM((rows, width), BF16),
-            pltpu.SemaphoreType.DMA((2, hi)),
-            pltpu.SemaphoreType.DMA((2, 2 * (hi - 1))),
-            pltpu.SemaphoreType.DMA((2, 1)),
-        ],
+        functools.partial(out_kernel, grid.n, grid.tensor),
+        out_shape=jax.ShapeDtypeStruct((grid.tensor, rows, width), BF16),
+        in_specs=[near] * 2,
+        out_specs=near,
+        scratch_shapes=[pltpu.VMEM(part.shape, BF16)] + rows_scratch(grid, rows, width) + rows_sems(grid),
         compiler_params=pltpu.CompilerParams(
-            collective_id=2 if second else 3, has_side_effects=True, vmem_limit_bytes=GRANT
+            collective_id=3, has_side_effects=True, vmem_limit_bytes=GRANT
         ),
-        name="sum_second" if second else "sum_feed",
-    )(part, resid, cot, gain)
+        name="block_output",
+    )(part, resid)
 
 
 RING = 4
@@ -1023,31 +1504,6 @@
 def rms_norm(values, gain):
     scale = lax.rsqrt(jnp.mean(values * values, axis=-1, keepdims=True) + 1e-06)
     return values * scale * gain
-
-
-def causal_conv(extended, marks, weight, bias):
-    margin = weight.shape[0] - 1
-    tok_count = extended.shape[1] - margin
-    current = marks[:, margin:]
-    total = bias + weight[0] * extended[:, margin:]
-    for offset in range(1, margin + 1):
-        moved = extended[:, margin - offset : margin - offset + tok_count]
-        same = (marks[:, margin - offset : margin - offset + tok_count] == current)[..., None]
-        total = total + jnp.where(same, weight[offset] * moved, 0.0)
-    return total
-
-
-def lru_terms(inlet_pre, forget_pre, conv_vals, rate, starts):
-    inlet = jax.nn.sigmoid(inlet_pre)
-    forget = jax.nn.sigmoid(forget_pre)
-    log_decay = -8.0 * forget * jax.nn.softplus(rate)
-    decay = jnp.where(starts, 0.0, jnp.exp(log_decay))
-    scaler = jnp.where(starts, 1.0, jnp.sqrt(-jnp.expm1(2.0 * log_decay)))
-    return (decay, scaler * inlet * conv_vals)
-
-
-def gelu_product(gate_pre, up_pre):
-    return jax.nn.gelu(gate_pre) * up_pre
 
 
 def dot(left, right):
@@ -1099,6 +1555,15 @@
     window_tiles = -(-unit_tiles // grid.hi)
     window = window_tiles * LANE
 
+    halo_rows = block_in[:, tok_count - HALO :]
+    marks = (segment_ids + 1).astype(BF16)
+    halo, rim_marks = shifted((halo_rows, marks[:, tok_count - margin :]), "wide", 1)
+    halo = halo.reshape(seq_count * HALO, width)
+    marks_ext = jnp.concatenate([rim_marks, marks], axis=1)
+    earlier = [marks_ext[:, margin - k : margin - k + tok_count] == marks for k in range(1, CONV)]
+    flags = jnp.stack([jnp.logical_not(earlier[0])] + earlier, axis=-1).astype(F32)
+    flags = jnp.pad(flags.reshape(rows_all, CONV), ((0, 0), (0, 8 - CONV)))
+
     rec_own = jnp.stack(
         [
             input_weight.reshape(d_own, channels),
@@ -1106,30 +1571,23 @@
             out_weight.reshape(channels, d_own).T,
         ]
     )
-    gates_own = jnp.stack([inlet_weight, forget_weight]).reshape(-1, block_size)
+    gates_own = jnp.stack([inlet_weight, forget_weight]).reshape(2 * head_count, lane_own, block_size)
+    per_lane = jnp.stack([gelu_bias, input_bias])
+    per_lane = jnp.concatenate(
+        [per_lane, conv_weight, jnp.stack([conv_bias, inlet_bias, forget_bias, decay_rate])]
+    )
+    lane_table = lax.dynamic_update_slice(
+        jnp.zeros((CONV + 6, head_count, block_size), BF16), per_lane, (0, 0, grid.w * lane_own)
+    )
+    per_width = jnp.stack([first_gain, out_bias, second_gain])
+    width_table = lax.dynamic_update_slice(
+        jnp.zeros((3, width), BF16), per_width, (0, grid.w * d_own)
+    )
     thin_own = jnp.concatenate(
-        [
-            v.reshape(-1)
-            for v in (
-                first_gain,
-                out_bias,
-                second_gain,
-                gelu_bias,
-                input_bias,
-                conv_weight,
-                conv_bias,
-                inlet_bias,
-                forget_bias,
-                decay_rate,
-            )
-        ]
-    )
-    gate_rows = gates_own.shape[0]
-    thin_size = thin_own.size
-    thin_rows = -(-thin_size // block_size)
-    spare = -(gate_rows + thin_rows) % 16
-    thin_own = jnp.pad(thin_own, (0, (thin_rows + spare) * block_size - thin_size))
-    gates_own = jnp.concatenate([gates_own, thin_own.reshape(-1, block_size)])
+        [lane_table.reshape(CONV + 6, channels), width_table.reshape(-1, channels)]
+    )
+    thin_count = thin_own.shape[0]
+    thin_own = jnp.pad(thin_own, ((0, -thin_count % 16), (0, 0)))
     feed_own = jnp.stack([mlp_gate, mlp_up, mlp_down.T])
     feed_windows = jnp.stack(
         [
@@ -1142,201 +1600,76 @@
     )
     cot_rows = cotangent.reshape(grid.tensor, rows_half, width)
     cot_own = pick(cot_rows, grid.t)
-    rec_all, gates_all, feed_all, cot_all = blank(
+    rec_all, gates_all, thin_all, feed_all, cot_all = blank(
         (3, grid.n, d_own, channels),
-        (grid.n,) + gates_own.shape,
+        (2 * head_count, grid.n, lane_own, block_size),
+        (grid.n,) + thin_own.shape,
         (3, grid.n + grid.hi, d_own, window),
         (grid.hi, grid.tensor, rows_half, width),
     )
     rec_all = lax.dynamic_update_slice(rec_all, rec_own[:, None], (0, grid.w, 0, 0))
-    gates_all = lax.dynamic_update_slice(gates_all, gates_own[None], (grid.w, 0, 0))
+    gates_all = lax.dynamic_update_slice(gates_all, gates_own[:, None], (0, grid.w, 0, 0))
+    thin_all = lax.dynamic_update_slice(thin_all, thin_own[None], (grid.w, 0, 0))
     feed_all = lax.dynamic_update_slice(feed_all, feed_windows, (0, grid.n, 0, 0))
     feed_all = lax.dynamic_update_slice(
         feed_all, lax.dynamic_slice_in_dim(feed_windows, grid.z, 1, 1), (0, grid.w, 0, 0)
     )
     cot_all = lax.dynamic_update_slice(cot_all, cot_own[None, None], (grid.z, grid.t, 0, 0))
-    rec_all, gates_all, feed_all, cot_all = bring_weights(
-        grid, rec_all, gates_all, feed_all, cot_all
-    )
-    feed_all = feed_all[:, : grid.n]
+    rec_all, gates_all, thin_all, feed_all, cot_all = bring_weights(
+        grid, rec_all, gates_all, thin_all, feed_all, cot_all
+    )
     rec_all = rec_all.reshape(3, width, channels)
-    input_full, gelu_full, out_turned = rec_all[0], rec_all[1], rec_all[2]
-    thin_all = gates_all[:, gate_rows:].reshape(grid.n, -1)[:, :thin_size]
-    gates_all = gates_all[:, :gate_rows]
-    gates_all = (
-        gates_all.reshape(grid.n, 2, head_count, lane_own, block_size)
-        .transpose(1, 2, 0, 3, 4)
-        .reshape(2, head_count, block_size, block_size)
-    )
+    input_full, gelu_full = rec_all[0], rec_all[1]
+    gates_all = gates_all.reshape(2, head_count, block_size, block_size)
     inlet_full, forget_full = gates_all[0], gates_all[1]
-
-    thin_all = thin_all.astype(F32)
-    gain_first, out_shift, gain_second = (
-        thin_all[:, i * d_own : (i + 1) * d_own].reshape(width) for i in range(3)
-    )
-    per = head_count * lane_own
-    lane_rows = (
-        thin_all[:, 3 * d_own :]
-        .reshape(grid.n, CONV + 6, head_count, lane_own)
-        .transpose(1, 2, 0, 3)
-        .reshape(CONV + 6, channels)
-    )
-    gelu_shift, input_shift = lane_rows[0], lane_rows[1]
-    conv_taps = lane_rows[2 : 2 + CONV]
-    conv_offset, inlet_shift, forget_shift, rate_wide = (lane_rows[2 + CONV + i] for i in range(4))
-    inlet_shift = inlet_shift.reshape(head_count, block_size)
-    forget_shift = forget_shift.reshape(head_count, block_size)
-    rate_wide = rate_wide.reshape(head_count, block_size)
-
-    feed_all = feed_all.reshape(3, width, window)
-    gate_full, up_full, down_turned = feed_all[0], feed_all[1], feed_all[2]
-    first_tile = jnp.minimum(grid.z * window_tiles, unit_tiles - window_tiles)
-    unit_place = lax.iota(jnp.int32, window) + first_tile * LANE
-    valid = (unit_place >= grid.z * window)[None, :]
-
-    inputs = block_in.astype(F32).reshape(rows_all, width)
-    normed = rms_norm(inputs, gain_first).astype(BF16)
-    input_pre = dot(normed, input_full) + input_shift
-    input_branch = input_pre.astype(BF16).reshape(seq_count, tok_count, channels)
-    marks = (segment_ids + 1).astype(BF16)
-    rim_values, rim_marks = shifted(
-        (input_branch[:, tok_count - margin :], marks[:, tok_count - margin :]), "wide", 1
-    )
-    extended = jnp.concatenate([rim_values, input_branch], axis=1).astype(F32)
-    marks_ext = jnp.concatenate([rim_marks, marks], axis=1).astype(F32)
-    conv_out = causal_conv(extended, marks_ext, conv_taps, conv_offset)
-    blocks = conv_out.astype(BF16).reshape(seq_count, tok_count, head_count, block_size)
-    inlet_pre = (
-        jnp.einsum("sthc,hcd->sthd", blocks, inlet_full, preferred_element_type=F32) + inlet_shift
-    )
-    forget_pre = (
-        jnp.einsum("sthc,hcd->sthd", blocks, forget_full, preferred_element_type=F32) + forget_shift
-    )
-    starts = (marks_ext[:, margin:] != marks_ext[:, margin - 1 : margin - 1 + tok_count])[
-        :, :, None, None
-    ]
-    blocks_wide = blocks.astype(F32)
-    decay, drive = lru_terms(inlet_pre, forget_pre, blocks_wide, rate_wide, starts)
-    flat = (seq_count, tok_count, channels)
-    decay_cum, local_state = local_scan(decay.reshape(flat), drive.reshape(flat), False)
-    gelu_pre = dot(normed, gelu_full) + gelu_shift
-    gelu_branch = jax.nn.gelu(gelu_pre).reshape(flat)
-    state_in = prefix_wide(grid, jnp.stack([decay_cum[:, -1], local_state[:, -1]]), False)
-    state = local_state + decay_cum * state_in[:, None]
-    mixed = (state * gelu_branch).astype(BF16).reshape(rows_all, channels)
-    branch_part = dot_nt(mixed, out_turned).reshape(grid.tensor, rows_half, width)
-    own_inputs = pick(inputs.reshape(grid.tensor, rows_half, width), grid.t)
-    resid, second_all = bring_second(
-        grid, branch_part, own_inputs, out_shift[None], gain_second[None]
+    table = jnp.sum(thin_all.astype(F32), axis=0)
+    lane_rows = table[: CONV + 6]
+    gain_first, out_shift, gain_second = table[CONV + 6 : thin_count].reshape(3, width)
+    rate = lane_rows[CONV + 5]
+    lanes = jnp.concatenate([lane_rows[: CONV + 5], jnp.stack([jax.nn.softplus(rate), jax.nn.sigmoid(rate)])])
+    lanes = jnp.pad(lanes, ((0, LANE_ROWS - lanes.shape[0]), (0, 0)))
+
+    x = block_in.reshape(rows_all, width)
+    normed, ext, conv, gelu_pre, inlet_pre, forget_pre, cum, local_state = enter_recurrence(
+        x, halo, gain_first[None], rec_all, inlet_full, forget_full, lanes, flags, seq_count
+    )
+    entered, mixed, resid, second_own = make_second(
+        grid, cum, local_state, gelu_pre, rec_all, x, out_shift[None], gain_second[None], seq_count
     )
 
     rows_feed = grid.hi * rows_all
-    second_all = second_all.reshape(rows_feed, width)
-    cot_all = cot_all.reshape(rows_feed, width)
-    gate_pre = dot(second_all, gate_full)
-    up_pre = dot(second_all, up_full)
-    product, pull_feed = jax.vjp(gelu_product, gate_pre, up_pre)
-    hidden = jnp.where(valid, product, 0.0).astype(BF16)
-    hidden_grad = jnp.where(valid, dot(cot_all, down_turned), 0.0)
-    gate_pre_grad, up_pre_grad = pull_feed(hidden_grad)
-    gate_low = gate_pre_grad.astype(BF16)
-    up_low = up_pre_grad.astype(BF16)
-    second_part = dot_nt(gate_low, gate_full) + dot_nt(up_low, up_full)
-    shape_rows = (grid.hi, grid.tensor, rows_half, width)
-    branch_low, gain_two_grad = sum_rows(
-        grid, True, second_part.astype(BF16).reshape(shape_rows), resid, cot_own, gain_second[None]
-    )
+    second_all, gate_low, up_low, hidden, branch_low, gain_two_grad = feed_forward(
+        grid, second_own, feed_all, cot_all, resid, gain_second[None], unit_tiles
+    )
+    second_all, cot_all = (v.reshape(rows_feed, width) for v in (second_all, cot_all))
+    gate_low, up_low, hidden = (v.reshape(rows_feed, window) for v in (gate_low, up_low, hidden))
     branch_low = branch_low.reshape(rows_all, width)
     gain_two_grad = jnp.sum(gain_two_grad, axis=0)
-    feed_part = dot_nt(hidden, down_turned).astype(BF16)
-    block_out, _ = sum_rows(
-        grid, False, feed_part.reshape(shape_rows), resid, cot_own, gain_second[None]
-    )
-    block_out = block_out.reshape(block_in.shape)
-
-    out_shift_grad = jnp.sum(branch_low.astype(F32), axis=0)
-    mixed_grad = dot(branch_low, out_turned).reshape(flat)
-    state_grad = mixed_grad * gelu_branch
-    _, pull_gelu = jax.vjp(jax.nn.gelu, gelu_pre)
-    (gelu_pre_grad,) = pull_gelu((mixed_grad * state).reshape(rows_all, channels))
-    gelu_low = gelu_pre_grad.astype(BF16)
-    gelu_b_grad = jnp.sum(gelu_low.astype(F32), axis=0)
-    decay_flat = decay.reshape(flat)
-    next_decay = jnp.concatenate([decay_flat[:, 1:], jnp.ones_like(decay_flat[:, :1])], axis=1)
-    tail_decay, local_carried = local_scan(next_decay, state_grad, True)
-    head_decay = decay_flat[:, 0]
-    from_right = prefix_wide(
-        grid,
-        jnp.stack([head_decay * tail_decay[:, 0], head_decay * local_carried[:, 0]]),
-        True,
-    )
-    carried = (local_carried + tail_decay * from_right[:, None]).reshape(blocks.shape)
-    prev_state = jnp.concatenate([state_in[:, None], state[:, :-1]], axis=1).reshape(blocks.shape)
-
-    def lru_local(inlet_arg, forget_arg, block_arg, rate_arg):
-        return lru_terms(inlet_arg, forget_arg, block_arg, rate_arg, starts)
-
-    _, pull_lru = jax.vjp(lru_local, inlet_pre, forget_pre, blocks_wide, rate_wide)
-    inlet_grad, forget_grad, block_direct, rate_grad = pull_lru((carried * prev_state, carried))
-    inlet_low = inlet_grad.astype(BF16)
-    forget_low = forget_grad.astype(BF16)
-    inlet_b_grad = jnp.sum(inlet_low.astype(F32), axis=(0, 1))
-    forget_b_grad = jnp.sum(forget_low.astype(F32), axis=(0, 1))
-    gate_w_grads = jnp.stack(
-        [
-            jnp.einsum("sthc,sthd->hcd", blocks, low, preferred_element_type=F32)
-            for low in (inlet_low, forget_low)
-        ]
-    )
+    feed_part = dot_nt(hidden, feed_all[2, : grid.n].reshape(width, window)).astype(BF16)
+    feed_part = feed_part.reshape(grid.hi, grid.tensor, rows_half, width)
+    block_out = block_output(grid, feed_part, resid).reshape(block_in.shape)
+
+    gelu_low, input_low, gate_w_grads, lane_grads, out_shift_grad = leave_recurrence(
+        grid, branch_low, rec_all, gelu_pre, local_state, cum, inlet_pre, forget_pre, conv, ext, entered,
+        inlet_full, forget_full, lanes, flags, seq_count,
+    )
+    out_shift_grad = jnp.sum(out_shift_grad, axis=0)
     gate_w_grads = (
         gate_w_grads.reshape(2, head_count, grid.n, lane_own, block_size)
         .transpose(2, 0, 1, 3, 4)
         .reshape(width, block_size)
-        .astype(BF16)
-    )
-    conv_grad = (
-        block_direct
-        + jnp.einsum("sthd,hcd->sthc", inlet_low, inlet_full, preferred_element_type=F32)
-        + jnp.einsum("sthd,hcd->sthc", forget_low, forget_full, preferred_element_type=F32)
-    )
-
-    def conv_local(ext_arg, taps_arg, offset_arg):
-        return causal_conv(ext_arg, marks_ext, taps_arg, offset_arg)
-
-    _, pull_conv = jax.vjp(conv_local, extended, conv_taps, conv_offset)
-    ext_grad, taps_grad, offset_grad = pull_conv(conv_grad.reshape(flat))
-    rim_grad = shifted(ext_grad[:, :margin], "wide", -1)
-    branch_input_grad = ext_grad[:, margin:] + jnp.concatenate(
-        [jnp.zeros((seq_count, tok_count - margin, channels), F32), rim_grad], axis=1
-    )
-    input_low = branch_input_grad.astype(BF16).reshape(rows_all, channels)
-    input_b_grad = jnp.sum(input_low.astype(F32), axis=0)
+    )
     first_part = dot_nt(input_low, input_full) + dot_nt(gelu_low, gelu_full)
+    inputs = x.astype(F32)
     scale_first = lax.rsqrt(jnp.mean(inputs * inputs, axis=-1, keepdims=True) + 1e-06)
     gain_one_grad = jnp.sum(first_part * inputs * scale_first, axis=0)
     first_part = first_part.astype(BF16)
     gain_grads = jnp.stack([gain_one_grad, gain_two_grad])
     gain_grads = gain_grads + grid.swap(gain_grads)
 
-    lane_grads = jnp.stack(
-        [
-            v.reshape(channels)
-            for v in (
-                gelu_b_grad,
-                input_b_grad,
-                taps_grad[0],
-                taps_grad[1],
-                taps_grad[2],
-                taps_grad[3],
-                offset_grad,
-                inlet_b_grad,
-                forget_b_grad,
-                rate_grad,
-            )
-        ]
-    )
     lane_grads = (
-        lane_grads.reshape(CONV + 6, head_count, grid.n, lane_own)
+        lane_grads[: CONV + 6]
+        .reshape(CONV + 6, head_count, grid.n, lane_own)
         .transpose(2, 0, 1, 3)
         .reshape(grid.n, -1)
     )

time: 1040 us -> 906 us (0.87)
  matrix products: 106 us -> 21 us
  Pallas kernels: 724 us -> 802 us
  local copies, waits for them, and re-layouts: 107 us -> 53 us
  other arithmetic: 54.6 us -> 23 us
  starting transfers between devices: 19.9 us -> 2.32 us
  waiting for transfers between devices: 13.3 us -> 0.01 us
    pallas_call x5, Pallas kernels: 245 us -> 321 us  [the longest x1 148 us: feed_forward(): pl.pallas_call(functools.partial(feed_kernel, grid.n, tensor, unit_tiles)...]
    dot_general x12 -> x0, matrix products: 60.2 us -> none  [the longest x6 52.4 us: dot(): return jnp.dot(left, right, preferred_element_type=F32)]
    dot_general x6 -> x3, matrix products: 46.2 us -> 21 us  [dot_nt(): return jnp.einsum('ik,jk->ij', left, right, preferred_element_type=F32)]
    slice x12 -> x3, local copies, waits for them, and re-layouts: 36.8 us -> 16.6 us  [the longest x1 9.49 us: local(): input_full, gelu_full = (rec_all[0], rec_all[1])]
    reduce_sum x7 -> x3, other arithmetic: 15.8 us -> 1.65 us  [the longest x1 1.29 us: local(): table = jnp.sum(thin_all.astype(F32), axis=0)]
    ppermute x8 -> x0, starting transfers between devices: 13.4 us -> none  [flip(): return lax.ppermute(value, 'wide', [(i, i ^ bit) for i in range(self.n)])]
    ppermute x8 -> x0, waiting for transfers between devices: 12.1 us -> none  [flip(): return lax.ppermute(value, 'wide', [(i, i ^ bit) for i in range(self.n)])]
  transfers between devices with their start and end apart: 12 -> 3, of which waited for: 7 -> 0; matrix products, arithmetic and copies ran while one was open for 6% -> 7% of each run, Pallas kernels for 8% -> 36%
where the time goes in v3:
time: 906 us; the launch traced here: 903 us
  Pallas kernels  802 us (89%)
  local copies, waits for them, and re-layouts  53 us (6%)
  other arithmetic  23 us (3%)
  matrix products  21 us (2%)
    pallas_call x1, Pallas kernels, bring_weights(): pl.pallas_call(functools.partial(weights_kernel, n, tensor), out_shape=[j...  241 us
    pallas_call x1, Pallas kernels, send_grads(): pl.pallas_call(functools.partial(grads_kernel, grid.n, grid.tensor, spans...  241 us
    pallas_call x1, Pallas kernels, feed_forward(): pl.pallas_call(functools.partial(feed_kernel, grid.n, tensor, unit_tiles)...  148 us
    pallas_call x1, Pallas kernels, block_output(): pl.pallas_call(functools.partial(out_kernel, grid.n, grid.tensor), out_sh...  80.2 us
    pallas_call x1, Pallas kernels, leave_recurrence(): pl.pallas_call(functools.partial(leave_kernel, grid.n, grid.tensor, seqs)...  39.3 us
    pallas_call x1, Pallas kernels, make_second(): pl.pallas_call(functools.partial(second_kernel, grid.n, grid.tensor, seqs...  35.2 us
    dot_general x3, matrix products, dot_nt(): return jnp.einsum('ik,jk->ij', left, right, preferred_element_type=F32)  21 us
  transfers between devices with their start and end apart: 3, of which 0 were waited for; matrix products, arithmetic and copies ran while one was open for 7% of the time, Pallas kernels for 36%

profile of v3, /device:TPU:27, one launch (start us, length us, event | category | flops | bytes accessed | tf_op | source)
XLA Modules:
  0.0 903.1 jit_solution(17417659364610817799)
XLA Ops:
  0.7 0.7 add_convert_fusion
  1.4 1.8 collective-permute-start.1
  3.2 1.5 slice.195
  4.7 2.2 pad_maximum_fusion.1
  7.1 1.5 slice_bitcast_fusion.6
  8.8 1.6 dynamic_update_slice.26
  10.6 0.3 dynamic_update_slice.27
  10.9 1.1 copy.88
  12.0 2.3 stack_reshape.6
  14.3 2.1 copy.89
  16.4 2.3 stack_reshape.7
  18.6 1.0 copy.111
  19.7 0.8 pad_maximum_fusion.5
  20.5 3.4 pad_maximum_fusion
  23.9 1.0 dynamic-slice_dynamic-update-slice_fusion.feed
  24.9 0.9 bitcast_dynamic-update-slice_fusion.cot
  25.8 0.6 constant_dynamic-update-slice_fusion.1.gates
  26.4 0.6 fusion.5.thin
  27.1 1.1 fusion.4.rec
  28.2 241.2 %bring_weights.1 = (bf16[3,16,160,1280]{3,2,1,0:T(8,128)(2,1)}, bf16[10,16,16,256]{3,2,1,0:T(8,128)(2,1)}, bf16[16,16,1280]{2,1,0:T(8,128)(2,1)}, bf16[3,20,160,...) custom-call(bf16[3,16,160,1280]{3,2,1,0:T(8,128)(2,1)} %fusion.4.rec, ...), custom_call_target="tpu_custom_call", output_to_operand_aliasing={{0}: (0, {}), {1}: (1, {}), {2}: (2, {}), {3}: (3, {}), {4}... | custom-call | tf_op jit(solution)/shard_map/bring_weights/pallas_call | solution.py:350
  269.4 1.3 convert_reduce_fusion
  270.7 0.3 multiply_reduce_fusion
  271.1 1.2 fusion.12
  272.3 0.6 copy.113
  272.9 0.6 copy.118
  273.5 0.6 copy.119
  274.2 9.5 %fusion.11 = (bf16[1,16,160,1280]{3,2,1,0:T(8,128)(2,1)}, bf16[1,16,160,1280]{3,2,1,0:T(8,128)(2,1)}) fusion(bf16[3,16,160,1280]{3,2,1,0:T(8,128)(2,1)} %get-tuple-element.63), kind=kLoop, calls=%fused_computation.100 | loop fusion | bytes 26214400 | tf_op jit(solution)/shard_map/slice | solution.py:1622
  283.7 5.6 slice.208
  289.2 0.7 select_maximum_fusion.lanes
  290.2 0.7 pad_convert_fusion.flags
  290.9 0.6 select_bitcast_fusion.halo
  291.5 17.8 %enter_recurrence.1 = (bf16[256,2560]{1,0:T(8,128)(2,1)}, bf16[2,136,1280]{2,1,0:T(8,128)(2,1)}, bf16[256,1280]{1,0:T(8,128)(2,1)}, f32[256,1280]{1,0:T(8,128)},...) custom-call(bf16[256,2560]{1,0:T(8,128)(2,1)} %bitcast.203, ...), custom_call_target="tpu_custom_call" | custom-call | tf_op jit(solution)/shard_map/enter_recurrence/pallas_call | solution.py:518
  309.3 35.2 %make_second.1 = (f32[8,1280]{1,0:T(8,128)}, bf16[256,1280]{1,0:T(8,128)(2,1)}, f32[128,2560]{1,0:T(8,128)}, bf16[128,2560]{1,0:T(8,128)(2,1)}) custom-call(f32[256,1280]{1,0:T(8,128)} %get-tuple-element.65.cum, f32[256,1280]{1,0:T(8,128)} %get-tuple-element.66.local, f32[256,1280]{1,0:T(8,128)} %get-tuple-element.67.gelu_pre, ...), custom_call_target="tpu_custom_call" | custom-call | tf_op jit(solution)/shard_map/make_second/pallas_call | solution.py:667
  344.5 148.1 %feed_forward.1 = (bf16[4,2,128,2560]{3,2,1,0:T(8,128)(2,1)}, bf16[4,256,1024]{2,1,0:T(8,128)(2,1)}, bf16[4,256,1024]{2,1,0:T(8,128)(2,1)}, bf16[4,256,1024]{2,1...) custom-call(bf16[128,2560]{1,0:T(8,128)(2,1)} %get-tuple-element.68.own, ...), custom_call_target="tpu_custom_call" | custom-call | tf_op jit(solution)/shard_map/feed_forward/pallas_call | solution.py:1108
  492.6 39.3 %leave_recurrence.1 = (bf16[256,1280]{1,0:T(8,128)(2,1)}, bf16[256,1280]{1,0:T(8,128)(2,1)}, bf16[2,5,256,256]{3,2,1,0:T(8,128)(2,1)}, f32[16,1280]{1,0:T(8,128)}, f32[8,2560]{1,0:T(8,128)}) custom-call(bf16[256,2560]{1,0:T(8,128)(2,1)} %bitcast.205, bf16[3,2560,1280]{2,1,0:T(8,128)(2,1)} %bitcast.199, f32[256,1280]{1,0:T(8,128)} %get-tuple-element.67.gelu_pre, ...), custom_call_target="tpu_custom_call" | custom-call | tf_op jit(solution)/shard_map/leave_recurrence/pallas_call | solution.py:832
  532.0 5.1 fusion.16
  537.1 6.1 fusion.1
  543.3 0.5 collective-permute-start.2
  543.8 9.9 %convolution_convert_fusion = bf16[1024,2560]{1,0:T(8,128)(2,1)} fusion(bf16[1024,1024]{1,0:T(8,128)(2,1)S(1)} %bitcast.225, bf16[2560,1024]{1,0:T(8,128)(2,1)} %bitcast.214), kind=kOutput, calls=%fused_computation | convolution fusion | flops 5371330560 | bytes 12582912 | tf_op jit(solution)/shard_map/ik,jk->ij/dot_general | solution.py:1514
  553.7 1.1 reshape.206
  555.2 2.5 copy.102
  557.8 80.2 %block_output.1 = bf16[2,128,2560]{2,1,0:T(8,128)(2,1)} custom-call(bf16[4,2,128,2560]{3,2,1,0:T(8,128)(2,1)} %bitcast.215, f32[128,2560]{1,0:T(8,128)} %get-tuple-element.71.resid), custom_call_target="tpu_custom_call" | custom-call | tf_op jit(solution)/shard_map/block_output/pallas_call | solution.py:1161
  638.0 0.8 fusion.9
  639.0 0.8 reshape.208.thin
  639.8 240.6 %send_grads.1 = (bf16[3,4,160,1024]{3,2,1,0:T(8,128)(2,1)}, f32[4,160,1024]{2,1,0:T(8,128)}, bf16[256,2560]{1,0:T(8,128)(2,1)}, f32[8,160]{1,0:T(8,128)}) custom-call(bf16[1024,2560]{1,0:T(8,128)(2,1)} %bitcast.216, bf16[1024,2560]{1,0:T(8,128)(2,1)} %bitcast.38.cot, bf16[256,2560]{1,0:T(8,128)(2,1)} %get-tuple-element.82.normed, ...), custom_call_target="tpu_custom_call" | custom-call | tf_op jit(solution)/shard_map/send_grads/pallas_call | solution.py:1469
  880.5 2.7 slice_bitcast_fusion
  883.1 0.6 copy-done.2
  883.7 1.2 slice_bitcast_fusion.13
  884.9 0.6 fusion.15
  885.5 0.7 slice_bitcast_fusion.20
  886.2 0.7 slice_bitcast_fusion.21
  887.1 0.7 fusion.13
  888.0 1.0 copy.128
  889.0 1.0 copy.129
  889.9 1.0 copy.130
  890.9 0.7 fusion.2
  891.6 2.6 fusion.3
  894.3 0.6 slice_bitcast_fusion.25
  895.0 0.6 copy.106
  895.6 2.9 convert_bitcast_fusion
  898.5 1.6 maximum_convert_fusion.1
  900.1 1.6 maximum_convert_fusion
  901.7 0.3 copy-done.7
  902.0 1.1 copy.146
  (117 shorter events, 2.2 us)
Async XLA Ops:
  1.4 288.5 %collective-permute-start.1 = (bf16[2,3]{1,0:T(2,128)(2,1)S(1)}, bf16[2,3]{1,0:T(2,128)(2,1)S(1)}, u32[]{:S(2)}, u32[]{:S(2)}) collective-permute-start(bf16[2,3]{1,0:T(2,128)(2,1)S(1)} %slice.204), channel_id=1, source_target_pairs={{0,2},{2,4},{4,6},{6,8},{8,10},{10,12},{12,14},{14,16},{16,18},{18... | collective-permute-start | bytes 44 | tf_op jit(solution)/shard_map/ppermute | solution.py:44
  4.7 286.2 %collective-permute-start = (bf16[2,8,2560]{2,1,0:T(8,128)(2,1)}, bf16[2,8,2560]{2,1,0:T(8,128)(2,1)S(1)}, u32[]{:S(2)}, u32[]{:S(2)}) collective-permute-start(bf16[2,8,2560]{2,1,0:T(8,128)(2,1)} %slice.195), channel_id=1, source_target_pairs={{0,2},{2,4},{4,6},{6,8},{8,10},{10,12},{12,14},{14,16},{16,18},{18... | collective-permute-start | bytes 245768 | tf_op jit(solution)/shard_map/ppermute | solution.py:44
  7.0 1.6 copy-start.24
  7.0 1.6 copy-start.25
  7.0 1.6 copy-start.26
  7.0 1.6 copy-start.27
  7.0 1.7 copy-start.28
  7.0 1.7 copy-start.29
  7.0 1.7 copy-start.21
  7.1 3.4 copy-start.30
  7.1 3.4 copy-start.31
  7.1 3.4 copy-start.32
  7.1 3.8 copy-start.14
  20.5 4.4 copy-start.15
  23.9 3.2 copy-start.10
  23.9 3.2 copy-start.11
  28.2 242.6 %copy-start = (bf16[2,128,2560]{2,1,0:T(8,128)(2,1)S(1)}, bf16[2,128,2560]{2,1,0:T(8,128)(2,1)}, u32[]{:S(2)}) copy-start(bf16[2,128,2560]{2,1,0:T(8,128)(2,1)} %param.21) | copy-start | bytes 3932164
  269.4 1.7 copy-start.5
  271.1 12.6 %copy-start.19 = (f32[2,128]{1,0:T(2,128)}, f32[2,128]{1,0:T(2,128)S(1)}, u32[]{:S(2)}) copy-start(f32[2,128]{1,0:T(2,128)S(1)} %multiply_reduce_fusion) | copy-start | bytes 3076
  283.7 253.4 %copy-start.22 = (f32[256]{0:T(256)}, f32[256]{0:T(256)S(1)}, u32[]{:S(2)}) copy-start(f32[256]{0:T(256)S(1)} %bitcast_rsqrt_fusion) | copy-start | bytes 3076
  532.0 5.1 copy-start.1
  532.0 5.1 copy-start.13
  537.1 6.1 copy-start.17
  537.1 6.7 copy-start.9
  543.3 94.7 %collective-permute-start.2 = (f32[2,2560]{1,0:T(2,128)S(1)}, f32[2,2560]{1,0:T(2,128)}, u32[]{:S(2)}, u32[]{:S(2)}) collective-permute-start(f32[2,2560]{1,0:T(2,128)S(1)} %pad_maximum_fusion.6), channel_id=1, source_target_pairs={{0,1},{1,0},{2,3},{3,2},{4,5},{5,4},{6,7},{7,6},{8,9},{9,8},{10,11... | collective-permute-start | bytes 61448 | tf_op jit(solution)/shard_map/ppermute | solution.py:36
  543.8 11.3 %copy-start.16 = (f32[8,2560]{1,0:T(8,128)S(1)}, f32[8,2560]{1,0:T(8,128)}, u32[]{:S(2)}) copy-start(f32[8,2560]{1,0:T(8,128)} %get-tuple-element.88) | copy-start | bytes 245764
  880.4 3.3 copy-start.2
  883.7 1.2 copy-start.18
  883.7 3.2 copy-start.8
  888.0 2.9 copy-start.4
  888.0 2.9 copy-start.6
  889.9 1.6 copy-start.20
  889.9 1.7 copy-start.3
  889.9 1.7 copy-start.23
  894.3 4.3 copy-start.12
  900.1 1.9 copy-start.7

commit v4 on v3

--- a/solution.py
+++ b/solution.py
@@ -164,6 +164,10 @@
         return remote(ref, ref, self.sems, (s - 1) if up else hi + s - 2, spot.line(other))
 
     def first(self):
+        self.first_line()
+        self.fans.hand_on(self.spot.z, 0)
+
+    def first_line(self):
         spot, hi = self.spot, self.spot.hi
 
         @pl.when(spot.z < hi - 1)
@@ -173,8 +177,6 @@
         @pl.when(spot.z > 0)
         def _():
             self.line_copy(1, False).start()
-
-        self.fans.hand_on(spot.z, 0)
 
     def onward(self, s):
         spot, hi = self.spot, self.spot.hi
@@ -252,8 +254,9 @@
 
 
 class Turns:
-    def __init__(self, spot, window_of, at, sems, sides):
+    def __init__(self, spot, distances, window_of, at, sems, sides):
         self.spot, self.window_of, self.at, self.sems = spot, window_of, at, sems
+        self.distances = distances
         self.fans = Fans(spot, at, sems, spot.hi, sides)
 
     def line_copy(self, distance):
@@ -270,29 +273,54 @@
         return remote(ref, ref, self.sems, distance, self.spot.line(place))
 
     def first(self):
-        for distance in range(1, self.spot.hi):
+        for distance in self.distances:
+            self.start(distance)
+
+    def start(self, distance):
+        if distance:
             self.line_copy(distance).start()
-        self.fans.hand_on(self.spot.z, 0)
+        else:
+            self.fans.hand_on(self.spot.z, 0)
 
     def onward(self, distance):
-        self.line_here(distance).wait_recv()
-        self.fans.hand_on(self.back(distance), 0)
+        if distance in self.distances:
+            self.line_here(distance).wait_recv()
+            self.fans.hand_on(self.back(distance), 0)
 
     def second(self, distance):
-        self.fans.pass_on(self.back(distance))
+        if distance in self.distances:
+            self.fans.pass_on(self.back(distance))
 
     def finish(self):
-        for distance in range(self.spot.hi):
+        for distance in self.distances:
             self.fans.finish(self.back(distance))
             if distance:
                 self.line_copy(distance).wait_send()
 
 
+EARLY = (2,)
+LATE = (0, 1, 3)
+
+
+def feed_turns(spot, distances, feed, sems, cube):
+    def index(place, k):
+        return place * spot.inner_size + jnp.bitwise_xor(spot.inner, k)
+
+    return Turns(
+        spot,
+        distances,
+        lambda place: feed.at[:, spot.n + place],
+        lambda place, k: feed.at[:, index(place, k)],
+        sems,
+        cube,
+    )
+
+
 def weights_kernel(
-    n, tensor, rec, gates, thin, feed, cot, rec_all, gates_all, thin_all, feed_all, cot_all,
-    rec_sems, gates_sems, thin_sems, feed_sems, cot_sems,
+    n, tensor, rec, gates, thin, feed, rec_all, gates_all, thin_all, feed_all,
+    rec_sems, gates_sems, thin_sems, feed_sems,
 ):
-    del rec, gates, thin, feed, cot
+    del rec, gates, thin, feed
     spot = Spot(n, tensor)
     hi = spot.hi
 
@@ -304,21 +332,9 @@
         Chain(spot, lambda place, k: thin_all.at[index(place, k)], thin_sems, cube),
         Chain(spot, lambda place, k: gates_all.at[:, index(place, k)], gates_sems, cube),
         Chain(spot, lambda place, k: rec_all.at[:, index(place, k)], rec_sems, cube),
-        Turns(
-            spot,
-            lambda place: feed_all.at[:, n + place],
-            lambda place, k: feed_all.at[:, index(place, k)],
-            feed_sems,
-            cube,
-        ),
-        Chain(
-            spot,
-            lambda place, k: cot_all.at[place, lax.rem(spot.t + k, tensor)],
-            cot_sems,
-            [spot.cross],
-        ),
+        feed_turns(spot, EARLY, feed_all, feed_sems, cube),
     ]
-    spot.greet(*cube, spot.cross)
+    spot.greet(*cube)
     for move in moves:
         move.first()
     for s in range(1, hi):
@@ -332,6 +348,10 @@
         move.finish()
 
 
+def turn_sems(grid):
+    return pltpu.SemaphoreType.DMA((2, grid.n))
+
+
 def blank(*shapes):
     return pl.pallas_call(
         lambda *refs: None,
@@ -342,10 +362,10 @@
     )()
 
 
-def bring_weights(grid, rec, gates, thin, feed, cot):
+def bring_weights(grid, rec, gates, thin, feed):
     n, hi, tensor = grid.n, grid.hi, grid.tensor
     far = pl.BlockSpec(memory_space=pl.ANY)
-    arrays = (rec, gates, thin, feed, cot)
+    arrays = (rec, gates, thin, feed)
     cube = grid.inner_size.bit_length() - 1
     return pl.pallas_call(
         functools.partial(weights_kernel, n, tensor),
@@ -357,8 +377,7 @@
             chain_sems(cube),
             chain_sems(cube),
             chain_sems(cube),
-            pltpu.SemaphoreType.DMA((2, grid.inner_size * hi)),
-            chain_sems(1),
+            turn_sems(grid),
         ],
         compiler_params=pltpu.CompilerParams(
             collective_id=0, has_side_effects=True, vmem_limit_bytes=GRANT
@@ -437,109 +456,35 @@
     lax.fori_loop(0, tiles, one, (start,) * seqs)
 
 
-def enter_kernel(
-    seqs, x, halo, gain, w_input, w_gelu, w_inlet, w_forget, lanes, flags,
-    normed, ext, conv, gelu_pre, inlet_pre, forget_pre, cum, local, held, factor, addend,
-):
-    rows = x.shape[0]
-    length = rows // seqs
-    width = conv.shape[1]
-
-    @pl.when(pl.program_id(0) == 0)
-    def _():
-        def norm(source, at, to):
-            value = source[at, :].astype(F32)
-            scale = lax.rsqrt(jnp.mean(value * value, axis=-1, keepdims=True) + 1e-06)
-            value = (value * scale * gain[...]).astype(BF16)
-            held[pl.ds(pl.multiple_of(at.start + to, STEP), STEP), :] = value
-            return value
-
-        def main(at):
-            normed[at, :] = norm(x, at, 0)
-
-        by_rows(rows, STEP, main)
-        by_rows(halo.shape[0], STEP, lambda at: norm(halo, at, rows))
-
-    table = lanes[...]
-
-    def row(i):
-        return table[i : i + 1]
-
-    branch = (dot(held[...], w_input[0]) + row(INPUT_SHIFT)).astype(BF16)
-    gelu_pre[...] = dot(held[0:rows, :], w_gelu[0]) + row(GELU_SHIFT)
-    for s in range(seqs):
-        here = slice(s * length, (s + 1) * length)
-        front = rows + s * HALO
-        longer = jnp.concatenate(
-            [branch[front : front + HALO].astype(F32), branch[here].astype(F32)], axis=0
-        )
-        ext[s] = longer.astype(BF16)
-        total = row(CONV_SHIFT) + row(TAPS) * longer[HALO:]
-        for k in range(1, CONV):
-            moved = pltpu.roll(longer, k, 0)[HALO:]
-            total = total + jnp.where(flags[here, k : k + 1] > 0.5, row(TAPS + k) * moved, 0.0)
-        conv[here, :] = total.astype(BF16)
-    blocks = conv[...]
-    inlet_pre[...] = dot(blocks, w_inlet[0]) + row(INLET_SHIFT)
-    forget_pre[...] = dot(blocks, w_forget[0]) + row(FORGET_SHIFT)
-
-    def terms(at):
-        starts = flags[at, 0:1] > 0.5
-        decay, scaler = decay_of(jax.nn.sigmoid(forget_pre[at, :]), row(RATE_SOFT), starts)
-        factor[at, :] = decay
-        addend[at, :] = scaler * jax.nn.sigmoid(inlet_pre[at, :]) * conv[at, :].astype(F32)
-
-    by_rows(rows, 32, terms)
-
-    def write(at, a, b):
-        cum[at, :] = a
-        local[at, :] = b
-
-    scan_rows(seqs, length, width, lambda at: (factor[at, :], addend[at, :]), write, False)
-
-
-def enter_recurrence(x, halo, gain, rec, inlet, forget, lanes, flags, seqs):
+def first_kernel(x, input_low, gelu_low, w_input, w_gelu, scale, part, gained):
+    value = dot_nt(input_low[...], w_input[0]) + dot_nt(gelu_low[...], w_gelu[0])
+    part[...] = value.astype(BF16)
+    gained[...] = jnp.sum(
+        (value * x[...].astype(F32) * scale[:, 0:1]).reshape(-1, 8, value.shape[1]), axis=0
+    )
+
+
+def first_gradient(x, input_low, gelu_low, rec, scale):
     rows, d = x.shape
-    heads, width = inlet.shape[:2]
-    channels = heads * width
-    longer = rows // seqs + HALO
+    channels = input_low.shape[1]
+    chunk = 512
 
     def fixed(a):
-        return pl.BlockSpec(a.shape, lambda h: (0, 0))
-
-    def column(count):
-        return pl.BlockSpec((count, width), lambda h: (0, h))
+        return pl.BlockSpec(a.shape, lambda i: (0, 0))
 
     def weight(k):
-        return pl.BlockSpec((1, d, width), lambda h: (k, 0, h))
-
-    head = pl.BlockSpec((1, width, width), lambda h: (h, 0, 0))
-    wide = jax.ShapeDtypeStruct((rows, channels), F32)
+        return pl.BlockSpec((1, chunk, channels), lambda i: (k, i, 0))
+
+    column = pl.BlockSpec((rows, chunk), lambda i: (0, i))
     return pl.pallas_call(
-        functools.partial(enter_kernel, seqs),
-        grid=(heads,),
-        out_shape=[
-            jax.ShapeDtypeStruct((rows, d), BF16),
-            jax.ShapeDtypeStruct((seqs, longer, channels), BF16),
-            jax.ShapeDtypeStruct((rows, channels), BF16),
-        ]
-        + [wide] * 5,
-        in_specs=[fixed(x), fixed(halo), fixed(gain), weight(0), weight(1), head, head]
-        + [column(LANE_ROWS), fixed(flags)],
-        out_specs=[
-            fixed(x),
-            pl.BlockSpec((seqs, longer, width), lambda h: (0, 0, h)),
-            column(rows),
-        ]
-        + [column(rows)] * 5,
-        scratch_shapes=[
-            pltpu.VMEM((rows + halo.shape[0], d), BF16),
-            pltpu.VMEM((rows, width), F32),
-            pltpu.VMEM((rows, width), F32),
-        ],
+        first_kernel,
+        grid=(d // chunk,),
+        out_shape=[jax.ShapeDtypeStruct((rows, d), BF16), jax.ShapeDtypeStruct((8, d), F32)],
+        in_specs=[column, fixed(input_low), fixed(gelu_low), weight(0), weight(1), fixed(scale)],
+        out_specs=[column, pl.BlockSpec((8, chunk), lambda i: (0, i))],
         compiler_params=pltpu.CompilerParams(vmem_limit_bytes=GRANT),
-        name="enter_recurrence",
-    )(x, halo, gain, rec, rec, inlet, forget, lanes, flags)
+        name="first_gradient",
+    )(x, input_low, gelu_low, rec, rec, scale)
 
 
 class Prefix:
@@ -604,96 +549,231 @@
     ]
 
 
-def second_kernel(
-    n, tensor, seqs, cum, local, gelu_pre, w_out, x, shift, gain,
-    entered, mixed, resid, second,
-    part, out, got, tots, gots, line, cube_sems, line_sems, swap_sems,
+def forward_kernel(
+    n, tensor, seqs, heads,
+    x, halo, gain, w_input, w_gelu, w_inlet, w_forget, lanes, flags, w_out, shift, gain_second, feed, cot,
+    normed, ext, conv, gelu_pre, inlet_pre, forget_pre, cum, local, entered, mixed, resid, second,
+    feed_all, cot_all,
+    held, factor, addend, part, out, got, tots, gots, line, cube_sems, line_sems, swap_sems, feed_sems, cot_sems,
 ):
+    del feed, cot
     spot = Spot(n, tensor)
-    rows = resid.shape[0]
-    every = x.shape[0]
-    length = every // seqs
-    spot.greet(*[spot.flip(bit) for bit in spot.bits], spot.cross)
-    tots[0] = jnp.zeros_like(tots[0])
-    for s in range(seqs):
-        last = slice((s + 1) * length - 1, (s + 1) * length)
-        tots[0, s : s + 1, :] = cum[last, :]
-        tots[0, seqs + s : seqs + s + 1, :] = local[last, :]
-    enter = Prefix(spot, seqs, False, tots, gots, line, cube_sems, line_sems).run()
-    entered[...] = jnp.zeros_like(entered)
-    entered[0:seqs, :] = enter
-    for s in range(seqs):
-
-        def mix(at, s=s):
-            here = pl.ds(pl.multiple_of(s * length + at.start, STEP), STEP)
-            state = local[here, :] + cum[here, :] * enter[s : s + 1]
-            mixed[here, :] = (state * gelu_of(gelu_pre[here, :])[0]).astype(BF16)
-
-        by_rows(length, STEP, mix)
-    values = mixed[...]
-
-    def branch(j, carry):
-        at = pl.ds(pl.multiple_of(j * 256, 256), 256)
-        value = dot_nt(values, w_out[0, at, :])
-        for side in range(tensor):
-            part[side, :, at] = value[side * rows : (side + 1) * rows]
-        return carry
-
-    lax.fori_loop(0, x.shape[1] // 256, branch, 0)
-
-    def put(at):
-        out[at, :] = part[1 - spot.t, at, :].astype(BF16)
-
-    by_rows(rows, STEP, put)
-    copy = remote(out, got, swap_sems, 0, spot.cross)
-    copy.start()
-    copy.wait()
-
-    def norm(at):
-        own = x[pl.ds(pl.multiple_of(spot.t * rows + at.start, STEP), STEP), :].astype(F32)
-        value = own + (part[spot.t, at, :] + got[at, :].astype(F32) + shift[...])
-        resid[at, :] = value
-        scale = lax.rsqrt(jnp.mean(value * value, axis=-1, keepdims=True) + 1e-06)
-        second[at, :] = (value * scale * gain[...]).astype(BF16)
-
-    by_rows(rows, STEP, norm)
-
-
-def make_second(grid, cum, local, gelu_pre, rec, x, shift, gain, seqs):
-    every, d = x.shape
-    channels = cum.shape[1]
-    rows = every // grid.tensor
-    near = pl.BlockSpec(memory_space=pltpu.VMEM)
+    hi = spot.hi
+    rows = x.shape[0]
+    length = rows // seqs
+    width = conv.shape[1]
+    step = pl.program_id(0)
+    cube = [spot.flip(bit) for bit in spot.bits]
+    turns = feed_turns(spot, LATE, feed_all, feed_sems, cube)
+    chain = Chain(
+        spot,
+        lambda place, k: cot_all.at[place, lax.rem(spot.t + k, tensor)],
+        cot_sems,
+        [spot.cross],
+    )
+
+    @pl.when(step == 0)
+    def _():
+        spot.greet(*cube, spot.cross)
+        turns.start(1)
+        turns.start(0)
+        chain.fans.hand_on(spot.z, 0)
+
+        def norm(source, at, to):
+            value = source[at, :].astype(F32)
+            scale = lax.rsqrt(jnp.mean(value * value, axis=-1, keepdims=True) + 1e-06)
+            value = (value * scale * gain[...]).astype(BF16)
+            held[pl.ds(pl.multiple_of(at.start + to, STEP), STEP), :] = value
+            return value
+
+        def main(at):
+            normed[at, :] = norm(x, at, 0)
+
+        by_rows(rows, STEP, main)
+        by_rows(halo.shape[0], STEP, lambda at: norm(halo, at, rows))
+
+    @pl.when(step < heads)
+    def _():
+        table = lanes[...]
+        cols = pl.ds(pl.multiple_of(step * width, width), width)
+
+        def row(i):
+            return table[i : i + 1]
+
+        branch = (dot(held[...], w_input[0]) + row(INPUT_SHIFT)).astype(BF16)
+        gelu_pre[:, cols] = dot(held[0:rows, :], w_gelu[0]) + row(GELU_SHIFT)
+        for s in range(seqs):
+            here = slice(s * length, (s + 1) * length)
+            front = rows + s * HALO
+            longer = jnp.concatenate(
+                [branch[front : front + HALO].astype(F32), branch[here].astype(F32)], axis=0
+            )
+            ext[s] = longer.astype(BF16)
+            total = row(CONV_SHIFT) + row(TAPS) * longer[HALO:]
+            for k in range(1, CONV):
+                moved = pltpu.roll(longer, k, 0)[HALO:]
+                total = total + jnp.where(flags[here, k : k + 1] > 0.5, row(TAPS + k) * moved, 0.0)
+            conv[here, :] = total.astype(BF16)
+        blocks = conv[...]
+        inlet_pre[...] = dot(blocks, w_inlet[0]) + row(INLET_SHIFT)
+        forget_pre[...] = dot(blocks, w_forget[0]) + row(FORGET_SHIFT)
+
+        def terms(at):
+            starts = flags[at, 0:1] > 0.5
+            decay, scaler = decay_of(jax.nn.sigmoid(forget_pre[at, :]), row(RATE_SOFT), starts)
+            factor[at, :] = decay
+            addend[at, :] = scaler * jax.nn.sigmoid(inlet_pre[at, :]) * conv[at, :].astype(F32)
+
+        by_rows(rows, 32, terms)
+
+        def write(at, a, b):
+            cum[at, cols] = a
+            local[at, cols] = b
+
+        scan_rows(seqs, length, width, lambda at: (factor[at, :], addend[at, :]), write, False)
+
+    @pl.when(step == heads)
+    def _():
+        chain.first_line()
+        tots[0] = jnp.zeros_like(tots[0])
+        for s in range(seqs):
+            tots[0, s : s + 1, :] = cum[(s + 1) * length - 8 : (s + 1) * length, :][7:8]
+            tots[0, seqs + s : seqs + s + 1, :] = local[(s + 1) * length - 8 : (s + 1) * length, :][7:8]
+        enter = Prefix(spot, seqs, False, tots, gots, line, cube_sems, line_sems).run()
+        entered[...] = jnp.zeros_like(entered)
+        entered[0:seqs, :] = enter
+        for s in range(seqs):
+
+            def mix(at, s=s):
+                here = pl.ds(pl.multiple_of(s * length + at.start, STEP), STEP)
+                state = local[here, :] + cum[here, :] * enter[s : s + 1]
+                mixed[here, :] = (state * gelu_of(gelu_pre[here, :])[0]).astype(BF16)
+
+            by_rows(length, STEP, mix)
+        turns.onward(1)
+        turns.start(3)
+        values = mixed[...]
+        own_rows = resid.shape[0]
+
+        def branch(j, carry):
+            at = pl.ds(pl.multiple_of(j * 256, 256), 256)
+            value = dot_nt(values, w_out[0, at, :])
+            for side in range(tensor):
+                part[side, :, at] = value[side * own_rows : (side + 1) * own_rows]
+            return carry
+
+        lax.fori_loop(0, x.shape[1] // 256, branch, 0)
+
+        def put(at):
+            out[at, :] = part[1 - spot.t, at, :].astype(BF16)
+
+        by_rows(own_rows, STEP, put)
+        copy = remote(out, got, swap_sems, 0, spot.cross)
+        copy.start()
+        chain.onward(1)
+        copy.wait()
+
+        def norm(at):
+            own = x[pl.ds(pl.multiple_of(spot.t * own_rows + at.start, STEP), STEP), :].astype(F32)
+            value = own + (part[spot.t, at, :] + got[at, :].astype(F32) + shift[...])
+            resid[at, :] = value
+            scale = lax.rsqrt(jnp.mean(value * value, axis=-1, keepdims=True) + 1e-06)
+            second[at, :] = (value * scale * gain_second[...]).astype(BF16)
+
+        by_rows(own_rows, STEP, norm)
+        turns.second(0)
+        turns.onward(3)
+        chain.onward(2)
+        turns.second(1)
+        chain.onward(3)
+        turns.second(3)
+        turns.finish()
+        chain.finish()
+
+
+def forward_recurrence(
+    grid, x, halo, gain, rec, inlet, forget, lanes, flags, shift, gain_second, feed, cot, seqs
+):
+    rows, d = x.shape
+    heads, width = inlet.shape[:2]
+    channels = heads * width
+    longer = rows // seqs + HALO
+    own_rows = rows // grid.tensor
+
+    def head_of(i):
+        return jnp.minimum(i, heads - 1)
+
+    def fixed(a):
+        zeros = (0,) * len(a.shape)
+        return pl.BlockSpec(a.shape, lambda i: zeros, pipeline_mode=pl.Buffered(1))
+
+    def column(count):
+        return pl.BlockSpec((count, width), lambda i: (0, head_of(i)))
+
+    def weight(k):
+        return pl.BlockSpec((1, d, width), lambda i: (k, 0, head_of(i)))
+
+    head = pl.BlockSpec((1, width, width), lambda i: (head_of(i), 0, 0))
+    far = pl.BlockSpec(memory_space=pl.ANY)
+    wide = jax.ShapeDtypeStruct((rows, channels), F32)
+    outs = [
+        jax.ShapeDtypeStruct((rows, d), BF16),
+        jax.ShapeDtypeStruct((seqs, longer, channels), BF16),
+        jax.ShapeDtypeStruct((rows, channels), BF16),
+        wide,
+        wide,
+        wide,
+        wide,
+        wide,
+        jax.ShapeDtypeStruct((8, channels), F32),
+        jax.ShapeDtypeStruct((rows, channels), BF16),
+        jax.ShapeDtypeStruct((own_rows, d), F32),
+        jax.ShapeDtypeStruct((own_rows, d), BF16),
+        jax.ShapeDtypeStruct(feed.shape, BF16),
+        jax.ShapeDtypeStruct(cot.shape, BF16),
+    ]
     return pl.pallas_call(
-        functools.partial(second_kernel, grid.n, grid.tensor, seqs),
-        grid=(1,),
-        out_shape=[
-            jax.ShapeDtypeStruct((8, channels), F32),
-            jax.ShapeDtypeStruct((every, channels), BF16),
-            jax.ShapeDtypeStruct((rows, d), F32),
-            jax.ShapeDtypeStruct((rows, d), BF16),
-        ],
-        in_specs=[near] * 3 + [pl.BlockSpec((1, d, channels), lambda i: (2, 0, 0))] + [near] * 3,
-        out_specs=[near] * 4,
+        functools.partial(forward_kernel, grid.n, grid.tensor, seqs, heads),
+        grid=(heads + 1,),
+        out_shape=outs,
+        in_specs=[fixed(x), fixed(halo), fixed(gain), weight(0), weight(1), head, head]
+        + [column(LANE_ROWS), fixed(flags)]
+        + [pl.BlockSpec((1, d, channels), lambda i: (2, 0, 0), pipeline_mode=pl.Buffered(1))]
+        + [fixed(shift), fixed(gain_second), far, far],
+        out_specs=[
+            fixed(outs[0]),
+            pl.BlockSpec((seqs, longer, width), lambda i: (0, 0, head_of(i))),
+            column(rows),
+            fixed(wide),
+            column(rows),
+            column(rows),
+        ]
+        + [fixed(a) for a in outs[6:12]]
+        + [far, far],
+        input_output_aliases={12: 12, 13: 13},
         scratch_shapes=[
-            pltpu.VMEM((grid.tensor, rows, d), F32),
-            pltpu.VMEM((rows, d), BF16),
-            pltpu.VMEM((rows, d), BF16),
+            pltpu.VMEM((rows + halo.shape[0], d), BF16),
+            pltpu.VMEM((rows, width), F32),
+            pltpu.VMEM((rows, width), F32),
+            pltpu.VMEM((grid.tensor, own_rows, d), F32),
+            pltpu.VMEM((own_rows, d), BF16),
+            pltpu.VMEM((own_rows, d), BF16),
         ]
         + prefix_scratch(grid, channels)
-        + [pltpu.SemaphoreType.DMA((2, 1))],
+        + [pltpu.SemaphoreType.DMA((2, 1)), turn_sems(grid), chain_sems(1)],
         compiler_params=pltpu.CompilerParams(
             collective_id=1, has_side_effects=True, vmem_limit_bytes=GRANT
         ),
-        name="make_second",
-    )(cum, local, gelu_pre, rec, x, shift, gain)
+        name="forward_recurrence",
+    )(x, halo, gain, rec, rec, inlet, forget, lanes, flags, rec, shift, gain_second, feed, cot)
 
 
 def leave_kernel(
     n, tensor, seqs, branch, w_out, gelu_pre, local, cum, inlet_pre, forget_pre, conv, ext, entered,
-    w_inlet, w_forget, lanes, flags,
-    gelu_low, input_low, gate_grads, lane_grads, shift_grad,
+    w_inlet, w_forget, lanes, flags, feed_part, resid,
+    gelu_low, input_low, gate_grads, lane_grads, shift_grad, own_out,
     tail, carried, factor, addend, back, rim, tots, gots, line, cube_sems, line_sems, rim_sems,
+    part, sums_got, sums_line, sums_cross, sums_sems,
 ):
     spot = Spot(n, tensor)
     every, channels = conv.shape
@@ -701,7 +781,16 @@
     heads, width = w_inlet.shape[:2]
     behind = {"wide": lax.rem(spot.w + n - 1, n)}
     ahead = {"wide": lax.rem(spot.w + 1, n)}
-    spot.greet(*[spot.flip(bit) for bit in spot.bits], behind, ahead)
+    spot.greet(*[spot.flip(bit) for bit in spot.bits], behind, ahead, spot.cross)
+    for place in range(spot.hi):
+        for side in range(tensor):
+
+            def put(at, place=place, side=side):
+                part[place, side, at, :] = feed_part[place, side, at, :]
+
+            by_rows(resid.shape[0], STEP, put)
+    sums = Rows(spot, part, sums_got, sums_line, sums_cross, sums_sems)
+    sums.start()
     tots[0] = jnp.zeros_like(tots[0])
     lane_grads[...] = jnp.zeros_like(lane_grads)
     shift_grad[...] = jnp.zeros_like(shift_grad)
@@ -742,7 +831,10 @@
             tots[0, seqs + s : seqs + s + 1, cols] = decay[0:1] * carried[first, cols][0:1]
         return none
 
-    lax.fori_loop(0, heads, upward, 0)
+    lax.fori_loop(0, heads // 2, upward, 0)
+    sums.along(1)
+    lax.fori_loop(heads // 2, heads, upward, 0)
+    sums.along(2)
     come = Prefix(spot, seqs, True, tots, gots, line, cube_sems, line_sems).run()
     tots[0, 0:seqs, :] = come
 
@@ -800,6 +892,8 @@
         return none
 
     lax.fori_loop(0, heads, downward, 0)
+    for s in range(3, spot.hi):
+        sums.along(s)
     copy = remote(back.at[:, 0:HALO, :], rim, rim_sems, 0, behind)
     copy.start()
     copy.wait()
@@ -819,10 +913,16 @@
 
     lax.fori_loop(0, heads, give, 0)
 
+    def done(at, total):
+        own_out[at, :] = (resid[at, :] + total).astype(BF16)
+
+    sums.end(done)
+    sums.finish()
+
 
 def leave_recurrence(
     grid, branch, rec, gelu_pre, local, cum, inlet_pre, forget_pre, conv, ext, entered, inlet, forget, lanes,
-    flags, seqs,
+    flags, feed_part, resid, seqs,
 ):
     every, channels = conv.shape
     d = branch.shape[1]
@@ -838,9 +938,10 @@
             jax.ShapeDtypeStruct((2, heads, width, width), BF16),
             jax.ShapeDtypeStruct((LANE_ROWS, channels), F32),
             jax.ShapeDtypeStruct((8, d), F32),
+            jax.ShapeDtypeStruct(resid.shape, BF16),
         ],
-        in_specs=[near, pl.BlockSpec((1, d, channels), lambda i: (2, 0, 0))] + [near] * 12,
-        out_specs=[near] * 5,
+        in_specs=[near, pl.BlockSpec((1, d, channels), lambda i: (2, 0, 0))] + [near] * 14,
+        out_specs=[near] * 6,
         scratch_shapes=[
             pltpu.VMEM((every, channels), F32),
             pltpu.VMEM((every, channels), F32),
@@ -850,14 +951,16 @@
             pltpu.VMEM((seqs, HALO, channels), F32),
         ]
         + prefix_scratch(grid, channels)
-        + [pltpu.SemaphoreType.DMA((2, 1))],
+        + [pltpu.SemaphoreType.DMA((2, 1)), pltpu.VMEM(feed_part.shape, BF16)]
+        + rows_scratch(grid, *resid.shape)[:2]
+        + rows_sems(grid)[:2],
         compiler_params=pltpu.CompilerParams(
             collective_id=5, has_side_effects=True, vmem_limit_bytes=GRANT
         ),
         name="leave_recurrence",
     )(
         branch, rec, gelu_pre, local, cum, inlet_pre, forget_pre, conv, ext, entered, inlet, forget,
-        lanes, flags,
+        lanes, flags, feed_part, resid,
     )
 
 
@@ -933,18 +1036,19 @@
     def sends_down(self, s):
         return self.spot.z >= self.spot.hi - s
 
-    def run(self, done):
+    def along(self, s):
         spot, hi = self.spot, self.spot.hi
-        for s in range(1, hi):
-
-            @pl.when(jnp.logical_and(self.sends_up(s), spot.z < hi - 1))
-            def _():
-                self.send(s, True)
-
-            @pl.when(jnp.logical_and(self.sends_down(s), spot.z > 0))
-            def _():
-                self.send(s, False)
-
+
+        @pl.when(jnp.logical_and(self.sends_up(s), spot.z < hi - 1))
+        def _():
+            self.send(s, True)
+
+        @pl.when(jnp.logical_and(self.sends_down(s), spot.z > 0))
+        def _():
+            self.send(s, False)
+
+    def end(self, done):
+        spot, hi = self.spot, self.spot.hi
         self.cross_copy(spot.z).wait_recv()
 
         @pl.when(spot.z > 0)
@@ -981,7 +1085,7 @@
 
 def feed_kernel(
     n, tensor, unit_tiles, own, w_gate, w_up, w_down, cot, resid, gain,
-    whole, gate_low, up_low, hidden, both, gain_grad,
+    whole, gate_low, up_low, hidden, both, gain_grad, feed_part,
     part, got, line, mine, other, sems, cross_sems, line_sems, swap_sems,
 ):
     spot = Spot(n, tensor)
@@ -1041,6 +1145,16 @@
     chain.places(hi - 1, come_and_work)
     sums = Rows(spot, part, got, line, cross_sems, line_sems)
     sums.start()
+
+    def give(i, none):
+        place, j = i // (d // chunk), lax.rem(i, d // chunk)
+        cols = pl.ds(pl.multiple_of(j * chunk, chunk), chunk)
+        value = dot_nt(hidden[place], w_down[0, cols, :]).astype(BF16)
+        for side in range(tensor):
+            feed_part[place, side, :, cols] = value[side * rows : (side + 1) * rows]
+        return none
+
+    lax.fori_loop(0, hi * (d // chunk), give, 0)
     chain.finish_sends()
 
     def done(at, total):
@@ -1054,7 +1168,9 @@
         gain_grad[...] += jnp.sum(gained.reshape(2, 8, -1), axis=0)
         mine[at, :] = grad.astype(BF16)
 
-    sums.run(done)
+    for s in range(1, hi):
+        sums.along(s)
+    sums.end(done)
     copy = remote(mine, other, swap_sems, 0, spot.cross)
     copy.start()
     sums.finish()
@@ -1115,9 +1231,10 @@
             low,
             jax.ShapeDtypeStruct((tensor, rows, d), BF16),
             jax.ShapeDtypeStruct((8, d), F32),
+            whole,
         ],
         in_specs=[near] + [weight(k) for k in range(3)] + [near] * 3,
-        out_specs=[near] * 6,
+        out_specs=[near] * 7,
         scratch_shapes=[pltpu.VMEM(whole.shape, BF16)]
         + rows_scratch(grid, rows, d)
         + [chain_sems(1)]
@@ -1129,48 +1246,6 @@
     )(own, feed, feed, feed, cot, resid, gain)
 
 
-def out_kernel(
-    n, tensor, part_in, resid, both, part, got, line, mine, other, cross_sems, line_sems, swap_sems
-):
-    spot = Spot(n, tensor)
-    spot.greet(spot.cross)
-    rows = resid.shape[0]
-    for place in range(spot.hi):
-        for side in range(tensor):
-
-            def put(at, place=place, side=side):
-                part[place, side, at, :] = part_in[place, side, at, :]
-
-            by_rows(rows, STEP, put)
-    sums = Rows(spot, part, got, line, cross_sems, line_sems)
-    sums.start()
-
-    def done(at, total):
-        mine[at, :] = (resid[at, :] + total).astype(BF16)
-
-    sums.run(done)
-    copy = remote(mine, other, swap_sems, 0, spot.cross)
-    copy.start()
-    sums.finish()
-    share(spot, copy, mine, other, both)
-
-
-def block_output(grid, part, resid):
-    rows, width = resid.shape
-    near = pl.BlockSpec(memory_space=pltpu.VMEM)
-    return pl.pallas_call(
-        functools.partial(out_kernel, grid.n, grid.tensor),
-        out_shape=jax.ShapeDtypeStruct((grid.tensor, rows, width), BF16),
-        in_specs=[near] * 2,
-        out_specs=near,
-        scratch_shapes=[pltpu.VMEM(part.shape, BF16)] + rows_scratch(grid, rows, width) + rows_sems(grid),
-        compiler_params=pltpu.CompilerParams(
-            collective_id=3, has_side_effects=True, vmem_limit_bytes=GRANT
-        ),
-        name="block_output",
-    )(part, resid)
-
-
 RING = 4
 
 
@@ -1178,10 +1253,19 @@
     return 16 if rows % 16 == 0 else 8
 
 
+SENDING = 8
+HELD = 2
+
+
+def place_at(j, hi):
+    return lax.rem(2 * j + hi // 2 + (2 * j) // hi, hi)
+
+
 def grads_kernel(
     n, tensor, spans, kept,
-    second, cot, normed, branch, gate_low, up_low, hidden, gelu_low, input_low, mixed, gates, first, thin,
-    apart, summed, first_other, thin_own, *refs,
+    unit_tiles,
+    second, cot, normed, branch, gate_low, up_low, hidden, gelu_low, input_low, mixed, gates, first, own_out, thin,
+    apart, summed, first_other, block_out, thin_own, *refs,
 ):
     stages = (n // LINE).bit_length() - 1
     lists = [refs[i * stages : (i + 1) * stages] for i in range(6)]
@@ -1196,8 +1280,14 @@
     units = all_spans * hi
     step = pl.program_id(0)
     rows = ready.shape[1]
+    width = ready.shape[2]
     each = tile_rows(rows)
     last_step = units + stages - 1
+    first_rows, out_rows = first.shape[0], own_out.shape[0]
+
+    def place_of(unit):
+        return place_at(lax.rem(unit, hi), hi)
+
     sources = {
         "gate": (second, gate_low),
         "up": (second, up_low),
@@ -1217,15 +1307,56 @@
             spot.flip(spot.bits[stage]),
         )
 
-    def line_copy(span, place, sender):
+    def line_copy(unit):
+        slot = lax.rem(unit, SENDING)
+        span = unit // hi
         return pltpu.make_async_remote_copy(
-            src_ref=ready.at[span * hi + place],
-            dst_ref=got_line.at[span, sender],
-            send_sem=line_sems.at[0, span * hi + place],
-            recv_sem=line_sems.at[1, span * hi + sender],
-            device_id=spot.line(place),
+            src_ref=ready.at[slot],
+            dst_ref=got_line.at[span, spot.z],
+            send_sem=line_sems.at[0, slot],
+            recv_sem=line_sems.at[1, span * hi + spot.z],
+            device_id=spot.line(place_of(unit)),
             device_id_type=MESH,
         )
+
+    def line_here(span, sender):
+        here = got_line.at[span, sender]
+        return pltpu.make_async_remote_copy(
+            src_ref=here,
+            dst_ref=here,
+            send_sem=line_sems.at[0, 0],
+            recv_sem=line_sems.at[1, span * hi + sender],
+            device_id=spot.line(sender),
+            device_id_type=MESH,
+        )
+
+    def line_sent(unit):
+        @pl.when(jnp.logical_and(unit >= 0, place_of(unit) != spot.z))
+        def _():
+            line_copy(unit).wait_send()
+
+    def settle(span):
+        for distance in range(1, hi):
+            line_here(span, spot.away(distance)).wait_recv()
+
+        def give(at):
+            if span < kept:
+                tiles = width // LANE
+                for place in range(hi):
+                    skip = place * tiles - min(place * tiles, unit_tiles - tiles)
+                    if skip < tiles:
+                        value = got_line[span, place, at, skip * LANE :].astype(F32)
+                        apart[span, at, place * width : (place + 1) * width - skip * LANE] = value
+            else:
+                value = got_line[span, 0, at, :].astype(F32)
+                for place in range(1, hi):
+                    value = value + got_line[span, place, at, :].astype(F32)
+                blocks = width // summed.shape[2]
+                for j in range(blocks):
+                    cols = slice(j * summed.shape[2], (j + 1) * summed.shape[2])
+                    summed[(span - kept) * blocks + j, at, :] = value[:, cols]
+
+        by_rows(rows, each, give)
 
     def thin_copy(stage):
         return remote(
@@ -1251,7 +1382,13 @@
         def put(at):
             first_out[at, :] = first[at, :]
 
-        by_rows(first.shape[0], STEP, put)
+        by_rows(first_rows, STEP, put)
+
+        def put_out(at):
+            to = pl.ds(pl.multiple_of(first_rows + at.start, STEP), STEP)
+            first_out[to, :] = own_out[at, :]
+
+        by_rows(out_rows, STEP, put_out)
         first_copy.start()
         mine = spot.bit(1)
         for place in range(hi):
@@ -1326,7 +1463,7 @@
                     return made[at_made, :].astype(BF16)
 
                 sends[0][slot, k, at, :] = block(2 * k + 1 - mine)
-                keeps[0][slot, k, at, :] = block(2 * k + mine)
+                keeps[0][lax.rem(step, HELD), k, at, :] = block(2 * k + mine)
 
             by_rows(rows, each, put)
         cube_copy(0, step).start()
@@ -1337,11 +1474,12 @@
         @pl.when(jnp.logical_and(unit >= 0, unit < units))
         def _(stage=stage, unit=unit):
             slot = lax.rem(unit, RING)
+            held = lax.rem(unit, HELD)
             cube_copy(stage, unit).wait_recv()
 
             def total(k, at):
                 return (
-                    keeps[stage][slot, k, at, :].astype(F32) + gots[stage][slot, k, at, :].astype(F32)
+                    keeps[stage][held, k, at, :].astype(F32) + gots[stage][slot, k, at, :].astype(F32)
                 ).astype(BF16)
 
             if stage < stages - 1:
@@ -1355,43 +1493,45 @@
 
                     def put(at, k=k):
                         sends[stage + 1][slot, k, at, :] = total(2 * k + 1 - mine, at)
-                        keeps[stage + 1][slot, k, at, :] = total(2 * k + mine, at)
+                        keeps[stage + 1][held, k, at, :] = total(2 * k + mine, at)
 
                     by_rows(rows, each, put)
                 cube_copy(stage + 1, unit).start()
             else:
-                span, place = unit // hi, lax.rem(unit, hi)
-
-                def put(at):
-                    ready[unit, at, :] = total(0, at)
-
-                by_rows(rows, each, put)
+                line_sent(unit - SENDING)
+                place = place_of(unit)
 
                 @pl.when(place != spot.z)
                 def _():
-                    line_copy(span, place, spot.z).start()
+                    def put(at):
+                        ready[lax.rem(unit, SENDING), at, :] = total(0, at)
+
+                    by_rows(rows, each, put)
+                    line_copy(unit).start()
+
+                @pl.when(place == spot.z)
+                def _():
+                    def put(at):
+                        got_line[unit // hi, spot.z, at, :] = total(0, at)
+
+                    by_rows(rows, each, put)
+
+    late = 2 * hi + stages - 1
+    for span in range(all_spans):
+        when = span * hi + hi - 1 + late
+        if when < last_step:
+
+            @pl.when(step == when)
+            def _(span=span):
+                settle(span)
 
     @pl.when(step == last_step)
     def _():
         for span in range(all_spans):
-            for distance in range(1, hi):
-                place = spot.away(distance)
-                line_copy(span, place, place).wait_recv()
-                line_copy(span, place, spot.z).wait_send()
-
-            def give(at, span=span):
-                own = ready[span * hi + spot.z, at, :]
-                if span < kept:
-                    for distance in range(hi):
-                        place = spot.away(distance)
-                        apart[span, place, at, :] = got_line[span, place, at, :] if distance else own
-                else:
-                    value = own.astype(F32)
-                    for distance in range(1, hi):
-                        value = value + got_line[span, spot.away(distance), at, :].astype(F32)
-                    summed[span - kept, at, :] = value
-
-            by_rows(rows, each, give)
+            if span * hi + hi - 1 + late >= last_step:
+                settle(span)
+        for unit in range(units - SENDING, units):
+            line_sent(unit)
         for stage in range(stages):
             for unit in range(units - RING, units):
                 cube_copy(stage, unit).wait_send()
@@ -1408,7 +1548,14 @@
         def take(at):
             first_other[at, :] = first_got[at, :]
 
-        by_rows(first.shape[0], STEP, take)
+        by_rows(first_rows, STEP, take)
+
+        def take_out(at):
+            other = pl.ds(pl.multiple_of(first_rows + at.start, STEP), STEP)
+            block_out[spot.t, at, :] = own_out[at, :]
+            block_out[1 - spot.t, at, :] = first_got[other, :]
+
+        by_rows(out_rows, STEP, take_out)
 
 
 def column_spans(widths, width):
@@ -1425,7 +1572,7 @@
     return spans
 
 
-def send_grads(grid, feed, rec, gates, first, thin):
+def send_grads(grid, feed, rec, gates, first, own_out, thin, unit_tiles):
     hi, inner = grid.hi, grid.inner_size
     second, cot, gate_low, up_low, hidden = feed
     normed, branch, gelu_low, input_low, mixed = rec
@@ -1443,7 +1590,7 @@
     stages = inner.bit_length() - 1
 
     def place_of(i):
-        return lax.rem(jnp.minimum(i, units - 1), hi)
+        return place_at(lax.rem(jnp.minimum(i, units - 1), hi), hi)
 
     def slab_of(a):
         return pl.BlockSpec((a.shape[0], slab), lambda i: (0, place_of(i)))
@@ -1452,13 +1599,16 @@
         zeros = (0,) * a.ndim
         return pl.BlockSpec(a.shape, lambda i: zeros, pipeline_mode=pl.Buffered(1))
 
-    apart = jax.ShapeDtypeStruct((kept, hi, rows, width), BF16)
-    summed = jax.ShapeDtypeStruct((all_spans - kept, rows, width), F32)
+    block = gates.shape[1]
+    apart = jax.ShapeDtypeStruct((kept, rows, unit_tiles * LANE), F32)
+    summed = jax.ShapeDtypeStruct(((all_spans - kept) * (width // block), rows, block), F32)
+    both = jax.ShapeDtypeStruct((grid.tensor,) + own_out.shape, BF16)
     other = jax.ShapeDtypeStruct(first.shape, BF16)
     thin = thin.reshape(hi, inner, 8, thin.shape[1] // 8)
     thin_shape = thin.shape[2:]
     thin_own = jax.ShapeDtypeStruct(thin_shape, F32)
-    outs = [apart, summed, other, thin_own]
+    outs = [apart, summed, other, both, thin_own]
+    swapped = (first.shape[0] + own_out.shape[0], d)
 
     def halves(lead, tail, kind):
         return [
@@ -1467,22 +1617,24 @@
 
     gates = gates.reshape(hi, slab, gates.shape[1])
     return pl.pallas_call(
-        functools.partial(grads_kernel, grid.n, grid.tensor, spans, kept),
+        functools.partial(grads_kernel, grid.n, grid.tensor, spans, kept, unit_tiles),
         grid=(units + stages,),
         out_shape=outs,
         in_specs=[slab_of(a) for a in (second, cot, normed, branch)]
         + [whole(a) for a in (gate_low, up_low, hidden, gelu_low, input_low, mixed)]
         + [pl.BlockSpec((1,) + gates.shape[1:], lambda i: (place_of(i), 0, 0))]
-        + [whole(first), whole(thin)],
+        + [whole(first), whole(own_out), whole(thin)],
         out_specs=[whole(a) for a in outs],
-        scratch_shapes=halves(RING, (rows, width), BF16) * 3
+        scratch_shapes=halves(RING, (rows, width), BF16)
+        + halves(HELD, (rows, width), BF16)
+        + halves(RING, (rows, width), BF16)
         + halves(hi, thin_shape, F32) * 3
         + [
             pltpu.VMEM((slab, width), BF16 if rows % 16 == 0 else F32),
-            pltpu.VMEM((units, rows, width), BF16),
+            pltpu.VMEM((SENDING, rows, width), BF16),
             pltpu.VMEM((all_spans, hi, rows, width), BF16),
-            pltpu.VMEM(first.shape, BF16),
-            pltpu.VMEM(first.shape, BF16),
+            pltpu.VMEM(swapped, BF16),
+            pltpu.VMEM(swapped, BF16),
             pltpu.VMEM((hi,) + thin_shape, F32),
             pltpu.VMEM((hi,) + thin_shape, F32),
             pltpu.SemaphoreType.DMA((stages, 2, RING)),
@@ -1497,7 +1649,7 @@
         name="send_grads",
     )(
         second, cot, normed, branch, gate_low, up_low, hidden, gelu_low, input_low, mixed, gates,
-        first, thin,
+        first, own_out, thin,
     )
 
 
@@ -1615,11 +1767,10 @@
         feed_all, lax.dynamic_slice_in_dim(feed_windows, grid.z, 1, 1), (0, grid.w, 0, 0)
     )
     cot_all = lax.dynamic_update_slice(cot_all, cot_own[None, None], (grid.z, grid.t, 0, 0))
-    rec_all, gates_all, thin_all, feed_all, cot_all = bring_weights(
-        grid, rec_all, gates_all, thin_all, feed_all, cot_all
+    rec_all, gates_all, thin_all, feed_all = bring_weights(
+        grid, rec_all, gates_all, thin_all, feed_all
     )
     rec_all = rec_all.reshape(3, width, channels)
-    input_full, gelu_full = rec_all[0], rec_all[1]
     gates_all = gates_all.reshape(2, head_count, block_size, block_size)
     inlet_full, forget_full = gates_all[0], gates_all[1]
     table = jnp.sum(thin_all.astype(F32), axis=0)
@@ -1630,28 +1781,38 @@
     lanes = jnp.pad(lanes, ((0, LANE_ROWS - lanes.shape[0]), (0, 0)))
 
     x = block_in.reshape(rows_all, width)
-    normed, ext, conv, gelu_pre, inlet_pre, forget_pre, cum, local_state = enter_recurrence(
-        x, halo, gain_first[None], rec_all, inlet_full, forget_full, lanes, flags, seq_count
-    )
-    entered, mixed, resid, second_own = make_second(
-        grid, cum, local_state, gelu_pre, rec_all, x, out_shift[None], gain_second[None], seq_count
+    (
+        normed,
+        ext,
+        conv,
+        gelu_pre,
+        inlet_pre,
+        forget_pre,
+        cum,
+        local_state,
+        entered,
+        mixed,
+        resid,
+        second_own,
+        feed_all,
+        cot_all,
+    ) = forward_recurrence(
+        grid, x, halo, gain_first[None], rec_all, inlet_full, forget_full, lanes, flags, out_shift[None],
+        gain_second[None], feed_all, cot_all, seq_count,
     )
 
     rows_feed = grid.hi * rows_all
-    second_all, gate_low, up_low, hidden, branch_low, gain_two_grad = feed_forward(
+    second_all, gate_low, up_low, hidden, branch_low, gain_two_grad, feed_part = feed_forward(
         grid, second_own, feed_all, cot_all, resid, gain_second[None], unit_tiles
     )
     second_all, cot_all = (v.reshape(rows_feed, width) for v in (second_all, cot_all))
     gate_low, up_low, hidden = (v.reshape(rows_feed, window) for v in (gate_low, up_low, hidden))
     branch_low = branch_low.reshape(rows_all, width)
     gain_two_grad = jnp.sum(gain_two_grad, axis=0)
-    feed_part = dot_nt(hidden, feed_all[2, : grid.n].reshape(width, window)).astype(BF16)
-    feed_part = feed_part.reshape(grid.hi, grid.tensor, rows_half, width)
-    block_out = block_output(grid, feed_part, resid).reshape(block_in.shape)
-
-    gelu_low, input_low, gate_w_grads, lane_grads, out_shift_grad = leave_recurrence(
+
+    gelu_low, input_low, gate_w_grads, lane_grads, out_shift_grad, own_out = leave_recurrence(
         grid, branch_low, rec_all, gelu_pre, local_state, cum, inlet_pre, forget_pre, conv, ext, entered,
-        inlet_full, forget_full, lanes, flags, seq_count,
+        inlet_full, forget_full, lanes, flags, feed_part, resid, seq_count,
     )
     out_shift_grad = jnp.sum(out_shift_grad, axis=0)
     gate_w_grads = (
@@ -1659,11 +1820,12 @@
         .transpose(2, 0, 1, 3, 4)
         .reshape(width, block_size)
     )
-    first_part = dot_nt(input_low, input_full) + dot_nt(gelu_low, gelu_full)
     inputs = x.astype(F32)
     scale_first = lax.rsqrt(jnp.mean(inputs * inputs, axis=-1, keepdims=True) + 1e-06)
-    gain_one_grad = jnp.sum(first_part * inputs * scale_first, axis=0)
-    first_part = first_part.astype(BF16)
+    first_part, gain_one_grad = first_gradient(
+        x, input_low, gelu_low, rec_all, jnp.broadcast_to(scale_first, (rows_all, 8))
+    )
+    gain_one_grad = jnp.sum(gain_one_grad, axis=0)
     gain_grads = jnp.stack([gain_one_grad, gain_two_grad])
     gain_grads = gain_grads + grid.swap(gain_grads)
 
@@ -1678,32 +1840,23 @@
         + [lane_grads],
         axis=1,
     )
-    feed_grads, rec_grads, first_other, thin = send_grads(
+    feed_grads, rec_grads, first_other, block_out, thin = send_grads(
         grid,
         (second_all, cot_all, gate_low, up_low, hidden),
         (normed, branch_low, gelu_low, input_low, mixed),
         gate_w_grads,
         first_part,
+        own_out,
         thin_grads,
-    )
+        unit_tiles,
+    )
+    block_out = block_out.reshape(block_in.shape)
     thin = thin.reshape(-1)
-    rec_grads = jnp.concatenate(list(rec_grads), axis=1)
-    gelu_w_grad = rec_grads[:, :channels]
-    input_w_grad = rec_grads[:, channels : 2 * channels]
-    out_grad = rec_grads[:, 2 * channels : 3 * channels]
-    gate_w_grads = rec_grads[:, 3 * channels :].reshape(2, head_count, lane_own, block_size)
-
-    def feed_weight_grad(got):
-        pieces = []
-        for place in range(grid.hi):
-            begin = min(place * window_tiles, unit_tiles - window_tiles)
-            skip = min(place * window_tiles - begin, window_tiles)
-            if skip < window_tiles:
-                pieces.append(got[place, :, skip * LANE :])
-        return jnp.concatenate(pieces, axis=1).astype(F32)
-
-    gate_grad, up_grad, down_grad = (feed_weight_grad(got) for got in feed_grads)
-    down_grad = down_grad.T
+    gate_grad, up_grad, down_grad = feed_grads[0], feed_grads[1], feed_grads[2].T
+    gelu_w_grad = rec_grads[:head_count].transpose(1, 0, 2)
+    input_w_grad = rec_grads[head_count : 2 * head_count].transpose(1, 0, 2)
+    out_grad = rec_grads[2 * head_count : 3 * head_count].transpose(0, 2, 1)
+    gate_w_grads = rec_grads[3 * head_count].reshape(2, head_count, lane_own, block_size)
     first_grad = first_part.astype(F32) + first_other.astype(F32)
     _, pull_first = jax.vjp(rms_norm, inputs, gain_first)
     input_norm_grad, _ = pull_first(first_grad)
@@ -1712,14 +1865,13 @@
         thin[i * d_own : (i + 1) * d_own] for i in range(3)
     )
     lanes = thin[3 * d_own :].reshape(CONV + 6, head_count, lane_own)
-    weight_shape = gelu_weight.shape
     return (
         block_out,
         block_grad,
         gain_one_own,
-        gelu_w_grad.reshape(weight_shape),
+        gelu_w_grad,
         lanes[0],
-        input_w_grad.reshape(weight_shape),
+        input_w_grad,
         lanes[1],
         lanes[2 : 2 + CONV],
         lanes[2 + CONV],
@@ -1728,7 +1880,7 @@
         gate_w_grads[1],
         lanes[4 + CONV],
         lanes[5 + CONV],
-        out_grad.T.reshape(out_weight.shape),
+        out_grad,
         out_shift_own,
         gain_two_own,
         gate_grad,

time: 906 us -> 830 us (0.916)
  Pallas kernels: 802 us -> 766 us
  matrix products: 21 us -> 0 us
  local copies, waits for them, and re-layouts: 53 us -> 38.5 us
    pallas_call x1, Pallas kernels: 241 us -> 163 us  [bring_weights(): pl.pallas_call(functools.partial(weights_kernel, n, tensor), out_shape=[j...]
    pallas_call x1, Pallas kernels: 39.3 us -> 77.4 us  [leave_recurrence(): pl.pallas_call(functools.partial(leave_kernel, grid.n, grid.tensor, seqs)...]
    dot_general x3 -> x0, matrix products: 21 us -> none  [dot_nt(): return jnp.einsum('ik,jk->ij', left, right, preferred_element_type=F32)]
    slice x2 -> x0, local copies, waits for them, and re-layouts: 15.1 us -> none  [the longest x1 9.49 us: local(): input_full, gelu_full = (rec_all[0], rec_all[1])]
    transpose x0 -> x2, local copies, waits for them, and re-layouts: none -> 9.68 us  [the longest x1 6.53 us: local(): feed_grads[2]]
    pallas_call x3 -> x2, Pallas kernels: 133 us -> 131 us  [the longest x1 121 us: forward_recurrence(): pl.pallas_call(functools.partial(forward_kernel, grid.n, grid.tensor, seq...]
  transfers between devices with their start and end apart: 3 -> 3, of which waited for: 0 -> 0; matrix products, arithmetic and copies ran while one was open for 7% -> 4% of each run, Pallas kernels for 36% -> 20%
where the time goes in v4:
time: 830 us; the launch traced here: 828 us
  Pallas kernels  766 us (92%)
  local copies, waits for them, and re-layouts  38.5 us (5%)
  other arithmetic  17.1 us (2%)
    pallas_call x1, Pallas kernels, send_grads(): pl.pallas_call(functools.partial(grads_kernel, grid.n, grid.tensor, spans...  244 us
    pallas_call x1, Pallas kernels, bring_weights(): pl.pallas_call(functools.partial(weights_kernel, n, tensor), out_shape=[j...  163 us
    pallas_call x1, Pallas kernels, feed_forward(): pl.pallas_call(functools.partial(feed_kernel, grid.n, tensor, unit_tiles)...  150 us
    pallas_call x1, Pallas kernels, forward_recurrence(): pl.pallas_call(functools.partial(forward_kernel, grid.n, grid.tensor, seq...  121 us
    pallas_call x1, Pallas kernels, leave_recurrence(): pl.pallas_call(functools.partial(leave_kernel, grid.n, grid.tensor, seqs)...  77.4 us
  transfers between devices with their start and end apart: 3, of which 0 were waited for; matrix products, arithmetic and copies ran while one was open for 4% of the time, Pallas kernels for 20%

profile of v4, /device:TPU:27, one launch (start us, length us, event | category | flops | bytes accessed | tf_op | source)
XLA Modules:
  0.0 827.6 jit_solution(3812704897557113)
XLA Ops:
  0.7 0.7 add_convert_fusion
  1.3 0.1 slice.145
  1.4 1.8 collective-permute-start.1
  3.2 1.5 slice.136
  4.7 2.2 pad_maximum_fusion.1
  7.0 0.0 copy-start.17
  7.1 1.5 slice_bitcast_fusion.6
  8.7 0.1 concatenate.16
  8.8 1.6 dynamic_update_slice.26
  10.6 0.3 dynamic_update_slice.27
  10.9 1.1 copy.83
  12.0 2.3 stack_reshape.6
  14.3 2.1 copy.84
  16.4 2.3 stack_reshape.7
  18.6 1.0 copy.100
  19.7 0.8 pad_maximum_fusion.2
  20.5 0.7 constant_dynamic-update-slice_fusion.1.gates
  21.2 0.6 fusion.3.thin
  21.8 3.4 pad_maximum_fusion
  25.2 1.0 dynamic-slice_dynamic-update-slice_fusion.feed
  26.3 1.1 fusion.2.rec
  27.4 163.4 %bring_weights.1 = (bf16[3,16,160,1280]{3,2,1,0:T(8,128)(2,1)}, bf16[10,16,16,256]{3,2,1,0:T(8,128)(2,1)}, bf16[16,16,1280]{2,1,0:T(8,128)(2,1)}, bf16[3,20,160,1024]{3,2,1,0:T(8,128)(2,1)}) custom-call(bf16[3,16,160,1280]{3,2,1,0:T(8,128)(2,1)} %fusion.2.rec, ...), custom_call_target="tpu_custom_call", output_to_operand_aliasing={{0}: (0, {}), {1}: (1, {}), {2}: (2, {}), {3}: (3, {})} | custom-call | tf_op jit(solution)/shard_map/bring_weights/pallas_call | solution.py:370
  190.8 1.3 convert_reduce_fusion
  192.2 0.3 multiply_reduce_fusion
  192.5 1.2 fusion.10
  193.7 0.6 copy.102
  194.3 0.6 copy.107
  194.9 0.6 copy.108
  195.5 0.7 select_maximum_fusion.lanes
  196.2 0.9 bitcast_dynamic-update-slice_fusion.cot
  197.1 0.1 not_bitcast_fusion
  197.2 0.2 copy.96
  197.4 0.7 pad_convert_fusion.flags
  198.1 0.6 select_bitcast_fusion.halo
  198.7 121.2 %forward_recurrence.1 = (bf16[256,2560]{1,0:T(8,128)(2,1)}, bf16[2,136,1280]{2,1,0:T(8,128)(2,1)}, bf16[256,1280]{1,0:T(8,128)(2,1)}, f32[256,1280]{1,0:T(8,128)...) custom-call(bf16[256,2560]{1,0:T(8,128)(2,1)} %bitcast.156, ...), custom_call_target="tpu_custom_call", output_to_operand_aliasing={{12}: (12, {}), {13}: (13, {})} | custom-call | tf_op jit(solution)/shard_map/forward_recurrence/pallas_call | solution.py:735
  319.9 150.1 %feed_forward.1 = (bf16[4,2,128,2560]{3,2,1,0:T(8,128)(2,1)}, bf16[4,256,1024]{2,1,0:T(8,128)(2,1)}, bf16[4,256,1024]{2,1,0:T(8,128)(2,1)}, bf16[4,256,1024]{2,1...) custom-call(bf16[128,2560]{1,0:T(8,128)(2,1)} %get-tuple-element.72.own, ...), custom_call_target="tpu_custom_call" | custom-call | tf_op jit(solution)/shard_map/feed_forward/pallas_call | solution.py:1224
  470.0 77.4 %leave_recurrence.1 = (bf16[256,1280]{1,0:T(8,128)(2,1)}, bf16[256,1280]{1,0:T(8,128)(2,1)}, bf16[2,5,256,256]{3,2,1,0:T(8,128)(2,1)}, f32[16,1280]{1,0:T(8,128)...) custom-call(bf16[256,2560]{1,0:T(8,128)(2,1)} %bitcast.158, bf16[3,2560,1280]{2,1,0:T(8,128)(2,1)} %bitcast.149, ...), custom_call_target="tpu_custom_call" | custom-call | tf_op jit(solution)/shard_map/leave_recurrence/pallas_call | solution.py:932
  547.4 0.8 broadcast_in_dim.34.scale
  548.2 9.9 %first_gradient.1 = (bf16[256,2560]{1,0:T(8,128)(2,1)}, f32[8,2560]{1,0:T(8,128)}) custom-call(bf16[256,2560]{1,0:T(8,128)(2,1)} %bitcast.157, bf16[256,1280]{1,0:T(8,128)(2,1)} %get-tuple-element.92.input_low, bf16[256,1280]{1,0:T(8,128)(2,1)} %get-tuple-element.91.gelu_low, bf16[3,2560,1280]{2,1,0:T(8,128)(2,1)} %bitcast.150, ...), custom_call_target="tpu_custom_call" | custom-call | tf_op jit(solution)/shard_map/first_gradient/pallas_call | solution.py:479
  558.1 1.0 reduce_sum.64
  559.3 3.3 collective-permute-start.2
  562.6 0.2 reshape.170
  562.7 0.2 copy.114
  562.9 0.2 reshape.171
  563.2 0.1 reshape.169
  563.2 1.2 copy.97
  564.5 0.1 slice_reduce_fusion
  564.5 0.1 reshape_squeeze.7
  564.6 0.1 reshape_squeeze.8
  564.7 0.1 concatenate.20
  564.8 0.8 reshape.172.thin
  565.6 243.7 %send_grads.1 = (f32[3,160,3840]{2,1,0:T(8,128)}, f32[16,160,256]{2,1,0:T(8,128)}, bf16[256,2560]{1,0:T(8,128)(2,1)}, bf16[2,128,2560]{2,1,0:T(8,128)(2,1)}, f32[8,160]{1,0:T(8,128)}) custom-call(bf16[1024,2560]{1,0:T(8,128)(2,1)} %bitcast.165, bf16[1024,2560]{1,0:T(8,128)(2,1)} %bitcast.155, bf16[256,2560]{1,0:T(8,128)(2,1)} %get-tuple-element.77.normed, ...), custom_call_target="tpu_custom_call" | custom-call | tf_op jit(solution)/shard_map/send_grads/pallas_call | solution.py:1619
  809.3 3.2 slice_bitcast_fusion.7
  812.4 1.6 fusion.9
  814.0 0.6 fusion.12
  814.6 6.5 slice_bitcast_fusion
  821.2 0.7 fusion
  821.9 0.6 copy-done.3
  822.5 2.6 fusion.1
  825.1 0.1 reshape.174
  825.2 0.6 slice_bitcast_fusion.12
  825.8 0.1 slice.160
  825.9 0.6 copy.99
  826.5 1.1 copy.130
  (88 shorter events, 0.5 us)
Async XLA Ops:
  1.4 195.7 %collective-permute-start.1 = (bf16[2,3]{1,0:T(2,128)(2,1)S(1)}, bf16[2,3]{1,0:T(2,128)(2,1)S(1)}, u32[]{:S(2)}, u32[]{:S(2)}) collective-permute-start(bf16[2,3]{1,0:T(2,128)(2,1)S(1)} %slice.145), channel_id=1, source_target_pairs={{0,2},{2,4},{4,6},{6,8},{8,10},{10,12},{12,14},{14,16},{16,18},{18... | collective-permute-start | bytes 44 | tf_op jit(solution)/shard_map/ppermute | solution.py:44
  4.7 193.3 %collective-permute-start = (bf16[2,8,2560]{2,1,0:T(8,128)(2,1)}, bf16[2,8,2560]{2,1,0:T(8,128)(2,1)S(1)}, u32[]{:S(2)}, u32[]{:S(2)}) collective-permute-start(bf16[2,8,2560]{2,1,0:T(8,128)(2,1)} %slice.136), channel_id=1, source_target_pairs={{0,2},{2,4},{4,6},{6,8},{8,10},{10,12},{12,14},{14,16},{16,18},{18... | collective-permute-start | bytes 245768 | tf_op jit(solution)/shard_map/ppermute | solution.py:44
  7.0 1.6 copy-start.17
  7.0 1.6 copy-start.18
  7.0 1.6 copy-start.19
  7.0 1.6 copy-start.20
  7.0 1.7 copy-start.21
  7.0 1.7 copy-start.22
  7.0 1.7 copy-start.16
  7.1 3.4 copy-start.23
  7.1 3.4 copy-start.24
  7.1 3.4 copy-start.25
  7.1 3.8 copy-start.10
  21.8 4.4 copy-start.6
  21.8 4.4 copy-start.7
  27.4 164.8 %copy-start = (bf16[2,128,2560]{2,1,0:T(8,128)(2,1)S(1)}, bf16[2,128,2560]{2,1,0:T(8,128)(2,1)}, u32[]{:S(2)}) copy-start(bf16[2,128,2560]{2,1,0:T(8,128)(2,1)} %param.21) | copy-start | bytes 3932164
  190.8 1.7 copy-start.4
  192.5 3.7 copy-start.11
  548.2 11.0 %copy-start.13 = (f32[8,2560]{1,0:T(8,128)S(1)}, f32[8,2560]{1,0:T(8,128)}, u32[]{:S(2)}) copy-start(f32[8,2560]{1,0:T(8,128)} %get-tuple-element.98) | copy-start | bytes 245764
  548.2 14.4 %copy-start.14 = (f32[16,1280]{1,0:T(8,128)S(1)}, f32[16,1280]{1,0:T(8,128)}, u32[]{:S(2)}) copy-start(f32[16,1280]{1,0:T(8,128)} %get-tuple-element.100) | copy-start | bytes 245764
  558.1 5.0 copy-start.12
  558.1 5.1 copy-start.9
  559.3 5.2 collective-permute-start.2
  809.3 4.8 copy-start.15
  814.6 6.5 copy-start.1
  814.6 6.5 copy-start.2
  814.6 6.5 copy-start.5
  821.2 1.3 copy-start.3
  822.5 4.0 copy-start.8

commit v5 on v4

--- a/solution.py
+++ b/solution.py
@@ -249,8 +249,8 @@
                 self.line_copy(s, False).wait_send()
 
 
-def chain_sems(sides):
-    return pltpu.SemaphoreType.DMA((2, 2 * (LINE - 1) + ((1 << sides) - 1) * LINE))
+def chain_sems(sides, *lead):
+    return pltpu.SemaphoreType.DMA(lead + (2, 2 * (LINE - 1) + ((1 << sides) - 1) * LINE))
 
 
 class Turns:
@@ -298,29 +298,48 @@
                 self.line_copy(distance).wait_send()
 
 
-EARLY = (2,)
-LATE = (0, 1, 3)
-
-
-def feed_turns(spot, distances, feed, sems, cube):
-    def index(place, k):
-        return place * spot.inner_size + jnp.bitwise_xor(spot.inner, k)
-
-    return Turns(
-        spot,
-        distances,
-        lambda place: feed.at[:, spot.n + place],
-        lambda place, k: feed.at[:, index(place, k)],
-        sems,
-        cube,
-    )
+LATE = (0, 1, 2, 3)
+
+
+class FeedTurns:
+    def __init__(self, spot, feed, sems, cube):
+        def index(place, k):
+            return place * spot.inner_size + jnp.bitwise_xor(spot.inner, k)
+
+        self.each = [
+            Turns(
+                spot,
+                LATE,
+                lambda place, m=m: feed.at[m, spot.n + place],
+                lambda place, k, m=m: feed.at[m, index(place, k)],
+                sems.at[m],
+                cube,
+            )
+            for m in range(feed.shape[0])
+        ]
+
+    def start(self, distance):
+        for turns in self.each:
+            turns.start(distance)
+
+    def onward(self, distance):
+        for turns in self.each:
+            turns.onward(distance)
+
+    def second(self, distance):
+        for turns in self.each:
+            turns.second(distance)
+
+    def finish(self):
+        for turns in self.each:
+            turns.finish()
 
 
 def weights_kernel(
-    n, tensor, rec, gates, thin, feed, rec_all, gates_all, thin_all, feed_all,
-    rec_sems, gates_sems, thin_sems, feed_sems,
+    n, tensor, rec, gates, thin, cot, rec_all, gates_all, thin_all, cot_all,
+    rec_sems, gates_sems, thin_sems, cot_sems,
 ):
-    del rec, gates, thin, feed
+    del rec, gates, thin, cot
     spot = Spot(n, tensor)
     hi = spot.hi
 
@@ -331,41 +350,119 @@
     moves = [
         Chain(spot, lambda place, k: thin_all.at[index(place, k)], thin_sems, cube),
         Chain(spot, lambda place, k: gates_all.at[:, index(place, k)], gates_sems, cube),
-        Chain(spot, lambda place, k: rec_all.at[:, index(place, k)], rec_sems, cube),
-        feed_turns(spot, EARLY, feed_all, feed_sems, cube),
+        *[
+            Chain(
+                spot, lambda place, k, m=m: rec_all.at[m, index(place, k)], rec_sems.at[m], cube
+            )
+            for m in range(rec_all.shape[0])
+        ],
+        Chain(
+            spot,
+            lambda place, k: cot_all.at[place, lax.rem(spot.t + k, tensor)],
+            cot_sems,
+            [spot.cross],
+        ),
     ]
-    spot.greet(*cube)
-    for move in moves:
+    spot.greet(*cube, spot.cross)
+    last = moves[-1]
+    for move in moves[:-1]:
         move.first()
+    last.fans.hand_on(spot.z, 0)
     for s in range(1, hi):
-        for move in moves:
+        for move in moves[:-1]:
             move.onward(s)
+        if s == 1:
+            last.first_line()
+        else:
+            last.onward(s - 1)
         for move in moves:
             move.second(s - 1)
+    last.onward(hi - 1)
     for move in moves:
         move.second(hi - 1)
     for move in moves:
         move.finish()
 
 
-def turn_sems(grid):
-    return pltpu.SemaphoreType.DMA((2, grid.n))
-
-
-def blank(*shapes):
+def turn_sems(grid, count):
+    return pltpu.SemaphoreType.DMA((count, 2, grid.n))
+
+
+def place_kernel(
+    unit_tiles, spot, wide_in, gelu_in, out_in, gate, up, down, inlet, forget, thin, cot,
+    rec_all, gates_all, thin_all, feed_all, cot_all,
+):
+    step = pl.program_id(0)
+    hi = LINE
+    width = feed_all.shape[3]
+    tiles = width // LANE
+
+    @pl.when(step == 0)
+    def _():
+        heads, _, lanes = wide_in.shape
+        for m, source in enumerate((wide_in, gelu_in, out_in)):
+            for h in range(heads):
+                rec_all[m, 0, :, h * lanes : (h + 1) * lanes] = source[h]
+        for m, source in enumerate((inlet, forget)):
+            for h in range(heads):
+                gates_all[m * heads + h, 0] = source[h]
+        thin_all[0] = thin[...]
+        cot_all[0, 0] = cot[0]
+
+    place = jnp.where(step < hi, step, spot[1])
+    tile = jnp.minimum(place * tiles, unit_tiles - tiles)
+    for m, source in enumerate((gate, up, down)):
+        feed_all[m, 0] = source[:, pl.ds(pl.multiple_of(tile * LANE, LANE), width)]
+
+
+def place_own(grid, rec, feed, gates, thin, cot):
+    n, hi = grid.n, grid.hi
+    heads, d_own, lanes = rec[0].shape
+    units = feed[0].shape[1]
+    unit_tiles = units // LANE
+    window = -(-unit_tiles // hi) * LANE
+    lane_own, block = gates[0].shape[1:]
+    spot = jnp.stack([grid.w, grid.z, grid.t])
+
+    def fixed(a):
+        zeros = (0,) * a.ndim
+        return pl.BlockSpec(a.shape, lambda i, spot: zeros)
+
+    outs = [
+        (3, n, d_own, heads * lanes),
+        (2 * heads, n, lane_own, block),
+        (n,) + thin.shape,
+        (3, n + hi, d_own, window),
+        (hi,) + cot.shape,
+    ]
     return pl.pallas_call(
-        lambda *refs: None,
-        out_shape=[jax.ShapeDtypeStruct(shape, BF16) for shape in shapes],
-        out_specs=[pl.BlockSpec(memory_space=pl.ANY)] * len(shapes),
+        functools.partial(place_kernel, unit_tiles),
+        grid_spec=pltpu.PrefetchScalarGridSpec(
+            num_scalar_prefetch=1,
+            grid=(hi + 1,),
+            in_specs=[fixed(a) for a in rec + feed + gates + (thin,)]
+            + [pl.BlockSpec((1,) + cot.shape[1:], lambda i, spot: (spot[2], 0, 0))],
+            out_specs=[
+                pl.BlockSpec((3, 1, d_own, heads * lanes), lambda i, spot: (0, spot[0], 0, 0)),
+                pl.BlockSpec((2 * heads, 1, lane_own, block), lambda i, spot: (0, spot[0], 0, 0)),
+                pl.BlockSpec((1,) + thin.shape, lambda i, spot: (spot[0], 0, 0)),
+                pl.BlockSpec(
+                    (3, 1, d_own, window),
+                    lambda i, spot: (0, jnp.where(i < hi, n + i, spot[0]), 0, 0),
+                ),
+                pl.BlockSpec((1, 1) + cot.shape[1:], lambda i, spot: (spot[1], spot[2], 0, 0)),
+            ],
+        ),
+        out_shape=[jax.ShapeDtypeStruct(shape, BF16) for shape in outs],
         compiler_params=pltpu.CompilerParams(vmem_limit_bytes=GRANT),
-        name="blank",
-    )()
-
-
-def bring_weights(grid, rec, gates, thin, feed):
+        name="place",
+    )(spot, *rec, *feed, *gates, thin, cot)
+
+
+def bring_weights(grid, rec, gates, thin, cot):
     n, hi, tensor = grid.n, grid.hi, grid.tensor
     far = pl.BlockSpec(memory_space=pl.ANY)
-    arrays = (rec, gates, thin, feed)
+    arrays = (rec, gates, thin, cot)
     cube = grid.inner_size.bit_length() - 1
     return pl.pallas_call(
         functools.partial(weights_kernel, n, tensor),
@@ -374,10 +471,10 @@
         out_specs=[far] * len(arrays),
         input_output_aliases={i: i for i in range(len(arrays))},
         scratch_shapes=[
+            chain_sems(cube, rec.shape[0]),
             chain_sems(cube),
             chain_sems(cube),
-            chain_sems(cube),
-            turn_sems(grid),
+            chain_sems(1),
         ],
         compiler_params=pltpu.CompilerParams(
             collective_id=0, has_side_effects=True, vmem_limit_bytes=GRANT
@@ -395,6 +492,7 @@
 
 
 STEP = 16
+HALVES = 2
 
 
 GELU_SLOPE = 0.7978845608028654
@@ -551,12 +649,12 @@
 
 def forward_kernel(
     n, tensor, seqs, heads,
-    x, halo, gain, w_input, w_gelu, w_inlet, w_forget, lanes, flags, w_out, shift, gain_second, feed, cot,
+    x, halo, gain, w_input, w_gelu, w_inlet, w_forget, lanes, flags, w_out, shift, gain_second, feed,
     normed, ext, conv, gelu_pre, inlet_pre, forget_pre, cum, local, entered, mixed, resid, second,
-    feed_all, cot_all,
-    held, factor, addend, part, out, got, tots, gots, line, cube_sems, line_sems, swap_sems, feed_sems, cot_sems,
+    feed_all,
+    held, factor, addend, part, out, got, tots, gots, line, cube_sems, line_sems, swap_sems, feed_sems,
 ):
-    del feed, cot
+    del feed
     spot = Spot(n, tensor)
     hi = spot.hi
     rows = x.shape[0]
@@ -564,20 +662,12 @@
     width = conv.shape[1]
     step = pl.program_id(0)
     cube = [spot.flip(bit) for bit in spot.bits]
-    turns = feed_turns(spot, LATE, feed_all, feed_sems, cube)
-    chain = Chain(
-        spot,
-        lambda place, k: cot_all.at[place, lax.rem(spot.t + k, tensor)],
-        cot_sems,
-        [spot.cross],
-    )
-
+    turns = FeedTurns(spot, feed_all, feed_sems, cube)
     @pl.when(step == 0)
     def _():
         spot.greet(*cube, spot.cross)
         turns.start(1)
         turns.start(0)
-        chain.fans.hand_on(spot.z, 0)
 
         def norm(source, at, to):
             value = source[at, :].astype(F32)
@@ -634,12 +724,13 @@
 
     @pl.when(step == heads)
     def _():
-        chain.first_line()
         tots[0] = jnp.zeros_like(tots[0])
         for s in range(seqs):
             tots[0, s : s + 1, :] = cum[(s + 1) * length - 8 : (s + 1) * length, :][7:8]
             tots[0, seqs + s : seqs + s + 1, :] = local[(s + 1) * length - 8 : (s + 1) * length, :][7:8]
         enter = Prefix(spot, seqs, False, tots, gots, line, cube_sems, line_sems).run()
+        turns.start(3)
+        turns.onward(1)
         entered[...] = jnp.zeros_like(entered)
         entered[0:seqs, :] = enter
         for s in range(seqs):
@@ -650,8 +741,7 @@
                 mixed[here, :] = (state * gelu_of(gelu_pre[here, :])[0]).astype(BF16)
 
             by_rows(length, STEP, mix)
-        turns.onward(1)
-        turns.start(3)
+        turns.start(2)
         values = mixed[...]
         own_rows = resid.shape[0]
 
@@ -670,7 +760,6 @@
         by_rows(own_rows, STEP, put)
         copy = remote(out, got, swap_sems, 0, spot.cross)
         copy.start()
-        chain.onward(1)
         copy.wait()
 
         def norm(at):
@@ -683,16 +772,15 @@
         by_rows(own_rows, STEP, norm)
         turns.second(0)
         turns.onward(3)
-        chain.onward(2)
         turns.second(1)
-        chain.onward(3)
+        turns.onward(2)
         turns.second(3)
+        turns.second(2)
         turns.finish()
-        chain.finish()
 
 
 def forward_recurrence(
-    grid, x, halo, gain, rec, inlet, forget, lanes, flags, shift, gain_second, feed, cot, seqs
+    grid, x, halo, gain, rec, inlet, forget, lanes, flags, shift, gain_second, feed, seqs
 ):
     rows, d = x.shape
     heads, width = inlet.shape[:2]
@@ -730,7 +818,6 @@
         jax.ShapeDtypeStruct((own_rows, d), F32),
         jax.ShapeDtypeStruct((own_rows, d), BF16),
         jax.ShapeDtypeStruct(feed.shape, BF16),
-        jax.ShapeDtypeStruct(cot.shape, BF16),
     ]
     return pl.pallas_call(
         functools.partial(forward_kernel, grid.n, grid.tensor, seqs, heads),
@@ -739,7 +826,7 @@
         in_specs=[fixed(x), fixed(halo), fixed(gain), weight(0), weight(1), head, head]
         + [column(LANE_ROWS), fixed(flags)]
         + [pl.BlockSpec((1, d, channels), lambda i: (2, 0, 0), pipeline_mode=pl.Buffered(1))]
-        + [fixed(shift), fixed(gain_second), far, far],
+        + [fixed(shift), fixed(gain_second), far],
         out_specs=[
             fixed(outs[0]),
             pl.BlockSpec((seqs, longer, width), lambda i: (0, 0, head_of(i))),
@@ -749,8 +836,8 @@
             column(rows),
         ]
         + [fixed(a) for a in outs[6:12]]
-        + [far, far],
-        input_output_aliases={12: 12, 13: 13},
+        + [far],
+        input_output_aliases={12: 12},
         scratch_shapes=[
             pltpu.VMEM((rows + halo.shape[0], d), BF16),
             pltpu.VMEM((rows, width), F32),
@@ -760,12 +847,12 @@
             pltpu.VMEM((own_rows, d), BF16),
         ]
         + prefix_scratch(grid, channels)
-        + [pltpu.SemaphoreType.DMA((2, 1)), turn_sems(grid), chain_sems(1)],
+        + [pltpu.SemaphoreType.DMA((2, 1)), turn_sems(grid, feed.shape[0])],
         compiler_params=pltpu.CompilerParams(
             collective_id=1, has_side_effects=True, vmem_limit_bytes=GRANT
         ),
         name="forward_recurrence",
-    )(x, halo, gain, rec, rec, inlet, forget, lanes, flags, rec, shift, gain_second, feed, cot)
+    )(x, halo, gain, rec, rec, inlet, forget, lanes, flags, rec, shift, gain_second, feed)
 
 
 def leave_kernel(
@@ -789,8 +876,14 @@
                 part[place, side, at, :] = feed_part[place, side, at, :]
 
             by_rows(resid.shape[0], STEP, put)
-    sums = Rows(spot, part, sums_got, sums_line, sums_cross, sums_sems)
-    sums.start()
+    half = resid.shape[0] // HALVES
+    sums = [
+        Rows(spot, part, sums_got, sums_line, sums_cross.at[i], sums_sems.at[i], i * half, half)
+        for i in range(HALVES)
+    ]
+    for k in range(spot.hi):
+        for each in sums:
+            each.start(k)
     tots[0] = jnp.zeros_like(tots[0])
     lane_grads[...] = jnp.zeros_like(lane_grads)
     shift_grad[...] = jnp.zeros_like(shift_grad)
@@ -832,10 +925,12 @@
         return none
 
     lax.fori_loop(0, heads // 2, upward, 0)
-    sums.along(1)
+    for each in sums:
+        each.along(1)
     lax.fori_loop(heads // 2, heads, upward, 0)
-    sums.along(2)
     come = Prefix(spot, seqs, True, tots, gots, line, cube_sems, line_sems).run()
+    for each in sums:
+        each.along(2)
     tots[0, 0:seqs, :] = come
 
     def downward(h, none):
@@ -892,10 +987,11 @@
         return none
 
     lax.fori_loop(0, heads, downward, 0)
-    for s in range(3, spot.hi):
-        sums.along(s)
     copy = remote(back.at[:, 0:HALO, :], rim, rim_sems, 0, behind)
     copy.start()
+    for s in range(3, spot.hi):
+        for each in sums:
+            each.along(s)
     copy.wait()
 
     def give(h, none):
@@ -916,8 +1012,10 @@
     def done(at, total):
         own_out[at, :] = (resid[at, :] + total).astype(BF16)
 
-    sums.end(done)
-    sums.finish()
+    for each in sums:
+        each.end(done)
+    for each in sums:
+        each.finish()
 
 
 def leave_recurrence(
@@ -965,10 +1063,17 @@
 
 
 class Rows:
-    def __init__(self, spot, part, got, line, cross_sems, line_sems):
+    def __init__(self, spot, part, got, line, cross_sems, line_sems, first, rows):
         self.spot, self.part, self.got, self.line = spot, part, got, line
         self.cross_sems, self.line_sems = cross_sems, line_sems
-        self.rows = got.shape[1]
+        self.first, self.rows = first, rows
+        self.span = pl.ds(first, rows)
+
+    def by_rows(self, act):
+        def one(at):
+            act(pl.ds(pl.multiple_of(self.first + at.start, STEP), STEP))
+
+        by_rows(self.rows, STEP, one)
 
     def place(self, k):
         spot, hi = self.spot, self.spot.hi
@@ -984,19 +1089,26 @@
     def cross_copy(self, place):
         spot = self.spot
         return remote(
-            self.part.at[place, 1 - spot.t], self.got.at[place], self.cross_sems, place, spot.cross
+            self.part.at[place, 1 - spot.t, self.span],
+            self.got.at[place, self.span],
+            self.cross_sems,
+            place,
+            spot.cross,
         )
 
-    def start(self):
-        for k in range(self.spot.hi):
-            self.cross_copy(self.place(k)).start()
+    def start(self, k):
+        self.cross_copy(self.place(k)).start()
 
     def line_copy(self, s, up, here=False):
         spot, hi = self.spot, self.spot.hi
         slot = (s - 1) if up else hi + s - 2
         step = 1 if up != here else -1
         return remote(
-            self.line.at[0, slot], self.line.at[1, slot], self.line_sems, slot, spot.line(spot.z + step)
+            self.line.at[0, slot, self.span],
+            self.line.at[1, slot, self.span],
+            self.line_sems,
+            slot,
+            spot.line(spot.z + step),
         )
 
     def own(self, place, at):
@@ -1014,7 +1126,7 @@
             def put(at):
                 self.line[0, slot, at, :] = self.own(place, at).astype(BF16)
 
-            by_rows(self.rows, STEP, put)
+            self.by_rows(put)
 
         if s > 1:
 
@@ -1026,7 +1138,7 @@
                     before = self.line[1, slot - 1, at, :].astype(F32)
                     self.line[0, slot, at, :] = (self.own(place, at) + before).astype(BF16)
 
-                by_rows(self.rows, STEP, put)
+                self.by_rows(put)
 
         self.line_copy(s, up).start()
 
@@ -1066,7 +1178,7 @@
             value = value + jnp.where(spot.z > 0, below, 0.0)
             done(at, value + jnp.where(spot.z < hi - 1, above, 0.0))
 
-        by_rows(self.rows, STEP, total)
+        self.by_rows(total)
 
     def finish(self):
         spot, hi = self.spot, self.spot.hi
@@ -1099,10 +1211,20 @@
         whole[spot.z, spot.t, at, :] = own[at, :]
 
     by_rows(rows, STEP, put)
-    chain = Chain(
-        spot, lambda place, k: whole.at[place, lax.rem(spot.t + k, tensor)], sems, [spot.cross]
-    )
-    chain.first()
+    half = rows // HALVES
+    chains = [
+        Chain(
+            spot,
+            lambda place, k, i=i: whole.at[
+                place, lax.rem(spot.t + k, tensor), pl.ds(i * half, half)
+            ],
+            sems.at[i],
+            [spot.cross],
+        )
+        for i in range(HALVES)
+    ]
+    for chain in chains:
+        chain.first()
     gain_grad[...] = jnp.zeros_like(gain_grad)
     tiles = width // LANE
     skip = spot.z * tiles - jnp.minimum(spot.z * tiles, unit_tiles - tiles)
@@ -1136,15 +1258,22 @@
         lax.fori_loop(0, d // chunk, back, 0)
 
     def come_and_work(place):
-        chain.fans.arrive(place, 1)
+        for chain in chains:
+            chain.fans.arrive(place, 1)
         work(place)
 
     for s in range(1, hi):
-        chain.onward(s)
-        chain.places(s - 1, come_and_work)
-    chain.places(hi - 1, come_and_work)
-    sums = Rows(spot, part, got, line, cross_sems, line_sems)
-    sums.start()
+        for chain in chains:
+            chain.onward(s)
+        chains[0].places(s - 1, come_and_work)
+    chains[0].places(hi - 1, come_and_work)
+    sums = [
+        Rows(spot, part, got, line, cross_sems.at[i], line_sems.at[i], i * half, half)
+        for i in range(HALVES)
+    ]
+    for k in range(hi):
+        for each in sums:
+            each.start(k)
 
     def give(i, none):
         place, j = i // (d // chunk), lax.rem(i, d // chunk)
@@ -1155,7 +1284,8 @@
         return none
 
     lax.fori_loop(0, hi * (d // chunk), give, 0)
-    chain.finish_sends()
+    for chain in chains:
+        chain.finish_sends()
 
     def done(at, total):
         value = resid[at, :]
@@ -1169,20 +1299,26 @@
         mine[at, :] = grad.astype(BF16)
 
     for s in range(1, hi):
-        sums.along(s)
-    sums.end(done)
-    copy = remote(mine, other, swap_sems, 0, spot.cross)
-    copy.start()
-    sums.finish()
-    share(spot, copy, mine, other, both)
-
-
-def share(spot, copy, mine, other, both):
+        for each in sums:
+            each.along(s)
+    swaps = []
+    for i, each in enumerate(sums):
+        each.end(done)
+        span = pl.ds(i * half, half)
+        swaps.append(remote(mine.at[span], other.at[span], swap_sems, i, spot.cross))
+        swaps[-1].start()
+    for each in sums:
+        each.finish()
+    share(spot, swaps, mine, other, both)
+
+
+def share(spot, copies, mine, other, both):
     def keep(at):
         both[spot.t, at, :] = mine[at, :]
 
     by_rows(mine.shape[0], STEP, keep)
-    copy.wait()
+    for copy in copies:
+        copy.wait()
 
     def take(at):
         both[1 - spot.t, at, :] = other[at, :]
@@ -1203,9 +1339,9 @@
 def rows_sems(grid):
     hi = grid.hi
     return [
-        pltpu.SemaphoreType.DMA((2, hi)),
-        pltpu.SemaphoreType.DMA((2, 2 * (hi - 1))),
-        pltpu.SemaphoreType.DMA((2, 1)),
+        pltpu.SemaphoreType.DMA((HALVES, 2, hi)),
+        pltpu.SemaphoreType.DMA((HALVES, 2, 2 * (hi - 1))),
+        pltpu.SemaphoreType.DMA((2, HALVES)),
     ]
 
 
@@ -1237,7 +1373,7 @@
         out_specs=[near] * 7,
         scratch_shapes=[pltpu.VMEM(whole.shape, BF16)]
         + rows_scratch(grid, rows, d)
-        + [chain_sems(1)]
+        + [chain_sems(1, HALVES)]
         + rows_sems(grid),
         compiler_params=pltpu.CompilerParams(
             collective_id=2, has_side_effects=True, vmem_limit_bytes=GRANT
@@ -1345,7 +1481,7 @@
                 for place in range(hi):
                     skip = place * tiles - min(place * tiles, unit_tiles - tiles)
                     if skip < tiles:
-                        value = got_line[span, place, at, skip * LANE :].astype(F32)
+                        value = got_line[span, place, at, skip * LANE :]
                         apart[span, at, place * width : (place + 1) * width - skip * LANE] = value
             else:
                 value = got_line[span, 0, at, :].astype(F32)
@@ -1600,7 +1736,7 @@
         return pl.BlockSpec(a.shape, lambda i: zeros, pipeline_mode=pl.Buffered(1))
 
     block = gates.shape[1]
-    apart = jax.ShapeDtypeStruct((kept, rows, unit_tiles * LANE), F32)
+    apart = jax.ShapeDtypeStruct((kept, rows, unit_tiles * LANE), BF16)
     summed = jax.ShapeDtypeStruct(((all_spans - kept) * (width // block), rows, block), F32)
     both = jax.ShapeDtypeStruct((grid.tensor,) + own_out.shape, BF16)
     other = jax.ShapeDtypeStruct(first.shape, BF16)
@@ -1716,14 +1852,6 @@
     flags = jnp.stack([jnp.logical_not(earlier[0])] + earlier, axis=-1).astype(F32)
     flags = jnp.pad(flags.reshape(rows_all, CONV), ((0, 0), (0, 8 - CONV)))
 
-    rec_own = jnp.stack(
-        [
-            input_weight.reshape(d_own, channels),
-            gelu_weight.reshape(d_own, channels),
-            out_weight.reshape(channels, d_own).T,
-        ]
-    )
-    gates_own = jnp.stack([inlet_weight, forget_weight]).reshape(2 * head_count, lane_own, block_size)
     per_lane = jnp.stack([gelu_bias, input_bias])
     per_lane = jnp.concatenate(
         [per_lane, conv_weight, jnp.stack([conv_bias, inlet_bias, forget_bias, decay_rate])]
@@ -1740,35 +1868,21 @@
     )
     thin_count = thin_own.shape[0]
     thin_own = jnp.pad(thin_own, ((0, -thin_count % 16), (0, 0)))
-    feed_own = jnp.stack([mlp_gate, mlp_up, mlp_down.T])
-    feed_windows = jnp.stack(
-        [
-            feed_own[:, :, tile * LANE : tile * LANE + window]
-            for tile in (
-                min(place * window_tiles, unit_tiles - window_tiles) for place in range(grid.hi)
-            )
-        ],
-        axis=1,
-    )
     cot_rows = cotangent.reshape(grid.tensor, rows_half, width)
-    cot_own = pick(cot_rows, grid.t)
-    rec_all, gates_all, thin_all, feed_all, cot_all = blank(
-        (3, grid.n, d_own, channels),
-        (2 * head_count, grid.n, lane_own, block_size),
-        (grid.n,) + thin_own.shape,
-        (3, grid.n + grid.hi, d_own, window),
-        (grid.hi, grid.tensor, rows_half, width),
-    )
-    rec_all = lax.dynamic_update_slice(rec_all, rec_own[:, None], (0, grid.w, 0, 0))
-    gates_all = lax.dynamic_update_slice(gates_all, gates_own[:, None], (0, grid.w, 0, 0))
-    thin_all = lax.dynamic_update_slice(thin_all, thin_own[None], (grid.w, 0, 0))
-    feed_all = lax.dynamic_update_slice(feed_all, feed_windows, (0, grid.n, 0, 0))
-    feed_all = lax.dynamic_update_slice(
-        feed_all, lax.dynamic_slice_in_dim(feed_windows, grid.z, 1, 1), (0, grid.w, 0, 0)
-    )
-    cot_all = lax.dynamic_update_slice(cot_all, cot_own[None, None], (grid.z, grid.t, 0, 0))
-    rec_all, gates_all, thin_all, feed_all = bring_weights(
-        grid, rec_all, gates_all, thin_all, feed_all
+    rec_all, gates_all, thin_all, feed_all, cot_all = place_own(
+        grid,
+        (
+            input_weight.transpose(1, 0, 2),
+            gelu_weight.transpose(1, 0, 2),
+            out_weight.transpose(0, 2, 1),
+        ),
+        (mlp_gate, mlp_up, mlp_down.T),
+        (inlet_weight, forget_weight),
+        thin_own,
+        cot_rows,
+    )
+    rec_all, gates_all, thin_all, cot_all = bring_weights(
+        grid, rec_all, gates_all, thin_all, cot_all
     )
     rec_all = rec_all.reshape(3, width, channels)
     gates_all = gates_all.reshape(2, head_count, block_size, block_size)
@@ -1795,10 +1909,9 @@
         resid,
         second_own,
         feed_all,
-        cot_all,
     ) = forward_recurrence(
         grid, x, halo, gain_first[None], rec_all, inlet_full, forget_full, lanes, flags, out_shift[None],
-        gain_second[None], feed_all, cot_all, seq_count,
+        gain_second[None], feed_all, seq_count,
     )
 
     rows_feed = grid.hi * rows_all
@@ -1852,7 +1965,8 @@
     )
     block_out = block_out.reshape(block_in.shape)
     thin = thin.reshape(-1)
-    gate_grad, up_grad, down_grad = feed_grads[0], feed_grads[1], feed_grads[2].T
+    gate_grad, up_grad, down_grad = (feed_grads[m].astype(F32) for m in range(3))
+    down_grad = down_grad.T
     gelu_w_grad = rec_grads[:head_count].transpose(1, 0, 2)
     input_w_grad = rec_grads[head_count : 2 * head_count].transpose(1, 0, 2)
     out_grad = rec_grads[2 * head_count : 3 * head_count].transpose(0, 2, 1)

time: 830 us -> 783 us (0.943)
  Pallas kernels: 766 us -> 736 us
  local copies, waits for them, and re-layouts: 38.5 us -> 25.4 us
    pallas_call x1, Pallas kernels: 163 us -> 148 us  [bring_weights(): pl.pallas_call(functools.partial(weights_kernel, n, tensor), out_shape=[j...]
    pallas_call x1, Pallas kernels: 244 us -> 233 us  [send_grads(): pl.pallas_call(functools.partial(grads_kernel, grid.n, grid.tensor, spans...]
    pallas_call x1, Pallas kernels: 77.4 us -> 69.1 us  [leave_recurrence(): pl.pallas_call(functools.partial(leave_kernel, grid.n, grid.tensor, seqs)...]
  transfers between devices with their start and end apart: 3 -> 3, of which waited for: 0 -> 0; matrix products, arithmetic and copies ran while one was open for 4% -> 2% of each run, Pallas kernels for 20% -> 20%
where the time goes in v5:
time: 783 us; the launch traced here: 779 us
  Pallas kernels  736 us (94%)
  local copies, waits for them, and re-layouts  25.4 us (3%)
  other arithmetic  13.9 us (2%)
    pallas_call x1, Pallas kernels, send_grads(): pl.pallas_call(functools.partial(grads_kernel, grid.n, grid.tensor, spans...  233 us
    pallas_call x1, Pallas kernels, feed_forward(): pl.pallas_call(functools.partial(feed_kernel, grid.n, tensor, unit_tiles)...  154 us
    pallas_call x1, Pallas kernels, bring_weights(): pl.pallas_call(functools.partial(weights_kernel, n, tensor), out_shape=[j...  148 us
    pallas_call x1, Pallas kernels, forward_recurrence(): pl.pallas_call(functools.partial(forward_kernel, grid.n, grid.tensor, seq...  115 us
    pallas_call x1, Pallas kernels, leave_recurrence(): pl.pallas_call(functools.partial(leave_kernel, grid.n, grid.tensor, seqs)...  69.1 us
  transfers between devices with their start and end apart: 3, of which 0 were waited for; matrix products, arithmetic and copies ran while one was open for 2% of the time, Pallas kernels for 20%

profile of v5, /device:TPU:27, one launch (start us, length us, event | category | flops | bytes accessed | tf_op | source)
XLA Modules:
  0.0 779.2 jit_solution(14207247607398462549)
XLA Ops:
  0.7 0.7 add_convert_fusion
  1.3 0.1 slice.129
  1.4 1.8 collective-permute-start.1
  3.2 0.9 slice.124
  4.1 0.0 collective-permute-start
  4.1 0.7 copy.70
  4.8 0.7 copy.71
  5.5 0.7 copy.72
  6.2 0.7 copy.73
  6.9 0.7 copy.74
  7.6 0.7 copy.75
  8.2 0.8 concatenate.16
  9.0 1.6 dynamic_update_slice.6
  10.7 0.7 stack.78
  11.3 0.7 stack.79
  12.0 0.7 stack.80
  12.7 0.3 dynamic_update_slice.7
  13.0 0.6 pad_maximum_fusion.thin
  13.6 0.6 pad_add_fusion.1.spot
  14.2 7.3 place.1
  21.6 147.6 %bring_weights.1 = (bf16[3,16,160,1280]{3,2,1,0:T(8,128)(2,1)}, bf16[10,16,16,256]{3,2,1,0:T(8,128)(2,1)}, bf16[16,16,1280]{2,1,0:T(8,128)(2,1)}, bf16[4,2,128,2560]{3,2,1,0:T(8,128)(2,1)}) custom-call(bf16[3,16,160,1280]{3,2,1,0:T(8,128)(2,1)} %get-tuple-element.62.rec, ...), custom_call_target="tpu_custom_call", output_to_operand_aliasing={{0}: (0, {}), {1}: (1, {}), {2}: (2, {}), {3}: (3, {})} | custom-call | tf_op jit(solution)/shard_map/bring_weights/pallas_call | solution.py:467
  169.2 1.3 convert_reduce_fusion
  170.6 0.3 multiply_reduce_fusion
  170.9 1.2 fusion.8
  172.1 0.6 copy.82
  172.7 0.6 copy.87
  173.3 0.6 copy.88
  173.9 0.7 select_maximum_fusion.lanes
  174.6 0.0 collective-permute-done.1
  174.6 0.1 not_bitcast_fusion
  174.7 0.2 copy.77
  174.9 0.7 pad_convert_fusion.flags
  175.6 0.0 collective-permute-done
  175.6 0.6 select_bitcast_fusion.halo
  176.2 114.9 %forward_recurrence.1 = (bf16[256,2560]{1,0:T(8,128)(2,1)}, bf16[2,136,1280]{2,1,0:T(8,128)(2,1)}, bf16[256,1280]{1,0:T(8,128)(2,1)}, f32[256,1280]{1,0:T(8,128)...) custom-call(bf16[256,2560]{1,0:T(8,128)(2,1)} %bitcast.128, ...), custom_call_target="tpu_custom_call", output_to_operand_aliasing={{12}: (12, {})} | custom-call | tf_op jit(solution)/shard_map/forward_recurrence/pallas_call | solution.py:822
  291.1 154.3 %feed_forward.1 = (bf16[4,2,128,2560]{3,2,1,0:T(8,128)(2,1)}, bf16[4,256,1024]{2,1,0:T(8,128)(2,1)}, bf16[4,256,1024]{2,1,0:T(8,128)(2,1)}, bf16[4,256,1024]{2,1...) custom-call(bf16[128,2560]{1,0:T(8,128)(2,1)} %get-tuple-element.70.own, ...), custom_call_target="tpu_custom_call" | custom-call | tf_op jit(solution)/shard_map/feed_forward/pallas_call | solution.py:1360
  445.4 69.1 %leave_recurrence.1 = (bf16[256,1280]{1,0:T(8,128)(2,1)}, bf16[256,1280]{1,0:T(8,128)(2,1)}, bf16[2,5,256,256]{3,2,1,0:T(8,128)(2,1)}, f32[16,1280]{1,0:T(8,128)...) custom-call(bf16[256,2560]{1,0:T(8,128)(2,1)} %bitcast.130, bf16[3,2560,1280]{2,1,0:T(8,128)(2,1)} %bitcast.121, ...), custom_call_target="tpu_custom_call" | custom-call | tf_op jit(solution)/shard_map/leave_recurrence/pallas_call | solution.py:1030
  514.5 0.8 broadcast_in_dim.22.scale
  515.3 10.0 %first_gradient.1 = (bf16[256,2560]{1,0:T(8,128)(2,1)}, f32[8,2560]{1,0:T(8,128)}) custom-call(bf16[256,2560]{1,0:T(8,128)(2,1)} %bitcast.129, bf16[256,1280]{1,0:T(8,128)(2,1)} %get-tuple-element.90.input_low, bf16[256,1280]{1,0:T(8,128)(2,1)} %get-tuple-element.89.gelu_low, bf16[3,2560,1280]{2,1,0:T(8,128)(2,1)} %bitcast.122, ...), custom_call_target="tpu_custom_call" | custom-call | tf_op jit(solution)/shard_map/first_gradient/pallas_call | solution.py:577
  525.3 1.0 reduce_sum.64
  526.4 0.9 collective-permute-start.2
  527.4 0.2 reshape.171
  527.5 0.2 copy.94
  527.7 0.2 reshape.172
  527.9 0.1 reshape.170
  528.0 1.2 copy.78
  529.3 0.1 slice_reduce_fusion
  529.3 0.1 reshape_squeeze.7
  529.4 0.1 reshape_squeeze.8
  529.5 0.1 concatenate.20
  529.6 0.8 reshape.173.thin
  530.3 233.0 %send_grads.1 = (bf16[3,160,3840]{2,1,0:T(8,128)(2,1)}, f32[16,160,256]{2,1,0:T(8,128)}, bf16[256,2560]{1,0:T(8,128)(2,1)}, bf16[2,128,2560]{2,1,0:T(8,128)(2,1)}, f32[8,160]{1,0:T(8,128)}) custom-call(bf16[1024,2560]{1,0:T(8,128)(2,1)} %bitcast.137, bf16[1024,2560]{1,0:T(8,128)(2,1)} %bitcast.127, bf16[256,2560]{1,0:T(8,128)(2,1)} %get-tuple-element.75.normed, ...), custom_call_target="tpu_custom_call" | custom-call | tf_op jit(solution)/shard_map/send_grads/pallas_call | solution.py:1755
  763.3 3.3 slice_bitcast_fusion
  766.6 1.6 fusion.7
  768.2 0.6 fusion.10
  768.8 3.7 convert_bitcast_fusion
  772.6 0.8 copy-done.5
  773.3 0.7 fusion
  774.1 2.7 fusion.1
  776.8 0.1 reshape.175
  776.8 0.6 slice_bitcast_fusion.5
  777.4 0.1 slice.144
  777.5 0.6 copy.80
  778.1 1.1 copy.103
  (50 shorter events, 0.4 us)
Async XLA Ops:
  1.4 173.2 %collective-permute-start.1 = (bf16[2,3]{1,0:T(2,128)(2,1)S(1)}, bf16[2,3]{1,0:T(2,128)(2,1)S(1)}, u32[]{:S(2)}, u32[]{:S(2)}) collective-permute-start(bf16[2,3]{1,0:T(2,128)(2,1)S(1)} %slice.129), channel_id=1, source_target_pairs={{0,2},{2,4},{4,6},{6,8},{8,10},{10,12},{12,14},{14,16},{16,18},{18... | collective-permute-start | bytes 44 | tf_op jit(solution)/shard_map/ppermute | solution.py:44
  4.1 171.5 %collective-permute-start = (bf16[2,8,2560]{2,1,0:T(8,128)(2,1)S(1)}, bf16[2,8,2560]{2,1,0:T(8,128)(2,1)S(1)}, u32[]{:S(2)}, u32[]{:S(2)}) collective-permute-start(bf16[2,8,2560]{2,1,0:T(8,128)(2,1)S(1)} %slice.124), channel_id=1, source_target_pairs={{0,2},{2,4},{4,6},{6,8},{8,10},{10,12},{12,14},{14,16},{16,18},{18... | collective-permute-start | bytes 245768 | tf_op jit(solution)/shard_map/ppermute | solution.py:44
  21.6 149.0 %copy-start = (bf16[2,128,2560]{2,1,0:T(8,128)(2,1)S(1)}, bf16[2,128,2560]{2,1,0:T(8,128)(2,1)}, u32[]{:S(2)}) copy-start(bf16[2,128,2560]{2,1,0:T(8,128)(2,1)} %param.21) | copy-start | bytes 3932164
  169.2 1.7 copy-start.4
  515.3 11.1 %copy-start.10 = (f32[8,2560]{1,0:T(8,128)S(1)}, f32[8,2560]{1,0:T(8,128)}, u32[]{:S(2)}) copy-start(f32[8,2560]{1,0:T(8,128)} %get-tuple-element.96) | copy-start | bytes 245764
  515.3 12.1 %copy-start.11 = (f32[16,1280]{1,0:T(8,128)S(1)}, f32[16,1280]{1,0:T(8,128)}, u32[]{:S(2)}) copy-start(f32[16,1280]{1,0:T(8,128)} %get-tuple-element.98) | copy-start | bytes 245764
  525.3 2.6 copy-start.9
  525.3 2.7 copy-start.8
  526.4 2.8 collective-permute-start.2
  763.3 4.9 copy-start.12
  763.3 5.5 copy-start.6
  768.8 3.8 copy-start.1
  768.8 3.8 copy-start.2
  768.8 4.5 copy-start.5
  772.6 1.5 copy-start.3
  774.1 4.1 copy-start.7

commit v6 on v5

--- a/solution.py
+++ b/solution.py
@@ -855,6 +855,314 @@
     )(x, halo, gain, rec, rec, inlet, forget, lanes, flags, rec, shift, gain_second, feed)
 
 
+def place_feed_kernel(unit_tiles, spot, gate, up, down, cot, feed_all, cot_all):
+    step = pl.program_id(0)
+    width = feed_all.shape[3]
+    tiles = width // LANE
+
+    @pl.when(step == 0)
+    def _():
+        cot_all[0, 0] = cot[0]
+
+    place = jnp.where(step < LINE, step, spot[1])
+    tile = jnp.minimum(place * tiles, unit_tiles - tiles)
+    for m, source in enumerate((gate, up, down)):
+        feed_all[m, 0] = source[:, pl.ds(pl.multiple_of(tile * LANE, LANE), width)]
+
+
+def place_feed(grid, feed, cot):
+    n, hi = grid.n, grid.hi
+    d_own, units = feed[0].shape
+    unit_tiles = units // LANE
+    window = -(-unit_tiles // hi) * LANE
+    spot = jnp.stack([grid.w, grid.z, grid.t])
+    outs = [(3, n + hi, d_own, window), (hi,) + cot.shape]
+    return pl.pallas_call(
+        functools.partial(place_feed_kernel, unit_tiles),
+        grid_spec=pltpu.PrefetchScalarGridSpec(
+            num_scalar_prefetch=1,
+            grid=(hi + 1,),
+            in_specs=[pl.BlockSpec(a.shape, lambda i, spot: (0, 0)) for a in feed]
+            + [pl.BlockSpec((1,) + cot.shape[1:], lambda i, spot: (spot[2], 0, 0))],
+            out_specs=[
+                pl.BlockSpec(
+                    (3, 1, d_own, window),
+                    lambda i, spot: (0, jnp.where(i < hi, n + i, spot[0]), 0, 0),
+                ),
+                pl.BlockSpec((1, 1) + cot.shape[1:], lambda i, spot: (spot[1], spot[2], 0, 0)),
+            ],
+        ),
+        out_shape=[jax.ShapeDtypeStruct(shape, BF16) for shape in outs],
+        compiler_params=pltpu.CompilerParams(vmem_limit_bytes=GRANT),
+        name="place",
+    )(spot, *feed, cot)
+
+
+def gather_kernel(
+    n, tensor, seqs, thin_lanes,
+    x, halo, flags, wide_in, gelu_in, out_in, inlet_in, forget_in, thin_in, feed, cot,
+    normed, ext, conv, gelu_pre, inlet_pre, forget_pre, cum, local, entered, mixed, resid, second,
+    lanes, table, gates_out, rec_out, feed_all, cot_all,
+    rec, gates, thin, held, factor, addend, part, out, got, tots, gots, line,
+    rec_sems, gates_sems, thin_sems, feed_sems, cot_sems, cube_sems, line_sems, swap_sems, own_sem,
+):
+    del feed, cot
+    spot = Spot(n, tensor)
+    hi = spot.hi
+    rows, d = x.shape
+    length = rows // seqs
+    heads, d_own, width = wide_in.shape
+    cube = [spot.flip(bit) for bit in spot.bits]
+
+    def index(place, k):
+        return place * spot.inner_size + jnp.bitwise_xor(spot.inner, k)
+
+    chains = [
+        Chain(spot, lambda place, k: thin.at[index(place, k)], thin_sems, cube),
+        Chain(spot, lambda place, k: gates.at[:, index(place, k)], gates_sems, cube),
+    ] + [
+        Chain(spot, lambda place, k, m=m: rec.at[m, index(place, k)], rec_sems.at[m], cube)
+        for m in range(3)
+    ]
+    turns = FeedTurns(spot, feed_all, feed_sems, cube)
+    cots = Chain(
+        spot,
+        lambda place, k: cot_all.at[place, lax.rem(spot.t + k, tensor)],
+        cot_sems,
+        [spot.cross],
+    )
+    for m, source in enumerate((wide_in, gelu_in, out_in)):
+        for h in range(heads):
+            rec[m, spot.w, :, h * width : (h + 1) * width] = source[h]
+    for m, source in enumerate((inlet_in, forget_in)):
+        for h in range(heads):
+            gates[m * heads + h, spot.w] = source[h]
+    thin[spot.w] = thin_in[...]
+    spot.greet(*cube, spot.cross)
+    for chain in chains:
+        chain.first()
+    cots.fans.hand_on(spot.z, 0)
+    for s in range(1, hi):
+        for chain in chains:
+            chain.onward(s)
+        if s == 1:
+            cots.first_line()
+        else:
+            cots.onward(s - 1)
+        for chain in chains:
+            chain.second(s - 1)
+    turns.start(1)
+    for chain in chains:
+        chain.second(hi - 1)
+    for chain in chains:
+        chain.finish()
+    turns.start(0)
+    keep = pltpu.make_async_copy(rec, rec_out, own_sem)
+    keep.start()
+
+    sums = thin[0].astype(F32)
+    for i in range(1, n):
+        sums = sums + thin[i].astype(F32)
+    table[...] = sums
+    rate = sums[RATE_SOFT : RATE_SOFT + 1]
+    lanes[0:RATE_SOFT, :] = sums[0:RATE_SOFT]
+    soft = jnp.maximum(rate, 0.0) + jnp.log1p(jnp.exp(-jnp.abs(rate)))
+    lanes[RATE_SOFT : RATE_SOFT + 1, :] = soft
+    lanes[RATE_SIGMOID : RATE_SIGMOID + 1, :] = jax.nn.sigmoid(rate)
+    lanes[RATE_SIGMOID + 1 :, :] = jnp.zeros((LANE_ROWS - RATE_SIGMOID - 1, sums.shape[1]), F32)
+    per = d // sums.shape[1]
+
+    def across(i):
+        first = thin_lanes + i * per
+        return jnp.concatenate([sums[first + j : first + j + 1] for j in range(per)], axis=1)
+
+    gain, shift, gain_second = across(0), across(1), across(2)
+
+    def norm_first(source, at, to):
+        value = source[at, :].astype(F32)
+        scale = lax.rsqrt(jnp.mean(value * value, axis=-1, keepdims=True) + 1e-06)
+        value = (value * scale * gain).astype(BF16)
+        held[pl.ds(pl.multiple_of(at.start + to, STEP), STEP), :] = value
+        return value
+
+    def main(at):
+        normed[at, :] = norm_first(x, at, 0)
+
+    by_rows(rows, STEP, main)
+    by_rows(halo.shape[0], STEP, lambda at: norm_first(halo, at, rows))
+
+    def work(step, none):
+        cols = pl.ds(pl.multiple_of(step * width, width), width)
+
+        def row(i):
+            return lanes[i : i + 1, cols]
+
+        def matrix(m):
+            return rec[m, :, :, cols].reshape(d, width)
+
+        branch = (dot(held[...], matrix(0)) + row(INPUT_SHIFT)).astype(BF16)
+        gelu_pre[:, cols] = dot(held[0:rows, :], matrix(1)) + row(GELU_SHIFT)
+        for s in range(seqs):
+            here = slice(s * length, (s + 1) * length)
+            front = rows + s * HALO
+            longer = jnp.concatenate(
+                [branch[front : front + HALO].astype(F32), branch[here].astype(F32)], axis=0
+            )
+            ext[s, :, cols] = longer.astype(BF16)
+            total = row(CONV_SHIFT) + row(TAPS) * longer[HALO:]
+            for k in range(1, CONV):
+                moved = pltpu.roll(longer, k, 0)[HALO:]
+                total = total + jnp.where(flags[here, k : k + 1] > 0.5, row(TAPS + k) * moved, 0.0)
+            conv[here, cols] = total.astype(BF16)
+        blocks = conv[:, cols]
+        for m, (to, bias) in enumerate(((inlet_pre, INLET_SHIFT), (forget_pre, FORGET_SHIFT))):
+            gate = gates[m * heads + step].reshape(width, width)
+            gates_out[m * heads + step] = gate
+            to[:, cols] = dot(blocks, gate) + row(bias)
+
+        def terms(at):
+            starts = flags[at, 0:1] > 0.5
+            decay, scaler = decay_of(jax.nn.sigmoid(forget_pre[at, cols]), row(RATE_SOFT), starts)
+            factor[at, :] = decay
+            addend[at, :] = scaler * jax.nn.sigmoid(inlet_pre[at, cols]) * conv[at, cols].astype(F32)
+
+        by_rows(rows, 32, terms)
+
+        def write(at, a, b):
+            cum[at, cols] = a
+            local[at, cols] = b
+
+        scan_rows(seqs, length, width, lambda at: (factor[at, :], addend[at, :]), write, False)
+        return none
+
+    lax.fori_loop(0, heads, work, 0)
+    tots[0] = jnp.zeros_like(tots[0])
+    for s in range(seqs):
+        tots[0, s : s + 1, :] = cum[(s + 1) * length - 8 : (s + 1) * length, :][7:8]
+        tots[0, seqs + s : seqs + s + 1, :] = local[(s + 1) * length - 8 : (s + 1) * length, :][7:8]
+    enter = Prefix(spot, seqs, False, tots, gots, line, cube_sems, line_sems).run()
+    turns.start(3)
+    turns.onward(1)
+    cots.onward(3)
+    turns.start(2)
+    entered[...] = jnp.zeros_like(entered)
+    entered[0:seqs, :] = enter
+    for s in range(seqs):
+
+        def mix(at, s=s):
+            here = pl.ds(pl.multiple_of(s * length + at.start, STEP), STEP)
+            state = local[here, :] + cum[here, :] * enter[s : s + 1]
+            mixed[here, :] = (state * gelu_of(gelu_pre[here, :])[0]).astype(BF16)
+
+        by_rows(length, STEP, mix)
+    values = mixed[...]
+    own_rows = resid.shape[0]
+    each, slab = n // hi, d // hi
+
+    def branch(j, none):
+        at = pl.ds(pl.multiple_of(j * slab, LANE), slab)
+        weights = rec[2, pl.ds(j * each, each)].reshape(slab, heads * width)
+        value = dot_nt(values, weights)
+        for side in range(tensor):
+            part[side, :, at] = value[side * own_rows : (side + 1) * own_rows]
+        return none
+
+    lax.fori_loop(0, hi, branch, 0)
+
+    def put(at):
+        out[at, :] = part[1 - spot.t, at, :].astype(BF16)
+
+    by_rows(own_rows, STEP, put)
+    copy = remote(out, got, swap_sems, 0, spot.cross)
+    copy.start()
+    copy.wait()
+
+    def norm(at):
+        own = x[pl.ds(pl.multiple_of(spot.t * own_rows + at.start, STEP), STEP), :].astype(F32)
+        value = own + (part[spot.t, at, :] + got[at, :].astype(F32) + shift)
+        resid[at, :] = value
+        scale = lax.rsqrt(jnp.mean(value * value, axis=-1, keepdims=True) + 1e-06)
+        second[at, :] = (value * scale * gain_second).astype(BF16)
+
+    by_rows(own_rows, STEP, norm)
+    turns.onward(3)
+    turns.second(0)
+    turns.second(1)
+    turns.onward(2)
+    turns.second(3)
+    turns.second(2)
+    turns.finish()
+    cots.finish()
+    keep.wait()
+
+
+def gather_recurrence(grid, x, halo, flags, rec, gates, thin, thin_lanes, feed, cot, seqs):
+    rows, d = x.shape
+    heads, d_own, width = rec[0].shape
+    lane_own = gates[0].shape[1]
+    n = grid.n
+    channels = heads * width
+    longer = rows // seqs + HALO
+    own_rows = rows // grid.tensor
+    near = pl.BlockSpec(memory_space=pltpu.VMEM)
+    far = pl.BlockSpec(memory_space=pl.ANY)
+    wide = jax.ShapeDtypeStruct((rows, channels), F32)
+    whole = (3, n, d_own, channels)
+    cube = grid.inner_size.bit_length() - 1
+    outs = [
+        jax.ShapeDtypeStruct((rows, d), BF16),
+        jax.ShapeDtypeStruct((seqs, longer, channels), BF16),
+        jax.ShapeDtypeStruct((rows, channels), BF16),
+        wide,
+        wide,
+        wide,
+        wide,
+        wide,
+        jax.ShapeDtypeStruct((8, channels), F32),
+        jax.ShapeDtypeStruct((rows, channels), BF16),
+        jax.ShapeDtypeStruct((own_rows, d), F32),
+        jax.ShapeDtypeStruct((own_rows, d), BF16),
+        jax.ShapeDtypeStruct((LANE_ROWS, channels), F32),
+        jax.ShapeDtypeStruct(thin.shape, F32),
+        jax.ShapeDtypeStruct((2 * heads, width, width), BF16),
+        jax.ShapeDtypeStruct(whole, BF16),
+        jax.ShapeDtypeStruct(feed.shape, BF16),
+        jax.ShapeDtypeStruct(cot.shape, BF16),
+    ]
+    return pl.pallas_call(
+        functools.partial(gather_kernel, n, grid.tensor, seqs, thin_lanes),
+        out_shape=outs,
+        in_specs=[near] * 9 + [far] * 2,
+        out_specs=[near] * 15 + [far] * 3,
+        input_output_aliases={9: 16, 10: 17},
+        scratch_shapes=[
+            pltpu.VMEM(whole, BF16),
+            pltpu.VMEM((2 * heads, n, lane_own, width), BF16),
+            pltpu.VMEM((n,) + thin.shape, BF16),
+            pltpu.VMEM((rows + halo.shape[0], d), BF16),
+            pltpu.VMEM((rows, width), F32),
+            pltpu.VMEM((rows, width), F32),
+            pltpu.VMEM((grid.tensor, own_rows, d), F32),
+            pltpu.VMEM((own_rows, d), BF16),
+            pltpu.VMEM((own_rows, d), BF16),
+        ]
+        + prefix_scratch(grid, channels)[:3]
+        + [
+            chain_sems(cube, 3),
+            chain_sems(cube),
+            chain_sems(cube),
+            turn_sems(grid, feed.shape[0]),
+            chain_sems(1),
+        ]
+        + prefix_scratch(grid, channels)[3:]
+        + [pltpu.SemaphoreType.DMA((2, 1)), pltpu.SemaphoreType.DMA],
+        compiler_params=pltpu.CompilerParams(
+            collective_id=6, has_side_effects=True, vmem_limit_bytes=GRANT
+        ),
+        name="gather_recurrence",
+    )(x, halo, flags, *rec, *gates, thin, feed, cot)
+
+
 def leave_kernel(
     n, tensor, seqs, branch, w_out, gelu_pre, local, cum, inlet_pre, forget_pre, conv, ext, entered,
     w_inlet, w_forget, lanes, flags, feed_part, resid,
@@ -1019,12 +1327,12 @@
 
 
 def leave_recurrence(
-    grid, branch, rec, gelu_pre, local, cum, inlet_pre, forget_pre, conv, ext, entered, inlet, forget, lanes,
+    grid, branch, rec, gelu_pre, local, cum, inlet_pre, forget_pre, conv, ext, entered, gates, lanes,
     flags, feed_part, resid, seqs,
 ):
     every, channels = conv.shape
     d = branch.shape[1]
-    heads, width = inlet.shape[:2]
+    heads, width = gates.shape[0] // 2, gates.shape[1]
     near = pl.BlockSpec(memory_space=pltpu.VMEM)
     low = jax.ShapeDtypeStruct((every, channels), BF16)
     return pl.pallas_call(
@@ -1038,7 +1346,10 @@
             jax.ShapeDtypeStruct((8, d), F32),
             jax.ShapeDtypeStruct(resid.shape, BF16),
         ],
-        in_specs=[near, pl.BlockSpec((1, d, channels), lambda i: (2, 0, 0))] + [near] * 14,
+        in_specs=[near, pl.BlockSpec((1, d, channels), lambda i: (2, 0, 0))]
+        + [near] * 8
+        + [pl.BlockSpec((heads, width, width), lambda i, m=m: (m, 0, 0)) for m in range(2)]
+        + [near] * 4,
         out_specs=[near] * 6,
         scratch_shapes=[
             pltpu.VMEM((every, channels), F32),
@@ -1057,7 +1368,7 @@
         ),
         name="leave_recurrence",
     )(
-        branch, rec, gelu_pre, local, cum, inlet_pre, forget_pre, conv, ext, entered, inlet, forget,
+        branch, rec, gelu_pre, local, cum, inlet_pre, forget_pre, conv, ext, entered, gates, gates,
         lanes, flags, feed_part, resid,
     )
 
@@ -1869,50 +2180,75 @@
     thin_count = thin_own.shape[0]
     thin_own = jnp.pad(thin_own, ((0, -thin_count % 16), (0, 0)))
     cot_rows = cotangent.reshape(grid.tensor, rows_half, width)
-    rec_all, gates_all, thin_all, feed_all, cot_all = place_own(
-        grid,
+    rec_own = (
+        input_weight.transpose(1, 0, 2),
+        gelu_weight.transpose(1, 0, 2),
+        out_weight.transpose(0, 2, 1),
+    )
+    feed_own = (mlp_gate, mlp_up, mlp_down.T)
+    gates_own = (inlet_weight, forget_weight)
+    x = block_in.reshape(rows_all, width)
+
+    if d_own % STEP == 0 and lane_own % STEP == 0:
+        feed_all, cot_all = place_feed(grid, feed_own, cot_rows)
         (
-            input_weight.transpose(1, 0, 2),
-            gelu_weight.transpose(1, 0, 2),
-            out_weight.transpose(0, 2, 1),
-        ),
-        (mlp_gate, mlp_up, mlp_down.T),
-        (inlet_weight, forget_weight),
-        thin_own,
-        cot_rows,
-    )
-    rec_all, gates_all, thin_all, cot_all = bring_weights(
-        grid, rec_all, gates_all, thin_all, cot_all
-    )
-    rec_all = rec_all.reshape(3, width, channels)
-    gates_all = gates_all.reshape(2, head_count, block_size, block_size)
-    inlet_full, forget_full = gates_all[0], gates_all[1]
-    table = jnp.sum(thin_all.astype(F32), axis=0)
-    lane_rows = table[: CONV + 6]
-    gain_first, out_shift, gain_second = table[CONV + 6 : thin_count].reshape(3, width)
-    rate = lane_rows[CONV + 5]
-    lanes = jnp.concatenate([lane_rows[: CONV + 5], jnp.stack([jax.nn.softplus(rate), jax.nn.sigmoid(rate)])])
-    lanes = jnp.pad(lanes, ((0, LANE_ROWS - lanes.shape[0]), (0, 0)))
-
-    x = block_in.reshape(rows_all, width)
-    (
-        normed,
-        ext,
-        conv,
-        gelu_pre,
-        inlet_pre,
-        forget_pre,
-        cum,
-        local_state,
-        entered,
-        mixed,
-        resid,
-        second_own,
-        feed_all,
-    ) = forward_recurrence(
-        grid, x, halo, gain_first[None], rec_all, inlet_full, forget_full, lanes, flags, out_shift[None],
-        gain_second[None], feed_all, seq_count,
-    )
+            normed,
+            ext,
+            conv,
+            gelu_pre,
+            inlet_pre,
+            forget_pre,
+            cum,
+            local_state,
+            entered,
+            mixed,
+            resid,
+            second_own,
+            lanes,
+            table,
+            gates_all,
+            rec_all,
+            feed_all,
+            cot_all,
+        ) = gather_recurrence(
+            grid, x, halo, flags, rec_own, gates_own, thin_own, CONV + 6, feed_all, cot_all, seq_count
+        )
+        rec_all = rec_all.reshape(3, width, channels)
+        gain_first, _, gain_second = table[CONV + 6 : thin_count].reshape(3, width)
+    else:
+        rec_all, gates_all, thin_all, feed_all, cot_all = place_own(
+            grid, rec_own, feed_own, gates_own, thin_own, cot_rows
+        )
+        rec_all, gates_all, thin_all, cot_all = bring_weights(
+            grid, rec_all, gates_all, thin_all, cot_all
+        )
+        rec_all = rec_all.reshape(3, width, channels)
+        gates_all = gates_all.reshape(2 * head_count, block_size, block_size)
+        table = jnp.sum(thin_all.astype(F32), axis=0)
+        gain_first, out_shift, gain_second = table[CONV + 6 : thin_count].reshape(3, width)
+        rate = table[CONV + 5]
+        lanes = jnp.concatenate(
+            [table[: CONV + 5], jnp.stack([jax.nn.softplus(rate), jax.nn.sigmoid(rate)])]
+        )
+        lanes = jnp.pad(lanes, ((0, LANE_ROWS - lanes.shape[0]), (0, 0)))
+        (
+            normed,
+            ext,
+            conv,
+            gelu_pre,
+            inlet_pre,
+            forget_pre,
+            cum,
+            local_state,
+            entered,
+            mixed,
+            resid,
+            second_own,
+            feed_all,
+        ) = forward_recurrence(
+            grid, x, halo, gain_first[None], rec_all, gates_all[:head_count], gates_all[head_count:],
+            lanes, flags, out_shift[None], gain_second[None], feed_all, seq_count,
+        )
 
     rows_feed = grid.hi * rows_all
     second_all, gate_low, up_low, hidden, branch_low, gain_two_grad, feed_part = feed_forward(
@@ -1925,7 +2261,7 @@
 
     gelu_low, input_low, gate_w_grads, lane_grads, out_shift_grad, own_out = leave_recurrence(
         grid, branch_low, rec_all, gelu_pre, local_state, cum, inlet_pre, forget_pre, conv, ext, entered,
-        inlet_full, forget_full, lanes, flags, feed_part, resid, seq_count,
+        gates_all, lanes, flags, feed_part, resid, seq_count,
     )
     out_shift_grad = jnp.sum(out_shift_grad, axis=0)
     gate_w_grads = (

time: 783 us -> 761 us (0.972)
  Pallas kernels: 736 us -> 717 us
    pallas_call x3 -> x2, Pallas kernels: 270 us -> 247 us  [the longest x1 241 us: gather_recurrence(): pl.pallas_call(functools.partial(gather_kernel, n, grid.tensor, seqs, thi...]
  transfers between devices with their start and end apart: 3 -> 3, of which waited for: 0 -> 1; matrix products, arithmetic and copies ran while one was open for 2% -> 2% of each run, Pallas kernels for 20% -> 1%
where the time goes in v6:
time: 761 us; the launch traced here: 758 us
  Pallas kernels  717 us (94%)
  local copies, waits for them, and re-layouts  23.8 us (3%)
  other arithmetic  13.3 us (2%)
    pallas_call x1, Pallas kernels, gather_recurrence(): pl.pallas_call(functools.partial(gather_kernel, n, grid.tensor, seqs, thi...  241 us
    pallas_call x1, Pallas kernels, send_grads(): pl.pallas_call(functools.partial(grads_kernel, grid.n, grid.tensor, spans...  234 us
    pallas_call x1, Pallas kernels, feed_forward(): pl.pallas_call(functools.partial(feed_kernel, grid.n, tensor, unit_tiles)...  157 us
    pallas_call x1, Pallas kernels, leave_recurrence(): pl.pallas_call(functools.partial(leave_kernel, grid.n, grid.tensor, seqs)...  69.6 us
  transfers between devices with their start and end apart: 3, of which 1 were waited for; matrix products, arithmetic and copies ran while one was open for 2% of the time, Pallas kernels for 1%

profile of v6, /device:TPU:27, one launch (start us, length us, event | category | flops | bytes accessed | tf_op | source)
XLA Modules:
  0.0 757.7 jit_solution(12549639838899797950)
XLA Ops:
  0.7 0.7 add_convert_fusion
  1.3 0.1 slice.106
  1.4 1.8 collective-permute-start.1
  3.2 0.9 slice.105
  4.1 0.0 collective-permute-start
  4.1 1.7 multiply_reduce_fusion
  5.8 0.7 copy.68
  6.5 0.7 copy.69
  7.2 0.7 copy.70
  7.8 0.7 copy.71
  8.5 0.7 copy.72
  9.2 0.7 copy.73
  9.9 0.8 concatenate.14
  10.7 1.6 dynamic_update_slice.6
  12.3 0.7 stack.77
  13.0 0.7 stack.78
  13.7 0.7 stack.79
  14.3 0.3 dynamic_update_slice.7
  14.7 0.6 pad_maximum_fusion.thin_in
  15.3 0.6 pad_add_fusion.1.spot
  15.9 6.3 place.1
  22.2 0.0 collective-permute-done.1
  22.2 0.1 not_bitcast_fusion
  22.3 0.2 copy.67
  22.5 0.7 pad_convert_fusion.flags
  23.2 0.0 collective-permute-done
  23.2 0.6 select_bitcast_fusion.halo
  23.9 240.8 %gather_recurrence.1 = (bf16[256,2560]{1,0:T(8,128)(2,1)}, bf16[2,136,1280]{2,1,0:T(8,128)(2,1)}, bf16[256,1280]{1,0:T(8,128)(2,1)}, f32[256,1280]{1,0:T(8,128)}...) custom-call(bf16[256,2560]{1,0:T(8,128)(2,1)} %bitcast.114, ...), custom_call_target="tpu_custom_call", output_to_operand_aliasing={{16}: (9, {}), {17}: (10, {})} | custom-call | tf_op jit(solution)/shard_map/gather_recurrence/pallas_call | solution.py:1132
  264.7 0.9 fusion.8
  265.5 0.6 copy.83
  266.1 156.9 %feed_forward.1 = (bf16[4,2,128,2560]{3,2,1,0:T(8,128)(2,1)}, bf16[4,256,1024]{2,1,0:T(8,128)(2,1)}, bf16[4,256,1024]{2,1,0:T(8,128)(2,1)}, bf16[4,256,1024]{2,1...) custom-call(bf16[128,2560]{1,0:T(8,128)(2,1)} %get-tuple-element.62.own, ...), custom_call_target="tpu_custom_call" | custom-call | tf_op jit(solution)/shard_map/feed_forward/pallas_call | solution.py:1671
  423.1 69.6 %leave_recurrence.1 = (bf16[256,1280]{1,0:T(8,128)(2,1)}, bf16[256,1280]{1,0:T(8,128)(2,1)}, bf16[2,5,256,256]{3,2,1,0:T(8,128)(2,1)}, f32[16,1280]{1,0:T(8,128)...) custom-call(bf16[256,2560]{1,0:T(8,128)(2,1)} %bitcast.116, bf16[3,2560,1280]{2,1,0:T(8,128)(2,1)} %bitcast.110, ...), custom_call_target="tpu_custom_call" | custom-call | tf_op jit(solution)/shard_map/leave_recurrence/pallas_call | solution.py:1338
  492.7 0.8 broadcast_in_dim.22.scale
  493.4 9.9 %first_gradient.1 = (bf16[256,2560]{1,0:T(8,128)(2,1)}, f32[8,2560]{1,0:T(8,128)}) custom-call(bf16[256,2560]{1,0:T(8,128)(2,1)} %bitcast.115, bf16[256,1280]{1,0:T(8,128)(2,1)} %get-tuple-element.86.input_low, bf16[256,1280]{1,0:T(8,128)(2,1)} %get-tuple-element.85.gelu_low, bf16[3,2560,1280]{2,1,0:T(8,128)(2,1)} %bitcast.111, ...), custom_call_target="tpu_custom_call" | custom-call | tf_op jit(solution)/shard_map/first_gradient/pallas_call | solution.py:577
  503.4 1.0 reduce_sum.44
  504.4 0.0 copy-done.8
  504.5 0.2 collective-permute-start.2
  504.7 0.0 copy-done.9
  504.7 0.2 reshape.165
  504.9 0.2 copy.89
  505.1 0.2 reshape.166
  505.3 0.0 copy-done.7
  505.3 0.1 reshape.164
  505.4 1.2 copy.75
  506.6 0.6 collective-permute-done.2
  507.2 0.1 slice_reduce_fusion
  507.3 0.1 reshape_squeeze.7
  507.4 0.1 reshape_squeeze.8
  507.4 0.1 concatenate.16
  507.6 0.8 reshape.167.thin
  508.3 233.5 %send_grads.1 = (bf16[3,160,3840]{2,1,0:T(8,128)(2,1)}, f32[16,160,256]{2,1,0:T(8,128)}, bf16[256,2560]{1,0:T(8,128)(2,1)}, bf16[2,128,2560]{2,1,0:T(8,128)(2,1)}, f32[8,160]{1,0:T(8,128)}) custom-call(bf16[1024,2560]{1,0:T(8,128)(2,1)} %bitcast.119, bf16[1024,2560]{1,0:T(8,128)(2,1)} %bitcast.113, bf16[256,2560]{1,0:T(8,128)(2,1)} %get-tuple-element.68.normed, ...), custom_call_target="tpu_custom_call" | custom-call | tf_op jit(solution)/shard_map/send_grads/pallas_call | solution.py:2066
  741.9 3.3 slice_bitcast_fusion
  745.2 1.6 fusion.7
  746.8 0.6 fusion.9
  747.4 3.7 convert_bitcast_fusion
  751.1 0.0 copy-done
  751.1 0.8 copy-done.3
  751.9 0.7 fusion
  752.6 2.7 fusion.1
  755.3 0.1 reshape.169
  755.3 0.6 slice_bitcast_fusion.4
  756.0 0.1 slice.121
  756.0 0.6 copy.77
  756.7 1.1 copy.95
  (39 shorter events, 0.3 us)
Async XLA Ops:
  1.4 20.8 %collective-permute-start.1 = (bf16[2,3]{1,0:T(2,128)(2,1)S(1)}, bf16[2,3]{1,0:T(2,128)(2,1)S(1)}, u32[]{:S(2)}, u32[]{:S(2)}) collective-permute-start(bf16[2,3]{1,0:T(2,128)(2,1)S(1)} %slice.106), channel_id=1, source_target_pairs={{0,2},{2,4},{4,6},{6,8},{8,10},{10,12},{12,14},{14,16},{16,18},{18... | collective-permute-start | bytes 44 | tf_op jit(solution)/shard_map/ppermute | solution.py:44
  4.1 19.1 %collective-permute-start = (bf16[2,8,2560]{2,1,0:T(8,128)(2,1)S(1)}, bf16[2,8,2560]{2,1,0:T(8,128)(2,1)S(1)}, u32[]{:S(2)}, u32[]{:S(2)}) collective-permute-start(bf16[2,8,2560]{2,1,0:T(8,128)(2,1)S(1)} %slice.105), channel_id=1, source_target_pairs={{0,2},{2,4},{4,6},{6,8},{8,10},{10,12},{12,14},{14,16},{16,18},{18... | collective-permute-start | bytes 245768 | tf_op jit(solution)/shard_map/ppermute | solution.py:44
  493.4 11.0 %copy-start.8 = (f32[8,2560]{1,0:T(8,128)S(1)}, f32[8,2560]{1,0:T(8,128)}, u32[]{:S(2)}) copy-start(f32[8,2560]{1,0:T(8,128)} %get-tuple-element.92) | copy-start | bytes 245764
  493.4 11.3 %copy-start.9 = (f32[16,1280]{1,0:T(8,128)S(1)}, f32[16,1280]{1,0:T(8,128)}, u32[]{:S(2)}) copy-start(f32[16,1280]{1,0:T(8,128)} %get-tuple-element.94) | copy-start | bytes 245764
  503.4 1.9 copy-start.7
  503.4 2.0 copy-start.6
  504.5 2.7 collective-permute-start.2
  741.8 4.9 copy-start.10
  741.8 5.5 copy-start.4
  747.3 3.8 copy-start
  747.3 3.8 copy-start.2
  747.3 4.5 copy-start.3
  751.1 1.5 copy-start.1
  752.6 4.1 copy-start.5

commit v7 on v6

--- a/solution.py
+++ b/solution.py
@@ -552,37 +552,6 @@
 
     start = (jnp.ones((8, width), F32), jnp.zeros((8, width), F32))
     lax.fori_loop(0, tiles, one, (start,) * seqs)
-
-
-def first_kernel(x, input_low, gelu_low, w_input, w_gelu, scale, part, gained):
-    value = dot_nt(input_low[...], w_input[0]) + dot_nt(gelu_low[...], w_gelu[0])
-    part[...] = value.astype(BF16)
-    gained[...] = jnp.sum(
-        (value * x[...].astype(F32) * scale[:, 0:1]).reshape(-1, 8, value.shape[1]), axis=0
-    )
-
-
-def first_gradient(x, input_low, gelu_low, rec, scale):
-    rows, d = x.shape
-    channels = input_low.shape[1]
-    chunk = 512
-
-    def fixed(a):
-        return pl.BlockSpec(a.shape, lambda i: (0, 0))
-
-    def weight(k):
-        return pl.BlockSpec((1, chunk, channels), lambda i: (k, i, 0))
-
-    column = pl.BlockSpec((rows, chunk), lambda i: (0, i))
-    return pl.pallas_call(
-        first_kernel,
-        grid=(d // chunk,),
-        out_shape=[jax.ShapeDtypeStruct((rows, d), BF16), jax.ShapeDtypeStruct((8, d), F32)],
-        in_specs=[column, fixed(input_low), fixed(gelu_low), weight(0), weight(1), fixed(scale)],
-        out_specs=[column, pl.BlockSpec((8, chunk), lambda i: (0, i))],
-        compiler_params=pltpu.CompilerParams(vmem_limit_bytes=GRANT),
-        name="first_gradient",
-    )(x, input_low, gelu_low, rec, rec, scale)
 
 
 class Prefix:
@@ -901,8 +870,9 @@
 def gather_kernel(
     n, tensor, seqs, thin_lanes,
     x, halo, flags, wide_in, gelu_in, out_in, inlet_in, forget_in, thin_in, feed, cot,
-    normed, ext, conv, gelu_pre, inlet_pre, forget_pre, cum, local, entered, mixed, resid, second,
-    lanes, table, gates_out, rec_out, feed_all, cot_all,
+    entered, mixed, resid, second, lanes, table, gates_out,
+    normed_out, ext_out, conv_out, gelu_out, inlet_out, forget_out, cum_out, local_out, rec_out, feed_all, cot_all,
+    normed, ext, conv, gelu_pre, inlet_pre, forget_pre, cum, local, out_sems,
     rec, gates, thin, held, factor, addend, part, out, got, tots, gots, line,
     rec_sems, gates_sems, thin_sems, feed_sems, cot_sems, cube_sems, line_sems, swap_sems, own_sem,
 ):
@@ -1040,6 +1010,23 @@
     for s in range(seqs):
         tots[0, s : s + 1, :] = cum[(s + 1) * length - 8 : (s + 1) * length, :][7:8]
         tots[0, seqs + s : seqs + s + 1, :] = local[(s + 1) * length - 8 : (s + 1) * length, :][7:8]
+    outs = [
+        pltpu.make_async_copy(held_here, to, out_sems.at[i])
+        for i, (held_here, to) in enumerate(
+            (
+                (normed, normed_out),
+                (ext, ext_out),
+                (conv, conv_out),
+                (gelu_pre, gelu_out),
+                (inlet_pre, inlet_out),
+                (forget_pre, forget_out),
+                (cum, cum_out),
+                (local, local_out),
+            )
+        )
+    ]
+    for copy in outs:
+        copy.start()
     enter = Prefix(spot, seqs, False, tots, gots, line, cube_sems, line_sems).run()
     turns.start(3)
     turns.onward(1)
@@ -1094,6 +1081,8 @@
     turns.finish()
     cots.finish()
     keep.wait()
+    for copy in outs:
+        copy.wait()
 
 
 def gather_recurrence(grid, x, halo, flags, rec, gates, thin, thin_lanes, feed, cot, seqs):
@@ -1109,15 +1098,12 @@
     wide = jax.ShapeDtypeStruct((rows, channels), F32)
     whole = (3, n, d_own, channels)
     cube = grid.inner_size.bit_length() - 1
-    outs = [
+    saved = [
         jax.ShapeDtypeStruct((rows, d), BF16),
         jax.ShapeDtypeStruct((seqs, longer, channels), BF16),
         jax.ShapeDtypeStruct((rows, channels), BF16),
-        wide,
-        wide,
-        wide,
-        wide,
-        wide,
+    ] + [wide] * 5
+    outs = [
         jax.ShapeDtypeStruct((8, channels), F32),
         jax.ShapeDtypeStruct((rows, channels), BF16),
         jax.ShapeDtypeStruct((own_rows, d), F32),
@@ -1125,17 +1111,21 @@
         jax.ShapeDtypeStruct((LANE_ROWS, channels), F32),
         jax.ShapeDtypeStruct(thin.shape, F32),
         jax.ShapeDtypeStruct((2 * heads, width, width), BF16),
+    ]
+    moved = [
         jax.ShapeDtypeStruct(whole, BF16),
         jax.ShapeDtypeStruct(feed.shape, BF16),
         jax.ShapeDtypeStruct(cot.shape, BF16),
     ]
     return pl.pallas_call(
         functools.partial(gather_kernel, n, grid.tensor, seqs, thin_lanes),
-        out_shape=outs,
+        out_shape=outs + saved + moved,
         in_specs=[near] * 9 + [far] * 2,
-        out_specs=[near] * 15 + [far] * 3,
+        out_specs=[near] * len(outs) + [far] * (len(saved) + len(moved)),
         input_output_aliases={9: 16, 10: 17},
-        scratch_shapes=[
+        scratch_shapes=[pltpu.VMEM(a.shape, a.dtype) for a in saved]
+        + [pltpu.SemaphoreType.DMA((len(saved),))]
+        + [
             pltpu.VMEM(whole, BF16),
             pltpu.VMEM((2 * heads, n, lane_own, width), BF16),
             pltpu.VMEM((n,) + thin.shape, BF16),
@@ -1508,7 +1498,8 @@
 
 def feed_kernel(
     n, tensor, unit_tiles, own, w_gate, w_up, w_down, cot, resid, gain,
-    whole, gate_low, up_low, hidden, both, gain_grad, feed_part,
+    whole_out, gate_out, up_out, hidden_out, feed_out, both, gain_grad,
+    whole, gate_low, up_low, hidden, feed_part, out_sems,
     part, got, line, mine, other, sems, cross_sems, line_sems, swap_sems,
 ):
     spot = Spot(n, tensor)
@@ -1585,6 +1576,20 @@
     for k in range(hi):
         for each in sums:
             each.start(k)
+    outs = [
+        pltpu.make_async_copy(held, to, out_sems.at[i])
+        for i, (held, to) in enumerate(
+            (
+                (gate_low, gate_out),
+                (up_low, up_out),
+                (hidden, hidden_out),
+                (whole, whole_out),
+                (feed_part, feed_out),
+            )
+        )
+    ]
+    for copy in outs[:3]:
+        copy.start()
 
     def give(i, none):
         place, j = i // (d // chunk), lax.rem(i, d // chunk)
@@ -1597,6 +1602,8 @@
     lax.fori_loop(0, hi * (d // chunk), give, 0)
     for chain in chains:
         chain.finish_sends()
+    for copy in outs[3:]:
+        copy.start()
 
     def done(at, total):
         value = resid[at, :]
@@ -1621,6 +1628,8 @@
     for each in sums:
         each.finish()
     share(spot, swaps, mine, other, both)
+    for copy in outs:
+        copy.wait()
 
 
 def share(spot, copies, mine, other, both):
@@ -1676,13 +1685,14 @@
             low,
             low,
             low,
+            whole,
             jax.ShapeDtypeStruct((tensor, rows, d), BF16),
             jax.ShapeDtypeStruct((8, d), F32),
-            whole,
         ],
         in_specs=[near] + [weight(k) for k in range(3)] + [near] * 3,
-        out_specs=[near] * 7,
-        scratch_shapes=[pltpu.VMEM(whole.shape, BF16)]
+        out_specs=[pl.BlockSpec(memory_space=pl.ANY)] * 5 + [near] * 2,
+        scratch_shapes=[pltpu.VMEM(a.shape, BF16) for a in (whole, low, low, low, whole)]
+        + [pltpu.SemaphoreType.DMA((5,)), pltpu.VMEM(whole.shape, BF16)]
         + rows_scratch(grid, rows, d)
         + [chain_sems(1, HALVES)]
         + rows_sems(grid),
@@ -1711,15 +1721,16 @@
 def grads_kernel(
     n, tensor, spans, kept,
     unit_tiles,
-    second, cot, normed, branch, gate_low, up_low, hidden, gelu_low, input_low, mixed, gates, first, own_out, thin,
-    apart, summed, first_other, block_out, thin_own, *refs,
+    second, cot, normed, branch, gate_low, up_low, hidden, gelu_low, input_low, mixed, gates,
+    w_input, w_gelu, x, scale, own_out, thin,
+    gate_rows, up_rows, down_rows, summed, first_grad, block_out, thin_own, *refs,
 ):
     stages = (n // LINE).bit_length() - 1
     lists = [refs[i * stages : (i + 1) * stages] for i in range(6)]
     sends, keeps, gots, thin_sends, thin_keeps, thin_gots = lists
     (
-        made, ready, got_line, first_out, first_got, thin_ready, thin_line,
-        cube_sems, line_sems, first_sems, thin_sems, thin_line_sems,
+        made, ready, got_line, first_out, first_got, thin_ready, thin_line, gained, thin_all, thin_send, thin_got,
+        cube_sems, line_sems, first_sems, thin_sems, thin_line_sems, gain_sems,
     ) = refs[6 * stages :]
     spot = Spot(n, tensor)
     hi = spot.hi
@@ -1730,7 +1741,9 @@
     width = ready.shape[2]
     each = tile_rows(rows)
     last_step = units + stages - 1
-    first_rows, out_rows = first.shape[0], own_out.shape[0]
+    first_rows, out_rows = first_grad.shape[0], own_out.shape[0]
+    chunk = w_input.shape[1]
+    begin_thin = first_grad.shape[1] // chunk
 
     def place_of(unit):
         return place_at(lax.rem(unit, hi), hi)
@@ -1793,7 +1806,8 @@
                     skip = place * tiles - min(place * tiles, unit_tiles - tiles)
                     if skip < tiles:
                         value = got_line[span, place, at, skip * LANE :]
-                        apart[span, at, place * width : (place + 1) * width - skip * LANE] = value
+                        cols = slice(place * width, (place + 1) * width - skip * LANE)
+                        (gate_rows, up_rows, down_rows)[span][at, cols] = value
             else:
                 value = got_line[span, 0, at, :].astype(F32)
                 for place in range(1, hi):
@@ -1826,27 +1840,41 @@
     def _():
         spot.greet(*[spot.flip(bit) for bit in spot.bits], spot.cross)
 
-        def put(at):
-            first_out[at, :] = first[at, :]
-
-        by_rows(first_rows, STEP, put)
-
         def put_out(at):
             to = pl.ds(pl.multiple_of(first_rows + at.start, STEP), STEP)
             first_out[to, :] = own_out[at, :]
 
         by_rows(out_rows, STEP, put_out)
+
+    @pl.when(step < begin_thin)
+    def _():
+        cols = pl.ds(pl.multiple_of(step * chunk, chunk), chunk)
+        value = dot_nt(input_low[...], w_input[0]) + dot_nt(gelu_low[...], w_gelu[0])
+        first_out[0:first_rows, cols] = value.astype(BF16)
+        gained[:, cols] = jnp.sum(
+            (value * x[...].astype(F32) * scale[:, 0:1]).reshape(-1, 8, chunk), axis=0
+        )
+
+    @pl.when(step == begin_thin)
+    def _():
         first_copy.start()
+        gain = jnp.sum(gained[...], axis=0, keepdims=True)
+        size = thin.shape[3]
+        for place in range(hi):
+            for inner in range(spot.inner_size):
+                at = (place * spot.inner_size + inner) * size
+                thin_all[place, inner] = thin[place, inner]
+                thin_all[place, inner, 0:1, :] = gain[:, at : at + size]
         mine = spot.bit(1)
         for place in range(hi):
             for k in range(thin_sends[0].shape[1]):
-                thin_sends[0][place, k] = thin[place, 2 * k + 1 - mine]
-                thin_keeps[0][place, k] = thin[place, 2 * k + mine]
+                thin_sends[0][place, k] = thin_all[place, 2 * k + 1 - mine]
+                thin_keeps[0][place, k] = thin_all[place, 2 * k + mine]
         thin_copy(0).start()
 
     for stage in range(stages):
 
-        @pl.when(step == stage + 1)
+        @pl.when(step == begin_thin + stage + 1)
         def _(stage=stage):
             thin_copy(stage).wait_recv()
             if stage < stages - 1:
@@ -1989,11 +2017,13 @@
             thin_line_copy(place, place).wait_recv()
             thin_line_copy(place, spot.z).wait_send()
             value = value + thin_line[place]
-        thin_own[...] = value
+        thin_send[...] = value
+        copy = remote(thin_send, thin_got, gain_sems, 0, spot.cross)
+        copy.start()
         first_copy.wait()
 
         def take(at):
-            first_other[at, :] = first_got[at, :]
+            first_grad[at, :] = first_out[at, :].astype(F32) + first_got[at, :].astype(F32)
 
         by_rows(first_rows, STEP, take)
 
@@ -2003,6 +2033,10 @@
             block_out[1 - spot.t, at, :] = first_got[other, :]
 
         by_rows(out_rows, STEP, take_out)
+        copy.wait()
+        row = lax.broadcasted_iota(jnp.int32, thin_own.shape, 0)
+        part = jnp.logical_or(row == 0, row == 2)
+        thin_own[...] = thin_send[...] + jnp.where(part, thin_got[...], 0.0)
 
 
 def column_spans(widths, width):
@@ -2019,7 +2053,7 @@
     return spans
 
 
-def send_grads(grid, feed, rec, gates, first, own_out, thin, unit_tiles):
+def send_grads(grid, feed, rec, gates, weights, x, scale, own_out, thin, unit_tiles):
     hi, inner = grid.hi, grid.inner_size
     second, cot, gate_low, up_low, hidden = feed
     normed, branch, gelu_low, input_low, mixed = rec
@@ -2047,14 +2081,16 @@
         return pl.BlockSpec(a.shape, lambda i: zeros, pipeline_mode=pl.Buffered(1))
 
     block = gates.shape[1]
-    apart = jax.ShapeDtypeStruct((kept, rows, unit_tiles * LANE), BF16)
+    apart = [jax.ShapeDtypeStruct((rows, unit_tiles * LANE), BF16)] * kept
     summed = jax.ShapeDtypeStruct(((all_spans - kept) * (width // block), rows, block), F32)
     both = jax.ShapeDtypeStruct((grid.tensor,) + own_out.shape, BF16)
-    other = jax.ShapeDtypeStruct(first.shape, BF16)
+    first = jax.ShapeDtypeStruct(x.shape, F32)
+    chunk = 256
+    chunks = d // chunk
     thin = thin.reshape(hi, inner, 8, thin.shape[1] // 8)
     thin_shape = thin.shape[2:]
     thin_own = jax.ShapeDtypeStruct(thin_shape, F32)
-    outs = [apart, summed, other, both, thin_own]
+    outs = apart + [summed, first, both, thin_own]
     swapped = (first.shape[0] + own_out.shape[0], d)
 
     def halves(lead, tail, kind):
@@ -2070,7 +2106,12 @@
         in_specs=[slab_of(a) for a in (second, cot, normed, branch)]
         + [whole(a) for a in (gate_low, up_low, hidden, gelu_low, input_low, mixed)]
         + [pl.BlockSpec((1,) + gates.shape[1:], lambda i: (place_of(i), 0, 0))]
-        + [whole(first), whole(own_out), whole(thin)],
+        + [
+            pl.BlockSpec((1, chunk, channels), lambda i, m=m: (m, jnp.minimum(i, chunks - 1), 0))
+            for m in range(2)
+        ]
+        + [pl.BlockSpec((x.shape[0], chunk), lambda i: (0, jnp.minimum(i, chunks - 1)))]
+        + [whole(scale), whole(own_out), whole(thin)],
         out_specs=[whole(a) for a in outs],
         scratch_shapes=halves(RING, (rows, width), BF16)
         + halves(HELD, (rows, width), BF16)
@@ -2084,11 +2125,16 @@
             pltpu.VMEM(swapped, BF16),
             pltpu.VMEM((hi,) + thin_shape, F32),
             pltpu.VMEM((hi,) + thin_shape, F32),
+            pltpu.VMEM((8, d), F32),
+            pltpu.VMEM((hi, inner) + thin_shape, F32),
+            pltpu.VMEM(thin_shape, F32),
+            pltpu.VMEM(thin_shape, F32),
             pltpu.SemaphoreType.DMA((stages, 2, RING)),
             pltpu.SemaphoreType.DMA((2, units)),
             pltpu.SemaphoreType.DMA((2, 1)),
             pltpu.SemaphoreType.DMA((2, stages)),
             pltpu.SemaphoreType.DMA((2, hi)),
+            pltpu.SemaphoreType.DMA((2, 1)),
         ],
         compiler_params=pltpu.CompilerParams(
             collective_id=4, has_side_effects=True, vmem_limit_bytes=GRANT
@@ -2096,7 +2142,7 @@
         name="send_grads",
     )(
         second, cot, normed, branch, gate_low, up_low, hidden, gelu_low, input_low, mixed, gates,
-        first, own_out, thin,
+        weights, weights, x, scale, own_out, thin,
     )
 
 
@@ -2163,12 +2209,13 @@
     flags = jnp.stack([jnp.logical_not(earlier[0])] + earlier, axis=-1).astype(F32)
     flags = jnp.pad(flags.reshape(rows_all, CONV), ((0, 0), (0, 8 - CONV)))
 
-    per_lane = jnp.stack([gelu_bias, input_bias])
     per_lane = jnp.concatenate(
-        [per_lane, conv_weight, jnp.stack([conv_bias, inlet_bias, forget_bias, decay_rate])]
+        [gelu_bias, input_bias]
+        + [conv_weight[k] for k in range(CONV)]
+        + [conv_bias, inlet_bias, forget_bias, decay_rate]
     )
     lane_table = lax.dynamic_update_slice(
-        jnp.zeros((CONV + 6, head_count, block_size), BF16), per_lane, (0, 0, grid.w * lane_own)
+        jnp.zeros(((CONV + 6) * head_count, block_size), BF16), per_lane, (0, grid.w * lane_own)
     )
     per_width = jnp.stack([first_gain, out_bias, second_gain])
     width_table = lax.dynamic_update_slice(
@@ -2192,6 +2239,13 @@
     if d_own % STEP == 0 and lane_own % STEP == 0:
         feed_all, cot_all = place_feed(grid, feed_own, cot_rows)
         (
+            entered,
+            mixed,
+            resid,
+            second_own,
+            lanes,
+            table,
+            gates_all,
             normed,
             ext,
             conv,
@@ -2200,13 +2254,6 @@
             forget_pre,
             cum,
             local_state,
-            entered,
-            mixed,
-            resid,
-            second_own,
-            lanes,
-            table,
-            gates_all,
             rec_all,
             feed_all,
             cot_all,
@@ -2251,7 +2298,7 @@
         )
 
     rows_feed = grid.hi * rows_all
-    second_all, gate_low, up_low, hidden, branch_low, gain_two_grad, feed_part = feed_forward(
+    second_all, gate_low, up_low, hidden, feed_part, branch_low, gain_two_grad = feed_forward(
         grid, second_own, feed_all, cot_all, resid, gain_second[None], unit_tiles
     )
     second_all, cot_all = (v.reshape(rows_feed, width) for v in (second_all, cot_all))
@@ -2271,13 +2318,6 @@
     )
     inputs = x.astype(F32)
     scale_first = lax.rsqrt(jnp.mean(inputs * inputs, axis=-1, keepdims=True) + 1e-06)
-    first_part, gain_one_grad = first_gradient(
-        x, input_low, gelu_low, rec_all, jnp.broadcast_to(scale_first, (rows_all, 8))
-    )
-    gain_one_grad = jnp.sum(gain_one_grad, axis=0)
-    gain_grads = jnp.stack([gain_one_grad, gain_two_grad])
-    gain_grads = gain_grads + grid.swap(gain_grads)
-
     lane_grads = (
         lane_grads[: CONV + 6]
         .reshape(CONV + 6, head_count, grid.n, lane_own)
@@ -2285,29 +2325,30 @@
         .reshape(grid.n, -1)
     )
     thin_grads = jnp.concatenate(
-        [v.reshape(grid.n, d_own) for v in (gain_grads[0], out_shift_grad, gain_grads[1])]
+        [v.reshape(grid.n, d_own) for v in (jnp.zeros_like(gain_two_grad), out_shift_grad, gain_two_grad)]
         + [lane_grads],
         axis=1,
     )
-    feed_grads, rec_grads, first_other, block_out, thin = send_grads(
+    gate_grad, up_grad, down_grad, rec_grads, first_grad, block_out, thin = send_grads(
         grid,
         (second_all, cot_all, gate_low, up_low, hidden),
         (normed, branch_low, gelu_low, input_low, mixed),
         gate_w_grads,
-        first_part,
+        rec_all,
+        x,
+        jnp.broadcast_to(scale_first, (rows_all, 8)),
         own_out,
         thin_grads,
         unit_tiles,
     )
     block_out = block_out.reshape(block_in.shape)
     thin = thin.reshape(-1)
-    gate_grad, up_grad, down_grad = (feed_grads[m].astype(F32) for m in range(3))
-    down_grad = down_grad.T
+    gate_grad, up_grad = gate_grad.astype(F32), up_grad.astype(F32)
+    down_grad = down_grad.astype(F32).T
     gelu_w_grad = rec_grads[:head_count].transpose(1, 0, 2)
     input_w_grad = rec_grads[head_count : 2 * head_count].transpose(1, 0, 2)
     out_grad = rec_grads[2 * head_count : 3 * head_count].transpose(0, 2, 1)
     gate_w_grads = rec_grads[3 * head_count].reshape(2, head_count, lane_own, block_size)
-    first_grad = first_part.astype(F32) + first_other.astype(F32)
     _, pull_first = jax.vjp(rms_norm, inputs, gain_first)
     input_norm_grad, _ = pull_first(first_grad)
     block_grad = (branch_low.astype(F32) + input_norm_grad).reshape(block_in.shape)

time: 761 us -> 746 us (0.980)
  Pallas kernels: 717 us -> 698 us
    pallas_call x1 -> x0, Pallas kernels: 9.94 us -> none  [first_gradient(): pl.pallas_call(first_kernel, grid=(d // chunk,), out_shape=[jax.ShapeDtyp...]
    pallas_call x1, Pallas kernels: 157 us -> 149 us  [feed_forward(): pl.pallas_call(functools.partial(feed_kernel, grid.n, tensor, unit_tiles)...]
  transfers between devices with their start and end apart: 3 -> 2, of which waited for: 1 -> 0; matrix products, arithmetic and copies ran while one was open for 2% -> 2% of each run, Pallas kernels for 1% -> 1%
where the time goes in v7:
time: 746 us; the launch traced here: 740 us
  Pallas kernels  698 us (94%)
  local copies, waits for them, and re-layouts  23.7 us (3%)
  other arithmetic  15.5 us (2%)
    pallas_call x1, Pallas kernels, gather_recurrence(): pl.pallas_call(functools.partial(gather_kernel, n, grid.tensor, seqs, thi...  238 us
    pallas_call x1, Pallas kernels, send_grads(): pl.pallas_call(functools.partial(grads_kernel, grid.n, grid.tensor, spans...  234 us
    pallas_call x1, Pallas kernels, feed_forward(): pl.pallas_call(functools.partial(feed_kernel, grid.n, tensor, unit_tiles)...  149 us
    pallas_call x1, Pallas kernels, leave_recurrence(): pl.pallas_call(functools.partial(leave_kernel, grid.n, grid.tensor, seqs)...  71.5 us
  transfers between devices with their start and end apart: 2, of which 0 were waited for; matrix products, arithmetic and copies ran while one was open for 2% of the time, Pallas kernels for 1%

profile of v7, /device:TPU:27, one launch (start us, length us, event | category | flops | bytes accessed | tf_op | source)
XLA Modules:
  0.0 740.1 jit_solution(5519046269151125248)
XLA Ops:
  0.7 0.7 add_convert_fusion
  1.3 0.1 slice.103
  1.4 1.8 collective-permute-start.1
  3.2 0.9 slice.102
  4.1 0.0 collective-permute-start
  4.1 1.7 multiply_reduce_fusion
  5.8 0.9 fusion.9
  6.7 4.6 concatenate.14
  11.3 0.3 dynamic_update_slice.6
  11.7 0.7 stack.44
  12.4 0.7 stack.45
  13.0 0.7 stack.46
  13.7 0.3 dynamic_update_slice.7
  14.0 0.6 pad_maximum_fusion.thin_in
  14.7 0.6 pad_add_fusion.1.spot
  15.3 6.2 place.1
  21.5 0.0 collective-permute-done.1
  21.5 0.1 not_bitcast_fusion
  21.7 0.2 copy.80
  21.8 0.7 pad_convert_fusion.flags
  22.5 0.0 collective-permute-done
  22.5 0.6 select_bitcast_fusion.halo
  23.2 237.7 %gather_recurrence.1 = (f32[8,1280]{1,0:T(8,128)}, bf16[256,1280]{1,0:T(8,128)(2,1)}, f32[128,2560]{1,0:T(8,128)}, bf16[128,2560]{1,0:T(8,128)(2,1)}, f32[16,128...) custom-call(bf16[256,2560]{1,0:T(8,128)(2,1)} %bitcast.104, ...), custom_call_target="tpu_custom_call", output_to_operand_aliasing={{16}: (9, {}), {17}: (10, {})} | custom-call | tf_op jit(solution)/shard_map/gather_recurrence/pallas_call | solution.py:1120
  260.9 0.9 fusion.7
  261.8 0.6 copy.96
  262.4 149.3 %feed_forward.1 = (bf16[4,2,128,2560]{3,2,1,0:T(8,128)(2,1)}, bf16[4,256,1024]{2,1,0:T(8,128)(2,1)}, bf16[4,256,1024]{2,1,0:T(8,128)(2,1)}, bf16[4,256,1024]{2,1...) custom-call(bf16[128,2560]{1,0:T(8,128)(2,1)} %get-tuple-element.62.own, ...), custom_call_target="tpu_custom_call" | custom-call | tf_op jit(solution)/shard_map/feed_forward/pallas_call | solution.py:1680
  411.7 71.5 %leave_recurrence.1 = (bf16[256,1280]{1,0:T(8,128)(2,1)}, bf16[256,1280]{1,0:T(8,128)(2,1)}, bf16[2,5,256,256]{3,2,1,0:T(8,128)(2,1)}, f32[16,1280]{1,0:T(8,128)...) custom-call(bf16[256,2560]{1,0:T(8,128)(2,1)} %bitcast.106, bf16[3,2560,1280]{2,1,0:T(8,128)(2,1)} %bitcast.100, ...), custom_call_target="tpu_custom_call" | custom-call | tf_op jit(solution)/shard_map/leave_recurrence/pallas_call | solution.py:1328
  483.1 0.0 copy-start.8
  483.1 0.0 copy-start.4
  483.1 1.2 reshape.167
  484.3 0.2 copy.106
  484.5 0.2 reshape.168
  484.7 0.9 reduce_sum.36
  485.6 0.1 reshape.165
  485.7 0.0 copy-done.8
  485.7 0.1 reshape.166
  485.8 0.1 concatenate.16
  485.9 0.8 reshape.169.thin
  486.7 0.0 copy-done.4
  486.7 1.2 copy.85
  487.9 0.8 broadcast_in_dim.22.scale
  488.6 233.6 %send_grads.1 = (bf16[160,3840]{1,0:T(8,128)(2,1)}, bf16[160,3840]{1,0:T(8,128)(2,1)}, bf16[160,3840]{1,0:T(8,128)(2,1)}, f32[16,160,256]{2,1,0:T(8,128)}, f32[2...) custom-call(bf16[1024,2560]{1,0:T(8,128)(2,1)} %bitcast.108, bf16[1024,2560]{1,0:T(8,128)(2,1)} %bitcast.103, ...), custom_call_target="tpu_custom_call" | custom-call | tf_op jit(solution)/shard_map/send_grads/pallas_call | solution.py:2102
  722.2 0.0 copy-start.9
  722.2 0.0 copy-start
  722.2 3.3 slice_bitcast_fusion
  725.5 1.7 fusion.6
  727.2 0.0 copy-done.9
  727.2 0.6 fusion.8
  727.8 0.0 copy-start.2
  727.8 0.0 copy-done
  727.8 2.3 fusion
  730.1 0.0 copy-done.1
  730.1 0.2 copy-done.2
  730.3 2.4 fusion.1
  732.7 0.0 copy-done.7
  732.7 1.6 convert_bitcast_fusion
  734.3 0.2 copy-done.6
  734.5 1.6 convert_element_type.27
  736.1 1.6 convert_element_type.28
  737.7 0.1 reshape.171
  737.8 0.6 slice_bitcast_fusion.4
  738.4 0.1 slice.120
  738.5 0.6 copy.87
  739.1 1.1 copy.112
  (25 shorter events, 0.2 us)
Async XLA Ops:
  1.4 20.1 %collective-permute-start.1 = (bf16[2,3]{1,0:T(2,128)(2,1)S(1)}, bf16[2,3]{1,0:T(2,128)(2,1)S(1)}, u32[]{:S(2)}, u32[]{:S(2)}) collective-permute-start(bf16[2,3]{1,0:T(2,128)(2,1)S(1)} %slice.103), channel_id=1, source_target_pairs={{0,2},{2,4},{4,6},{6,8},{8,10},{10,12},{12,14},{14,16},{16,18},{18... | collective-permute-start | bytes 44 | tf_op jit(solution)/shard_map/ppermute | solution.py:44
  4.1 18.4 %collective-permute-start = (bf16[2,8,2560]{2,1,0:T(8,128)(2,1)S(1)}, bf16[2,8,2560]{2,1,0:T(8,128)(2,1)S(1)}, u32[]{:S(2)}, u32[]{:S(2)}) collective-permute-start(bf16[2,8,2560]{2,1,0:T(8,128)(2,1)S(1)} %slice.102), channel_id=1, source_target_pairs={{0,2},{2,4},{4,6},{6,8},{8,10},{10,12},{12,14},{14,16},{16,18},{18... | collective-permute-start | bytes 245768 | tf_op jit(solution)/shard_map/ppermute | solution.py:44
  483.1 2.6 copy-start.8
  483.1 3.5 copy-start.4
  722.2 5.0 copy-start.9
  722.2 5.6 copy-start
  725.5 4.7 copy-start.1
  727.8 2.5 copy-start.2
  730.3 2.4 copy-start.7
  732.7 1.8 copy-start.6
  734.3 1.8 copy-start.5
  736.1 3.0 copy-start.3

commit v8 on v7

--- a/solution.py
+++ b/solution.py
@@ -928,7 +928,6 @@
         chain.finish()
     turns.start(0)
     keep = pltpu.make_async_copy(rec, rec_out, own_sem)
-    keep.start()
 
     sums = thin[0].astype(F32)
     for i in range(1, n):
@@ -1025,13 +1024,13 @@
             )
         )
     ]
-    for copy in outs:
-        copy.start()
     enter = Prefix(spot, seqs, False, tots, gots, line, cube_sems, line_sems).run()
     turns.start(3)
     turns.onward(1)
     cots.onward(3)
     turns.start(2)
+    for copy in [keep] + outs:
+        copy.start()
     entered[...] = jnp.zeros_like(entered)
     entered[0:seqs, :] = enter
     for s in range(seqs):
@@ -1743,7 +1742,8 @@
     last_step = units + stages - 1
     first_rows, out_rows = first_grad.shape[0], own_out.shape[0]
     chunk = w_input.shape[1]
-    begin_thin = first_grad.shape[1] // chunk
+    begin_first = kept * hi
+    begin_thin = begin_first + first_grad.shape[1] // chunk
 
     def place_of(unit):
         return place_at(lax.rem(unit, hi), hi)
@@ -1846,9 +1846,9 @@
 
         by_rows(out_rows, STEP, put_out)
 
-    @pl.when(step < begin_thin)
+    @pl.when(jnp.logical_and(step >= begin_first, step < begin_thin))
     def _():
-        cols = pl.ds(pl.multiple_of(step * chunk, chunk), chunk)
+        cols = pl.ds(pl.multiple_of((step - begin_first) * chunk, chunk), chunk)
         value = dot_nt(input_low[...], w_input[0]) + dot_nt(gelu_low[...], w_gelu[0])
         first_out[0:first_rows, cols] = value.astype(BF16)
         gained[:, cols] = jnp.sum(
@@ -2087,6 +2087,10 @@
     first = jax.ShapeDtypeStruct(x.shape, F32)
     chunk = 256
     chunks = d // chunk
+
+    def chunk_of(i):
+        return jnp.clip(i - kept * hi, 0, chunks - 1)
+
     thin = thin.reshape(hi, inner, 8, thin.shape[1] // 8)
     thin_shape = thin.shape[2:]
     thin_own = jax.ShapeDtypeStruct(thin_shape, F32)
@@ -2107,10 +2111,10 @@
         + [whole(a) for a in (gate_low, up_low, hidden, gelu_low, input_low, mixed)]
         + [pl.BlockSpec((1,) + gates.shape[1:], lambda i: (place_of(i), 0, 0))]
         + [
-            pl.BlockSpec((1, chunk, channels), lambda i, m=m: (m, jnp.minimum(i, chunks - 1), 0))
+            pl.BlockSpec((1, chunk, channels), lambda i, m=m: (m, chunk_of(i), 0))
             for m in range(2)
         ]
-        + [pl.BlockSpec((x.shape[0], chunk), lambda i: (0, jnp.minimum(i, chunks - 1)))]
+        + [pl.BlockSpec((x.shape[0], chunk), lambda i: (0, chunk_of(i)))]
         + [whole(scale), whole(own_out), whole(thin)],
         out_specs=[whole(a) for a in outs],
         scratch_shapes=halves(RING, (rows, width), BF16)

time: 746 us -> 745 us (level)
  no operation moved by 1% of the time
where the time goes in v8:
time: 745 us; the launch traced here: 740 us
  Pallas kernels  698 us (94%)
  local copies, waits for them, and re-layouts  23.7 us (3%)
  other arithmetic  15.5 us (2%)
    pallas_call x1, Pallas kernels, gather_recurrence(): pl.pallas_call(functools.partial(gather_kernel, n, grid.tensor, seqs, thi...  238 us
    pallas_call x1, Pallas kernels, send_grads(): pl.pallas_call(functools.partial(grads_kernel, grid.n, grid.tensor, spans...  234 us
    pallas_call x1, Pallas kernels, feed_forward(): pl.pallas_call(functools.partial(feed_kernel, grid.n, tensor, unit_tiles)...  149 us
    pallas_call x1, Pallas kernels, leave_recurrence(): pl.pallas_call(functools.partial(leave_kernel, grid.n, grid.tensor, seqs)...  71.5 us
  transfers between devices with their start and end apart: 2, of which 0 were waited for; matrix products, arithmetic and copies ran while one was open for 2% of the time, Pallas kernels for 1%

profile of v8, /device:TPU:27, one launch (start us, length us, event | category | flops | bytes accessed | tf_op | source)
XLA Modules:
  0.0 740.3 jit_solution(12593513196395057956)
XLA Ops:
  0.7 0.7 add_convert_fusion
  1.3 0.1 slice.103
  1.4 1.8 collective-permute-start.1
  3.2 0.9 slice.102
  4.1 0.0 collective-permute-start
  4.1 1.7 multiply_reduce_fusion
  5.8 0.9 fusion.9
  6.7 4.6 concatenate.14
  11.3 0.3 dynamic_update_slice.6
  11.7 0.7 stack.44
  12.4 0.7 stack.45
  13.0 0.7 stack.46
  13.7 0.3 dynamic_update_slice.7
  14.0 0.6 pad_maximum_fusion.thin_in
  14.7 0.6 pad_add_fusion.1.spot
  15.3 6.2 place.1
  21.5 0.0 collective-permute-done.1
  21.5 0.1 not_bitcast_fusion
  21.7 0.2 copy.80
  21.8 0.7 pad_convert_fusion.flags
  22.5 0.0 collective-permute-done
  22.5 0.6 select_bitcast_fusion.halo
  23.2 237.7 %gather_recurrence.1 = (f32[8,1280]{1,0:T(8,128)}, bf16[256,1280]{1,0:T(8,128)(2,1)}, f32[128,2560]{1,0:T(8,128)}, bf16[128,2560]{1,0:T(8,128)(2,1)}, f32[16,128...) custom-call(bf16[256,2560]{1,0:T(8,128)(2,1)} %bitcast.104, ...), custom_call_target="tpu_custom_call", output_to_operand_aliasing={{16}: (9, {}), {17}: (10, {})} | custom-call | tf_op jit(solution)/shard_map/gather_recurrence/pallas_call | solution.py:1119
  260.9 0.9 fusion.7
  261.8 0.6 copy.96
  262.4 149.3 %feed_forward.1 = (bf16[4,2,128,2560]{3,2,1,0:T(8,128)(2,1)}, bf16[4,256,1024]{2,1,0:T(8,128)(2,1)}, bf16[4,256,1024]{2,1,0:T(8,128)(2,1)}, bf16[4,256,1024]{2,1...) custom-call(bf16[128,2560]{1,0:T(8,128)(2,1)} %get-tuple-element.62.own, ...), custom_call_target="tpu_custom_call" | custom-call | tf_op jit(solution)/shard_map/feed_forward/pallas_call | solution.py:1679
  411.7 71.5 %leave_recurrence.1 = (bf16[256,1280]{1,0:T(8,128)(2,1)}, bf16[256,1280]{1,0:T(8,128)(2,1)}, bf16[2,5,256,256]{3,2,1,0:T(8,128)(2,1)}, f32[16,1280]{1,0:T(8,128)...) custom-call(bf16[256,2560]{1,0:T(8,128)(2,1)} %bitcast.106, bf16[3,2560,1280]{2,1,0:T(8,128)(2,1)} %bitcast.100, ...), custom_call_target="tpu_custom_call" | custom-call | tf_op jit(solution)/shard_map/leave_recurrence/pallas_call | solution.py:1327
  483.1 0.0 copy-start.8
  483.1 0.0 copy-start.4
  483.1 1.2 reshape.167
  484.3 0.2 copy.106
  484.5 0.2 reshape.168
  484.7 0.9 reduce_sum.36
  485.6 0.1 reshape.165
  485.7 0.0 copy-done.8
  485.7 0.1 reshape.166
  485.8 0.1 concatenate.16
  485.9 0.8 reshape.169.thin
  486.7 0.0 copy-done.4
  486.7 1.2 copy.85
  487.9 0.8 broadcast_in_dim.22.scale
  488.6 233.7 %send_grads.1 = (bf16[160,3840]{1,0:T(8,128)(2,1)}, bf16[160,3840]{1,0:T(8,128)(2,1)}, bf16[160,3840]{1,0:T(8,128)(2,1)}, f32[16,160,256]{2,1,0:T(8,128)}, f32[2...) custom-call(bf16[1024,2560]{1,0:T(8,128)(2,1)} %bitcast.108, bf16[1024,2560]{1,0:T(8,128)(2,1)} %bitcast.103, ...), custom_call_target="tpu_custom_call" | custom-call | tf_op jit(solution)/shard_map/send_grads/pallas_call | solution.py:2106
  722.3 0.0 copy-start.9
  722.4 0.0 copy-start
  722.4 3.3 slice_bitcast_fusion
  725.6 1.7 fusion.6
  727.3 0.0 copy-done.9
  727.3 0.6 fusion.8
  727.9 0.0 copy-start.2
  727.9 0.0 copy-done
  727.9 2.3 fusion
  730.3 0.0 copy-done.1
  730.3 0.2 copy-done.2
  730.5 2.4 fusion.1
  732.9 0.0 copy-done.7
  732.9 1.6 convert_bitcast_fusion
  734.5 0.2 copy-done.6
  734.6 1.6 convert_element_type.27
  736.2 1.6 convert_element_type.28
  737.8 0.1 reshape.171
  737.9 0.6 slice_bitcast_fusion.4
  738.5 0.1 slice.120
  738.6 0.6 copy.87
  739.2 1.1 copy.112
  (25 shorter events, 0.2 us)
Async XLA Ops:
  1.4 20.1 %collective-permute-start.1 = (bf16[2,3]{1,0:T(2,128)(2,1)S(1)}, bf16[2,3]{1,0:T(2,128)(2,1)S(1)}, u32[]{:S(2)}, u32[]{:S(2)}) collective-permute-start(bf16[2,3]{1,0:T(2,128)(2,1)S(1)} %slice.103), channel_id=1, source_target_pairs={{0,2},{2,4},{4,6},{6,8},{8,10},{10,12},{12,14},{14,16},{16,18},{18... | collective-permute-start | bytes 44 | tf_op jit(solution)/shard_map/ppermute | solution.py:44
  4.1 18.4 %collective-permute-start = (bf16[2,8,2560]{2,1,0:T(8,128)(2,1)S(1)}, bf16[2,8,2560]{2,1,0:T(8,128)(2,1)S(1)}, u32[]{:S(2)}, u32[]{:S(2)}) collective-permute-start(bf16[2,8,2560]{2,1,0:T(8,128)(2,1)S(1)} %slice.102), channel_id=1, source_target_pairs={{0,2},{2,4},{4,6},{6,8},{8,10},{10,12},{12,14},{14,16},{16,18},{18... | collective-permute-start | bytes 245768 | tf_op jit(solution)/shard_map/ppermute | solution.py:44
  483.1 2.6 copy-start.8
  483.1 3.5 copy-start.4
  722.3 5.0 copy-start.9
  722.4 5.6 copy-start
  725.6 4.7 copy-start.1
  727.9 2.5 copy-start.2
  730.5 2.4 copy-start.7
  732.9 1.8 copy-start.6
  734.5 1.8 copy-start.5
  736.2 3.0 copy-start.3
